TPU v7x, 32 devices: a whole 2x2x4 slice. The times are simulated.
32 devices in a mesh: member: 8 (over y, x, core), lon: 4 (over z).
Axes of the slice: x: 2, y: 2, z: 4, core: 2. Of those that a mesh axis runs over, the one named last changes fastest.
Arguments:
- atmos: bfloat16 [8, 96, 96, 512], P('member', None, None, 'lon'), may hold values from -6 to 6
- ocean: bfloat16 [96, 96, 512], P(None, None, 'lon'), may hold values from -6 to 6
- land_mask: int32 [96, 512], P(None, 'lon'), may hold values 0 or 1
- ice_mask: int32 [96, 512], P(None, 'lon'), may hold values 0 or 1
- atm_kernel: float32 [2, 7, 7, 96], replicated, may hold values from -0.875 to 0.875
- atm_gain: float32 [2, 96], replicated, may hold values from 0.25 to 1.75
- atm_up: bfloat16 [2, 96, 384], replicated, may hold values from -0.625 to 0.625
- atm_down: bfloat16 [2, 384, 96], replicated, may hold values from -0.3125 to 0.3125
- atm_scale: float32 [2, 96], replicated, may hold values from 0.5 to 1.5
- flux_weight: bfloat16 [96, 32], replicated, may hold values from -0.625 to 0.625
- flux_lift: bfloat16 [2, 32, 96], replicated, may hold values from -1 to 1
- ocn_kernel: float32 [7, 7, 96], replicated, may hold values from -0.875 to 0.875
- ocn_gain: float32 [96], replicated, may hold values from 0.25 to 1.75
- ocn_up: bfloat16 [96, 384], replicated, may hold values from -0.625 to 0.625
- ocn_down: bfloat16 [384, 96], replicated, may hold values from -0.3125 to 0.3125
- ocn_scale: float32 [96], replicated, may hold values from 0.5 to 1.5
- surf_weight: bfloat16 [96, 8], replicated, may hold values from -0.625 to 0.625
- back_weight: bfloat16 [8, 96], replicated, may hold values from -2 to 2
Outputs:
- atmos_out: bfloat16 [8, 96, 96, 512], P('member', None, None, 'lon')
- ocean_new: bfloat16 [96, 96, 512], P('member', None, 'lon')
All inputs are finite; a program needn't handle non-finite values. No bound on the sum of `land_mask` or of `ice_mask` on one device may be relied on, other than what follows from the above.
Results may differ from a plain program's by a relative error of at most 0.017.
Values may be sent and summed in bfloat16 or wider, within the bound.
No kernel may reach another device: no remote copies, remote signals or barrier semaphores. Data moves between devices by JAX's collectives and lax.ppermute only.
A program may use at most 64 MiB of HBM per device.

v0:
```python
import jax
import jax.numpy as jnp
from jax import lax
from jax.sharding import PartitionSpec as P


def with_halo(cells, sides, width):
    for axis, dim in sides:
        count = lax.axis_size(axis)
        head = lax.slice_in_dim(cells, 0, width, axis=dim)
        tail = lax.slice_in_dim(cells, cells.shape[dim] - width, cells.shape[dim], axis=dim)
        cells = jnp.concatenate(
            [
                lax.ppermute(tail, axis, [(i, (i + 1) % count) for i in range(count)]),
                cells,
                lax.ppermute(head, axis, [((i + 1) % count, i) for i in range(count)]),
            ],
            axis=dim,
        )
    return cells


def contract(form, left, right):
    return jnp.einsum(form, left.astype(jnp.float32), right.astype(jnp.float32))


def mixer(field, padded, kernel, gain, up_proj, down_proj, scale, keep):
    rows = field.shape[0]
    cols = field.shape[2]
    acc = jnp.zeros(field.shape, jnp.float32)
    for i in range(7):
        for j in range(7):
            acc = (
                acc
                + padded[i : i + rows, :, j : j + cols].astype(jnp.float32) * kernel[i, j][:, None]
            )
    center = acc - jnp.mean(acc, axis=1, keepdims=True)
    spread = jnp.mean(center * center, axis=1, keepdims=True)
    normed = (center * lax.rsqrt(spread + 1e-06) * gain[:, None]).astype(jnp.bfloat16)
    hidden = jax.nn.gelu(contract("lcw,ch->lhw", normed, up_proj)).astype(jnp.bfloat16)
    branch = contract("lhw,hc->lcw", hidden, down_proj)
    result = field.astype(jnp.float32) + scale[:, None] * branch
    if keep is not None:
        result = result * keep[:, None, :]
    return result.astype(jnp.bfloat16)


def atmos_pad(state):
    tall = jnp.pad(state, ((3, 3), (0, 0), (0, 0)))
    return with_halo(tall, (("lon", 2),), 3)


def forced(ocean_part, flux_sum, count, sea, ice, flux_lift):
    flux_low = (flux_sum / count).astype(jnp.bfloat16)
    open_term = contract("lfw,fc->lcw", flux_low, flux_lift[0])
    ice_term = contract("lfw,fc->lcw", flux_low, flux_lift[1])
    forcing = sea[:, None, :] * ((1.0 - ice)[:, None, :] * open_term + ice[:, None, :] * ice_term)
    return (ocean_part.astype(jnp.float32) + forcing).astype(jnp.bfloat16)


def local(
    atmos,
    ocean,
    land_mask,
    ice_mask,
    atm_kernel,
    atm_gain,
    atm_up,
    atm_down,
    atm_scale,
    flux_weight,
    flux_lift,
    ocn_kernel,
    ocn_gain,
    ocn_up,
    ocn_down,
    ocn_scale,
    surf_weight,
    back_weight,
):
    sea = (1 - land_mask).astype(jnp.float32)
    ice = ice_mask.astype(jnp.float32)
    state = atmos[0]
    for layer in range(2):
        state = mixer(
            state,
            atmos_pad(state),
            atm_kernel[layer],
            atm_gain[layer],
            atm_up[layer],
            atm_down[layer],
            atm_scale[layer],
            None,
        )
    flux = jax.nn.gelu(contract("lcw,cf->lfw", state, flux_weight))
    members = lax.axis_size("member")
    rank = lax.axis_index("member")
    rows = state.shape[0] // members
    flux_sum = lax.psum(flux.astype(jnp.bfloat16), "member").astype(jnp.float32)
    ocean_mid = forced(ocean, flux_sum, members, sea, ice, flux_lift)
    tall = jnp.pad(ocean_mid, ((3, 3), (0, 0), (0, 0)))
    padded = with_halo(tall, (("lon", 2),), 3)
    ocean_full = mixer(ocean_mid, padded, ocn_kernel, ocn_gain, ocn_up, ocn_down, ocn_scale, sea)
    surface = contract("lcw,cs->lsw", ocean_full, surf_weight).astype(jnp.bfloat16)
    ocean_rows = lax.dynamic_slice_in_dim(ocean_full, rank * rows, rows, 0)
    coupling = sea[:, None, :] * contract("lsw,sc->lcw", surface, back_weight)
    atmos_out = (state.astype(jnp.float32) + coupling).astype(jnp.bfloat16)[None]
    return (atmos_out, ocean_rows)


def solution(mesh):
    in_specs = (
        P("member", None, None, "lon"),
        P(None, None, "lon"),
        P(None, "lon"),
        P(None, "lon"),
        P(),
        P(),
        P(),
        P(),
        P(),
        P(),
        P(),
        P(),
        P(),
        P(),
        P(),
        P(),
        P(),
        P(),
    )
    out_specs = (P("member", None, None, "lon"), P("member", None, "lon"))
    return jax.shard_map(local, mesh=mesh, in_specs=in_specs, out_specs=out_specs, check_vma=False)
```

profile of v0, /device:TPU:0, one launch (start us, length us, event | category | flops | bytes accessed | tf_op | source)
XLA Modules:
  0.0 445.3 jit_solution(18338120241749519731)
XLA Ops:
  7.2 0.0 copy-start
  7.2 0.0 all-reduce.5.cloned.1.call-start
  7.3 4.7 %pad_slice_fusion.245 = (bf16[102,96,3]{2,1,0:T(8,128)(2,1)}, bf16[102,96,3]{2,1,0:T(8,128)(2,1)S(1)}) fusion(bf16[96,96,128]{2,1,0:T(8,128)(2,1)} %bitcast.394), kind=kLoop, calls=%fused_computation.715 | loop fusion | bytes 2476800 | tf_op jit(solution)/shard_map/slice | solution.py:11
  12.0 3.3 copy.28
  15.3 3.1 collective-permute-start
  18.4 2.2 copy.31
  20.6 2.3 collective-permute-start.1
  23.1 1.8 pad.10
  25.0 0.0 collective-permute-done
  25.0 3.0 copy.29
  28.0 0.0 collective-permute-done.1
  28.0 3.0 copy.32
  31.0 83.8 %fusion.313 = (f32[96,128]{1,0:T(8,128)S(1)}, f32[96,96,128]{2,1,0:T(8,128)}) fusion(f32[96]{0:T(128)S(1)} %get-tuple-element.115, bf16[102,96,3]{2,1,0:T(8,128)(2,1)} %copy.32, bf16[102,96,128]{2,1,0:T(8,128)(2,1)S(1)} %pad.10, f32[96]{0:T(128)S(1)} %get-tuple-element.116, f32[96]{0:T(128)S(1)} %get-tuple-element.117, f32[96]{0:T(128)S(1)} %get-tuple-element.118, ...), kind=kLoop, calls=%fused_computation.718 | loop fusion | flops 322031616 | bytes 23932160 | tf_op jit(solution)/shard_map/reduce_sum | solution.py:37
  114.8 0.0 copy-start.3
  114.8 0.0 copy-start.16
  114.8 0.0 copy-start.18
  114.9 3.6 multiply_reduce_fusion.2
  118.4 0.0 copy-done.3
  118.4 0.0 copy-done.16
  118.5 10.9 %fusion.61 = bf16[96,96,128]{2,1,0:T(8,128)(2,1)} fusion(f32[96]{0:T(128)S(1)} %get-tuple-element.169, f32[96,96,128]{2,1,0:T(8,128)} %get-tuple-element.7, f32[96]{0:T(128)S(1)} %get-tuple-element.164, f32[96,128]{1,0:T(8,128)S(1)} %add_rsqrt_fusion.2, f32[96,128]{1,0:T(8,128)S(1)} %broadcast_multiply_fusion.2, bf16[2,384,96]{1,2,0:T(8,128)(2,1)S(1)} %copy-done.16, ...), kind=kOutput, calls=%fused_computation.304 | convolution fusion | flops 1863843840 | bytes 9683968 | tf_op jit(solution)/shard_map/lhw,hc->lcw/dot_general | solution.py:24
  129.4 4.6 %pad_slice_fusion.243 = (bf16[102,96,3]{2,1,0:T(8,128)(2,1)}, bf16[102,96,3]{2,1,0:T(8,128)(2,1)S(1)}) fusion(bf16[96,96,128]{2,1,0:T(8,128)(2,1)} %fusion.61), kind=kLoop, calls=%fused_computation.713 | loop fusion | bytes 2476800 | tf_op jit(solution)/shard_map/slice | solution.py:11
  134.0 3.3 copy.34
  137.3 0.1 collective-permute-start.2
  137.4 2.2 copy.37
  139.6 3.8 collective-permute-start.3
  143.5 1.8 pad.11
  145.3 0.0 collective-permute-done.2
  145.3 3.4 copy.35
  148.8 0.0 collective-permute-done.3
  148.8 3.0 copy.38
  151.8 83.9 %fusion.311 = (f32[96,128]{1,0:T(8,128)S(1)}, f32[96,96,128]{2,1,0:T(8,128)}) fusion(f32[96]{0:T(128)S(1)} %get-tuple-element.66, bf16[102,96,3]{2,1,0:T(8,128)(2,1)} %copy.38, bf16[102,96,128]{2,1,0:T(8,128)(2,1)S(1)} %pad.11, f32[96]{0:T(128)S(1)} %get-tuple-element.67, f32[96]{0:T(128)S(1)} %get-tuple-element.68, f32[96]{0:T(128)S(1)} %get-tuple-element.69, ...), kind=kLoop, calls=%fused_computation.717 | loop fusion | flops 322031616 | bytes 23932160 | tf_op jit(solution)/shard_map/reduce_sum | solution.py:37
  235.7 0.0 copy-start.4
  235.7 0.0 copy-start.17
  235.7 0.0 copy-start.19
  235.7 3.6 multiply_reduce_fusion.1
  239.4 0.0 copy-start.21
  239.4 10.8 %fusion.87 = bf16[96,96,128]{2,1,0:T(8,128)(2,1)} fusion(bf16[96,96,128]{2,1,0:T(8,128)(2,1)S(1)} %copy-done.4, f32[96]{0:T(128)S(1)} %get-tuple-element.170, f32[96,96,128]{2,1,0:T(8,128)} %get-tuple-element.5, f32[96]{0:T(128)S(1)} %get-tuple-element.163, f32[96,128]{1,0:T(8,128)S(1)} %add_rsqrt_fusion.1, f32[96,128]{1,0:T(8,128)S(1)} %broadcast_multiply_fusion.1, ...), kind=kOutput, calls=%fused_computation.330 | convolution fusion | flops 1863843840 | bytes 9683968 | tf_op jit(solution)/shard_map/lhw,hc->lcw/dot_general | solution.py:24
  250.2 0.0 copy-start.6
  250.2 3.4 fusion.267
  253.7 0.0 all-reduce.5.cloned.1.call-update
  253.7 54.3 %all-reduce.5.cloned.1.call-done = bf16[96,32,128]{2,1,0:T(8,128)(2,1)} async-done(((bf16[96,32,128]{2,1,0:T(8,128)(2,1)}), bf16[96,32,128]{2,1,0:T(8,128)(2,1)}) %all-reduce.5.cloned.1.call-update) | async-done | bytes 786448 | tf_op jit(solution)/shard_map/psum | solution.py:99
  308.1 2.0 fusion.271
  310.1 1.7 fusion.116
  311.8 1.4 copy-done.1
  313.2 2.3 pad_slice_fusion.241
  315.5 3.3 copy.40
  318.8 1.4 collective-permute-start.4
  320.2 2.2 copy.42
  322.4 2.5 collective-permute-start.5
  325.0 1.8 pad.12
  326.8 0.0 collective-permute-done.4
  326.8 3.3 copy.41
  330.1 0.0 collective-permute-done.5
  330.1 3.0 copy.43
  333.1 83.8 %fusion.309 = (f32[96,128]{1,0:T(8,128)S(1)}, f32[96,96,128]{2,1,0:T(8,128)}) fusion(f32[96]{0:T(128)S(1)} %get-tuple-element.63, bf16[102,96,3]{2,1,0:T(8,128)(2,1)} %copy.43, bf16[102,96,128]{2,1,0:T(8,128)(2,1)S(1)} %pad.12, f32[96]{0:T(128)S(1)} %get-tuple-element.64, f32[96]{0:T(128)S(1)} %get-tuple-element.17, f32[96]{0:T(128)S(1)} %get-tuple-element.18, ...), kind=kLoop, calls=%fused_computation.716 | loop fusion | flops 322031616 | bytes 23932160 | tf_op jit(solution)/shard_map/reduce_sum | solution.py:37
  416.9 0.0 copy-start.20
  416.9 0.0 copy-start.22
  416.9 0.0 copy-start.23
  416.9 3.6 multiply_reduce_fusion
  420.5 0.0 copy-start.12
  420.6 0.0 copy-start.13
  420.6 11.1 %fusion.114 = bf16[96,96,128]{2,1,0:T(8,128)(2,1)} fusion(bf16[96,96,128]{2,1,0:T(8,128)(2,1)S(1)} %copy-done.2, f32[96,128]{1,0:T(8,128)S(1)} %subtract_convert_fusion, f32[96]{0:T(128)S(1)} %copy-done.22, f32[96,96,128]{2,1,0:T(8,128)} %get-tuple-element.3, f32[96]{0:T(128)S(1)} %copy-done.23, f32[96,128]{1,0:T(8,128)S(1)} %add_rsqrt_fusion, ...), kind=kOutput, calls=%fused_computation.357 | convolution fusion | flops 1865023488 | bytes 9732864 | tf_op jit(solution)/shard_map/lhw,hc->lcw/dot_general | solution.py:24
  431.6 1.7 constant_dynamic-slice_fusion
  433.3 4.8 %fusion.117 = bf16[1,96,96,128]{3,2,1,0:T(8,128)(2,1)} fusion(bf16[96,96,128]{2,1,0:T(8,128)(2,1)} %fusion.87, f32[96,128]{1,0:T(8,128)S(1)} %subtract_convert_fusion, bf16[96,96,128]{2,1,0:T(8,128)(2,1)} %fusion.114, bf16[8,96]{1,0:T(8,128)(2,1)S(1)} %copy-done.12, bf16[96,8]{0,1:T(8,128)(2,1)S(1)} %copy-done.13), kind=kOutput, calls=%fused_computation.369 | convolution fusion | flops 42565632 | bytes 7130112 | tf_op jit(solution)/shard_map/lsw,sc->lcw/dot_general | solution.py:24
  (52 shorter events, 0.3 us)
Async XLA Ops:
  7.2 413.3 %copy-start = (bf16[384,96]{0,1:T(8,128)(2,1)S(1)}, bf16[384,96]{0,1:T(8,128)(2,1)}, u32[]{:S(2)}) copy-start(bf16[384,96]{0,1:T(8,128)(2,1)} %param.32) | copy-start | bytes 221188
  7.2 300.9 %all-reduce.5.cloned.1.call-start = ((), (), s32[]{:S(2)}) async-start(), calls=%async_computation | async-start | bytes 1572864 | tf_op jit(solution)/shard_map/psum | solution.py:99
  7.2 15.6 %copy-start.8 = (f32[2,7,7,96]{3,0,2,1:T(2,128)S(1)}, f32[2,7,7,96]{3,0,2,1:T(2,128)}, u32[]{:S(2)}) copy-start(f32[2,7,7,96]{3,0,2,1:T(2,128)} %param.22) | copy-start | bytes 112900
  7.2 15.8 %copy-start.7 = (s32[96,128]{1,0:T(8,128)S(1)}, s32[96,128]{1,0:T(8,128)}, u32[]{:S(2)}) copy-start(s32[96,128]{1,0:T(8,128)} %param.21) | copy-start | bytes 147460
  7.2 15.8 %copy-start.10 = (f32[7,7,96]{2,1,0:T(8,128)S(1)}, f32[7,7,96]{2,1,0:T(8,128)}, u32[]{:S(2)}) copy-start(f32[7,7,96]{2,1,0:T(8,128)} %param.29) | copy-start | bytes 56452
  7.3 15.8 %copy-start.14 = (f32[2,96]{1,0:T(2,128)S(1)}, f32[2,96]{1,0:T(2,128)}, u32[]{:S(2)}) copy-start(f32[2,96]{1,0:T(2,128)} %param.23) | copy-start | bytes 2308
  7.3 15.8 %copy-start.15 = (f32[2,96]{1,0:T(2,128)S(1)}, f32[2,96]{1,0:T(2,128)}, u32[]{:S(2)}) copy-start(f32[2,96]{1,0:T(2,128)} %param.26) | copy-start | bytes 2308
  15.3 9.7 %collective-permute-start = (bf16[102,96,3]{0,1,2:T(8,128)(2,1)S(1)}, bf16[102,96,3]{0,1,2:T(8,128)(2,1)S(1)}, u32[]{:S(2)}, u32[]{:S(2)}) collective-permute-start(bf16[102,96,3]{0,1,2:T(8,128)(2,1)S(1)} %copy.28), channel_id=1, source_target_pairs={{0,1},{1,2},{2,3},{3,0},{4,5},{5,6},{6,7},{7,4},{8,9},{9,10},{10,1... | collective-permute-start | bytes 176264 | tf_op jit(solution)/shard_map/ppermute | solution.py:14
  20.6 7.4 %collective-permute-start.1 = (bf16[102,96,3]{0,1,2:T(8,128)(2,1)S(1)}, bf16[102,96,3]{0,1,2:T(8,128)(2,1)S(1)}, u32[]{:S(2)}, u32[]{:S(2)}) collective-permute-start(bf16[102,96,3]{0,1,2:T(8,128)(2,1)S(1)} %copy.31), channel_id=1, source_target_pairs={{1,0},{2,1},{3,2},{0,3},{5,4},{6,5},{7,6},{4,7},{9,8},{10,9},{11,1... | collective-permute-start | bytes 176264 | tf_op jit(solution)/shard_map/ppermute | solution.py:16
  114.8 3.6 copy-start.3
  114.8 3.6 copy-start.16
  114.8 3.6 copy-start.18
  137.3 8.0 %collective-permute-start.2 = (bf16[102,96,3]{0,1,2:T(8,128)(2,1)S(1)}, bf16[102,96,3]{0,1,2:T(8,128)(2,1)S(1)}, u32[]{:S(2)}, u32[]{:S(2)}) collective-permute-start(bf16[102,96,3]{0,1,2:T(8,128)(2,1)S(1)} %copy.34), channel_id=1, source_target_pairs={{0,1},{1,2},{2,3},{3,0},{4,5},{5,6},{6,7},{7,4},{8,9},{9,10},{10,1... | collective-permute-start | bytes 176264 | tf_op jit(solution)/shard_map/ppermute | solution.py:14
  139.6 9.2 %collective-permute-start.3 = (bf16[102,96,3]{0,1,2:T(8,128)(2,1)S(1)}, bf16[102,96,3]{0,1,2:T(8,128)(2,1)S(1)}, u32[]{:S(2)}, u32[]{:S(2)}) collective-permute-start(bf16[102,96,3]{0,1,2:T(8,128)(2,1)S(1)} %copy.37), channel_id=1, source_target_pairs={{1,0},{2,1},{3,2},{0,3},{5,4},{6,5},{7,6},{4,7},{9,8},{10,9},{11,1... | collective-permute-start | bytes 176264 | tf_op jit(solution)/shard_map/ppermute | solution.py:16
  235.7 3.6 copy-start.4
  235.7 3.6 copy-start.17
  235.7 3.6 copy-start.19
  239.4 10.9 %copy-start.21 = (bf16[96,32]{0,1:T(8,128)(2,1)S(1)}, bf16[96,32]{0,1:T(8,128)(2,1)}, u32[]{:S(2)}) copy-start(bf16[96,32]{0,1:T(8,128)(2,1)} %param.27) | copy-start | bytes 18436
  250.2 3.5 copy-start.9
  250.2 57.8 %copy-start.11 = (bf16[2,32,96]{2,1,0:T(8,128)(2,1)S(1)}, bf16[2,32,96]{2,1,0:T(8,128)(2,1)}, u32[]{:S(2)}) copy-start(bf16[2,32,96]{2,1,0:T(8,128)(2,1)} %param.28) | copy-start | bytes 36868
  250.2 59.8 %copy-start.6 = (bf16[96,96,128]{2,1,0:T(8,128)(2,1)S(1)}, bf16[96,96,128]{2,1,0:T(8,128)(2,1)}, u32[]{:S(2)}) copy-start(bf16[96,96,128]{2,1,0:T(8,128)(2,1)} %param.19) | copy-start | bytes 7077892
  308.1 2.0 copy-start.5
  311.8 1.4 copy-start.1
  318.8 8.0 %collective-permute-start.4 = (bf16[102,96,3]{0,1,2:T(8,128)(2,1)S(1)}, bf16[102,96,3]{0,1,2:T(8,128)(2,1)S(1)}, u32[]{:S(2)}, u32[]{:S(2)}) collective-permute-start(bf16[102,96,3]{0,1,2:T(8,128)(2,1)S(1)} %copy.40), channel_id=1, source_target_pairs={{0,1},{1,2},{2,3},{3,0},{4,5},{5,6},{6,7},{7,4},{8,9},{9,10},{10,1... | collective-permute-start | bytes 176264 | tf_op jit(solution)/shard_map/ppermute | solution.py:14
  322.4 7.7 %collective-permute-start.5 = (bf16[102,96,3]{0,1,2:T(8,128)(2,1)S(1)}, bf16[102,96,3]{0,1,2:T(8,128)(2,1)S(1)}, u32[]{:S(2)}, u32[]{:S(2)}) collective-permute-start(bf16[102,96,3]{0,1,2:T(8,128)(2,1)S(1)} %copy.42), channel_id=1, source_target_pairs={{1,0},{2,1},{3,2},{0,3},{5,4},{6,5},{7,6},{4,7},{9,8},{10,9},{11,1... | collective-permute-start | bytes 176264 | tf_op jit(solution)/shard_map/ppermute | solution.py:16
  416.9 3.7 copy-start.2
  416.9 3.7 copy-start.20
  416.9 3.7 copy-start.22
  416.9 3.7 copy-start.23
  420.5 12.8 %copy-start.12 = (bf16[8,96]{1,0:T(8,128)(2,1)S(1)}, bf16[8,96]{1,0:T(8,128)(2,1)}, u32[]{:S(2)}) copy-start(bf16[8,96]{1,0:T(8,128)(2,1)} %param.35) | copy-start | bytes 4612
  420.6 12.8 %copy-start.13 = (bf16[96,8]{0,1:T(8,128)(2,1)S(1)}, bf16[96,8]{0,1:T(8,128)(2,1)}, u32[]{:S(2)}) copy-start(bf16[96,8]{0,1:T(8,128)(2,1)} %param.34) | copy-start | bytes 4612
Sparse Core Ops, SparseCore 0:
  253.8 54.1 all-reduce.4
where the time goes:
time: 449 us; the launch traced here: 445 us
  other arithmetic  262 us (58%)
  local copies, waits for them, and re-layouts  55.9 us (12%)
  waiting for transfers between devices  54.3 us (12%)
  matrix products  44.8 us (10%)
  between operations  14.9 us (3%)
  starting transfers between devices  13.2 us (3%)
    reduce_sum x3, other arithmetic, mixer(): center = acc - jnp.mean(acc, axis=1, keepdims=True)  251 us
    psum x1, waiting for transfers between devices, local(): flux_sum = lax.psum(flux.astype(jnp.bfloat16), 'member').astype(jnp.float32)  54.3 us
    dot_general x7, matrix products, contract(): return jnp.einsum(form, left.astype(jnp.float32), right.astype(jnp.float32))  44.8 us
    slice x6, local copies, waits for them, and re-layouts, with_halo(): lax.slice_in_dim(cells, cells.shape[dim] - width, cells.shape[dim], axis=...  21.6 us
    reduce_sum x3, other arithmetic, mixer(): spread = jnp.mean(center * center, axis=1, keepdims=True)  10.7 us
    ppermute x3, local copies, waits for them, and re-layouts, with_halo(): lax.ppermute(tail, axis, [(i, (i + 1) % count) for i in range(count)])  9.74 us
    ppermute x3, local copies, waits for them, and re-layouts, with_halo(): lax.ppermute(head, axis, [((i + 1) % count, i) for i in range(count)])  9.02 us
  transfers between devices with their start and end apart: 7, of which 1 were waited for; matrix products, arithmetic and copies ran while one was open for 5% of the time, Pallas kernels for 0%

commit v1 on v0

v1 whole, which is shorter than its diff:
```python
import functools

import jax
import jax.numpy as jnp
from jax import lax
from jax.experimental import pallas as pl
from jax.experimental.pallas import tpu as pltpu
from jax.sharding import PartitionSpec as P

BF = jnp.bfloat16
F32 = jnp.float32
TANH_A = 0.7978845608028654
TANH_B = TANH_A * 0.044715
TAPS = 7
HALO = 3
GROUP = 16
SPAN = 16
OUT = SPAN - TAPS + 1
DEPTH = GROUP * SPAN
SLOT = 8
PACK = 16
BY_DOT = (0, 1, 5, 6)
VMEM = pl.BlockSpec(memory_space=pltpu.VMEM)
ANY = pl.BlockSpec(memory_space=pl.ANY)


def params(mib):
    return pltpu.CompilerParams(vmem_limit_bytes=mib * 2**20)


def twice_gelu(z):
    return z + z * jnp.tanh(z * (TANH_A + TANH_B * (z * z)))


def spread(row, lanes):
    return jnp.broadcast_to(row.T, (row.shape[1], lanes))


def shift_matrix(lanes):
    shape = (2 * lanes, len(BY_DOT) * lanes)
    src = lax.broadcasted_iota(jnp.int32, shape, 0)
    dst = lax.broadcasted_iota(jnp.int32, shape, 1)
    hit = jnp.zeros(shape, jnp.bool_)
    for a, j in enumerate(BY_DOT):
        want = dst - a * lanes + (j - HALO)
        want = jnp.where(want < 0, want + 2 * lanes, want)
        hit = hit | ((dst >= a * lanes) & (dst < (a + 1) * lanes) & (src == want))
    return hit.astype(BF)


def make_shifts(rows, edges, xj, at, smat):
    count, chans, lanes = rows.shape
    lane = lax.broadcasted_iota(jnp.int32, (chans, lanes), 1)
    halo = [edges if t == 0 else pltpu.roll(edges, lanes - SLOT * t, 1) for t in range(count)]
    both = jnp.concatenate(
        [rows.reshape(count * chans, lanes), jnp.concatenate(halo, axis=0)], axis=1
    )
    moved = jnp.dot(both, smat, preferred_element_type=F32)
    for a, j in enumerate(BY_DOT):
        part = moved[:, a * lanes : (a + 1) * lanes].astype(BF)
        xj[j, pl.ds(at, count)] = part.reshape(count, chans, lanes)
    for t in range(count):
        for j in range(TAPS):
            d = j - HALO
            if j in BY_DOT:
                continue
            if d == 0:
                xj[j, at + t] = rows[t]
            else:
                mask = (lane < d) if d > 0 else (lane >= lanes + d)
                xj[j, at + t] = pltpu.roll(jnp.where(mask, halo[t], rows[t]), (-d) % lanes, 1)


def pick_edges(from_left, from_right):
    lane = lax.broadcasted_iota(jnp.int32, from_left.shape, 1)
    return jnp.where(lane % SLOT < SLOT // 2, from_right, from_left)


def pack_edges(rows):
    chans, lanes = rows[0].shape
    lane = lax.broadcasted_iota(jnp.int32, (chans, lanes), 1)
    place = (lane + HALO) // SLOT % PACK
    out = rows[0]
    for t in range(1, PACK):
        if t < len(rows):
            out = jnp.where(place == t, pltpu.roll(rows[t], SLOT * t, 1), out)
    return out


def build_band(taps, band):
    chans = band.shape[0] * GROUP
    wide = TAPS * DEPTH
    t = lax.broadcasted_iota(jnp.int32, (TAPS, wide), 0)
    n = lax.broadcasted_iota(jnp.int32, (TAPS, wide), 1)
    base = jnp.zeros((chans, wide), F32)
    for i in range(TAPS):
        put = ((t == n // DEPTH) & ((n % DEPTH) // GROUP == i)).astype(BF)
        base = base + jnp.dot(taps(i).T.astype(BF), put, preferred_element_type=F32)
    r = lax.broadcasted_iota(jnp.int32, (chans, wide), 0)
    c = lax.broadcasted_iota(jnp.int32, (chans, wide), 1)
    base = jnp.where(r % GROUP == c % GROUP, base, 0.0)
    for j in range(TAPS):
        one = base[:, j * DEPTH : (j + 1) * DEPTH]
        for r in range(OUT):
            moved = (pltpu.roll(one, GROUP * r, 1) if r else one).astype(BF)
            for g in range(band.shape[0]):
                band[g, GROUP * r : GROUP * (r + 1), j * DEPTH : (j + 1) * DEPTH] = moved[
                    GROUP * g : GROUP * (g + 1)
                ]


def convolve(xj, band, acc):
    rows, chans, lanes = acc.shape
    starts = [min(OUT * i, max(rows - OUT, 0)) for i in range(-(-rows // OUT))]

    def group(g, carry):
        at = pl.ds(pl.multiple_of(GROUP * g, GROUP), GROUP)
        field = jnp.concatenate(
            [
                jnp.concatenate(
                    [xj[j, s : s + SPAN, at, :].reshape(DEPTH, lanes) for j in range(TAPS)], axis=0
                )
                for s in starts
            ],
            axis=1,
        )
        out = jnp.dot(band[g], field, preferred_element_type=F32)
        for n, s in enumerate(starts):
            take = min(OUT, rows)
            part = out[: take * GROUP, n * lanes : (n + 1) * lanes]
            acc[s : s + take, at, :] = part.reshape(take, GROUP, lanes)
        return carry

    lax.fori_loop(0, chans // GROUP, group, 0)


def pointwise(acc, at, count, gain, up_t, down_t):
    normed = []
    for r in range(count):
        a = acc[at + r]
        center = a - jnp.mean(a, axis=0, keepdims=True)
        spread_ = jnp.mean(center * center, axis=0, keepdims=True)
        normed.append((center * lax.rsqrt(spread_ + 1e-06) * gain).astype(BF))
    n = jnp.concatenate(normed, axis=1)
    z = jnp.dot(up_t, n, preferred_element_type=F32)
    h = twice_gelu(z.astype(BF))
    return jnp.dot(down_t, h, preferred_element_type=F32)


def transposed(ref_value, factor):
    return (ref_value.astype(F32).T * factor).astype(BF)


def pack_kernel(x_ref, p_ref):
    p_ref[0] = pack_edges([x_ref[t] for t in range(PACK)])


def pack(x):
    rows, chans, lanes = x.shape
    return pl.pallas_call(
        pack_kernel,
        grid=(rows // PACK,),
        out_shape=jax.ShapeDtypeStruct((rows // PACK, chans, lanes), BF),
        in_specs=[pl.BlockSpec((PACK, chans, lanes), lambda i: (i, 0, 0))],
        out_specs=pl.BlockSpec((1, chans, lanes), lambda i: (i, 0, 0)),
        name="pack_edges",
    )(x)


def layer_kernel(layer, members, *refs):
    x_ref, left_ref, right_ref, k_ref, g_ref, up_ref, dn_ref, s_ref = refs[:8]
    if layer == 0:
        y_ref, p_ref, xj, acc, band, up_t, dn_t = refs[8:]
    else:
        fw_ref, y_ref = refs[8:10]
        flux_refs = refs[10 : 10 + members]
        xj, acc, band, up_t, dn_t, flux = refs[10 + members :]
    rows, chans, lanes = x_ref.shape
    blank = jnp.zeros((HALO, chans, lanes), BF)
    for j in range(TAPS):
        xj[j, 0:HALO] = blank
        xj[j, rows + HALO : rows + 2 * HALO] = blank
    smat = shift_matrix(lanes)

    def prep(q, carry):
        at = q * PACK
        edges = pick_edges(left_ref[q], right_ref[q])
        make_shifts(x_ref[pl.ds(at, PACK)], edges, xj, at + HALO, smat)
        return carry

    lax.fori_loop(0, rows // PACK, prep, 0)
    build_band(lambda i: k_ref[layer, i], band)
    up_t[...] = transposed(up_ref[layer], 1.0)
    dn_t[...] = transposed(dn_ref[layer], 0.5)
    gain = spread(g_ref[layer : layer + 1], lanes)
    scale = spread(s_ref[layer : layer + 1], lanes)
    convolve(xj, band, acc)
    if layer == 1:
        fw_t = transposed(fw_ref[...], 1.0)
        flux[0:HALO] = jnp.zeros((HALO,) + flux.shape[1:], BF)
        flux[rows + HALO : rows + 2 * HALO] = jnp.zeros((HALO,) + flux.shape[1:], BF)

    def mlp(q, carry):
        at = q * PACK
        branch = pointwise(acc, at, PACK, gain, up_t[...], dn_t[...])
        made = []
        for t in range(PACK):
            y = x_ref[at + t].astype(F32) + scale * branch[:, t * lanes : (t + 1) * lanes]
            made.append(y.astype(BF))
            y_ref[at + t] = made[t]
        if layer == 0:
            p_ref[q] = pack_edges(made)
        else:
            z = jnp.dot(fw_t, jnp.concatenate(made, axis=1), preferred_element_type=F32)
            f = (0.5 * twice_gelu(z)).astype(BF)
            for t in range(PACK):
                flux[at + HALO + t] = f[:, t * lanes : (t + 1) * lanes]
        return carry

    lax.fori_loop(0, rows // PACK, mlp, 0)
    if layer == 1:
        share = rows // members
        rank = lax.axis_index("member")
        for s in range(members):
            dst = lax.rem(rank + s, members)
            flux_refs[s][...] = flux[pl.ds(dst * share, share + 2 * HALO)]


def run_layer(layer, members, x, left, right, kernel, gain, up, down, scale, flux_weight=None):
    rows, chans, lanes = x.shape
    hid = up.shape[2]
    out = [jax.ShapeDtypeStruct(x.shape, BF)]
    args = [x, left, right, kernel, gain, up, down, scale]
    scratch = [
        pltpu.VMEM((TAPS, rows + 2 * HALO, chans, lanes), BF),
        pltpu.VMEM((rows, chans, lanes), F32),
        pltpu.VMEM((chans // GROUP, GROUP * OUT, TAPS * DEPTH), BF),
        pltpu.VMEM((hid, chans), BF),
        pltpu.VMEM((chans, hid), BF),
    ]
    if layer == 0:
        out.append(jax.ShapeDtypeStruct(left.shape, BF))
    else:
        args.append(flux_weight)
        flux = flux_weight.shape[1]
        share = rows // members
        out += [jax.ShapeDtypeStruct((share + 2 * HALO, flux, lanes), BF)] * members
        scratch.append(pltpu.VMEM((rows + 2 * HALO, flux, lanes), BF))
    return pl.pallas_call(
        functools.partial(layer_kernel, layer, members),
        out_shape=out,
        in_specs=[VMEM] * len(args),
        out_specs=[VMEM] * len(out),
        scratch_shapes=scratch,
        compiler_params=params(56),
        name="atmos_block",
    )(*args)


def force_kernel(members, *refs):
    flux_refs = refs[:members]
    ocean_ref, land_ref, ice_ref, lift_ref, mid_ref, p_ref, win, sem = refs[members:]
    span, flux, lanes = flux_refs[0].shape
    rows = land_ref.shape[0]
    chans = mid_ref.shape[1]
    share = rows // members
    first = lax.axis_index("member") * share - HALO
    start = jnp.clip(first, 0, rows - span)
    copy = pltpu.make_async_copy(ocean_ref.at[pl.ds(start, span)], win, sem)
    copy.start()
    total = flux_refs[0][...].astype(F32)
    for ref in flux_refs[1:]:
        total = total + ref[...].astype(F32)
    low = (total / members).astype(BF)
    lift = jnp.concatenate([transposed(lift_ref[0], 1.0), transposed(lift_ref[1], 1.0)], axis=0)
    terms = jnp.dot(
        lift, jnp.concatenate([low[r] for r in range(span)], axis=1), preferred_element_type=F32
    )
    copy.wait()
    for r in range(span, mid_ref.shape[0]):
        mid_ref[r] = jnp.zeros((chans, lanes), BF)
    for r in range(span):
        row = first + r
        safe = jnp.clip(row, 0, rows - 1)
        sea = (1 - land_ref[pl.ds(safe, 1), :]).astype(F32)
        ice = ice_ref[pl.ds(safe, 1), :].astype(F32)
        at = slice(r * lanes, (r + 1) * lanes)
        forcing = sea * ((1.0 - ice) * terms[:chans, at] + ice * terms[chans:, at])
        mid = win[jnp.clip(row - start, 0, span - 1)].astype(F32) + forcing
        inside = (row >= 0) & (row < rows)
        mid_ref[r] = jnp.where(inside, mid, 0.0).astype(BF)
    for q in range(mid_ref.shape[0] // PACK):
        p_ref[q] = pack_edges([mid_ref[q * PACK + t] for t in range(PACK)])


def run_force(members, chunks, ocean, land, ice, lift):
    span, _, lanes = chunks[0].shape
    chans = ocean.shape[1]
    tall = max(-(-span // PACK) * PACK, 2 * PACK)
    return pl.pallas_call(
        functools.partial(force_kernel, members),
        out_shape=[
            jax.ShapeDtypeStruct((tall, chans, lanes), BF),
            jax.ShapeDtypeStruct((tall // PACK, chans, lanes), BF),
        ],
        in_specs=[VMEM] * members + [ANY, VMEM, VMEM, VMEM],
        out_specs=[VMEM] * 2,
        scratch_shapes=[pltpu.VMEM((span, chans, lanes), BF), pltpu.SemaphoreType.DMA(())],
        compiler_params=params(40),
        name="ocean_forcing",
    )(*chunks, ocean, land, ice, lift)


def ocean_kernel(members, mid_ref, left_ref, right_ref, land_ref, k_ref, g_ref, up_ref, dn_ref, s_ref, sw_ref, new_ref, surf_ref, xj, acc, band):
    tall, chans, lanes = mid_ref.shape
    share = new_ref.shape[0]
    smat = shift_matrix(lanes)

    def prep(q, carry):
        at = q * PACK
        edges = pick_edges(left_ref[q], right_ref[q])
        make_shifts(mid_ref[pl.ds(at, PACK)], edges, xj, at, smat)
        return carry

    lax.fori_loop(0, tall // PACK, prep, 0)
    build_band(lambda i: k_ref[i], band)
    gain = spread(g_ref[...], lanes)
    scale = spread(s_ref[...], lanes)
    convolve(xj, band, acc)
    branch = pointwise(
        acc, 0, share, gain, transposed(up_ref[...], 1.0), transposed(dn_ref[...], 0.5)
    )
    first = lax.axis_index("member") * share
    made = []
    for r in range(share):
        sea = (1 - land_ref[pl.ds(first + r, 1), :]).astype(F32)
        y = mid_ref[HALO + r].astype(F32) + scale * branch[:, r * lanes : (r + 1) * lanes]
        made.append((y * sea).astype(BF))
        new_ref[r] = made[r]
    surf = jnp.dot(
        transposed(sw_ref[...], 1.0), jnp.concatenate(made, axis=1), preferred_element_type=F32
    )
    for r in range(share):
        surf_ref[r] = surf[:, r * lanes : (r + 1) * lanes].astype(BF)


def run_ocean(members, mid, left, right, land, kernel, gain, up, down, scale, surf_weight):
    tall, chans, lanes = mid.shape
    share = land.shape[0] // members
    return pl.pallas_call(
        functools.partial(ocean_kernel, members),
        out_shape=[
            jax.ShapeDtypeStruct((share, chans, lanes), BF),
            jax.ShapeDtypeStruct((share, surf_weight.shape[1], lanes), BF),
        ],
        in_specs=[VMEM] * 10,
        out_specs=[VMEM] * 2,
        scratch_shapes=[
            pltpu.VMEM((TAPS, tall, chans, lanes), BF),
            pltpu.VMEM((share, chans, lanes), F32),
            pltpu.VMEM((chans // GROUP, GROUP * OUT, TAPS * DEPTH), BF),
        ],
        compiler_params=params(40),
        name="ocean_block",
    )(mid, left, right, land, kernel, gain[None], up, down, scale[None], surf_weight)


def couple_kernel(y_ref, surf_ref, land_ref, bw_ref, o_ref):
    share, chans, lanes = y_ref.shape
    surf = jnp.concatenate([surf_ref[0, r] for r in range(share)], axis=1)
    back = jnp.dot(transposed(bw_ref[...], 1.0), surf, preferred_element_type=F32)
    first = pl.program_id(0) * share
    for r in range(share):
        sea = (1 - land_ref[pl.ds(first + r, 1), :]).astype(F32)
        out = y_ref[r].astype(F32) + sea * back[:, r * lanes : (r + 1) * lanes]
        o_ref[r] = out.astype(BF)


def couple(y, surface, land, back_weight):
    members, share, surf, lanes = surface.shape
    chans = y.shape[1]
    rows = pl.BlockSpec((share, chans, lanes), lambda i: (i, 0, 0))
    return pl.pallas_call(
        couple_kernel,
        grid=(members,),
        out_shape=jax.ShapeDtypeStruct(y.shape, BF),
        in_specs=[
            rows,
            pl.BlockSpec((1, share, surf, lanes), lambda i: (i, 0, 0, 0)),
            VMEM,
            VMEM,
        ],
        out_specs=rows,
        compiler_params=params(32),
        name="couple",
    )(y, surface, land, back_weight)


def neighbours(packed):
    count = lax.axis_size("lon")
    left = lax.ppermute(packed, "lon", [(i, (i + 1) % count) for i in range(count)])
    right = lax.ppermute(packed, "lon", [((i + 1) % count, i) for i in range(count)])
    return left, right


def local(
    atmos,
    ocean,
    land_mask,
    ice_mask,
    atm_kernel,
    atm_gain,
    atm_up,
    atm_down,
    atm_scale,
    flux_weight,
    flux_lift,
    ocn_kernel,
    ocn_gain,
    ocn_up,
    ocn_down,
    ocn_scale,
    surf_weight,
    back_weight,
):
    members = lax.axis_size("member")
    state = atmos[0]
    atm = (atm_kernel, atm_gain, atm_up, atm_down, atm_scale)
    left, right = neighbours(pack(state))
    state, packed = run_layer(0, members, state, left, right, *atm)
    left, right = neighbours(packed)
    state, *chunks = run_layer(1, members, state, left, right, *atm, flux_weight)
    for s in range(1, members):
        chunks[s] = lax.ppermute(
            chunks[s], "member", [(i, (i + s) % members) for i in range(members)]
        )
    mid, packed = run_force(members, chunks, ocean, land_mask, ice_mask, flux_lift)
    left, right = neighbours(packed)
    ocean_rows, surface = run_ocean(
        members, mid, left, right, land_mask, ocn_kernel, ocn_gain, ocn_up, ocn_down, ocn_scale, surf_weight
    )
    surface = lax.all_gather(surface, "member")
    out = couple(state, surface, land_mask, back_weight)
    return (out[None], ocean_rows)


def solution(mesh):
    in_specs = (
        P("member", None, None, "lon"),
        P(None, None, "lon"),
        P(None, "lon"),
        P(None, "lon"),
    ) + (P(),) * 14
    out_specs = (P("member", None, None, "lon"), P("member", None, "lon"))
    return jax.shard_map(local, mesh=mesh, in_specs=in_specs, out_specs=out_specs, check_vma=False)
```

time: 449 us -> 117 us (0.26)
  other arithmetic: 262 us -> 0 us
  Pallas kernels: 0 us -> 57.6 us
  local copies, waits for them, and re-layouts: 55.9 us -> 6.33 us
  matrix products: 44.8 us -> 0 us
  waiting for transfers between devices: 54.3 us -> 23.6 us
  between operations: 14.9 us -> 0.75 us
  blocking collectives: 0 us -> 9.67 us
  starting transfers between devices: 13.2 us -> 18.3 us
    reduce_sum x6 -> x0, other arithmetic: 262 us -> none  [the longest x3 251 us: mixer(): center = acc - jnp.mean(acc, axis=1, keepdims=True)]
    pallas_call x0 -> x6, Pallas kernels: none -> 57.6 us  [the longest x2 41.4 us: run_layer(): pl.pallas_call(functools.partial(layer_kernel, layer, members), out_shape...]
    psum x1 -> x0, waiting for transfers between devices: 54.3 us -> none  [local(): flux_sum = lax.psum(flux.astype(jnp.bfloat16), 'member').astype(jnp.float32)]
    dot_general x7 -> x0, matrix products: 44.8 us -> none  [contract(): return jnp.einsum(form, left.astype(jnp.float32), right.astype(jnp.float32))]
    slice x10 -> x0, local copies, waits for them, and re-layouts: 28.3 us -> none  [the longest x6 21.6 us: with_halo(): lax.slice_in_dim(cells, cells.shape[dim] - width, cells.shape[dim], axis=...]
    ppermute x6 -> x13, waiting for transfers between devices: 0.02 us -> 23.6 us  [the longest x7 11.1 us: local(): lax.ppermute(chunks[s], 'member', [(i, (i + s) % members) for i in range(...]
    ppermute x6 -> x0, local copies, waits for them, and re-layouts: 18.8 us -> none  [the longest x3 9.74 us: with_halo(): lax.ppermute(tail, axis, [(i, (i + 1) % count) for i in range(count)])]
    all_gather x0 -> x1, blocking collectives: none -> 9.67 us  [local(): surface = lax.all_gather(surface, 'member')]
  transfers between devices with their start and end apart: 7 -> 13, of which waited for: 1 -> 11; matrix products, arithmetic and copies ran while one was open for 5% -> 2% of each run, Pallas kernels for 0% -> 0%
where the time goes in v1:
time: 117 us; the launch traced here: 116 us
  Pallas kernels  57.6 us (49%)
  waiting for transfers between devices  23.6 us (20%)
  starting transfers between devices  18.3 us (16%)
  blocking collectives  9.67 us (8%)
  local copies, waits for them, and re-layouts  6.33 us (5%)
    pallas_call x2, Pallas kernels, run_layer(): pl.pallas_call(functools.partial(layer_kernel, layer, members), out_shape...  41.4 us
    ppermute x7, waiting for transfers between devices, local(): lax.ppermute(chunks[s], 'member', [(i, (i + s) % members) for i in range(...  11.1 us
    all_gather x1, blocking collectives, local(): surface = lax.all_gather(surface, 'member')  9.67 us
    ppermute x3, waiting for transfers between devices, neighbours(): lax.ppermute(packed, 'lon', [(i, (i + 1) % count) for i in range(count)])  9.66 us
    ppermute x3, starting transfers between devices, neighbours(): lax.ppermute(packed, 'lon', [((i + 1) % count, i) for i in range(count)])  8.26 us
    unnamed x45, local copies, waits for them, and re-layouts  6.33 us
    pallas_call x1, Pallas kernels, run_ocean(): pl.pallas_call(functools.partial(ocean_kernel, members), out_shape=[jax.S...  5.91 us
    ppermute x7, starting transfers between devices, local(): lax.ppermute(chunks[s], 'member', [(i, (i + s) % members) for i in range(...  5.54 us
  transfers between devices with their start and end apart: 13, of which 11 were waited for; matrix products, arithmetic and copies ran while one was open for 2% of the time, Pallas kernels for 0%

profile of v1, /device:TPU:0, one launch (start us, length us, event | category | flops | bytes accessed | tf_op | source)
XLA Modules:
  0.0 116.3 jit_solution(10847949188356336340)
XLA Ops:
  0.6 0.0 copy-start.11
  0.6 0.0 copy-start.17
  0.6 4.8 %pack_edges.1 = bf16[6,96,128]{2,1,0:T(8,128)(2,1)} custom-call(bf16[96,96,128]{2,1,0:T(8,128)(2,1)} %bitcast.8), custom_call_target="tpu_custom_call" | custom-call | tf_op jit(solution)/shard_map/pack_edges/pallas_call | solution.py:160
  5.5 0.0 copy-start.18
  5.5 3.0 %collective-permute-start = (bf16[6,96,128]{2,1,0:T(8,128)(2,1)}, bf16[6,96,128]{2,1,0:T(8,128)(2,1)S(1)}, u32[]{:S(2)}, u32[]{:S(2)}) collective-permute-start(bf16[6,96,128]{2,1,0:T(8,128)(2,1)} %pack_edges.1), channel_id=1, source_target_pairs={{0,1},{1,2},{2,3},{3,0},{4,5},{5,6},{6,7},{7,4},{8,9},{9,10},{10,1... | collective-permute-start | bytes 442376 | tf_op jit(solution)/shard_map/ppermute | solution.py:401
  8.5 2.0 %collective-permute-start.1 = (bf16[6,96,128]{2,1,0:T(8,128)(2,1)}, bf16[6,96,128]{2,1,0:T(8,128)(2,1)S(1)}, u32[]{:S(2)}, u32[]{:S(2)}) collective-permute-start(bf16[6,96,128]{2,1,0:T(8,128)(2,1)} %pack_edges.1), channel_id=1, source_target_pairs={{1,0},{2,1},{3,2},{0,3},{5,4},{6,5},{7,6},{4,7},{9,8},{10,9},{11,1... | collective-permute-start | bytes 442376 | tf_op jit(solution)/shard_map/ppermute | solution.py:402
  10.5 0.0 copy-done.11
  10.5 0.8 copy.28.refs_6_
  11.3 0.0 copy-done.17
  11.3 0.6 copy.27.refs_3_
  12.0 0.0 copy-start
  12.0 3.5 %collective-permute-done.refs_1_ = bf16[6,96,128]{2,1,0:T(8,128)(2,1)S(1)} collective-permute-done((bf16[6,96,128]{2,1,0:T(8,128)(2,1)}, bf16[6,96,128]{2,1,0:T(8,128)(2,1)S(1)}, u32[]{:S(2)}, u32[]{:S(2)}) %collective-permute-start) | collective-permute-done | bytes 147488 | tf_op jit(solution)/shard_map/ppermute | solution.py:401
  15.4 1.7 %collective-permute-done.1.refs_2_ = bf16[6,96,128]{2,1,0:T(8,128)(2,1)S(1)} collective-permute-done((bf16[6,96,128]{2,1,0:T(8,128)(2,1)}, bf16[6,96,128]{2,1,0:T(8,128)(2,1)S(1)}, u32[]{:S(2)}, u32[]{:S(2)}) %collective-permute-start.1) | collective-permute-done | bytes 147488 | tf_op jit(solution)/shard_map/ppermute | solution.py:402
  17.2 0.0 copy-done.14
  17.2 0.7 copy-done.15
  17.8 20.3 %atmos_block.2 = (bf16[96,96,128]{2,1,0:T(8,128)(2,1)}, bf16[6,96,128]{2,1,0:T(8,128)(2,1)}) custom-call(bf16[96,96,128]{2,1,0:T(8,128)(2,1)} %bitcast.9, bf16[6,96,128]{2,1,0:T(8,128)(2,1)} %copy-done.14, bf16[6,96,128]{2,1,0:T(8,128)(2,1)} %copy-done.15, f32[2,7,7,96]{3,2,1,0:T(8,128)} %copy.27.refs_3_, f32[2,96]{1,0:T(2,128)} %refs_4_.3, ...), custom_call_target="tpu_custom_call" | custom-call | tf_op jit(solution)/shard_map/atmos_block/pallas_call | solution.py:249
  38.1 1.1 collective-permute-start.2
  39.2 2.7 %collective-permute-start.3 = (bf16[6,96,128]{2,1,0:T(8,128)(2,1)}, bf16[6,96,128]{2,1,0:T(8,128)(2,1)S(1)}, u32[]{:S(2)}, u32[]{:S(2)}) collective-permute-start(bf16[6,96,128]{2,1,0:T(8,128)(2,1)} %get-tuple-element.18), channel_id=1, source_target_pairs={{1,0},{2,1},{3,2},{0,3},{5,4},{6,5},{7,6},{4,7},{9,8},{10,9},{11,1... | collective-permute-start | bytes 442376 | tf_op jit(solution)/shard_map/ppermute | solution.py:402
  41.9 0.0 copy-done.18
  41.9 0.7 copy.31.refs_8_
  42.6 4.3 %collective-permute-done.2.refs_1_ = bf16[6,96,128]{2,1,0:T(8,128)(2,1)S(1)} collective-permute-done((bf16[6,96,128]{2,1,0:T(8,128)(2,1)}, bf16[6,96,128]{2,1,0:T(8,128)(2,1)S(1)}, u32[]{:S(2)}, u32[]{:S(2)}) %collective-permute-start.2) | collective-permute-done | bytes 147488 | tf_op jit(solution)/shard_map/ppermute | solution.py:401
  46.9 1.2 %collective-permute-done.3.refs_2_ = bf16[6,96,128]{2,1,0:T(8,128)(2,1)S(1)} collective-permute-done((bf16[6,96,128]{2,1,0:T(8,128)(2,1)}, bf16[6,96,128]{2,1,0:T(8,128)(2,1)S(1)}, u32[]{:S(2)}, u32[]{:S(2)}) %collective-permute-start.3) | collective-permute-done | bytes 147488 | tf_op jit(solution)/shard_map/ppermute | solution.py:402
  48.1 0.0 copy-done.12
  48.1 0.7 copy-done.13
  48.7 21.1 %atmos_block.3 = (bf16[96,96,128]{2,1,0:T(8,128)(2,1)}, bf16[18,32,128]{2,1,0:T(8,128)(2,1)}, bf16[18,32,128]{2,1,0:T(8,128)(2,1)}, bf16[18,32,128]{2,1,0:T(8,12...) custom-call(bf16[96,96,128]{2,1,0:T(8,128)(2,1)} %get-tuple-element., ...), custom_call_target="tpu_custom_call" | custom-call | tf_op jit(solution)/shard_map/atmos_block/pallas_call | solution.py:249
  69.9 0.0 copy-start.10
  69.9 1.7 %collective-permute-start.10 = (bf16[18,32,128]{2,1,0:T(8,128)(2,1)}, bf16[18,32,128]{2,1,0:T(8,128)(2,1)S(1)}, u32[]{:S(2)}, u32[]{:S(2)}) collective-permute-start(bf16[18,32,128]{2,1,0:T(8,128)(2,1)} %get-tuple-element.27), channel_id=1, source_target_pairs={{0,28},{4,0},{8,4},{12,8},{16,12},{20,16},{24,20},{28,24},{1,29},{... | collective-permute-start | bytes 442376 | tf_op jit(solution)/shard_map/ppermute | solution.py:434
  71.6 0.0 collective-permute-start.4
  71.6 0.4 collective-permute-start.5
  72.0 2.0 %collective-permute-start.6 = (bf16[18,32,128]{2,1,0:T(8,128)(2,1)}, bf16[18,32,128]{2,1,0:T(8,128)(2,1)S(1)}, u32[]{:S(2)}, u32[]{:S(2)}) collective-permute-start(bf16[18,32,128]{2,1,0:T(8,128)(2,1)} %get-tuple-element.23), channel_id=1, source_target_pairs={{0,12},{4,16},{8,20},{12,24},{16,28},{20,0},{24,4},{28,8},{1,13},{... | collective-permute-start | bytes 442376 | tf_op jit(solution)/shard_map/ppermute | solution.py:434
  73.9 0.9 collective-permute-start.7
  74.9 1.3 %collective-permute-done.10.refs_7_ = bf16[18,32,128]{2,1,0:T(8,128)(2,1)S(1)} collective-permute-done((bf16[18,32,128]{2,1,0:T(8,128)(2,1)}, bf16[18,32,128]{2,1,0:T(8,128)(2,1)S(1)}, u32[]{:S(2)}, u32[]{:S(2)}) %collective-permute-start.10) | collective-permute-done | bytes 147488 | tf_op jit(solution)/shard_map/ppermute | solution.py:434
  76.1 0.0 collective-permute-start.8
  76.1 2.4 %collective-permute-done.4.refs_1_ = bf16[18,32,128]{2,1,0:T(8,128)(2,1)S(1)} collective-permute-done((bf16[18,32,128]{2,1,0:T(8,128)(2,1)}, bf16[18,32,128]{2,1,0:T(8,128)(2,1)S(1)}, u32[]{:S(2)}, u32[]{:S(2)}) %collective-permute-start.4) | collective-permute-done | bytes 147488 | tf_op jit(solution)/shard_map/ppermute | solution.py:434
  78.5 0.6 collective-permute-start.9
  79.1 0.4 collective-permute-done.5.refs_2_
  79.5 5.6 %collective-permute-done.6.refs_3_ = bf16[18,32,128]{2,1,0:T(8,128)(2,1)S(1)} collective-permute-done((bf16[18,32,128]{2,1,0:T(8,128)(2,1)}, bf16[18,32,128]{2,1,0:T(8,128)(2,1)S(1)}, u32[]{:S(2)}, u32[]{:S(2)}) %collective-permute-start.6) | collective-permute-done | bytes 147488 | tf_op jit(solution)/shard_map/ppermute | solution.py:434
  85.1 0.2 collective-permute-done.7.refs_4_
  85.3 1.2 %collective-permute-done.8.refs_5_ = bf16[18,32,128]{2,1,0:T(8,128)(2,1)S(1)} collective-permute-done((bf16[18,32,128]{2,1,0:T(8,128)(2,1)}, bf16[18,32,128]{2,1,0:T(8,128)(2,1)S(1)}, u32[]{:S(2)}, u32[]{:S(2)}) %collective-permute-start.8) | collective-permute-done | bytes 147488 | tf_op jit(solution)/shard_map/ppermute | solution.py:434
  86.5 0.0 collective-permute-done.9.refs_6_
  86.5 0.0 copy-done
  86.5 0.0 copy-done.2
  86.5 0.0 copy-done.5
  86.5 0.0 copy-done.7
  86.6 0.0 copy-start.3
  86.6 0.9 copy-done.3
  87.5 1.2 %ocean_forcing.1 = (bf16[32,96,128]{2,1,0:T(8,128)(2,1)S(1)}, bf16[2,96,128]{2,1,0:T(8,128)(2,1)S(1)}) custom-call(bf16[18,32,128]{2,1,0:T(8,128)(2,1)S(1)} %copy-done.3, bf16[18,32,128]{2,1,0:T(8,128)(2,1)S(1)} %collective-permute-done.4.refs_1_, bf16[18,32,128]{2,1,0:T(8,128)(2,1)S(1)} %collective-permute-done.5.refs_2_, ...), custom_call_target="tpu_custom_call" | custom-call | tf_op jit(solution)/shard_map/ocean_forcing/pallas_call | solution.py:300
  88.7 0.3 collective-permute-start.11
  89.0 3.5 %collective-permute-start.12 = (bf16[2,96,128]{2,1,0:T(8,128)(2,1)S(1)}, bf16[2,96,128]{2,1,0:T(8,128)(2,1)S(1)}, u32[]{:S(2)}, u32[]{:S(2)}) collective-permute-start(bf16[2,96,128]{2,1,0:T(8,128)(2,1)S(1)} %get-tuple-element.29), channel_id=1, source_target_pairs={{1,0},{2,1},{3,2},{0,3},{5,4},{6,5},{7,6},{4,7},{9,8},{10,9},{11,1... | collective-permute-start | bytes 147464 | tf_op jit(solution)/shard_map/ppermute | solution.py:402
  92.6 0.0 copy-done.16
  92.6 0.1 copy.32.dn_ref
  92.7 0.0 copy-done.19
  92.7 0.1 copy.33.sw_ref
  92.8 1.9 %collective-permute-done.11.left_ref = bf16[2,96,128]{2,1,0:T(8,128)(2,1)S(1)} collective-permute-done((bf16[2,96,128]{2,1,0:T(8,128)(2,1)S(1)}, bf16[2,96,128]{2,1,0:T(8,128)(2,1)S(1)}, u32[]{:S(2)}, u32[]{:S(2)}) %collective-permute-start.11) | collective-permute-done | bytes 49184 | tf_op jit(solution)/shard_map/ppermute | solution.py:401
  94.7 0.0 collective-permute-done.12.right_ref
  94.7 0.0 copy-done.4
  94.7 0.0 copy-done.6
  94.7 0.0 copy-done.9
  94.8 0.0 copy-done.10
  94.8 5.9 %ocean_block.1 = (bf16[12,96,128]{2,1,0:T(8,128)(2,1)}, bf16[12,8,128]{2,1,0:T(8,128)(2,1)S(1)}) custom-call(bf16[32,96,128]{2,1,0:T(8,128)(2,1)S(1)} %get-tuple-element.28.mid_ref, bf16[2,96,128]{2,1,0:T(8,128)(2,1)S(1)} %collective-permute-done.11.left_ref, bf16[2,96,128]{2,1,0:T(8,128)(2,1)S(1)} %collective-permute-done.12.right_ref, ...), custom_call_target="tpu_custom_call" | custom-call | tf_op jit(solution)/shard_map/ocean_block/pallas_call | solution.py:350
  100.7 9.7 %all-gather = bf16[96,8,128]{2,1,0:T(8,128)(2,1)S(1)} all-gather(bf16[12,8,128]{2,1,0:T(8,128)(2,1)S(1)} %get-tuple-element.30), channel_id=2, replica_groups=mesh['member'=8,'lon'=4] {'member'}, dimensions={0}, use_global_device_ids=true | all-gather | bytes 221184 | tf_op jit(solution)/shard_map/all_gather | solution.py:442
  110.3 0.0 copy-done.8
  110.3 1.7 %copy-done.1 = bf16[96,96,128]{2,1,0:T(8,128)(2,1)S(1)} copy-done((bf16[96,96,128]{2,1,0:T(8,128)(2,1)S(1)}, bf16[96,96,128]{2,1,0:T(8,128)(2,1)}, u32[]{:S(2)}) %copy-start.1) | copy-done | bytes 2359320
  112.0 4.3 %couple.1 = bf16[96,96,128]{2,1,0:T(8,128)(2,1)} custom-call(bf16[96,96,128]{2,1,0:T(8,128)(2,1)S(1)} %copy-done.1, bf16[8,12,8,128]{3,2,1,0:T(8,128)(2,1)S(1)} %bitcast.5, s32[96,128]{1,0:T(8,128)S(1)} %copy-done.2, bf16[8,96]{1,0:T(8,128)(2,1)S(1)} %copy-done.8), custom_call_target="tpu_custom_call" | custom-call | tf_op jit(solution)/shard_map/couple/pallas_call | solution.py:383
  (14 shorter events, 0.0 us)
Async XLA Ops:
  0.6 9.9 %copy-start.11 = (bf16[2,384,96]{1,2,0:T(8,128)(2,1)S(1)}, bf16[2,384,96]{1,2,0:T(8,128)(2,1)}, u32[]{:S(2)}) copy-start(bf16[2,384,96]{1,2,0:T(8,128)(2,1)} %param.25) | copy-start | bytes 442372
  0.6 10.7 %copy-start.17 = (f32[2,7,7,96]{3,0,2,1:T(2,128)S(1)}, f32[2,7,7,96]{3,0,2,1:T(2,128)}, u32[]{:S(2)}) copy-start(f32[2,7,7,96]{3,0,2,1:T(2,128)} %param.22) | copy-start | bytes 112900
  5.5 36.5 %copy-start.18 = (bf16[96,32]{0,1:T(8,128)(2,1)S(1)}, bf16[96,32]{0,1:T(8,128)(2,1)}, u32[]{:S(2)}) copy-start(bf16[96,32]{0,1:T(8,128)(2,1)} %param.27) | copy-start | bytes 18436
  5.5 10.0 %collective-permute-start = (bf16[6,96,128]{2,1,0:T(8,128)(2,1)}, bf16[6,96,128]{2,1,0:T(8,128)(2,1)S(1)}, u32[]{:S(2)}, u32[]{:S(2)}) collective-permute-start(bf16[6,96,128]{2,1,0:T(8,128)(2,1)} %pack_edges.1), channel_id=1, source_target_pairs={{0,1},{1,2},{2,3},{3,0},{4,5},{5,6},{6,7},{7,4},{8,9},{9,10},{10,1... | collective-permute-start | bytes 442376 | tf_op jit(solution)/shard_map/ppermute | solution.py:401
  8.5 8.7 %collective-permute-start.1 = (bf16[6,96,128]{2,1,0:T(8,128)(2,1)}, bf16[6,96,128]{2,1,0:T(8,128)(2,1)S(1)}, u32[]{:S(2)}, u32[]{:S(2)}) collective-permute-start(bf16[6,96,128]{2,1,0:T(8,128)(2,1)} %pack_edges.1), channel_id=1, source_target_pairs={{1,0},{2,1},{3,2},{0,3},{5,4},{6,5},{7,6},{4,7},{9,8},{10,9},{11,1... | collective-permute-start | bytes 442376 | tf_op jit(solution)/shard_map/ppermute | solution.py:402
  12.0 74.6 %copy-start = (bf16[96,96,128]{2,1,0:T(8,128)(2,1)S(1)}, bf16[96,96,128]{2,1,0:T(8,128)(2,1)}, u32[]{:S(2)}) copy-start(bf16[96,96,128]{2,1,0:T(8,128)(2,1)} %refs_8_.2) | copy-start | bytes 7077892
  12.0 74.6 %copy-start.2 = (s32[96,128]{1,0:T(8,128)S(1)}, s32[96,128]{1,0:T(8,128)}, u32[]{:S(2)}) copy-start(s32[96,128]{1,0:T(8,128)} %land_ref.3) | copy-start | bytes 147460
  12.0 74.6 %copy-start.5 = (s32[96,128]{1,0:T(8,128)S(1)}, s32[96,128]{1,0:T(8,128)}, u32[]{:S(2)}) copy-start(s32[96,128]{1,0:T(8,128)} %refs_10_.1) | copy-start | bytes 147460
  12.0 74.6 %copy-start.7 = (bf16[2,32,96]{2,1,0:T(8,128)(2,1)S(1)}, bf16[2,32,96]{2,1,0:T(8,128)(2,1)}, u32[]{:S(2)}) copy-start(bf16[2,32,96]{2,1,0:T(8,128)(2,1)} %refs_11_.1) | copy-start | bytes 36868
  15.4 1.7 %copy-start.14 = (bf16[6,96,128]{2,1,0:T(8,128)(2,1)}, bf16[6,96,128]{2,1,0:T(8,128)(2,1)S(1)}, u32[]{:S(2)}) copy-start(bf16[6,96,128]{2,1,0:T(8,128)(2,1)S(1)} %collective-permute-done.refs_1_) | copy-start | bytes 442372
  17.2 0.7 copy-start.15
  38.1 8.8 %collective-permute-start.2 = (bf16[6,96,128]{2,1,0:T(8,128)(2,1)}, bf16[6,96,128]{2,1,0:T(8,128)(2,1)S(1)}, u32[]{:S(2)}, u32[]{:S(2)}) collective-permute-start(bf16[6,96,128]{2,1,0:T(8,128)(2,1)} %get-tuple-element.18), channel_id=1, source_target_pairs={{0,1},{1,2},{2,3},{3,0},{4,5},{5,6},{6,7},{7,4},{8,9},{9,10},{10,1... | collective-permute-start | bytes 442376 | tf_op jit(solution)/shard_map/ppermute | solution.py:401
  39.2 8.8 %collective-permute-start.3 = (bf16[6,96,128]{2,1,0:T(8,128)(2,1)}, bf16[6,96,128]{2,1,0:T(8,128)(2,1)S(1)}, u32[]{:S(2)}, u32[]{:S(2)}) collective-permute-start(bf16[6,96,128]{2,1,0:T(8,128)(2,1)} %get-tuple-element.18), channel_id=1, source_target_pairs={{1,0},{2,1},{3,2},{0,3},{5,4},{6,5},{7,6},{4,7},{9,8},{10,9},{11,1... | collective-permute-start | bytes 442376 | tf_op jit(solution)/shard_map/ppermute | solution.py:402
  46.9 1.2 %copy-start.12 = (bf16[6,96,128]{2,1,0:T(8,128)(2,1)}, bf16[6,96,128]{2,1,0:T(8,128)(2,1)S(1)}, u32[]{:S(2)}) copy-start(bf16[6,96,128]{2,1,0:T(8,128)(2,1)S(1)} %collective-permute-done.2.refs_1_) | copy-start | bytes 442372
  48.1 0.7 copy-start.13
  48.7 43.8 %copy-start.16 = (bf16[384,96]{0,1:T(8,128)(2,1)S(1)}, bf16[384,96]{0,1:T(8,128)(2,1)}, u32[]{:S(2)}) copy-start(bf16[384,96]{0,1:T(8,128)(2,1)} %param.32) | copy-start | bytes 221188
  48.7 46.0 %copy-start.4 = (bf16[96,384]{1,0:T(8,128)(2,1)S(1)}, bf16[96,384]{1,0:T(8,128)(2,1)}, u32[]{:S(2)}) copy-start(bf16[96,384]{1,0:T(8,128)(2,1)} %up_ref.1) | copy-start | bytes 221188
  48.7 46.0 %copy-start.6 = (f32[7,7,96]{2,1,0:T(8,128)S(1)}, f32[7,7,96]{2,1,0:T(8,128)}, u32[]{:S(2)}) copy-start(f32[7,7,96]{2,1,0:T(8,128)} %k_ref.1) | copy-start | bytes 56452
  69.9 22.8 %copy-start.19 = (bf16[96,8]{0,1:T(8,128)(2,1)S(1)}, bf16[96,8]{0,1:T(8,128)(2,1)}, u32[]{:S(2)}) copy-start(bf16[96,8]{0,1:T(8,128)(2,1)} %param.34) | copy-start | bytes 4612
  69.9 24.9 %copy-start.9 = (f32[96]{0:T(128)S(1)}, f32[96]{0:T(128)}, u32[]{:S(2)}) copy-start(f32[96]{0:T(128)} %param.30) | copy-start | bytes 1156
  69.9 24.9 %copy-start.10 = (f32[96]{0:T(128)S(1)}, f32[96]{0:T(128)}, u32[]{:S(2)}) copy-start(f32[96]{0:T(128)} %param.33) | copy-start | bytes 1156
  69.9 6.2 %collective-permute-start.10 = (bf16[18,32,128]{2,1,0:T(8,128)(2,1)}, bf16[18,32,128]{2,1,0:T(8,128)(2,1)S(1)}, u32[]{:S(2)}, u32[]{:S(2)}) collective-permute-start(bf16[18,32,128]{2,1,0:T(8,128)(2,1)} %get-tuple-element.27), channel_id=1, source_target_pairs={{0,28},{4,0},{8,4},{12,8},{16,12},{20,16},{24,20},{28,24},{1,29},{... | collective-permute-start | bytes 442376 | tf_op jit(solution)/shard_map/ppermute | solution.py:434
  71.6 6.9 %collective-permute-start.4 = (bf16[18,32,128]{2,1,0:T(8,128)(2,1)}, bf16[18,32,128]{2,1,0:T(8,128)(2,1)S(1)}, u32[]{:S(2)}, u32[]{:S(2)}) collective-permute-start(bf16[18,32,128]{2,1,0:T(8,128)(2,1)} %get-tuple-element.21), channel_id=1, source_target_pairs={{0,4},{4,8},{8,12},{12,16},{16,20},{20,24},{24,28},{28,0},{1,5},{5... | collective-permute-start | bytes 442376 | tf_op jit(solution)/shard_map/ppermute | solution.py:434
  71.6 7.9 %collective-permute-start.5 = (bf16[18,32,128]{2,1,0:T(8,128)(2,1)}, bf16[18,32,128]{2,1,0:T(8,128)(2,1)S(1)}, u32[]{:S(2)}, u32[]{:S(2)}) collective-permute-start(bf16[18,32,128]{2,1,0:T(8,128)(2,1)} %get-tuple-element.22), channel_id=1, source_target_pairs={{0,8},{4,12},{8,16},{12,20},{16,24},{20,28},{24,0},{28,4},{1,9},{5... | collective-permute-start | bytes 442376 | tf_op jit(solution)/shard_map/ppermute | solution.py:434
  72.0 13.1 %collective-permute-start.6 = (bf16[18,32,128]{2,1,0:T(8,128)(2,1)}, bf16[18,32,128]{2,1,0:T(8,128)(2,1)S(1)}, u32[]{:S(2)}, u32[]{:S(2)}) collective-permute-start(bf16[18,32,128]{2,1,0:T(8,128)(2,1)} %get-tuple-element.23), channel_id=1, source_target_pairs={{0,12},{4,16},{8,20},{12,24},{16,28},{20,0},{24,4},{28,8},{1,13},{... | collective-permute-start | bytes 442376 | tf_op jit(solution)/shard_map/ppermute | solution.py:434
  73.9 11.4 %collective-permute-start.7 = (bf16[18,32,128]{2,1,0:T(8,128)(2,1)}, bf16[18,32,128]{2,1,0:T(8,128)(2,1)S(1)}, u32[]{:S(2)}, u32[]{:S(2)}) collective-permute-start(bf16[18,32,128]{2,1,0:T(8,128)(2,1)} %get-tuple-element.24), channel_id=1, source_target_pairs={{0,16},{4,20},{8,24},{12,28},{16,0},{20,4},{24,8},{28,12},{1,17},{... | collective-permute-start | bytes 442376 | tf_op jit(solution)/shard_map/ppermute | solution.py:434
  76.1 10.4 %collective-permute-start.8 = (bf16[18,32,128]{2,1,0:T(8,128)(2,1)}, bf16[18,32,128]{2,1,0:T(8,128)(2,1)S(1)}, u32[]{:S(2)}, u32[]{:S(2)}) collective-permute-start(bf16[18,32,128]{2,1,0:T(8,128)(2,1)} %get-tuple-element.25), channel_id=1, source_target_pairs={{0,20},{4,24},{8,28},{12,0},{16,4},{20,8},{24,12},{28,16},{1,21},{... | collective-permute-start | bytes 442376 | tf_op jit(solution)/shard_map/ppermute | solution.py:434
  78.5 8.0 %collective-permute-start.9 = (bf16[18,32,128]{2,1,0:T(8,128)(2,1)}, bf16[18,32,128]{2,1,0:T(8,128)(2,1)S(1)}, u32[]{:S(2)}, u32[]{:S(2)}) collective-permute-start(bf16[18,32,128]{2,1,0:T(8,128)(2,1)} %get-tuple-element.26), channel_id=1, source_target_pairs={{0,24},{4,28},{8,0},{12,4},{16,8},{20,12},{24,16},{28,20},{1,25},{... | collective-permute-start | bytes 442376 | tf_op jit(solution)/shard_map/ppermute | solution.py:434
  86.6 0.9 copy-start.3
  87.5 22.9 %copy-start.8 = (bf16[8,96]{1,0:T(8,128)(2,1)S(1)}, bf16[8,96]{1,0:T(8,128)(2,1)}, u32[]{:S(2)}) copy-start(bf16[8,96]{1,0:T(8,128)(2,1)} %bw_ref.1) | copy-start | bytes 4612
  88.7 6.1 %collective-permute-start.11 = (bf16[2,96,128]{2,1,0:T(8,128)(2,1)S(1)}, bf16[2,96,128]{2,1,0:T(8,128)(2,1)S(1)}, u32[]{:S(2)}, u32[]{:S(2)}) collective-permute-start(bf16[2,96,128]{2,1,0:T(8,128)(2,1)S(1)} %get-tuple-element.29), channel_id=1, source_target_pairs={{0,1},{1,2},{2,3},{3,0},{4,5},{5,6},{6,7},{7,4},{8,9},{9,10},{10,1... | collective-permute-start | bytes 147464 | tf_op jit(solution)/shard_map/ppermute | solution.py:401
  89.0 5.7 %collective-permute-start.12 = (bf16[2,96,128]{2,1,0:T(8,128)(2,1)S(1)}, bf16[2,96,128]{2,1,0:T(8,128)(2,1)S(1)}, u32[]{:S(2)}, u32[]{:S(2)}) collective-permute-start(bf16[2,96,128]{2,1,0:T(8,128)(2,1)S(1)} %get-tuple-element.29), channel_id=1, source_target_pairs={{1,0},{2,1},{3,2},{0,3},{5,4},{6,5},{7,6},{4,7},{9,8},{10,9},{11,1... | collective-permute-start | bytes 147464 | tf_op jit(solution)/shard_map/ppermute | solution.py:402
  110.3 1.7 %copy-start.1 = (bf16[96,96,128]{2,1,0:T(8,128)(2,1)S(1)}, bf16[96,96,128]{2,1,0:T(8,128)(2,1)}, u32[]{:S(2)}) copy-start(bf16[96,96,128]{2,1,0:T(8,128)(2,1)} %get-tuple-element.19.y_ref) | copy-start | bytes 7077892

commit v2 on v1

v2 whole, which is shorter than its diff:
```python
import functools

import jax
import jax.numpy as jnp
from jax import lax
from jax.experimental import pallas as pl
from jax.experimental.pallas import tpu as pltpu
from jax.sharding import PartitionSpec as P

BF = jnp.bfloat16
F32 = jnp.float32
TANH_A = 0.7978845608028654
TANH_B = TANH_A * 0.044715
TAPS = 7
HALO = 3
GROUP = 16
SPAN = 16
OUT = SPAN - TAPS + 1
DEPTH = GROUP * SPAN
SLOT = 8
SLOTS = 16
BY_DOT = (0, 1, 5, 6)
VMEM = pl.BlockSpec(memory_space=pltpu.VMEM)
ANY = pl.BlockSpec(memory_space=pl.ANY)


def params(mib):
    return pltpu.CompilerParams(vmem_limit_bytes=mib * 2**20)


def cost(gflop):
    return pl.CostEstimate(flops=int(gflop * 1e9), bytes_accessed=0, transcendentals=0)


def twice_gelu(z):
    return z + z * jnp.tanh(z * (TANH_A + TANH_B * (z * z)))


def transposed(value, factor):
    return (value.astype(F32).T * factor).astype(BF)


def spread(row, lanes):
    return jnp.broadcast_to(row.T, (row.shape[1], lanes))


def edge_lanes(shape):
    lane = lax.broadcasted_iota(jnp.int32, shape, len(shape) - 1)
    return (lane < HALO) | (lane >= shape[-1] - HALO)


def pack_kernel(x_ref, p_ref):
    step = pl.program_id(0)
    count, chans, lanes = x_ref.shape
    blocks = p_ref.shape[0]
    keep = edge_lanes((chans, lanes)).astype(F32).astype(BF)
    for q in range(blocks):
        total = None
        for c in range(count // blocks):
            slot = step * (count // blocks) + c
            moved = pltpu.roll(x_ref[c * blocks + q] * keep, SLOT * slot, 1)
            total = moved if total is None else total + moved
        if count // blocks < SLOTS:

            @pl.when(step == 0)
            def _():
                p_ref[q] = total

            @pl.when(step > 0)
            def _():
                p_ref[q] = p_ref[q] + total

        else:
            p_ref[q] = total


def pack(x, step):
    rows, chans, lanes = x.shape
    blocks = rows // SLOTS
    return pl.pallas_call(
        pack_kernel,
        grid=(rows // step,),
        out_shape=jax.ShapeDtypeStruct((blocks, chans, lanes), BF),
        in_specs=[pl.BlockSpec((step, chans, lanes), lambda i: (i, 0, 0))],
        out_specs=pl.BlockSpec((blocks, chans, lanes), lambda i: (0, 0, 0)),
        compiler_params=params(16),
        name="pack_edges",
    )(x)


def neighbours(packed):
    count = lax.axis_size("lon")
    left = lax.ppermute(packed, "lon", [(i, (i + 1) % count) for i in range(count)])
    right = lax.ppermute(packed, "lon", [((i + 1) % count, i) for i in range(count)])
    return left, right


def shift_matrix(lanes):
    shape = (lanes, len(BY_DOT) * lanes)
    src = lax.broadcasted_iota(jnp.int32, shape, 0)
    dst = lax.broadcasted_iota(jnp.int32, shape, 1)
    hit = jnp.zeros(shape, jnp.bool_)
    for a, j in enumerate(BY_DOT):
        hit = hit | ((dst >= a * lanes) & (dst < (a + 1) * lanes) & (src == dst - a * lanes + j - HALO))
    return hit.astype(F32).astype(BF)


def fill_base(taps, base):
    groups, _, wide = base.shape
    chans = groups * GROUP
    t = lax.broadcasted_iota(jnp.int32, (TAPS, wide), 0)
    n = lax.broadcasted_iota(jnp.int32, (TAPS, wide), 1)
    total = jnp.zeros((chans, wide), F32)
    for i in range(TAPS):
        put = ((t == n // DEPTH) & ((n % DEPTH) // GROUP == i)).astype(F32).astype(BF)
        total = total + jnp.dot(taps(i).T.astype(BF), put, preferred_element_type=F32)
    r = lax.broadcasted_iota(jnp.int32, (chans, wide), 0)
    c = lax.broadcasted_iota(jnp.int32, (chans, wide), 1)
    total = jnp.where(r % GROUP == c % GROUP, total, 0.0)
    for g in range(groups):
        base[g] = total[GROUP * g : GROUP * (g + 1)]


def conv_kernel(layer, pad, x_ref, k_ref, a_ref, band_ref, base, smat, xj, band):
    g = pl.program_id(0)
    count, _, lanes = x_ref.shape
    rows = a_ref.shape[0]
    tall = xj.shape[1]

    @pl.when(g == 0)
    def _():
        fill_base(lambda i: k_ref[layer, i] if layer is not None else k_ref[i], base)
        smat[...] = shift_matrix(lanes)
        for j in range(TAPS):
            if pad:
                xj[j, :pad] = jnp.zeros((pad, GROUP, lanes), BF)
            if tall > pad + count:
                xj[j, pad + count :] = jnp.zeros((tall - pad - count, GROUP, lanes), BF)

    for j in range(TAPS):
        one = base[g, :, j * DEPTH : (j + 1) * DEPTH]
        for r in range(OUT):
            moved = pltpu.roll(one, GROUP * r, 1) if r else one
            band[GROUP * r : GROUP * (r + 1), j * DEPTH : (j + 1) * DEPTH] = moved.astype(BF)
    band_ref[0] = band[: band_ref.shape[1]]

    x = x_ref[...]
    moved = jnp.dot(x.reshape(count * GROUP, lanes), smat[...], preferred_element_type=F32)
    for a, j in enumerate(BY_DOT):
        part = moved[:, a * lanes : (a + 1) * lanes].astype(BF)
        xj[j, pad : pad + count] = part.reshape(count, GROUP, lanes)
    lane = lax.broadcasted_iota(jnp.int32, (GROUP, lanes), 1)
    for j in range(TAPS):
        d = j - HALO
        if j in BY_DOT:
            continue
        if d == 0:
            xj[j, pad : pad + count] = x
        else:
            keep = ((lane < lanes - d) if d > 0 else (lane >= -d)).astype(F32).astype(BF)
            xj[j, pad : pad + count] = pltpu.roll(x, (-d) % lanes, 2) * keep[None]

    starts = [min(OUT * i, max(rows - OUT, 0)) for i in range(-(-rows // OUT))]
    field = jnp.concatenate(
        [
            jnp.concatenate([xj[j, s : s + SPAN].reshape(DEPTH, lanes) for j in range(TAPS)], axis=0)
            for s in starts
        ],
        axis=1,
    )
    out = jnp.dot(band[...], field, preferred_element_type=F32)
    take = min(OUT, rows)
    for n, s in enumerate(starts):
        part = out[: take * GROUP, n * lanes : (n + 1) * lanes]
        a_ref[s : s + take] = part.reshape(take, GROUP, lanes)


def convolve(layer, x, taps, pad, blocks):
    count, chans, lanes = x.shape
    rows = count + 2 * pad - 2 * HALO
    groups = chans // GROUP
    wide = TAPS * DEPTH
    tall = max(count + 2 * pad, SPAN)
    return pl.pallas_call(
        functools.partial(conv_kernel, layer, pad),
        grid=(groups,),
        out_shape=[
            jax.ShapeDtypeStruct((rows, chans, lanes), F32),
            jax.ShapeDtypeStruct((groups, blocks * GROUP, wide), BF),
        ],
        in_specs=[pl.BlockSpec((count, GROUP, lanes), lambda g: (0, g, 0)), VMEM],
        out_specs=[
            pl.BlockSpec((rows, GROUP, lanes), lambda g: (0, g, 0)),
            pl.BlockSpec((1, blocks * GROUP, wide), lambda g: (g, 0, 0)),
        ],
        scratch_shapes=[
            pltpu.VMEM((groups, GROUP, wide), F32),
            pltpu.VMEM((lanes, len(BY_DOT) * lanes), BF),
            pltpu.VMEM((TAPS, tall, GROUP, lanes), BF),
            pltpu.VMEM((GROUP * OUT, wide), BF),
        ],
        compiler_params=params(32),
        cost_estimate=cost(8 * rows / 96),
        name="conv",
    )(x, taps)


def halo_matrix(lanes):
    side = [j for j in range(TAPS) if j != HALO]
    shape = (2 * lanes, len(side) * lanes)
    src = lax.broadcasted_iota(jnp.int32, shape, 0)
    dst = lax.broadcasted_iota(jnp.int32, shape, 1)
    hit = jnp.zeros(shape, jnp.bool_)
    to = dst % lanes
    for a, j in enumerate(side):
        d = j - HALO
        here = (dst >= a * lanes) & (dst < (a + 1) * lanes)
        from_ = (to + d + lanes) % lanes
        if d > 0:
            ok = (src == from_) & (src % SLOT < HALO) & (to % SLOT >= SLOT - HALO)
        else:
            ok = (src == from_ + lanes) & (src % SLOT >= SLOT - HALO) & (to % SLOT < HALO)
        hit = hit | (here & ok)
    return hit.astype(F32).astype(BF)


def halo_conv(left, right, band, wrapped, xe, halo):
    blocks, chans, lanes = halo.shape
    wide = TAPS * DEPTH
    both = [jnp.concatenate([right[q], left[q]], axis=1) for q in range(blocks)]
    lane = lax.broadcasted_iota(jnp.int32, (chans, lanes), 1)
    slot = (lane + HALO) // SLOT % SLOTS

    def turned(value, shift, drop):
        keep = (slot != drop).astype(F32).astype(BF)
        parts = [pltpu.roll(value[:, n * lanes : (n + 1) * lanes], shift, 1) * keep for n in range(2)]
        return jnp.concatenate(parts, axis=1)

    if wrapped:
        tall = (
            [turned(both[q], SLOT, 0) for q in range(blocks - HALO, blocks)]
            + both
            + [turned(both[q], lanes - SLOT, SLOTS - 1) for q in range(HALO)]
        )
    else:
        tall = both + [turned(both[q], lanes - SLOT, SLOTS - 1) for q in range(2 * HALO)]
    field = jnp.concatenate(tall, axis=0)
    moved = jnp.dot(field, halo_matrix(lanes), preferred_element_type=F32)
    count = len(tall)
    for a in range(TAPS - 1):
        part = moved[:, a * lanes : (a + 1) * lanes].astype(BF)
        xe[a, :count] = part.reshape(count, chans, lanes)
        xe[a, count:] = jnp.zeros((SPAN - count, chans, lanes), BF)
    low = HALO * DEPTH
    for g in range(chans // GROUP):
        at = slice(GROUP * g, GROUP * (g + 1))
        rhs = jnp.concatenate([xe[a, :, at, :].reshape(DEPTH, lanes) for a in range(TAPS - 1)], axis=0)
        lhs = jnp.concatenate([band[g, :, :low], band[g, :, low + DEPTH : wide]], axis=1)
        out = jnp.dot(lhs, rhs, preferred_element_type=F32)
        halo[:, at, :] = out.reshape(blocks, GROUP, lanes)


def branch_of(a_ref, halo, slot0, gain, up_t, down_t):
    count, chans, lanes = a_ref.shape
    blocks = halo.shape[0]
    edge = edge_lanes((chans, lanes))
    normed = []
    for r in range(count):
        shift = lax.rem(lanes - SLOT * (slot0 + r // blocks), lanes)
        a = a_ref[r] + jnp.where(edge, pltpu.roll(halo[r % blocks], shift, 1), 0.0)
        center = a - jnp.mean(a, axis=0, keepdims=True)
        var = jnp.mean(center * center, axis=0, keepdims=True)
        normed.append((center * lax.rsqrt(var + 1e-06) * gain).astype(BF))
    z = jnp.dot(up_t, jnp.concatenate(normed, axis=1), preferred_element_type=F32)
    h = twice_gelu(z.astype(BF))
    return jnp.dot(down_t, h, preferred_element_type=F32)


def first_kernel(x_ref, a_ref, left_ref, right_ref, band_ref, g_ref, up_ref, dn_ref, s_ref, y_ref, p_ref, xe, halo, up_t, dn_t, gain, scale):
    step = pl.program_id(0)
    count, chans, lanes = x_ref.shape
    blocks = halo.shape[0]

    @pl.when(step == 0)
    def _():
        halo_conv(left_ref, right_ref, band_ref, True, xe, halo)
        up_t[...] = transposed(up_ref[0], 1.0)
        dn_t[...] = transposed(dn_ref[0], 0.5)
        gain[...] = spread(g_ref[0:1], lanes)
        scale[...] = spread(s_ref[0:1], lanes)
        p_ref[...] = jnp.zeros(p_ref.shape, BF)

    slot0 = step * (count // blocks)
    branch = branch_of(a_ref, halo, slot0, gain[...], up_t[...], dn_t[...])
    keep = edge_lanes((chans, lanes)).astype(F32).astype(BF)
    for r in range(count):
        y = x_ref[r].astype(F32) + scale[...] * branch[:, r * lanes : (r + 1) * lanes]
        y = y.astype(BF)
        y_ref[r] = y
        moved = pltpu.roll(y * keep, SLOT * (slot0 + r // blocks), 1)
        p_ref[r % blocks] = p_ref[r % blocks] + moved


def first_block(x, a, left, right, band, gain, up, down, scale, step):
    rows, chans, lanes = x.shape
    blocks = rows // SLOTS
    hid = up.shape[2]
    part = pl.BlockSpec((step, chans, lanes), lambda i: (i, 0, 0))
    return pl.pallas_call(
        first_kernel,
        grid=(rows // step,),
        out_shape=[
            jax.ShapeDtypeStruct(x.shape, BF),
            jax.ShapeDtypeStruct((blocks, chans, lanes), BF),
        ],
        in_specs=[part, part] + [VMEM] * 7,
        out_specs=[part, pl.BlockSpec((blocks, chans, lanes), lambda i: (0, 0, 0))],
        scratch_shapes=[
            pltpu.VMEM((TAPS - 1, SPAN, chans, lanes), BF),
            pltpu.VMEM((blocks, chans, lanes), F32),
            pltpu.VMEM((hid, chans), BF),
            pltpu.VMEM((chans, hid), BF),
            pltpu.VMEM((chans, lanes), F32),
            pltpu.VMEM((chans, lanes), F32),
        ],
        compiler_params=params(40),
        cost_estimate=cost(8),
        name="first_block",
    )(x, a, left, right, band, gain, up, down, scale)


def second_kernel(near, members, at_ref, *refs):
    x_ref, a_ref, left_ref, right_ref, band_ref, g_ref, up_ref, dn_ref, s_ref, fw_ref = refs[:10]
    refs = refs[10:]
    if near:
        old_ref = refs[1]
        refs = refs[2:]
    y_ref, refs = refs[0], refs[1:]
    half = members // 2
    chunk_refs, refs = refs[:half], refs[half:]
    flux, xe, halo, up_t, dn_t, fw_t, gain, scale = refs
    step = pl.program_id(0)
    count, chans, lanes = x_ref.shape
    blocks = halo.shape[0]
    tall = flux.shape[0]

    @pl.when(step == 0)
    def _():
        halo_conv(left_ref, right_ref, band_ref, True, xe, halo)
        up_t[...] = transposed(up_ref[1], 1.0)
        dn_t[...] = transposed(dn_ref[1], 0.5)
        fw_t[...] = transposed(fw_ref[...], 1.0)
        gain[...] = spread(g_ref[1:2], lanes)
        scale[...] = spread(s_ref[1:2], lanes)
        if near:
            flux[...] = old_ref[...]
        else:
            flux[0:HALO] = jnp.zeros((HALO,) + flux.shape[1:], BF)
            flux[tall - HALO : tall] = jnp.zeros((HALO,) + flux.shape[1:], BF)

    row0 = (at_ref[0] + step) * count
    slot0 = (at_ref[0] + step) * (count // blocks)
    branch = branch_of(a_ref, halo, slot0, gain[...], up_t[...], dn_t[...])
    made = []
    for r in range(count):
        y = x_ref[r].astype(F32) + scale[...] * branch[:, r * lanes : (r + 1) * lanes]
        made.append(y.astype(BF))
        y_ref[r] = made[r]
    z = jnp.dot(fw_t[...], jnp.concatenate(made, axis=1), preferred_element_type=F32)
    f = (0.5 * twice_gelu(z)).astype(BF)
    for r in range(count):
        flux[row0 + HALO + r] = f[:, r * lanes : (r + 1) * lanes]

    @pl.when(step == pl.num_programs(0) - 1)
    def _():
        rank = lax.axis_index("member")
        share = (tall - 2 * HALO) // members
        for k in range(half):
            dst = rank ^ (k if near else half + k)
            chunk_refs[k][...] = flux[pl.ds(dst * share, share + 2 * HALO)]


def second_block(near, members, at, x, a, left, right, band, gain, up, down, scale, flux_weight, earlier, step, steps):
    rows, chans, lanes = x.shape
    blocks = rows // SLOTS
    hid = up.shape[2]
    flux = flux_weight.shape[1]
    half = members // 2
    share = rows // members
    part = pl.BlockSpec((step, chans, lanes), lambda i, s: (s[0] + i, 0, 0))
    args = [at, x, a, left, right, band, gain, up, down, scale, flux_weight]
    in_specs = [part, part] + [VMEM] * 8
    alias = {}
    if near:
        alias = {len(args): 0}
        args += earlier
        in_specs += [ANY, VMEM]
    outs = [jax.ShapeDtypeStruct(x.shape, BF)]
    outs += [jax.ShapeDtypeStruct((share + 2 * HALO, flux, lanes), BF)] * half
    out_specs = [part] + [VMEM] * half
    scratch = [
        pltpu.VMEM((TAPS - 1, SPAN, chans, lanes), BF),
        pltpu.VMEM((blocks, chans, lanes), F32),
        pltpu.VMEM((hid, chans), BF),
        pltpu.VMEM((chans, hid), BF),
        pltpu.VMEM((flux, chans), BF),
        pltpu.VMEM((chans, lanes), F32),
        pltpu.VMEM((chans, lanes), F32),
    ]
    field = (rows + 2 * HALO, flux, lanes)
    if near:
        scratch = [pltpu.VMEM(field, BF)] + scratch
    else:
        outs.append(jax.ShapeDtypeStruct(field, BF))
        out_specs.append(VMEM)
    return pl.pallas_call(
        functools.partial(second_kernel, near, members),
        out_shape=outs,
        grid_spec=pltpu.PrefetchScalarGridSpec(
            num_scalar_prefetch=1,
            grid=(steps,),
            in_specs=in_specs,
            out_specs=out_specs,
            scratch_shapes=scratch,
        ),
        input_output_aliases=alias,
        compiler_params=params(40),
        cost_estimate=cost(8 * steps * step / rows),
        name="second_block",
    )(*args)


def force_kernel(members, *refs):
    flux_refs = refs[:members]
    ocean_ref, land_ref, ice_ref, lift_ref, mid_ref, p_ref, win, sem = refs[members:]
    span, flux, lanes = flux_refs[0].shape
    rows = land_ref.shape[0]
    chans = mid_ref.shape[1]
    share = rows // members
    blocks = p_ref.shape[0]
    first = lax.axis_index("member") * share - HALO
    start = jnp.clip(first, 0, rows - span)
    copy = pltpu.make_async_copy(ocean_ref.at[pl.ds(start, span)], win, sem)
    copy.start()
    total = flux_refs[0][...].astype(F32)
    for ref in flux_refs[1:]:
        total = total + ref[...].astype(F32)
    low = (total / members).astype(BF)
    lift = jnp.concatenate([transposed(lift_ref[0], 1.0), transposed(lift_ref[1], 1.0)], axis=0)
    terms = jnp.dot(
        lift, jnp.concatenate([low[r] for r in range(span)], axis=1), preferred_element_type=F32
    )
    keep = edge_lanes((chans, lanes)).astype(F32).astype(BF)
    packed = [None] * blocks
    copy.wait()
    for r in range(span):
        row = first + r
        safe = jnp.clip(row, 0, rows - 1)
        sea = (1 - land_ref[pl.ds(safe, 1), :]).astype(F32)
        ice = ice_ref[pl.ds(safe, 1), :].astype(F32)
        at = slice(r * lanes, (r + 1) * lanes)
        forcing = sea * ((1.0 - ice) * terms[:chans, at] + ice * terms[chans:, at])
        mid = win[jnp.clip(row - start, 0, span - 1)].astype(F32) + forcing
        inside = (row >= 0) & (row < rows)
        mid = jnp.where(inside, mid, 0.0).astype(BF)
        mid_ref[r] = mid
        q, slot = r % blocks, r // blocks
        moved = mid * keep
        if slot:
            moved = pltpu.roll(moved, SLOT * slot, 1)
        packed[q] = moved if packed[q] is None else packed[q] + moved
    for q in range(blocks):
        p_ref[q] = packed[q]


def force(members, chunks, ocean, land, ice, lift):
    span, _, lanes = chunks[0].shape
    rows, chans, _ = ocean.shape
    return pl.pallas_call(
        functools.partial(force_kernel, members),
        out_shape=[
            jax.ShapeDtypeStruct((span, chans, lanes), BF),
            jax.ShapeDtypeStruct((rows // SLOTS, chans, lanes), BF),
        ],
        in_specs=[VMEM] * members + [ANY, VMEM, VMEM, VMEM],
        out_specs=[VMEM] * 2,
        scratch_shapes=[pltpu.VMEM((span, chans, lanes), BF), pltpu.SemaphoreType.DMA(())],
        compiler_params=params(24),
        name="ocean_forcing",
    )(*chunks, ocean, land, ice, lift)


def ocean_kernel(mid_ref, a_ref, left_ref, right_ref, band_ref, land_ref, g_ref, up_ref, dn_ref, s_ref, sw_ref, new_ref, surf_ref, xe, halo):
    share, chans, lanes = new_ref.shape
    halo_conv(left_ref, right_ref, band_ref, False, xe, halo)
    gain = spread(g_ref[...], lanes)
    scale = spread(s_ref[...], lanes)
    branch = branch_of(
        a_ref, halo, 0, gain, transposed(up_ref[...], 1.0), transposed(dn_ref[...], 0.5)
    )
    first = lax.axis_index("member") * share
    made = []
    for r in range(share):
        sea = (1 - land_ref[pl.ds(first + r, 1), :]).astype(F32)
        y = mid_ref[HALO + r].astype(F32) + scale * branch[:, r * lanes : (r + 1) * lanes]
        made.append((y * sea).astype(BF))
        new_ref[r] = made[r]
    surf = jnp.dot(
        transposed(sw_ref[...], 1.0), jnp.concatenate(made, axis=1), preferred_element_type=F32
    )
    for r in range(share):
        surf_ref[r] = surf[:, r * lanes : (r + 1) * lanes].astype(BF)


def ocean_block(mid, a, left, right, band, land, gain, up, down, scale, surf_weight):
    share, chans, lanes = a.shape
    blocks = left.shape[0]
    return pl.pallas_call(
        ocean_kernel,
        out_shape=[
            jax.ShapeDtypeStruct((share, chans, lanes), BF),
            jax.ShapeDtypeStruct((share, surf_weight.shape[1], lanes), BF),
        ],
        in_specs=[VMEM] * 11,
        out_specs=[VMEM] * 2,
        scratch_shapes=[
            pltpu.VMEM((TAPS - 1, SPAN, chans, lanes), BF),
            pltpu.VMEM((blocks, chans, lanes), F32),
        ],
        compiler_params=params(24),
        name="ocean_block",
    )(mid, a, left, right, band, land, gain[None], up, down, scale[None], surf_weight)


def couple_kernel(y_ref, surf_ref, land_ref, bw_ref, o_ref):
    share, chans, lanes = y_ref.shape
    surf = jnp.concatenate([surf_ref[0, r] for r in range(share)], axis=1)
    back = jnp.dot(transposed(bw_ref[...], 1.0), surf, preferred_element_type=F32)
    first = pl.program_id(0) * share
    for r in range(share):
        sea = (1 - land_ref[pl.ds(first + r, 1), :]).astype(F32)
        out = y_ref[r].astype(F32) + sea * back[:, r * lanes : (r + 1) * lanes]
        o_ref[r] = out.astype(BF)


def couple(y, surface, land, back_weight):
    members, share, surf, lanes = surface.shape
    chans = y.shape[1]
    rows = pl.BlockSpec((share, chans, lanes), lambda i: (i, 0, 0))
    return pl.pallas_call(
        couple_kernel,
        grid=(members,),
        out_shape=jax.ShapeDtypeStruct(y.shape, BF),
        in_specs=[
            rows,
            pl.BlockSpec((1, share, surf, lanes), lambda i: (i, 0, 0, 0)),
            VMEM,
            VMEM,
        ],
        out_specs=rows,
        compiler_params=params(24),
        name="couple",
    )(y, surface, land, back_weight)


def local(
    atmos,
    ocean,
    land_mask,
    ice_mask,
    atm_kernel,
    atm_gain,
    atm_up,
    atm_down,
    atm_scale,
    flux_weight,
    flux_lift,
    ocn_kernel,
    ocn_gain,
    ocn_up,
    ocn_down,
    ocn_scale,
    surf_weight,
    back_weight,
):
    members = lax.axis_size("member")
    rank = lax.axis_index("member")
    half = members // 2
    state = atmos[0]
    rows = state.shape[0]
    blocks = rows // SLOTS
    big, small = 4 * blocks, 2 * blocks
    atm = (atm_gain, atm_up, atm_down, atm_scale)

    left, right = neighbours(pack(state, big))
    a, band = convolve(0, state, atm_kernel, HALO, blocks)
    state, packed = first_block(state, a, left, right, band, *atm, big)

    left, right = neighbours(packed)
    a, band = convolve(1, state, atm_kernel, HALO, blocks)
    near_steps = (rows // 2 - small) // small
    far_steps = rows // small - near_steps
    upper = rank >= half
    far_at = jnp.where(upper, 0, near_steps).astype(jnp.int32)[None]
    near_at = jnp.where(upper, far_steps, 0).astype(jnp.int32)[None]
    shared = (state, a, left, right, band, *atm, flux_weight)
    partly, *chunks, flux = second_block(False, members, far_at, *shared, [], small, far_steps)
    sent = [
        lax.ppermute(chunk, "member", [(i, i ^ (half + k)) for i in range(members)])
        for k, chunk in enumerate(chunks)
    ]
    state, *chunks = second_block(True, members, near_at, *shared, [partly, flux], small, near_steps)
    sent += [
        lax.ppermute(chunks[k], "member", [(i, i ^ k) for i in range(members)])
        for k in range(half - 1, 0, -1)
    ]
    sent.append(chunks[0])

    mid, packed = force(members, sent, ocean, land_mask, ice_mask, flux_lift)
    left, right = neighbours(packed)
    a, band = convolve(None, mid, ocn_kernel, 0, blocks)
    ocean_rows, surface = ocean_block(
        mid, a, left, right, band, land_mask, ocn_gain, ocn_up, ocn_down, ocn_scale, surf_weight
    )
    surface = lax.all_gather(surface, "member")
    out = couple(state, surface, land_mask, back_weight)
    return (out[None], ocean_rows)


def solution(mesh):
    in_specs = (
        P("member", None, None, "lon"),
        P(None, None, "lon"),
        P(None, "lon"),
        P(None, "lon"),
    ) + (P(),) * 14
    out_specs = (P("member", None, None, "lon"), P("member", None, "lon"))
    return jax.shard_map(local, mesh=mesh, in_specs=in_specs, out_specs=out_specs, check_vma=False)
```

time: 117 us -> 105 us (0.90)
  waiting for transfers between devices: 23.6 us -> 7.66 us
  local copies, waits for them, and re-layouts: 6.33 us -> 10.5 us
  Pallas kernels: 57.6 us -> 53.6 us
  starting transfers between devices: 18.3 us -> 22 us
    ppermute x3, waiting for transfers between devices: 9.66 us -> 0.01 us  [neighbours(): lax.ppermute(packed, 'lon', [(i, (i + 1) % count) for i in range(count)])]
    unnamed x45 -> x49, local copies, waits for them, and re-layouts: 6.33 us -> 10.5 us
    pallas_call x5 -> x9, Pallas kernels: 53.3 us -> 49.4 us  [the longest x3 22.7 us: convolve(): pl.pallas_call(functools.partial(conv_kernel, layer, pad), grid=(groups,)...]
    ppermute x7, waiting for transfers between devices: 11.1 us -> 7.32 us  [the longest x4 6.44 us: local(): lax.ppermute(chunk, 'member', [(i, i ^ half + k) for i in range(members)])]
    ppermute x7, starting transfers between devices: 5.54 us -> 9.12 us  [the longest x4 6.91 us: local(): lax.ppermute(chunk, 'member', [(i, i ^ half + k) for i in range(members)])]
    ppermute x3, waiting for transfers between devices: 2.89 us -> 0.33 us  [neighbours(): lax.ppermute(packed, 'lon', [((i + 1) % count, i) for i in range(count)])]
    ppermute x3, starting transfers between devices: 8.26 us -> 9.71 us  [neighbours(): lax.ppermute(packed, 'lon', [((i + 1) % count, i) for i in range(count)])]
    ppermute x3, starting transfers between devices: 4.49 us -> 3.19 us  [neighbours(): lax.ppermute(packed, 'lon', [(i, (i + 1) % count) for i in range(count)])]
  transfers between devices with their start and end apart: 13 -> 13, of which waited for: 11 -> 3; matrix products, arithmetic and copies ran while one was open for 2% -> 1% of each run, Pallas kernels for 0% -> 22%
where the time goes in v2:
time: 105 us; the launch traced here: 104 us
  Pallas kernels  53.6 us (51%)
  starting transfers between devices  22 us (21%)
  local copies, waits for them, and re-layouts  10.5 us (10%)
  blocking collectives  9.37 us (9%)
  waiting for transfers between devices  7.66 us (7%)
    pallas_call x3, Pallas kernels, convolve(): pl.pallas_call(functools.partial(conv_kernel, layer, pad), grid=(groups,)...  22.7 us
    pallas_call x2, Pallas kernels, second_block(): pl.pallas_call(functools.partial(second_kernel, near, members), out_shape...  11.6 us
    unnamed x49, local copies, waits for them, and re-layouts  10.5 us
    ppermute x3, starting transfers between devices, neighbours(): lax.ppermute(packed, 'lon', [((i + 1) % count, i) for i in range(count)])  9.71 us
    all_gather x1, blocking collectives, local(): surface = lax.all_gather(surface, 'member')  9.37 us
    pallas_call x1, Pallas kernels, first_block(): pl.pallas_call(first_kernel, grid=(rows // step,), out_shape=[jax.ShapeDt...  8.56 us
    ppermute x4, starting transfers between devices, local(): lax.ppermute(chunk, 'member', [(i, i ^ half + k) for i in range(members)])  6.91 us
    ppermute x4, waiting for transfers between devices, local(): lax.ppermute(chunk, 'member', [(i, i ^ half + k) for i in range(members)])  6.44 us
  transfers between devices with their start and end apart: 13, of which 3 were waited for; matrix products, arithmetic and copies ran while one was open for 1% of the time, Pallas kernels for 22%

profile of v2, /device:TPU:0, one launch (start us, length us, event | category | flops | bytes accessed | tf_op | source)
XLA Modules:
  0.0 104.2 jit_solution(13730820513119832793)
XLA Ops:
  0.6 0.0 copy-start
  0.6 1.7 %copy-done = bf16[1,96,96,128]{3,2,1,0:T(8,128)(2,1)S(1)} copy-done((bf16[1,96,96,128]{3,2,1,0:T(8,128)(2,1)S(1)}, bf16[1,96,96,128]{3,2,1,0:T(8,128)(2,1)}, u32[]{:S(2)}) %copy-start) | copy-done | bytes 2359320
  2.3 2.4 %pack_edges.1 = bf16[6,96,128]{2,1,0:T(8,128)(2,1)S(1)} custom-call(bf16[96,96,128]{2,1,0:T(8,128)(2,1)S(1)} %bitcast.7), custom_call_target="tpu_custom_call" | custom-call | tf_op jit(solution)/shard_map/pack_edges/pallas_call | solution.py:80
  4.8 3.1 %collective-permute-start = (bf16[6,96,128]{2,1,0:T(8,128)(2,1)S(1)}, bf16[6,96,128]{2,1,0:T(8,128)(2,1)S(1)}, u32[]{:S(2)}, u32[]{:S(2)}) collective-permute-start(bf16[6,96,128]{2,1,0:T(8,128)(2,1)S(1)} %pack_edges.1), channel_id=1, source_target_pairs={{0,1},{1,2},{2,3},{3,0},{4,5},{5,6},{6,7},{7,4},{8,9},{9,10},{10,1... | collective-permute-start | bytes 442376 | tf_op jit(solution)/shard_map/ppermute | solution.py:93
  7.8 2.1 %collective-permute-start.1 = (bf16[6,96,128]{2,1,0:T(8,128)(2,1)S(1)}, bf16[6,96,128]{2,1,0:T(8,128)(2,1)S(1)}, u32[]{:S(2)}, u32[]{:S(2)}) collective-permute-start(bf16[6,96,128]{2,1,0:T(8,128)(2,1)S(1)} %pack_edges.1), channel_id=1, source_target_pairs={{1,0},{2,1},{3,2},{0,3},{5,4},{6,5},{7,6},{4,7},{9,8},{10,9},{11,1... | collective-permute-start | bytes 442376 | tf_op jit(solution)/shard_map/ppermute | solution.py:94
  9.9 0.0 copy-done.19
  9.9 0.0 copy-done.1
  9.9 0.0 copy-start.18
  10.0 0.0 copy-start.20
  10.0 0.0 copy-start.4
  10.0 0.0 copy-start.9
  10.0 0.0 copy-start.10
  10.0 9.2 %conv.3 = (f32[96,96,128]{2,1,0:T(8,128)S(1)}, bf16[6,96,1792]{2,1,0:T(8,128)(2,1)S(1)}) custom-call(bf16[96,96,128]{2,1,0:T(8,128)(2,1)S(1)} %bitcast.8, f32[2,7,7,96]{3,2,1,0:T(8,128)S(1)} %copy.30.k_ref), custom_call_target="tpu_custom_call" | custom-call | flops 8000000000 | tf_op jit(solution)/shard_map/conv/pallas_call | solution.py:184
  19.2 2.1 %copy-done.14 = f32[96,96,128]{2,1,0:T(8,128)} copy-done((f32[96,96,128]{2,1,0:T(8,128)}, f32[96,96,128]{2,1,0:T(8,128)S(1)}, u32[]{:S(2)}) %copy-start.14) | copy-done | bytes 4718616
  21.4 1.3 %copy-done.16 = bf16[6,96,1792]{2,1,0:T(8,128)(2,1)} copy-done((bf16[6,96,1792]{2,1,0:T(8,128)(2,1)}, bf16[6,96,1792]{2,1,0:T(8,128)(2,1)S(1)}, u32[]{:S(2)}) %copy-start.16) | copy-done | bytes 2064408
  22.7 0.2 copy.31.dn_ref.refs_7_
  22.8 0.1 copy.36.refs_9_
  23.0 0.0 collective-permute-done.left_ref
  23.0 0.0 collective-permute-done.1.right_ref
  23.0 2.3 %copy-done.15 = f32[96,96,128]{2,1,0:T(8,128)S(1)} copy-done((f32[96,96,128]{2,1,0:T(8,128)S(1)}, f32[96,96,128]{2,1,0:T(8,128)}, u32[]{:S(2)}) %copy-start.15) | copy-done | bytes 4718616
  25.4 1.6 %copy-done.17 = bf16[6,96,1792]{2,1,0:T(8,128)(2,1)S(1)} copy-done((bf16[6,96,1792]{2,1,0:T(8,128)(2,1)S(1)}, bf16[6,96,1792]{2,1,0:T(8,128)(2,1)}, u32[]{:S(2)}) %copy-start.17) | copy-done | bytes 2064408
  26.9 8.6 %first_block.1 = (bf16[96,96,128]{2,1,0:T(8,128)(2,1)S(1)}, bf16[6,96,128]{2,1,0:T(8,128)(2,1)S(1)}) custom-call(bf16[96,96,128]{2,1,0:T(8,128)(2,1)S(1)} %bitcast.9, f32[96,96,128]{2,1,0:T(8,128)S(1)} %copy-done.15, bf16[6,96,128]{2,1,0:T(8,128)(2,1)S(1)} %collective-permute-done.left_ref, bf16[6,96,128]{2,1,0:T(8,128)(2,1)S(1)} %collective-permute-done.1.right_ref, ...), custom_call_target="tpu_custom_call" | custom-call | flops 8000000000 | tf_op jit(solution)/shard_map/first_block/pallas_call | solution.py:309
  35.5 0.1 collective-permute-start.2
  35.6 3.8 %collective-permute-start.3 = (bf16[6,96,128]{2,1,0:T(8,128)(2,1)S(1)}, bf16[6,96,128]{2,1,0:T(8,128)(2,1)S(1)}, u32[]{:S(2)}, u32[]{:S(2)}) collective-permute-start(bf16[6,96,128]{2,1,0:T(8,128)(2,1)S(1)} %get-tuple-element.29), channel_id=1, source_target_pairs={{1,0},{2,1},{3,2},{0,3},{5,4},{6,5},{7,6},{4,7},{9,8},{10,9},{11,1... | collective-permute-start | bytes 442376 | tf_op jit(solution)/shard_map/ppermute | solution.py:94
  39.4 9.2 %conv.4 = (f32[96,96,128]{2,1,0:T(8,128)S(1)}, bf16[6,96,1792]{2,1,0:T(8,128)(2,1)S(1)}) custom-call(bf16[96,96,128]{2,1,0:T(8,128)(2,1)S(1)} %get-tuple-element.27.x_ref.refs_0_, f32[2,7,7,96]{3,2,1,0:T(8,128)S(1)} %copy.30.k_ref), custom_call_target="tpu_custom_call" | custom-call | flops 8000000000 | tf_op jit(solution)/shard_map/conv/pallas_call | solution.py:184
  48.6 0.0 collective-permute-done.2.refs_2_
  48.6 0.0 collective-permute-done.3.refs_3_
  48.6 6.8 %second_block.2 = (bf16[96,96,128]{2,1,0:T(8,128)(2,1)S(1)}, bf16[18,32,128]{2,1,0:T(8,128)(2,1)S(1)}, bf16[18,32,128]{2,1,0:T(8,128)(2,1)S(1)}, bf16[18,32,128]...) custom-call(s32[1]{0:T(128)} %bitcast.2.at_ref, ...), custom_call_target="tpu_custom_call" | custom-call | flops 5000000000 | tf_op jit(solution)/shard_map/second_block/pallas_call | solution.py:416
  55.4 0.0 copy-start.2
  55.4 0.0 copy-start.3
  55.5 0.0 copy-start.6
  55.5 0.0 copy-start.7
  55.5 4.8 %second_block.3 = (bf16[96,96,128]{2,1,0:T(8,128)(2,1)S(1)}, bf16[18,32,128]{2,1,0:T(8,128)(2,1)S(1)}, bf16[18,32,128]{2,1,0:T(8,128)(2,1)S(1)}, bf16[18,32,128]...) custom-call(s32[1]{0:T(128)} %bitcast.at_ref, ...), custom_call_target="tpu_custom_call", output_to_operand_aliasing={{0}: (11, {})} | custom-call | flops 3000000000 | tf_op jit(solution)/shard_map/second_block/pallas_call | solution.py:416
  60.2 0.0 copy-start.21
  60.3 0.0 copy-start.13
  60.3 0.1 collective-permute-start.10
  60.4 1.7 %collective-permute-start.8 = (bf16[18,32,128]{2,1,0:T(8,128)(2,1)S(1)}, bf16[18,32,128]{2,1,0:T(8,128)(2,1)S(1)}, u32[]{:S(2)}, u32[]{:S(2)}) collective-permute-start(bf16[18,32,128]{2,1,0:T(8,128)(2,1)S(1)} %get-tuple-element.38), channel_id=1, source_target_pairs={{0,12},{4,8},{8,4},{12,0},{16,28},{20,24},{24,20},{28,16},{1,13},{... | collective-permute-start | bytes 442376 | tf_op jit(solution)/shard_map/ppermute | solution.py:614
  62.1 0.4 collective-permute-start.9
  62.5 1.7 %collective-permute-start.4 = (bf16[18,32,128]{2,1,0:T(8,128)(2,1)S(1)}, bf16[18,32,128]{2,1,0:T(8,128)(2,1)S(1)}, u32[]{:S(2)}, u32[]{:S(2)}) collective-permute-start(bf16[18,32,128]{2,1,0:T(8,128)(2,1)S(1)} %get-tuple-element.34), channel_id=1, source_target_pairs={{0,16},{4,20},{8,24},{12,28},{16,0},{20,4},{24,8},{28,12},{1,17},{... | collective-permute-start | bytes 442376 | tf_op jit(solution)/shard_map/ppermute | solution.py:609
  64.2 0.0 collective-permute-start.5
  64.2 0.0 collective-permute-done.10.refs_6_
  64.2 2.0 %collective-permute-start.6 = (bf16[18,32,128]{2,1,0:T(8,128)(2,1)S(1)}, bf16[18,32,128]{2,1,0:T(8,128)(2,1)S(1)}, u32[]{:S(2)}, u32[]{:S(2)}) collective-permute-start(bf16[18,32,128]{2,1,0:T(8,128)(2,1)S(1)} %get-tuple-element.36), channel_id=1, source_target_pairs={{0,24},{4,28},{8,16},{12,20},{16,8},{20,12},{24,0},{28,4},{1,25},{... | collective-permute-start | bytes 442376 | tf_op jit(solution)/shard_map/ppermute | solution.py:609
  66.2 0.0 collective-permute-done.8.refs_4_
  66.3 3.2 %collective-permute-start.7 = (bf16[18,32,128]{2,1,0:T(8,128)(2,1)S(1)}, bf16[18,32,128]{2,1,0:T(8,128)(2,1)S(1)}, u32[]{:S(2)}, u32[]{:S(2)}) collective-permute-start(bf16[18,32,128]{2,1,0:T(8,128)(2,1)S(1)} %get-tuple-element.37), channel_id=1, source_target_pairs={{0,28},{4,24},{8,20},{12,16},{16,12},{20,8},{24,4},{28,0},{1,29},{... | collective-permute-start | bytes 442376 | tf_op jit(solution)/shard_map/ppermute | solution.py:609
  69.5 0.8 collective-permute-done.9.refs_5_
  70.3 0.0 collective-permute-done.4.refs_0_
  70.3 6.4 %collective-permute-done.5.refs_1_ = bf16[18,32,128]{2,1,0:T(8,128)(2,1)S(1)} collective-permute-done((bf16[18,32,128]{2,1,0:T(8,128)(2,1)S(1)}, bf16[18,32,128]{2,1,0:T(8,128)(2,1)S(1)}, u32[]{:S(2)}, u32[]{:S(2)}) %collective-permute-start.5) | collective-permute-done | bytes 147488 | tf_op jit(solution)/shard_map/ppermute | solution.py:609
  76.7 0.0 collective-permute-done.6.refs_2_
  76.7 0.0 collective-permute-done.7.refs_3_
  76.8 1.0 ocean_forcing.1
  77.8 0.0 copy-start.5
  77.8 0.0 copy-start.11
  77.8 0.0 copy-start.12
  77.8 0.1 collective-permute-start.11
  77.9 3.8 %collective-permute-start.12 = (bf16[6,96,128]{2,1,0:T(8,128)(2,1)S(1)}, bf16[6,96,128]{2,1,0:T(8,128)(2,1)S(1)}, u32[]{:S(2)}, u32[]{:S(2)}) collective-permute-start(bf16[6,96,128]{2,1,0:T(8,128)(2,1)S(1)} %get-tuple-element.44), channel_id=1, source_target_pairs={{1,0},{2,1},{3,2},{0,3},{5,4},{6,5},{7,6},{4,7},{9,8},{10,9},{11,1... | collective-permute-start | bytes 442376 | tf_op jit(solution)/shard_map/ppermute | solution.py:94
  81.7 1.0 copy.37.dn_ref
  82.7 0.1 copy.38.sw_ref
  82.8 4.3 %conv.5 = (f32[12,96,128]{2,1,0:T(8,128)S(1)}, bf16[6,96,1792]{2,1,0:T(8,128)(2,1)S(1)}) custom-call(bf16[18,96,128]{2,1,0:T(8,128)(2,1)S(1)} %get-tuple-element.42.x_ref.mid_ref, f32[7,7,96]{2,1,0:T(8,128)S(1)} %copy-done.13), custom_call_target="tpu_custom_call" | custom-call | flops 1000000000 | tf_op jit(solution)/shard_map/conv/pallas_call | solution.py:184
  87.1 0.0 copy-start.8
  87.1 0.0 collective-permute-done.11.left_ref
  87.1 0.3 collective-permute-done.12.right_ref
  87.5 3.1 %ocean_block.1 = (bf16[12,96,128]{2,1,0:T(8,128)(2,1)}, bf16[12,8,128]{2,1,0:T(8,128)(2,1)S(1)}) custom-call(bf16[18,96,128]{2,1,0:T(8,128)(2,1)S(1)} %get-tuple-element.42.x_ref.mid_ref, f32[12,96,128]{2,1,0:T(8,128)S(1)} %get-tuple-element.43.a_ref, bf16[6,96,128]{2,1,0:T(8,128)(2,1)S(1)} %collective-permute-done.11.left_ref, ...), custom_call_target="tpu_custom_call" | custom-call | tf_op jit(solution)/shard_map/ocean_block/pallas_call | solution.py:518
  90.6 9.4 %all-gather = bf16[96,8,128]{2,1,0:T(8,128)(2,1)S(1)} all-gather(bf16[12,8,128]{2,1,0:T(8,128)(2,1)S(1)} %get-tuple-element.46), channel_id=2, replica_groups=mesh['member'=8,'lon'=4] {'member'}, dimensions={0}, use_global_device_ids=true | all-gather | bytes 221184 | tf_op jit(solution)/shard_map/all_gather | solution.py:625
  100.0 4.3 %couple.1 = bf16[96,96,128]{2,1,0:T(8,128)(2,1)} custom-call(bf16[96,96,128]{2,1,0:T(8,128)(2,1)S(1)} %get-tuple-element.33.y_ref, bf16[8,12,8,128]{3,2,1,0:T(8,128)(2,1)S(1)} %bitcast.10, s32[96,128]{1,0:T(8,128)S(1)} %copy-done.3, bf16[8,96]{1,0:T(8,128)(2,1)S(1)} %copy-done.8), custom_call_target="tpu_custom_call" | custom-call | tf_op jit(solution)/shard_map/couple/pallas_call | solution.py:550
  (22 shorter events, 0.0 us)
Async XLA Ops:
  0.6 1.7 %copy-start = (bf16[1,96,96,128]{3,2,1,0:T(8,128)(2,1)S(1)}, bf16[1,96,96,128]{3,2,1,0:T(8,128)(2,1)}, u32[]{:S(2)}) copy-start(bf16[1,96,96,128]{3,2,1,0:T(8,128)(2,1)} %param.18) | copy-start | bytes 7077892
  2.3 7.6 %copy-start.19 = (f32[2,7,7,96]{3,0,2,1:T(2,128)S(1)}, f32[2,7,7,96]{3,0,2,1:T(2,128)}, u32[]{:S(2)}) copy-start(f32[2,7,7,96]{3,0,2,1:T(2,128)} %param.22) | copy-start | bytes 112900
  2.3 7.6 %copy-start.1 = (bf16[1,96,96,128]{3,2,1,0:T(8,128)(2,1)S(1)}, bf16[1,96,96,128]{3,2,1,0:T(8,128)(2,1)}, u32[]{:S(2)}) copy-start(bf16[1,96,96,128]{3,2,1,0:T(8,128)(2,1)} %param.18) | copy-start | bytes 7077892
  4.8 18.2 %collective-permute-start = (bf16[6,96,128]{2,1,0:T(8,128)(2,1)S(1)}, bf16[6,96,128]{2,1,0:T(8,128)(2,1)S(1)}, u32[]{:S(2)}, u32[]{:S(2)}) collective-permute-start(bf16[6,96,128]{2,1,0:T(8,128)(2,1)S(1)} %pack_edges.1), channel_id=1, source_target_pairs={{0,1},{1,2},{2,3},{3,0},{4,5},{5,6},{6,7},{7,4},{8,9},{9,10},{10,1... | collective-permute-start | bytes 442376 | tf_op jit(solution)/shard_map/ppermute | solution.py:93
  7.8 15.1 %collective-permute-start.1 = (bf16[6,96,128]{2,1,0:T(8,128)(2,1)S(1)}, bf16[6,96,128]{2,1,0:T(8,128)(2,1)S(1)}, u32[]{:S(2)}, u32[]{:S(2)}) collective-permute-start(bf16[6,96,128]{2,1,0:T(8,128)(2,1)S(1)} %pack_edges.1), channel_id=1, source_target_pairs={{1,0},{2,1},{3,2},{0,3},{5,4},{6,5},{7,6},{4,7},{9,8},{10,9},{11,1... | collective-permute-start | bytes 442376 | tf_op jit(solution)/shard_map/ppermute | solution.py:94
  9.9 12.7 %copy-start.18 = (bf16[2,384,96]{1,2,0:T(8,128)(2,1)S(1)}, bf16[2,384,96]{1,2,0:T(8,128)(2,1)}, u32[]{:S(2)}) copy-start(bf16[2,384,96]{1,2,0:T(8,128)(2,1)} %param.25) | copy-start | bytes 442372
  10.0 12.9 %copy-start.20 = (bf16[96,32]{0,1:T(8,128)(2,1)S(1)}, bf16[96,32]{0,1:T(8,128)(2,1)}, u32[]{:S(2)}) copy-start(bf16[96,32]{0,1:T(8,128)(2,1)} %param.27) | copy-start | bytes 18436
  10.0 13.0 %copy-start.4 = (bf16[2,96,384]{2,1,0:T(8,128)(2,1)S(1)}, bf16[2,96,384]{2,1,0:T(8,128)(2,1)}, u32[]{:S(2)}) copy-start(bf16[2,96,384]{2,1,0:T(8,128)(2,1)} %refs_6_.3) | copy-start | bytes 442372
  10.0 13.0 %copy-start.9 = (f32[2,96]{1,0:T(2,128)S(1)}, f32[2,96]{1,0:T(2,128)}, u32[]{:S(2)}) copy-start(f32[2,96]{1,0:T(2,128)} %refs_5_.3) | copy-start | bytes 2308
  10.0 13.0 %copy-start.10 = (f32[2,96]{1,0:T(2,128)S(1)}, f32[2,96]{1,0:T(2,128)}, u32[]{:S(2)}) copy-start(f32[2,96]{1,0:T(2,128)} %refs_8_.4) | copy-start | bytes 2308
  19.2 2.1 %copy-start.14 = (f32[96,96,128]{2,1,0:T(8,128)}, f32[96,96,128]{2,1,0:T(8,128)S(1)}, u32[]{:S(2)}) copy-start(f32[96,96,128]{2,1,0:T(8,128)S(1)} %get-tuple-element.25.a_ref) | copy-start | bytes 14155780
  21.4 1.3 %copy-start.16 = (bf16[6,96,1792]{2,1,0:T(8,128)(2,1)}, bf16[6,96,1792]{2,1,0:T(8,128)(2,1)S(1)}, u32[]{:S(2)}) copy-start(bf16[6,96,1792]{2,1,0:T(8,128)(2,1)S(1)} %get-tuple-element.26.band_ref) | copy-start | bytes 6193156
  23.0 2.3 %copy-start.15 = (f32[96,96,128]{2,1,0:T(8,128)S(1)}, f32[96,96,128]{2,1,0:T(8,128)}, u32[]{:S(2)}) copy-start(f32[96,96,128]{2,1,0:T(8,128)} %copy-done.14) | copy-start | bytes 14155780
  25.4 1.6 %copy-start.17 = (bf16[6,96,1792]{2,1,0:T(8,128)(2,1)S(1)}, bf16[6,96,1792]{2,1,0:T(8,128)(2,1)}, u32[]{:S(2)}) copy-start(bf16[6,96,1792]{2,1,0:T(8,128)(2,1)} %copy-done.16) | copy-start | bytes 6193156
  35.5 13.1 %collective-permute-start.2 = (bf16[6,96,128]{2,1,0:T(8,128)(2,1)S(1)}, bf16[6,96,128]{2,1,0:T(8,128)(2,1)S(1)}, u32[]{:S(2)}, u32[]{:S(2)}) collective-permute-start(bf16[6,96,128]{2,1,0:T(8,128)(2,1)S(1)} %get-tuple-element.29), channel_id=1, source_target_pairs={{0,1},{1,2},{2,3},{3,0},{4,5},{5,6},{6,7},{7,4},{8,9},{9,10},{10,1... | collective-permute-start | bytes 442376 | tf_op jit(solution)/shard_map/ppermute | solution.py:93
  35.6 13.0 %collective-permute-start.3 = (bf16[6,96,128]{2,1,0:T(8,128)(2,1)S(1)}, bf16[6,96,128]{2,1,0:T(8,128)(2,1)S(1)}, u32[]{:S(2)}, u32[]{:S(2)}) collective-permute-start(bf16[6,96,128]{2,1,0:T(8,128)(2,1)S(1)} %get-tuple-element.29), channel_id=1, source_target_pairs={{1,0},{2,1},{3,2},{0,3},{5,4},{6,5},{7,6},{4,7},{9,8},{10,9},{11,1... | collective-permute-start | bytes 442376 | tf_op jit(solution)/shard_map/ppermute | solution.py:94
  55.4 21.3 %copy-start.2 = (bf16[96,96,128]{2,1,0:T(8,128)(2,1)S(1)}, bf16[96,96,128]{2,1,0:T(8,128)(2,1)}, u32[]{:S(2)}) copy-start(bf16[96,96,128]{2,1,0:T(8,128)(2,1)} %refs_8_.5) | copy-start | bytes 7077892
  55.4 21.3 %copy-start.3 = (s32[96,128]{1,0:T(8,128)S(1)}, s32[96,128]{1,0:T(8,128)}, u32[]{:S(2)}) copy-start(s32[96,128]{1,0:T(8,128)} %land_ref.3) | copy-start | bytes 147460
  55.5 21.3 %copy-start.6 = (s32[96,128]{1,0:T(8,128)S(1)}, s32[96,128]{1,0:T(8,128)}, u32[]{:S(2)}) copy-start(s32[96,128]{1,0:T(8,128)} %refs_10_.1) | copy-start | bytes 147460
  55.5 21.3 %copy-start.7 = (bf16[2,32,96]{2,1,0:T(8,128)(2,1)S(1)}, bf16[2,32,96]{2,1,0:T(8,128)(2,1)}, u32[]{:S(2)}) copy-start(bf16[2,32,96]{2,1,0:T(8,128)(2,1)} %refs_11_.1) | copy-start | bytes 36868
  60.2 22.5 %copy-start.21 = (bf16[96,8]{0,1:T(8,128)(2,1)S(1)}, bf16[96,8]{0,1:T(8,128)(2,1)}, u32[]{:S(2)}) copy-start(bf16[96,8]{0,1:T(8,128)(2,1)} %param.34) | copy-start | bytes 4612
  60.3 22.6 %copy-start.13 = (f32[7,7,96]{2,1,0:T(8,128)S(1)}, f32[7,7,96]{2,1,0:T(8,128)}, u32[]{:S(2)}) copy-start(f32[7,7,96]{2,1,0:T(8,128)} %k_ref.3) | copy-start | bytes 56452
  60.3 3.9 %collective-permute-start.10 = (bf16[18,32,128]{2,1,0:T(8,128)(2,1)S(1)}, bf16[18,32,128]{2,1,0:T(8,128)(2,1)S(1)}, u32[]{:S(2)}, u32[]{:S(2)}) collective-permute-start(bf16[18,32,128]{2,1,0:T(8,128)(2,1)S(1)} %get-tuple-element.40), channel_id=1, source_target_pairs={{0,4},{4,0},{8,12},{12,8},{16,20},{20,16},{24,28},{28,24},{1,5},{5... | collective-permute-start | bytes 442376 | tf_op jit(solution)/shard_map/ppermute | solution.py:614
  60.4 5.9 %collective-permute-start.8 = (bf16[18,32,128]{2,1,0:T(8,128)(2,1)S(1)}, bf16[18,32,128]{2,1,0:T(8,128)(2,1)S(1)}, u32[]{:S(2)}, u32[]{:S(2)}) collective-permute-start(bf16[18,32,128]{2,1,0:T(8,128)(2,1)S(1)} %get-tuple-element.38), channel_id=1, source_target_pairs={{0,12},{4,8},{8,4},{12,0},{16,28},{20,24},{24,20},{28,16},{1,13},{... | collective-permute-start | bytes 442376 | tf_op jit(solution)/shard_map/ppermute | solution.py:614
  62.1 8.2 %collective-permute-start.9 = (bf16[18,32,128]{2,1,0:T(8,128)(2,1)S(1)}, bf16[18,32,128]{2,1,0:T(8,128)(2,1)S(1)}, u32[]{:S(2)}, u32[]{:S(2)}) collective-permute-start(bf16[18,32,128]{2,1,0:T(8,128)(2,1)S(1)} %get-tuple-element.39), channel_id=1, source_target_pairs={{0,8},{4,12},{8,0},{12,4},{16,24},{20,28},{24,16},{28,20},{1,9},{5... | collective-permute-start | bytes 442376 | tf_op jit(solution)/shard_map/ppermute | solution.py:614
  62.5 7.8 %collective-permute-start.4 = (bf16[18,32,128]{2,1,0:T(8,128)(2,1)S(1)}, bf16[18,32,128]{2,1,0:T(8,128)(2,1)S(1)}, u32[]{:S(2)}, u32[]{:S(2)}) collective-permute-start(bf16[18,32,128]{2,1,0:T(8,128)(2,1)S(1)} %get-tuple-element.34), channel_id=1, source_target_pairs={{0,16},{4,20},{8,24},{12,28},{16,0},{20,4},{24,8},{28,12},{1,17},{... | collective-permute-start | bytes 442376 | tf_op jit(solution)/shard_map/ppermute | solution.py:609
  64.2 12.5 %collective-permute-start.5 = (bf16[18,32,128]{2,1,0:T(8,128)(2,1)S(1)}, bf16[18,32,128]{2,1,0:T(8,128)(2,1)S(1)}, u32[]{:S(2)}, u32[]{:S(2)}) collective-permute-start(bf16[18,32,128]{2,1,0:T(8,128)(2,1)S(1)} %get-tuple-element.35), channel_id=1, source_target_pairs={{0,20},{4,16},{8,28},{12,24},{16,4},{20,0},{24,12},{28,8},{1,21},{... | collective-permute-start | bytes 442376 | tf_op jit(solution)/shard_map/ppermute | solution.py:609
  64.2 12.5 %collective-permute-start.6 = (bf16[18,32,128]{2,1,0:T(8,128)(2,1)S(1)}, bf16[18,32,128]{2,1,0:T(8,128)(2,1)S(1)}, u32[]{:S(2)}, u32[]{:S(2)}) collective-permute-start(bf16[18,32,128]{2,1,0:T(8,128)(2,1)S(1)} %get-tuple-element.36), channel_id=1, source_target_pairs={{0,24},{4,28},{8,16},{12,20},{16,8},{20,12},{24,0},{28,4},{1,25},{... | collective-permute-start | bytes 442376 | tf_op jit(solution)/shard_map/ppermute | solution.py:609
  66.3 10.5 %collective-permute-start.7 = (bf16[18,32,128]{2,1,0:T(8,128)(2,1)S(1)}, bf16[18,32,128]{2,1,0:T(8,128)(2,1)S(1)}, u32[]{:S(2)}, u32[]{:S(2)}) collective-permute-start(bf16[18,32,128]{2,1,0:T(8,128)(2,1)S(1)} %get-tuple-element.37), channel_id=1, source_target_pairs={{0,28},{4,24},{8,20},{12,16},{16,12},{20,8},{24,4},{28,0},{1,29},{... | collective-permute-start | bytes 442376 | tf_op jit(solution)/shard_map/ppermute | solution.py:609
  77.8 9.7 %copy-start.5 = (bf16[96,384]{1,0:T(8,128)(2,1)S(1)}, bf16[96,384]{1,0:T(8,128)(2,1)}, u32[]{:S(2)}) copy-start(bf16[96,384]{1,0:T(8,128)(2,1)} %up_ref.3) | copy-start | bytes 221188
  77.8 9.7 %copy-start.11 = (f32[96]{0:T(128)S(1)}, f32[96]{0:T(128)}, u32[]{:S(2)}) copy-start(f32[96]{0:T(128)} %param.30) | copy-start | bytes 1156
  77.8 9.7 %copy-start.12 = (f32[96]{0:T(128)S(1)}, f32[96]{0:T(128)}, u32[]{:S(2)}) copy-start(f32[96]{0:T(128)} %param.33) | copy-start | bytes 1156
  77.8 9.3 %collective-permute-start.11 = (bf16[6,96,128]{2,1,0:T(8,128)(2,1)S(1)}, bf16[6,96,128]{2,1,0:T(8,128)(2,1)S(1)}, u32[]{:S(2)}, u32[]{:S(2)}) collective-permute-start(bf16[6,96,128]{2,1,0:T(8,128)(2,1)S(1)} %get-tuple-element.44), channel_id=1, source_target_pairs={{0,1},{1,2},{2,3},{3,0},{4,5},{5,6},{6,7},{7,4},{8,9},{9,10},{10,1... | collective-permute-start | bytes 442376 | tf_op jit(solution)/shard_map/ppermute | solution.py:93
  77.9 9.6 %collective-permute-start.12 = (bf16[6,96,128]{2,1,0:T(8,128)(2,1)S(1)}, bf16[6,96,128]{2,1,0:T(8,128)(2,1)S(1)}, u32[]{:S(2)}, u32[]{:S(2)}) collective-permute-start(bf16[6,96,128]{2,1,0:T(8,128)(2,1)S(1)} %get-tuple-element.44), channel_id=1, source_target_pairs={{1,0},{2,1},{3,2},{0,3},{5,4},{6,5},{7,6},{4,7},{9,8},{10,9},{11,1... | collective-permute-start | bytes 442376 | tf_op jit(solution)/shard_map/ppermute | solution.py:94
  87.1 12.8 %copy-start.8 = (bf16[8,96]{1,0:T(8,128)(2,1)S(1)}, bf16[8,96]{1,0:T(8,128)(2,1)}, u32[]{:S(2)}) copy-start(bf16[8,96]{1,0:T(8,128)(2,1)} %bw_ref.1) | copy-start | bytes 4612

commit v3 on v2

--- a/solution.py
+++ b/solution.py
@@ -19,6 +19,7 @@
 DEPTH = GROUP * SPAN
 SLOT = 8
 SLOTS = 16
+OCEAN_BLOCKS = 2
 BY_DOT = (0, 1, 5, 6)
 VMEM = pl.BlockSpec(memory_space=pltpu.VMEM)
 ANY = pl.BlockSpec(memory_space=pl.ANY)
@@ -36,8 +37,12 @@
     return z + z * jnp.tanh(z * (TANH_A + TANH_B * (z * z)))
 
 
-def transposed(value, factor):
-    return (value.astype(F32).T * factor).astype(BF)
+def transposed(value):
+    return value.astype(F32).T.astype(BF)
+
+
+def halved(value):
+    return (0.5 * value.astype(F32)).astype(BF)
 
 
 def spread(row, lanes):
@@ -83,7 +88,7 @@
         out_shape=jax.ShapeDtypeStruct((blocks, chans, lanes), BF),
         in_specs=[pl.BlockSpec((step, chans, lanes), lambda i: (i, 0, 0))],
         out_specs=pl.BlockSpec((blocks, chans, lanes), lambda i: (0, 0, 0)),
-        compiler_params=params(16),
+        compiler_params=params(24),
         name="pack_edges",
     )(x)
 
@@ -129,7 +134,7 @@
 
     @pl.when(g == 0)
     def _():
-        fill_base(lambda i: k_ref[layer, i] if layer is not None else k_ref[i], base)
+        fill_base(lambda i: k_ref[i, :, layer, :] if layer is not None else k_ref[i], base)
         smat[...] = shift_matrix(lanes)
         for j in range(TAPS):
             if pad:
@@ -199,7 +204,7 @@
             pltpu.VMEM((TAPS, tall, GROUP, lanes), BF),
             pltpu.VMEM((GROUP * OUT, wide), BF),
         ],
-        compiler_params=params(32),
+        compiler_params=params(24),
         cost_estimate=cost(8 * rows / 96),
         name="conv",
     )(x, taps)
@@ -232,8 +237,10 @@
     slot = (lane + HALO) // SLOT % SLOTS
 
     def turned(value, shift, drop):
-        keep = (slot != drop).astype(F32).astype(BF)
-        parts = [pltpu.roll(value[:, n * lanes : (n + 1) * lanes], shift, 1) * keep for n in range(2)]
+        parts = [pltpu.roll(value[:, n * lanes : (n + 1) * lanes], shift, 1) for n in range(2)]
+        if drop >= 0:
+            keep = (slot != drop).astype(F32).astype(BF)
+            parts = [part * keep for part in parts]
         return jnp.concatenate(parts, axis=1)
 
     if wrapped:
@@ -243,7 +250,10 @@
             + [turned(both[q], lanes - SLOT, SLOTS - 1) for q in range(HALO)]
         )
     else:
-        tall = both + [turned(both[q], lanes - SLOT, SLOTS - 1) for q in range(2 * HALO)]
+        tall = both + [
+            turned(both[e % blocks], lanes - SLOT * (e // blocks), -1)
+            for e in range(blocks, blocks + 2 * HALO)
+        ]
     field = jnp.concatenate(tall, axis=0)
     moved = jnp.dot(field, halo_matrix(lanes), preferred_element_type=F32)
     count = len(tall)
@@ -284,8 +294,8 @@
     @pl.when(step == 0)
     def _():
         halo_conv(left_ref, right_ref, band_ref, True, xe, halo)
-        up_t[...] = transposed(up_ref[0], 1.0)
-        dn_t[...] = transposed(dn_ref[0], 0.5)
+        up_t[...] = transposed(up_ref[0])
+        dn_t[...] = halved(dn_ref[0])
         gain[...] = spread(g_ref[0:1], lanes)
         scale[...] = spread(s_ref[0:1], lanes)
         p_ref[...] = jnp.zeros(p_ref.shape, BF)
@@ -323,7 +333,7 @@
             pltpu.VMEM((chans, lanes), F32),
             pltpu.VMEM((chans, lanes), F32),
         ],
-        compiler_params=params(40),
+        compiler_params=params(24),
         cost_estimate=cost(8),
         name="first_block",
     )(x, a, left, right, band, gain, up, down, scale)
@@ -338,7 +348,7 @@
     y_ref, refs = refs[0], refs[1:]
     half = members // 2
     chunk_refs, refs = refs[:half], refs[half:]
-    flux, xe, halo, up_t, dn_t, fw_t, gain, scale = refs
+    flux, xe, halo, up_t, dn_t, gain, scale = refs
     step = pl.program_id(0)
     count, chans, lanes = x_ref.shape
     blocks = halo.shape[0]
@@ -347,9 +357,8 @@
     @pl.when(step == 0)
     def _():
         halo_conv(left_ref, right_ref, band_ref, True, xe, halo)
-        up_t[...] = transposed(up_ref[1], 1.0)
-        dn_t[...] = transposed(dn_ref[1], 0.5)
-        fw_t[...] = transposed(fw_ref[...], 1.0)
+        up_t[...] = transposed(up_ref[1])
+        dn_t[...] = halved(dn_ref[1])
         gain[...] = spread(g_ref[1:2], lanes)
         scale[...] = spread(s_ref[1:2], lanes)
         if near:
@@ -366,7 +375,7 @@
         y = x_ref[r].astype(F32) + scale[...] * branch[:, r * lanes : (r + 1) * lanes]
         made.append(y.astype(BF))
         y_ref[r] = made[r]
-    z = jnp.dot(fw_t[...], jnp.concatenate(made, axis=1), preferred_element_type=F32)
+    z = jnp.dot(fw_ref[...], jnp.concatenate(made, axis=1), preferred_element_type=F32)
     f = (0.5 * twice_gelu(z)).astype(BF)
     for r in range(count):
         flux[row0 + HALO + r] = f[:, r * lanes : (r + 1) * lanes]
@@ -384,7 +393,7 @@
     rows, chans, lanes = x.shape
     blocks = rows // SLOTS
     hid = up.shape[2]
-    flux = flux_weight.shape[1]
+    flux = flux_weight.shape[0]
     half = members // 2
     share = rows // members
     part = pl.BlockSpec((step, chans, lanes), lambda i, s: (s[0] + i, 0, 0))
@@ -403,7 +412,6 @@
         pltpu.VMEM((blocks, chans, lanes), F32),
         pltpu.VMEM((hid, chans), BF),
         pltpu.VMEM((chans, hid), BF),
-        pltpu.VMEM((flux, chans), BF),
         pltpu.VMEM((chans, lanes), F32),
         pltpu.VMEM((chans, lanes), F32),
     ]
@@ -424,7 +432,7 @@
             scratch_shapes=scratch,
         ),
         input_output_aliases=alias,
-        compiler_params=params(40),
+        compiler_params=params(24),
         cost_estimate=cost(8 * steps * step / rows),
         name="second_block",
     )(*args)
@@ -446,7 +454,7 @@
     for ref in flux_refs[1:]:
         total = total + ref[...].astype(F32)
     low = (total / members).astype(BF)
-    lift = jnp.concatenate([transposed(lift_ref[0], 1.0), transposed(lift_ref[1], 1.0)], axis=0)
+    lift = jnp.concatenate([transposed(lift_ref[0]), transposed(lift_ref[1])], axis=0)
     terms = jnp.dot(
         lift, jnp.concatenate([low[r] for r in range(span)], axis=1), preferred_element_type=F32
     )
@@ -480,7 +488,7 @@
         functools.partial(force_kernel, members),
         out_shape=[
             jax.ShapeDtypeStruct((span, chans, lanes), BF),
-            jax.ShapeDtypeStruct((rows // SLOTS, chans, lanes), BF),
+            jax.ShapeDtypeStruct((OCEAN_BLOCKS, chans, lanes), BF),
         ],
         in_specs=[VMEM] * members + [ANY, VMEM, VMEM, VMEM],
         out_specs=[VMEM] * 2,
@@ -496,7 +504,7 @@
     gain = spread(g_ref[...], lanes)
     scale = spread(s_ref[...], lanes)
     branch = branch_of(
-        a_ref, halo, 0, gain, transposed(up_ref[...], 1.0), transposed(dn_ref[...], 0.5)
+        a_ref, halo, 0, gain, transposed(up_ref[...]), halved(dn_ref[...])
     )
     first = lax.axis_index("member") * share
     made = []
@@ -506,7 +514,7 @@
         made.append((y * sea).astype(BF))
         new_ref[r] = made[r]
     surf = jnp.dot(
-        transposed(sw_ref[...], 1.0), jnp.concatenate(made, axis=1), preferred_element_type=F32
+        sw_ref[...], jnp.concatenate(made, axis=1), preferred_element_type=F32
     )
     for r in range(share):
         surf_ref[r] = surf[:, r * lanes : (r + 1) * lanes].astype(BF)
@@ -519,7 +527,7 @@
         ocean_kernel,
         out_shape=[
             jax.ShapeDtypeStruct((share, chans, lanes), BF),
-            jax.ShapeDtypeStruct((share, surf_weight.shape[1], lanes), BF),
+            jax.ShapeDtypeStruct((share, surf_weight.shape[0], lanes), BF),
         ],
         in_specs=[VMEM] * 11,
         out_specs=[VMEM] * 2,
@@ -535,7 +543,7 @@
 def couple_kernel(y_ref, surf_ref, land_ref, bw_ref, o_ref):
     share, chans, lanes = y_ref.shape
     surf = jnp.concatenate([surf_ref[0, r] for r in range(share)], axis=1)
-    back = jnp.dot(transposed(bw_ref[...], 1.0), surf, preferred_element_type=F32)
+    back = jnp.dot(transposed(bw_ref[...]), surf, preferred_element_type=F32)
     first = pl.program_id(0) * share
     for r in range(share):
         sea = (1 - land_ref[pl.ds(first + r, 1), :]).astype(F32)
@@ -590,20 +598,21 @@
     rows = state.shape[0]
     blocks = rows // SLOTS
     big, small = 4 * blocks, 2 * blocks
-    atm = (atm_gain, atm_up, atm_down, atm_scale)
+    atm = (atm_gain, atm_up, atm_down.transpose(0, 2, 1), atm_scale)
+    taps = atm_kernel.transpose(1, 2, 0, 3)
 
     left, right = neighbours(pack(state, big))
-    a, band = convolve(0, state, atm_kernel, HALO, blocks)
+    a, band = convolve(0, state, taps, HALO, blocks)
     state, packed = first_block(state, a, left, right, band, *atm, big)
 
     left, right = neighbours(packed)
-    a, band = convolve(1, state, atm_kernel, HALO, blocks)
+    a, band = convolve(1, state, taps, HALO, blocks)
     near_steps = (rows // 2 - small) // small
     far_steps = rows // small - near_steps
     upper = rank >= half
     far_at = jnp.where(upper, 0, near_steps).astype(jnp.int32)[None]
     near_at = jnp.where(upper, far_steps, 0).astype(jnp.int32)[None]
-    shared = (state, a, left, right, band, *atm, flux_weight)
+    shared = (state, a, left, right, band, *atm, flux_weight.T)
     partly, *chunks, flux = second_block(False, members, far_at, *shared, [], small, far_steps)
     sent = [
         lax.ppermute(chunk, "member", [(i, i ^ (half + k)) for i in range(members)])
@@ -618,9 +627,9 @@
 
     mid, packed = force(members, sent, ocean, land_mask, ice_mask, flux_lift)
     left, right = neighbours(packed)
-    a, band = convolve(None, mid, ocn_kernel, 0, blocks)
+    a, band = convolve(None, mid, ocn_kernel, 0, OCEAN_BLOCKS)
     ocean_rows, surface = ocean_block(
-        mid, a, left, right, band, land_mask, ocn_gain, ocn_up, ocn_down, ocn_scale, surf_weight
+        mid, a, left, right, band, land_mask, ocn_gain, ocn_up, ocn_down.T, ocn_scale, surf_weight.T
     )
     surface = lax.all_gather(surface, "member")
     out = couple(state, surface, land_mask, back_weight)

time: 105 us -> 104 us (level)
  waiting for transfers between devices: 7.66 us -> 10.8 us
  starting transfers between devices: 22 us -> 20.2 us
  local copies, waits for them, and re-layouts: 10.5 us -> 9.1 us
    ppermute x3, starting transfers between devices: 3.19 us -> 0.01 us  [neighbours(): lax.ppermute(packed, 'lon', [(i, (i + 1) % count) for i in range(count)])]
    ppermute x3, starting transfers between devices: 9.71 us -> 12.9 us  [neighbours(): lax.ppermute(packed, 'lon', [((i + 1) % count, i) for i in range(count)])]
    ppermute x3, waiting for transfers between devices: 0.88 us -> 3.36 us  [local(): lax.ppermute(chunks[k], 'member', [(i, i ^ k) for i in range(members)])]
    ppermute x3, waiting for transfers between devices: 0.01 us -> 1.57 us  [neighbours(): lax.ppermute(packed, 'lon', [(i, (i + 1) % count) for i in range(count)])]
    ppermute x4, starting transfers between devices: 6.91 us -> 5.43 us  [local(): lax.ppermute(chunk, 'member', [(i, i ^ half + k) for i in range(members)])]
    unnamed x49 -> x46, local copies, waits for them, and re-layouts: 10.5 us -> 9.1 us
  transfers between devices with their start and end apart: 13 -> 13, of which waited for: 3 -> 5; matrix products, arithmetic and copies ran while one was open for 1% -> 0% of each run, Pallas kernels for 22% -> 22%
where the time goes in v3:
time: 104 us
  Pallas kernels  53.5 us (51%)
  starting transfers between devices  20.2 us (19%)
  waiting for transfers between devices  10.8 us (10%)
  blocking collectives  9.43 us (9%)
  local copies, waits for them, and re-layouts  9.1 us (9%)
    pallas_call x3, Pallas kernels, convolve(): pl.pallas_call(functools.partial(conv_kernel, layer, pad), grid=(groups,)...  22.7 us
    ppermute x3, starting transfers between devices, neighbours(): lax.ppermute(packed, 'lon', [((i + 1) % count, i) for i in range(count)])  12.9 us
    pallas_call x2, Pallas kernels, second_block(): pl.pallas_call(functools.partial(second_kernel, near, members), out_shape...  11.6 us
    all_gather x1, blocking collectives, local(): surface = lax.all_gather(surface, 'member')  9.43 us
    unnamed x46, local copies, waits for them, and re-layouts  9.1 us
    pallas_call x1, Pallas kernels, first_block(): pl.pallas_call(first_kernel, grid=(rows // step,), out_shape=[jax.ShapeDt...  8.55 us
    ppermute x4, waiting for transfers between devices, local(): lax.ppermute(chunk, 'member', [(i, i ^ half + k) for i in range(members)])  5.81 us
    ppermute x4, starting transfers between devices, local(): lax.ppermute(chunk, 'member', [(i, i ^ half + k) for i in range(members)])  5.43 us
  transfers between devices with their start and end apart: 13, of which 5 were waited for; matrix products, arithmetic and copies ran while one was open for 0% of the time, Pallas kernels for 22%

profile of v3, /device:TPU:0, one launch (start us, length us, event | category | flops | bytes accessed | tf_op | source)
XLA Modules:
  0.0 103.9 jit_solution(1354170447186631287)
XLA Ops:
  0.6 0.0 copy-start
  0.6 1.7 %copy-done = bf16[1,96,96,128]{3,2,1,0:T(8,128)(2,1)S(1)} copy-done((bf16[1,96,96,128]{3,2,1,0:T(8,128)(2,1)S(1)}, bf16[1,96,96,128]{3,2,1,0:T(8,128)(2,1)}, u32[]{:S(2)}) %copy-start) | copy-done | bytes 2359320
  2.3 2.4 %pack_edges.1 = bf16[6,96,128]{2,1,0:T(8,128)(2,1)S(1)} custom-call(bf16[96,96,128]{2,1,0:T(8,128)(2,1)S(1)} %bitcast.12), custom_call_target="tpu_custom_call" | custom-call | tf_op jit(solution)/shard_map/pack_edges/pallas_call | solution.py:85
  4.8 5.1 %collective-permute-start.1 = (bf16[6,96,128]{2,1,0:T(8,128)(2,1)S(1)}, bf16[6,96,128]{2,1,0:T(8,128)(2,1)S(1)}, u32[]{:S(2)}, u32[]{:S(2)}) collective-permute-start(bf16[6,96,128]{2,1,0:T(8,128)(2,1)S(1)} %pack_edges.1), channel_id=1, source_target_pairs={{1,0},{2,1},{3,2},{0,3},{5,4},{6,5},{7,6},{4,7},{9,8},{10,9},{11,1... | collective-permute-start | bytes 442376 | tf_op jit(solution)/shard_map/ppermute | solution.py:99
  9.9 0.0 collective-permute-start
  9.9 0.0 copy-done.17
  9.9 0.0 copy-start.5
  9.9 0.0 copy-start.13
  9.9 0.0 copy-start.14
  9.9 9.2 %conv.3 = (f32[96,96,128]{2,1,0:T(8,128)S(1)}, bf16[6,96,1792]{2,1,0:T(8,128)(2,1)S(1)}) custom-call(bf16[96,96,128]{2,1,0:T(8,128)(2,1)S(1)} %bitcast.13, f32[7,7,2,96]{3,2,1,0:T(2,128)S(1)} %bitcast.25), custom_call_target="tpu_custom_call" | custom-call | flops 8000000000 | tf_op jit(solution)/shard_map/conv/pallas_call | solution.py:189
  19.1 0.0 copy-start.19
  19.1 2.1 %copy-done.19 = f32[96,96,128]{2,1,0:T(8,128)} copy-done((f32[96,96,128]{2,1,0:T(8,128)}, f32[96,96,128]{2,1,0:T(8,128)S(1)}, u32[]{:S(2)}) %copy-start.19) | copy-done | bytes 4718616
  21.3 1.3 %copy-done.21 = bf16[6,96,1792]{2,1,0:T(8,128)(2,1)} copy-done((bf16[6,96,1792]{2,1,0:T(8,128)(2,1)}, bf16[6,96,1792]{2,1,0:T(8,128)(2,1)S(1)}, u32[]{:S(2)}) %copy-start.21) | copy-done | bytes 2064408
  22.6 0.0 collective-permute-done.1.right_ref
  22.6 0.0 collective-permute-done.left_ref
  22.6 0.0 copy-done.1
  22.6 0.0 copy-done.4
  22.6 0.0 copy-done.5
  22.6 0.0 copy-done.13
  22.6 2.3 %copy-done.20 = f32[96,96,128]{2,1,0:T(8,128)S(1)} copy-done((f32[96,96,128]{2,1,0:T(8,128)S(1)}, f32[96,96,128]{2,1,0:T(8,128)}, u32[]{:S(2)}) %copy-start.20) | copy-done | bytes 4718616
  25.0 1.6 %copy-done.22 = bf16[6,96,1792]{2,1,0:T(8,128)(2,1)S(1)} copy-done((bf16[6,96,1792]{2,1,0:T(8,128)(2,1)S(1)}, bf16[6,96,1792]{2,1,0:T(8,128)(2,1)}, u32[]{:S(2)}) %copy-start.22) | copy-done | bytes 2064408
  26.5 8.6 %first_block.1 = (bf16[96,96,128]{2,1,0:T(8,128)(2,1)S(1)}, bf16[6,96,128]{2,1,0:T(8,128)(2,1)S(1)}) custom-call(bf16[96,96,128]{2,1,0:T(8,128)(2,1)S(1)} %bitcast.14, f32[96,96,128]{2,1,0:T(8,128)S(1)} %copy-done.20, bf16[6,96,128]{2,1,0:T(8,128)(2,1)S(1)} %collective-permute-done.left_ref, bf16[6,96,128]{2,1,0:T(8,128)(2,1)S(1)} %collective-permute-done.1.right_ref, ...), custom_call_target="tpu_custom_call" | custom-call | flops 8000000000 | tf_op jit(solution)/shard_map/first_block/pallas_call | solution.py:319
  35.1 3.9 %collective-permute-start.3 = (bf16[6,96,128]{2,1,0:T(8,128)(2,1)S(1)}, bf16[6,96,128]{2,1,0:T(8,128)(2,1)S(1)}, u32[]{:S(2)}, u32[]{:S(2)}) collective-permute-start(bf16[6,96,128]{2,1,0:T(8,128)(2,1)S(1)} %get-tuple-element.29), channel_id=1, source_target_pairs={{1,0},{2,1},{3,2},{0,3},{5,4},{6,5},{7,6},{4,7},{9,8},{10,9},{11,1... | collective-permute-start | bytes 442376 | tf_op jit(solution)/shard_map/ppermute | solution.py:99
  39.0 0.0 collective-permute-start.2
  39.0 9.2 %conv.4 = (f32[96,96,128]{2,1,0:T(8,128)S(1)}, bf16[6,96,1792]{2,1,0:T(8,128)(2,1)S(1)}) custom-call(bf16[96,96,128]{2,1,0:T(8,128)(2,1)S(1)} %get-tuple-element.27.x_ref.refs_0_, f32[7,7,2,96]{3,2,1,0:T(2,128)S(1)} %bitcast.26), custom_call_target="tpu_custom_call" | custom-call | flops 8000000000 | tf_op jit(solution)/shard_map/conv/pallas_call | solution.py:189
  48.2 0.0 collective-permute-done.3.refs_3_
  48.2 0.0 collective-permute-done.2.refs_2_
  48.2 6.8 %second_block.2 = (bf16[96,96,128]{2,1,0:T(8,128)(2,1)S(1)}, bf16[18,32,128]{2,1,0:T(8,128)(2,1)S(1)}, bf16[18,32,128]{2,1,0:T(8,128)(2,1)S(1)}, bf16[18,32,128]...) custom-call(s32[1]{0:T(128)} %bitcast.5.at_ref, ...), custom_call_target="tpu_custom_call" | custom-call | flops 5000000000 | tf_op jit(solution)/shard_map/second_block/pallas_call | solution.py:424
  55.1 0.0 copy-start.2
  55.1 0.0 copy-start.3
  55.1 0.0 copy-start.8
  55.1 0.0 copy-start.9
  55.1 4.8 %second_block.3 = (bf16[96,96,128]{2,1,0:T(8,128)(2,1)S(1)}, bf16[18,32,128]{2,1,0:T(8,128)(2,1)S(1)}, bf16[18,32,128]{2,1,0:T(8,128)(2,1)S(1)}, bf16[18,32,128]...) custom-call(s32[1]{0:T(128)} %bitcast.at_ref, ...), custom_call_target="tpu_custom_call", output_to_operand_aliasing={{0}: (11, {})} | custom-call | flops 3000000000 | tf_op jit(solution)/shard_map/second_block/pallas_call | solution.py:424
  59.9 0.0 copy-start.18
  59.9 0.2 collective-permute-start.8
  60.1 1.5 %collective-permute-start.9 = (bf16[18,32,128]{2,1,0:T(8,128)(2,1)S(1)}, bf16[18,32,128]{2,1,0:T(8,128)(2,1)S(1)}, u32[]{:S(2)}, u32[]{:S(2)}) collective-permute-start(bf16[18,32,128]{2,1,0:T(8,128)(2,1)S(1)} %get-tuple-element.39), channel_id=1, source_target_pairs={{0,8},{4,12},{8,0},{12,4},{16,24},{20,28},{24,16},{28,20},{1,9},{5... | collective-permute-start | bytes 442376 | tf_op jit(solution)/shard_map/ppermute | solution.py:623
  61.6 0.3 collective-permute-start.10
  61.8 1.5 %collective-permute-start.4 = (bf16[18,32,128]{2,1,0:T(8,128)(2,1)S(1)}, bf16[18,32,128]{2,1,0:T(8,128)(2,1)S(1)}, u32[]{:S(2)}, u32[]{:S(2)}) collective-permute-start(bf16[18,32,128]{2,1,0:T(8,128)(2,1)S(1)} %get-tuple-element.34), channel_id=1, source_target_pairs={{0,16},{4,20},{8,24},{12,28},{16,0},{20,4},{24,8},{28,12},{1,17},{... | collective-permute-start | bytes 442376 | tf_op jit(solution)/shard_map/ppermute | solution.py:618
  63.4 0.1 collective-permute-start.5
  63.4 2.6 %collective-permute-done.8.refs_4_ = bf16[18,32,128]{2,1,0:T(8,128)(2,1)S(1)} collective-permute-done((bf16[18,32,128]{2,1,0:T(8,128)(2,1)S(1)}, bf16[18,32,128]{2,1,0:T(8,128)(2,1)S(1)}, u32[]{:S(2)}, u32[]{:S(2)}) %collective-permute-start.8) | collective-permute-done | bytes 147488 | tf_op jit(solution)/shard_map/ppermute | solution.py:623
  66.1 2.5 %collective-permute-start.6 = (bf16[18,32,128]{2,1,0:T(8,128)(2,1)S(1)}, bf16[18,32,128]{2,1,0:T(8,128)(2,1)S(1)}, u32[]{:S(2)}, u32[]{:S(2)}) collective-permute-start(bf16[18,32,128]{2,1,0:T(8,128)(2,1)S(1)} %get-tuple-element.36), channel_id=1, source_target_pairs={{0,24},{4,28},{8,16},{12,20},{16,8},{20,12},{24,0},{28,4},{1,25},{... | collective-permute-start | bytes 442376 | tf_op jit(solution)/shard_map/ppermute | solution.py:618
  68.6 0.7 collective-permute-done.9.refs_5_
  69.3 1.3 %collective-permute-start.7 = (bf16[18,32,128]{2,1,0:T(8,128)(2,1)S(1)}, bf16[18,32,128]{2,1,0:T(8,128)(2,1)S(1)}, u32[]{:S(2)}, u32[]{:S(2)}) collective-permute-start(bf16[18,32,128]{2,1,0:T(8,128)(2,1)S(1)} %get-tuple-element.37), channel_id=1, source_target_pairs={{0,28},{4,24},{8,20},{12,16},{16,12},{20,8},{24,4},{28,0},{1,29},{... | collective-permute-start | bytes 442376 | tf_op jit(solution)/shard_map/ppermute | solution.py:618
  70.6 0.0 collective-permute-done.10.refs_6_
  70.6 0.0 collective-permute-done.4.refs_0_
  70.6 5.7 %collective-permute-done.5.refs_1_ = bf16[18,32,128]{2,1,0:T(8,128)(2,1)S(1)} collective-permute-done((bf16[18,32,128]{2,1,0:T(8,128)(2,1)S(1)}, bf16[18,32,128]{2,1,0:T(8,128)(2,1)S(1)}, u32[]{:S(2)}, u32[]{:S(2)}) %collective-permute-start.5) | collective-permute-done | bytes 147488 | tf_op jit(solution)/shard_map/ppermute | solution.py:618
  76.3 0.0 collective-permute-done.6.refs_2_
  76.3 0.1 collective-permute-done.7.refs_3_
  76.5 0.0 copy-done.8
  76.5 1.1 %ocean_forcing.1 = (bf16[18,96,128]{2,1,0:T(8,128)(2,1)S(1)}, bf16[2,96,128]{2,1,0:T(8,128)(2,1)S(1)}) custom-call(bf16[18,32,128]{2,1,0:T(8,128)(2,1)S(1)} %collective-permute-done.4.refs_0_, bf16[18,32,128]{2,1,0:T(8,128)(2,1)S(1)} %collective-permute-done.5.refs_1_, bf16[18,32,128]{2,1,0:T(8,128)(2,1)S(1)} %collective-permute-done.6.refs_2_, ...), custom_call_target="tpu_custom_call" | custom-call | tf_op jit(solution)/shard_map/ocean_forcing/pallas_call | solution.py:487
  77.5 0.0 copy-start.6
  77.6 0.0 copy-start.7
  77.6 0.0 copy-start.12
  77.6 0.0 copy-start.15
  77.6 0.0 copy-start.16
  77.6 3.9 %collective-permute-start.12 = (bf16[2,96,128]{2,1,0:T(8,128)(2,1)S(1)}, bf16[2,96,128]{2,1,0:T(8,128)(2,1)S(1)}, u32[]{:S(2)}, u32[]{:S(2)}) collective-permute-start(bf16[2,96,128]{2,1,0:T(8,128)(2,1)S(1)} %get-tuple-element.44), channel_id=1, source_target_pairs={{1,0},{2,1},{3,2},{0,3},{5,4},{6,5},{7,6},{4,7},{9,8},{10,9},{11,1... | collective-permute-start | bytes 147464 | tf_op jit(solution)/shard_map/ppermute | solution.py:99
  81.5 0.0 collective-permute-start.11
  81.5 4.3 %conv.5 = (f32[12,96,128]{2,1,0:T(8,128)S(1)}, bf16[6,32,1792]{2,1,0:T(8,128)(2,1)S(1)}) custom-call(bf16[18,96,128]{2,1,0:T(8,128)(2,1)S(1)} %get-tuple-element.42.x_ref.mid_ref, f32[7,7,96]{2,1,0:T(8,128)S(1)} %copy-done.18), custom_call_target="tpu_custom_call" | custom-call | flops 1000000000 | tf_op jit(solution)/shard_map/conv/pallas_call | solution.py:189
  85.8 0.0 collective-permute-done.12.right_ref
  85.8 1.6 %collective-permute-done.11.left_ref = bf16[2,96,128]{2,1,0:T(8,128)(2,1)S(1)} collective-permute-done((bf16[2,96,128]{2,1,0:T(8,128)(2,1)S(1)}, bf16[2,96,128]{2,1,0:T(8,128)(2,1)S(1)}, u32[]{:S(2)}, u32[]{:S(2)}) %collective-permute-start.11) | collective-permute-done | bytes 49184 | tf_op jit(solution)/shard_map/ppermute | solution.py:98
  87.4 0.0 copy-done.7
  87.4 2.8 %ocean_block.1 = (bf16[12,96,128]{2,1,0:T(8,128)(2,1)}, bf16[12,8,128]{2,1,0:T(8,128)(2,1)S(1)}) custom-call(bf16[18,96,128]{2,1,0:T(8,128)(2,1)S(1)} %get-tuple-element.42.x_ref.mid_ref, f32[12,96,128]{2,1,0:T(8,128)S(1)} %get-tuple-element.43.a_ref, bf16[2,96,128]{2,1,0:T(8,128)(2,1)S(1)} %collective-permute-done.11.left_ref, ...), custom_call_target="tpu_custom_call" | custom-call | tf_op jit(solution)/shard_map/ocean_block/pallas_call | solution.py:526
  90.2 9.4 %all-gather = bf16[96,8,128]{2,1,0:T(8,128)(2,1)S(1)} all-gather(bf16[12,8,128]{2,1,0:T(8,128)(2,1)S(1)} %get-tuple-element.46), channel_id=2, replica_groups=mesh['member'=8,'lon'=4] {'member'}, dimensions={0}, use_global_device_ids=true | all-gather | bytes 221184 | tf_op jit(solution)/shard_map/all_gather | solution.py:634
  99.7 4.3 %couple.1 = bf16[96,96,128]{2,1,0:T(8,128)(2,1)} custom-call(bf16[96,96,128]{2,1,0:T(8,128)(2,1)S(1)} %get-tuple-element.33.y_ref, bf16[8,12,8,128]{3,2,1,0:T(8,128)(2,1)S(1)} %bitcast.15, s32[96,128]{1,0:T(8,128)S(1)} %copy-done.3, bf16[8,96]{1,0:T(8,128)(2,1)S(1)} %copy-done.11), custom_call_target="tpu_custom_call" | custom-call | tf_op jit(solution)/shard_map/couple/pallas_call | solution.py:558
  (19 shorter events, 0.0 us)
Async XLA Ops:
  0.6 1.7 %copy-start = (bf16[1,96,96,128]{3,2,1,0:T(8,128)(2,1)S(1)}, bf16[1,96,96,128]{3,2,1,0:T(8,128)(2,1)}, u32[]{:S(2)}) copy-start(bf16[1,96,96,128]{3,2,1,0:T(8,128)(2,1)} %param.18) | copy-start | bytes 7077892
  2.3 7.6 %copy-start.17 = (f32[2,7,7,96]{3,0,2,1:T(2,128)S(1)}, f32[2,7,7,96]{3,0,2,1:T(2,128)}, u32[]{:S(2)}) copy-start(f32[2,7,7,96]{3,0,2,1:T(2,128)} %param.22) | copy-start | bytes 112900
  4.8 17.8 %collective-permute-start.1 = (bf16[6,96,128]{2,1,0:T(8,128)(2,1)S(1)}, bf16[6,96,128]{2,1,0:T(8,128)(2,1)S(1)}, u32[]{:S(2)}, u32[]{:S(2)}) collective-permute-start(bf16[6,96,128]{2,1,0:T(8,128)(2,1)S(1)} %pack_edges.1), channel_id=1, source_target_pairs={{1,0},{2,1},{3,2},{0,3},{5,4},{6,5},{7,6},{4,7},{9,8},{10,9},{11,1... | collective-permute-start | bytes 442376 | tf_op jit(solution)/shard_map/ppermute | solution.py:99
  9.9 12.7 %collective-permute-start = (bf16[6,96,128]{2,1,0:T(8,128)(2,1)S(1)}, bf16[6,96,128]{2,1,0:T(8,128)(2,1)S(1)}, u32[]{:S(2)}, u32[]{:S(2)}) collective-permute-start(bf16[6,96,128]{2,1,0:T(8,128)(2,1)S(1)} %pack_edges.1), channel_id=1, source_target_pairs={{0,1},{1,2},{2,3},{3,0},{4,5},{5,6},{6,7},{7,4},{8,9},{9,10},{10,1... | collective-permute-start | bytes 442376 | tf_op jit(solution)/shard_map/ppermute | solution.py:98
  9.9 12.7 %copy-start.1 = (bf16[1,96,96,128]{3,2,1,0:T(8,128)(2,1)S(1)}, bf16[1,96,96,128]{3,2,1,0:T(8,128)(2,1)}, u32[]{:S(2)}) copy-start(bf16[1,96,96,128]{3,2,1,0:T(8,128)(2,1)} %param.18) | copy-start | bytes 7077892
  9.9 12.7 %copy-start.4 = (bf16[2,96,384]{2,1,0:T(8,128)(2,1)S(1)}, bf16[2,96,384]{2,1,0:T(8,128)(2,1)}, u32[]{:S(2)}) copy-start(bf16[2,96,384]{2,1,0:T(8,128)(2,1)} %refs_6_.3) | copy-start | bytes 442372
  9.9 12.7 %copy-start.5 = (bf16[2,384,96]{1,2,0:T(8,128)(2,1)S(1)}, bf16[2,384,96]{1,2,0:T(8,128)(2,1)}, u32[]{:S(2)}) copy-start(bf16[2,384,96]{1,2,0:T(8,128)(2,1)} %param.25) | copy-start | bytes 442372
  9.9 12.7 %copy-start.13 = (f32[2,96]{1,0:T(2,128)S(1)}, f32[2,96]{1,0:T(2,128)}, u32[]{:S(2)}) copy-start(f32[2,96]{1,0:T(2,128)} %refs_5_.3) | copy-start | bytes 2308
  9.9 12.7 %copy-start.14 = (f32[2,96]{1,0:T(2,128)S(1)}, f32[2,96]{1,0:T(2,128)}, u32[]{:S(2)}) copy-start(f32[2,96]{1,0:T(2,128)} %refs_8_.4) | copy-start | bytes 2308
  19.1 2.1 %copy-start.19 = (f32[96,96,128]{2,1,0:T(8,128)}, f32[96,96,128]{2,1,0:T(8,128)S(1)}, u32[]{:S(2)}) copy-start(f32[96,96,128]{2,1,0:T(8,128)S(1)} %get-tuple-element.25.a_ref) | copy-start | bytes 14155780
  21.3 1.3 %copy-start.21 = (bf16[6,96,1792]{2,1,0:T(8,128)(2,1)}, bf16[6,96,1792]{2,1,0:T(8,128)(2,1)S(1)}, u32[]{:S(2)}) copy-start(bf16[6,96,1792]{2,1,0:T(8,128)(2,1)S(1)} %get-tuple-element.26.band_ref) | copy-start | bytes 6193156
  22.6 2.3 %copy-start.20 = (f32[96,96,128]{2,1,0:T(8,128)S(1)}, f32[96,96,128]{2,1,0:T(8,128)}, u32[]{:S(2)}) copy-start(f32[96,96,128]{2,1,0:T(8,128)} %copy-done.19) | copy-start | bytes 14155780
  25.0 1.6 %copy-start.22 = (bf16[6,96,1792]{2,1,0:T(8,128)(2,1)S(1)}, bf16[6,96,1792]{2,1,0:T(8,128)(2,1)}, u32[]{:S(2)}) copy-start(bf16[6,96,1792]{2,1,0:T(8,128)(2,1)} %copy-done.21) | copy-start | bytes 6193156
  35.1 13.1 %collective-permute-start.3 = (bf16[6,96,128]{2,1,0:T(8,128)(2,1)S(1)}, bf16[6,96,128]{2,1,0:T(8,128)(2,1)S(1)}, u32[]{:S(2)}, u32[]{:S(2)}) collective-permute-start(bf16[6,96,128]{2,1,0:T(8,128)(2,1)S(1)} %get-tuple-element.29), channel_id=1, source_target_pairs={{1,0},{2,1},{3,2},{0,3},{5,4},{6,5},{7,6},{4,7},{9,8},{10,9},{11,1... | collective-permute-start | bytes 442376 | tf_op jit(solution)/shard_map/ppermute | solution.py:99
  39.0 9.2 %collective-permute-start.2 = (bf16[6,96,128]{2,1,0:T(8,128)(2,1)S(1)}, bf16[6,96,128]{2,1,0:T(8,128)(2,1)S(1)}, u32[]{:S(2)}, u32[]{:S(2)}) collective-permute-start(bf16[6,96,128]{2,1,0:T(8,128)(2,1)S(1)} %get-tuple-element.29), channel_id=1, source_target_pairs={{0,1},{1,2},{2,3},{3,0},{4,5},{5,6},{6,7},{7,4},{8,9},{9,10},{10,1... | collective-permute-start | bytes 442376 | tf_op jit(solution)/shard_map/ppermute | solution.py:98
  39.0 9.2 %copy-start.10 = (bf16[96,32]{0,1:T(8,128)(2,1)S(1)}, bf16[96,32]{0,1:T(8,128)(2,1)}, u32[]{:S(2)}) copy-start(bf16[96,32]{0,1:T(8,128)(2,1)} %param.27) | copy-start | bytes 18436
  55.1 21.4 %copy-start.2 = (bf16[96,96,128]{2,1,0:T(8,128)(2,1)S(1)}, bf16[96,96,128]{2,1,0:T(8,128)(2,1)}, u32[]{:S(2)}) copy-start(bf16[96,96,128]{2,1,0:T(8,128)(2,1)} %refs_8_.5) | copy-start | bytes 7077892
  55.1 21.4 %copy-start.3 = (s32[96,128]{1,0:T(8,128)S(1)}, s32[96,128]{1,0:T(8,128)}, u32[]{:S(2)}) copy-start(s32[96,128]{1,0:T(8,128)} %land_ref.3) | copy-start | bytes 147460
  55.1 21.4 %copy-start.8 = (s32[96,128]{1,0:T(8,128)S(1)}, s32[96,128]{1,0:T(8,128)}, u32[]{:S(2)}) copy-start(s32[96,128]{1,0:T(8,128)} %refs_10_.1) | copy-start | bytes 147460
  55.1 21.4 %copy-start.9 = (bf16[2,32,96]{2,1,0:T(8,128)(2,1)S(1)}, bf16[2,32,96]{2,1,0:T(8,128)(2,1)}, u32[]{:S(2)}) copy-start(bf16[2,32,96]{2,1,0:T(8,128)(2,1)} %refs_11_.1) | copy-start | bytes 36868
  59.9 21.6 %copy-start.18 = (f32[7,7,96]{2,1,0:T(8,128)S(1)}, f32[7,7,96]{2,1,0:T(8,128)}, u32[]{:S(2)}) copy-start(f32[7,7,96]{2,1,0:T(8,128)} %k_ref.1) | copy-start | bytes 56452
  59.9 6.1 %collective-permute-start.8 = (bf16[18,32,128]{2,1,0:T(8,128)(2,1)S(1)}, bf16[18,32,128]{2,1,0:T(8,128)(2,1)S(1)}, u32[]{:S(2)}, u32[]{:S(2)}) collective-permute-start(bf16[18,32,128]{2,1,0:T(8,128)(2,1)S(1)} %get-tuple-element.38), channel_id=1, source_target_pairs={{0,12},{4,8},{8,4},{12,0},{16,28},{20,24},{24,20},{28,16},{1,13},{... | collective-permute-start | bytes 442376 | tf_op jit(solution)/shard_map/ppermute | solution.py:623
  60.1 9.2 %collective-permute-start.9 = (bf16[18,32,128]{2,1,0:T(8,128)(2,1)S(1)}, bf16[18,32,128]{2,1,0:T(8,128)(2,1)S(1)}, u32[]{:S(2)}, u32[]{:S(2)}) collective-permute-start(bf16[18,32,128]{2,1,0:T(8,128)(2,1)S(1)} %get-tuple-element.39), channel_id=1, source_target_pairs={{0,8},{4,12},{8,0},{12,4},{16,24},{20,28},{24,16},{28,20},{1,9},{5... | collective-permute-start | bytes 442376 | tf_op jit(solution)/shard_map/ppermute | solution.py:623
  61.6 9.1 %collective-permute-start.10 = (bf16[18,32,128]{2,1,0:T(8,128)(2,1)S(1)}, bf16[18,32,128]{2,1,0:T(8,128)(2,1)S(1)}, u32[]{:S(2)}, u32[]{:S(2)}) collective-permute-start(bf16[18,32,128]{2,1,0:T(8,128)(2,1)S(1)} %get-tuple-element.40), channel_id=1, source_target_pairs={{0,4},{4,0},{8,12},{12,8},{16,20},{20,16},{24,28},{28,24},{1,5},{5... | collective-permute-start | bytes 442376 | tf_op jit(solution)/shard_map/ppermute | solution.py:623
  61.8 8.8 %collective-permute-start.4 = (bf16[18,32,128]{2,1,0:T(8,128)(2,1)S(1)}, bf16[18,32,128]{2,1,0:T(8,128)(2,1)S(1)}, u32[]{:S(2)}, u32[]{:S(2)}) collective-permute-start(bf16[18,32,128]{2,1,0:T(8,128)(2,1)S(1)} %get-tuple-element.34), channel_id=1, source_target_pairs={{0,16},{4,20},{8,24},{12,28},{16,0},{20,4},{24,8},{28,12},{1,17},{... | collective-permute-start | bytes 442376 | tf_op jit(solution)/shard_map/ppermute | solution.py:618
  63.4 13.0 %collective-permute-start.5 = (bf16[18,32,128]{2,1,0:T(8,128)(2,1)S(1)}, bf16[18,32,128]{2,1,0:T(8,128)(2,1)S(1)}, u32[]{:S(2)}, u32[]{:S(2)}) collective-permute-start(bf16[18,32,128]{2,1,0:T(8,128)(2,1)S(1)} %get-tuple-element.35), channel_id=1, source_target_pairs={{0,20},{4,16},{8,28},{12,24},{16,4},{20,0},{24,12},{28,8},{1,21},{... | collective-permute-start | bytes 442376 | tf_op jit(solution)/shard_map/ppermute | solution.py:618
  66.1 10.3 %collective-permute-start.6 = (bf16[18,32,128]{2,1,0:T(8,128)(2,1)S(1)}, bf16[18,32,128]{2,1,0:T(8,128)(2,1)S(1)}, u32[]{:S(2)}, u32[]{:S(2)}) collective-permute-start(bf16[18,32,128]{2,1,0:T(8,128)(2,1)S(1)} %get-tuple-element.36), channel_id=1, source_target_pairs={{0,24},{4,28},{8,16},{12,20},{16,8},{20,12},{24,0},{28,4},{1,25},{... | collective-permute-start | bytes 442376 | tf_op jit(solution)/shard_map/ppermute | solution.py:618
  69.3 7.2 %collective-permute-start.7 = (bf16[18,32,128]{2,1,0:T(8,128)(2,1)S(1)}, bf16[18,32,128]{2,1,0:T(8,128)(2,1)S(1)}, u32[]{:S(2)}, u32[]{:S(2)}) collective-permute-start(bf16[18,32,128]{2,1,0:T(8,128)(2,1)S(1)} %get-tuple-element.37), channel_id=1, source_target_pairs={{0,28},{4,24},{8,20},{12,16},{16,12},{20,8},{24,4},{28,0},{1,29},{... | collective-permute-start | bytes 442376 | tf_op jit(solution)/shard_map/ppermute | solution.py:618
  77.5 9.8 %copy-start.6 = (bf16[96,384]{1,0:T(8,128)(2,1)S(1)}, bf16[96,384]{1,0:T(8,128)(2,1)}, u32[]{:S(2)}) copy-start(bf16[96,384]{1,0:T(8,128)(2,1)} %up_ref.3) | copy-start | bytes 221188
  77.6 9.8 %copy-start.7 = (bf16[384,96]{0,1:T(8,128)(2,1)S(1)}, bf16[384,96]{0,1:T(8,128)(2,1)}, u32[]{:S(2)}) copy-start(bf16[384,96]{0,1:T(8,128)(2,1)} %param.32) | copy-start | bytes 221188
  77.6 9.8 %copy-start.12 = (bf16[96,8]{0,1:T(8,128)(2,1)S(1)}, bf16[96,8]{0,1:T(8,128)(2,1)}, u32[]{:S(2)}) copy-start(bf16[96,8]{0,1:T(8,128)(2,1)} %param.34) | copy-start | bytes 4612
  77.6 9.8 %copy-start.15 = (f32[96]{0:T(128)S(1)}, f32[96]{0:T(128)}, u32[]{:S(2)}) copy-start(f32[96]{0:T(128)} %param.30) | copy-start | bytes 1156
  77.6 9.8 %copy-start.16 = (f32[96]{0:T(128)S(1)}, f32[96]{0:T(128)}, u32[]{:S(2)}) copy-start(f32[96]{0:T(128)} %param.33) | copy-start | bytes 1156
  77.6 8.2 %collective-permute-start.12 = (bf16[2,96,128]{2,1,0:T(8,128)(2,1)S(1)}, bf16[2,96,128]{2,1,0:T(8,128)(2,1)S(1)}, u32[]{:S(2)}, u32[]{:S(2)}) collective-permute-start(bf16[2,96,128]{2,1,0:T(8,128)(2,1)S(1)} %get-tuple-element.44), channel_id=1, source_target_pairs={{1,0},{2,1},{3,2},{0,3},{5,4},{6,5},{7,6},{4,7},{9,8},{10,9},{11,1... | collective-permute-start | bytes 147464 | tf_op jit(solution)/shard_map/ppermute | solution.py:99
  81.5 5.9 %collective-permute-start.11 = (bf16[2,96,128]{2,1,0:T(8,128)(2,1)S(1)}, bf16[2,96,128]{2,1,0:T(8,128)(2,1)S(1)}, u32[]{:S(2)}, u32[]{:S(2)}) collective-permute-start(bf16[2,96,128]{2,1,0:T(8,128)(2,1)S(1)} %get-tuple-element.44), channel_id=1, source_target_pairs={{0,1},{1,2},{2,3},{3,0},{4,5},{5,6},{6,7},{7,4},{8,9},{9,10},{10,1... | collective-permute-start | bytes 147464 | tf_op jit(solution)/shard_map/ppermute | solution.py:98
  81.5 18.2 %copy-start.11 = (bf16[8,96]{1,0:T(8,128)(2,1)S(1)}, bf16[8,96]{1,0:T(8,128)(2,1)}, u32[]{:S(2)}) copy-start(bf16[8,96]{1,0:T(8,128)(2,1)} %bw_ref.1) | copy-start | bytes 4612

commit v4 on v3

--- a/solution.py
+++ b/solution.py
@@ -23,6 +23,7 @@
 BY_DOT = (0, 1, 5, 6)
 VMEM = pl.BlockSpec(memory_space=pltpu.VMEM)
 ANY = pl.BlockSpec(memory_space=pl.ANY)
+HBM = pl.BlockSpec(memory_space=pltpu.HBM)
 
 
 def params(mib):
@@ -54,40 +55,38 @@
     return (lane < HALO) | (lane >= shape[-1] - HALO)
 
 
-def pack_kernel(x_ref, p_ref):
-    step = pl.program_id(0)
-    count, chans, lanes = x_ref.shape
+def pack_kernel(step, src_ref, x_ref, p_ref, sems):
+    rows, chans, lanes = x_ref.shape
     blocks = p_ref.shape[0]
+    copies = []
+    for n in range(rows // step):
+        at = slice(n * step, (n + 1) * step)
+        copies.append(pltpu.make_async_copy(src_ref.at[at], x_ref.at[at], sems.at[n]))
+        copies[n].start()
     keep = edge_lanes((chans, lanes)).astype(F32).astype(BF)
-    for q in range(blocks):
-        total = None
-        for c in range(count // blocks):
-            slot = step * (count // blocks) + c
-            moved = pltpu.roll(x_ref[c * blocks + q] * keep, SLOT * slot, 1)
-            total = moved if total is None else total + moved
-        if count // blocks < SLOTS:
-
-            @pl.when(step == 0)
-            def _():
-                p_ref[q] = total
-
-            @pl.when(step > 0)
-            def _():
-                p_ref[q] = p_ref[q] + total
-
-        else:
+    for n in range(rows // step):
+        copies[n].wait()
+        for q in range(blocks):
+            total = None if n == 0 else p_ref[q]
+            for slot in range(n * step // blocks, (n + 1) * step // blocks):
+                moved = x_ref[slot * blocks + q] * keep
+                if slot:
+                    moved = pltpu.roll(moved, SLOT * slot, 1)
+                total = moved if total is None else total + moved
             p_ref[q] = total
 
 
 def pack(x, step):
     rows, chans, lanes = x.shape
-    blocks = rows // SLOTS
-    return pl.pallas_call(
-        pack_kernel,
-        grid=(rows // step,),
-        out_shape=jax.ShapeDtypeStruct((blocks, chans, lanes), BF),
-        in_specs=[pl.BlockSpec((step, chans, lanes), lambda i: (i, 0, 0))],
-        out_specs=pl.BlockSpec((blocks, chans, lanes), lambda i: (0, 0, 0)),
+    return pl.pallas_call(
+        functools.partial(pack_kernel, step),
+        out_shape=[
+            jax.ShapeDtypeStruct(x.shape, BF),
+            jax.ShapeDtypeStruct((rows // SLOTS, chans, lanes), BF),
+        ],
+        in_specs=[HBM],
+        out_specs=[VMEM, VMEM],
+        scratch_shapes=[pltpu.SemaphoreType.DMA((rows // step,))],
         compiler_params=params(24),
         name="pack_edges",
     )(x)
@@ -126,31 +125,17 @@
         base[g] = total[GROUP * g : GROUP * (g + 1)]
 
 
-def conv_kernel(layer, pad, x_ref, k_ref, a_ref, band_ref, base, smat, xj, band):
-    g = pl.program_id(0)
-    count, _, lanes = x_ref.shape
-    rows = a_ref.shape[0]
-    tall = xj.shape[1]
-
-    @pl.when(g == 0)
-    def _():
-        fill_base(lambda i: k_ref[i, :, layer, :] if layer is not None else k_ref[i], base)
-        smat[...] = shift_matrix(lanes)
-        for j in range(TAPS):
-            if pad:
-                xj[j, :pad] = jnp.zeros((pad, GROUP, lanes), BF)
-            if tall > pad + count:
-                xj[j, pad + count :] = jnp.zeros((tall - pad - count, GROUP, lanes), BF)
-
+def fill_band(base, g, band):
     for j in range(TAPS):
         one = base[g, :, j * DEPTH : (j + 1) * DEPTH]
         for r in range(OUT):
             moved = pltpu.roll(one, GROUP * r, 1) if r else one
             band[GROUP * r : GROUP * (r + 1), j * DEPTH : (j + 1) * DEPTH] = moved.astype(BF)
-    band_ref[0] = band[: band_ref.shape[1]]
-
-    x = x_ref[...]
-    moved = jnp.dot(x.reshape(count * GROUP, lanes), smat[...], preferred_element_type=F32)
+
+
+def fill_shifts(x, pad, smat, xj):
+    count, _, lanes = x.shape
+    moved = jnp.dot(x.reshape(count * GROUP, lanes), smat, preferred_element_type=F32)
     for a, j in enumerate(BY_DOT):
         part = moved[:, a * lanes : (a + 1) * lanes].astype(BF)
         xj[j, pad : pad + count] = part.reshape(count, GROUP, lanes)
@@ -165,6 +150,18 @@
             keep = ((lane < lanes - d) if d > 0 else (lane >= -d)).astype(F32).astype(BF)
             xj[j, pad : pad + count] = pltpu.roll(x, (-d) % lanes, 2) * keep[None]
 
+
+def clear_pads(pad, count, xj):
+    tall, _, lanes = xj.shape[1:]
+    for j in range(TAPS):
+        if pad:
+            xj[j, :pad] = jnp.zeros((pad, GROUP, lanes), BF)
+        if tall > pad + count:
+            xj[j, pad + count :] = jnp.zeros((tall - pad - count, GROUP, lanes), BF)
+
+
+def apply_band(band, xj, a_ref):
+    rows, _, lanes = a_ref.shape
     starts = [min(OUT * i, max(rows - OUT, 0)) for i in range(-(-rows // OUT))]
     field = jnp.concatenate(
         [
@@ -173,41 +170,98 @@
         ],
         axis=1,
     )
-    out = jnp.dot(band[...], field, preferred_element_type=F32)
+    out = jnp.dot(band, field, preferred_element_type=F32)
     take = min(OUT, rows)
     for n, s in enumerate(starts):
         part = out[: take * GROUP, n * lanes : (n + 1) * lanes]
         a_ref[s : s + take] = part.reshape(take, GROUP, lanes)
 
 
-def convolve(layer, x, taps, pad, blocks):
-    count, chans, lanes = x.shape
-    rows = count + 2 * pad - 2 * HALO
+def conv_kernel(layer, x_ref, k_ref, a_ref, band_ref, base, smat, xj, band):
+    g = pl.program_id(0)
+    count, _, lanes = x_ref.shape
+
+    @pl.when(g == 0)
+    def _():
+        fill_base(lambda i: k_ref[i, :, layer, :], base)
+        smat[...] = shift_matrix(lanes)
+        clear_pads(HALO, count, xj)
+
+    fill_band(base, g, band)
+    band_ref[0] = band[: band_ref.shape[1]]
+    fill_shifts(x_ref[...], HALO, smat[...], xj)
+    apply_band(band[...], xj, a_ref)
+
+
+def convolve(layer, x, taps, blocks):
+    rows, chans, lanes = x.shape
     groups = chans // GROUP
     wide = TAPS * DEPTH
-    tall = max(count + 2 * pad, SPAN)
-    return pl.pallas_call(
-        functools.partial(conv_kernel, layer, pad),
+    part = pl.BlockSpec((rows, GROUP, lanes), lambda g: (0, g, 0))
+    return pl.pallas_call(
+        functools.partial(conv_kernel, layer),
         grid=(groups,),
         out_shape=[
             jax.ShapeDtypeStruct((rows, chans, lanes), F32),
             jax.ShapeDtypeStruct((groups, blocks * GROUP, wide), BF),
         ],
-        in_specs=[pl.BlockSpec((count, GROUP, lanes), lambda g: (0, g, 0)), VMEM],
-        out_specs=[
-            pl.BlockSpec((rows, GROUP, lanes), lambda g: (0, g, 0)),
-            pl.BlockSpec((1, blocks * GROUP, wide), lambda g: (g, 0, 0)),
-        ],
+        in_specs=[part, VMEM],
+        out_specs=[part, pl.BlockSpec((1, blocks * GROUP, wide), lambda g: (g, 0, 0))],
         scratch_shapes=[
             pltpu.VMEM((groups, GROUP, wide), F32),
             pltpu.VMEM((lanes, len(BY_DOT) * lanes), BF),
-            pltpu.VMEM((TAPS, tall, GROUP, lanes), BF),
+            pltpu.VMEM((TAPS, rows + 2 * HALO, GROUP, lanes), BF),
             pltpu.VMEM((GROUP * OUT, wide), BF),
         ],
         compiler_params=params(24),
-        cost_estimate=cost(8 * rows / 96),
+        cost_estimate=cost(8),
         name="conv",
     )(x, taps)
+
+
+def band_kernel(k_ref, band_ref, base):
+    fill_base(lambda i: k_ref[i], base)
+    for g in range(base.shape[0]):
+        fill_band(base, g, band_ref.at[g])
+
+
+def ocean_band(taps):
+    groups = taps.shape[2] // GROUP
+    wide = TAPS * DEPTH
+    return pl.pallas_call(
+        band_kernel,
+        out_shape=jax.ShapeDtypeStruct((groups, GROUP * OUT, wide), BF),
+        in_specs=[VMEM],
+        out_specs=VMEM,
+        scratch_shapes=[pltpu.VMEM((groups, GROUP, wide), F32)],
+        compiler_params=params(24),
+        cost_estimate=cost(3),
+        name="ocean_band",
+    )(taps)
+
+
+def ocean_conv_kernel(x_ref, band_ref, a_ref, xj):
+    count, chans, lanes = x_ref.shape
+    smat = shift_matrix(lanes)
+    clear_pads(0, count, xj)
+    for g in range(chans // GROUP):
+        at = slice(GROUP * g, GROUP * (g + 1))
+        fill_shifts(x_ref[:, at, :], 0, smat, xj)
+        apply_band(band_ref[g], xj, a_ref.at[:, at, :])
+
+
+def ocean_conv(x, band):
+    count, chans, lanes = x.shape
+    return pl.pallas_call(
+        ocean_conv_kernel,
+        out_shape=jax.ShapeDtypeStruct((count - 2 * HALO, chans, lanes), F32),
+        in_specs=[VMEM, VMEM],
+        out_specs=VMEM,
+        scratch_shapes=[pltpu.VMEM((TAPS, max(count, SPAN), GROUP, lanes), BF)],
+        compiler_params=params(24),
+        cost_estimate=cost(2),
+        name="ocean_conv",
+    )(x, band)
 
 
 def halo_matrix(lanes):
@@ -265,7 +319,8 @@
     for g in range(chans // GROUP):
         at = slice(GROUP * g, GROUP * (g + 1))
         rhs = jnp.concatenate([xe[a, :, at, :].reshape(DEPTH, lanes) for a in range(TAPS - 1)], axis=0)
-        lhs = jnp.concatenate([band[g, :, :low], band[g, :, low + DEPTH : wide]], axis=1)
+        tops = slice(0, blocks * GROUP)
+        lhs = jnp.concatenate([band[g, tops, :low], band[g, tops, low + DEPTH : wide]], axis=1)
         out = jnp.dot(lhs, rhs, preferred_element_type=F32)
         halo[:, at, :] = out.reshape(blocks, GROUP, lanes)
 
@@ -340,15 +395,20 @@
 
 
 def second_kernel(near, members, at_ref, *refs):
-    x_ref, a_ref, left_ref, right_ref, band_ref, g_ref, up_ref, dn_ref, s_ref, fw_ref = refs[:10]
-    refs = refs[10:]
+    x_ref, a_ref, g_ref, up_ref, dn_ref, s_ref, fw_ref = refs[:7]
+    refs = refs[7:]
     if near:
-        old_ref = refs[1]
-        refs = refs[2:]
-    y_ref, refs = refs[0], refs[1:]
+        _, old_ref, halo = refs[:3]
+        refs = refs[3:]
+    else:
+        left_ref, right_ref, band_ref = refs[:3]
+        refs = refs[3:]
+    y_ref, keep_ref, give_ref = refs[:3]
+    if near:
+        flux, up_t, dn_t, gain, scale = refs[3:]
+    else:
+        flux, halo, xe, up_t, dn_t, gain, scale = refs[3:]
     half = members // 2
-    chunk_refs, refs = refs[:half], refs[half:]
-    flux, xe, halo, up_t, dn_t, gain, scale = refs
     step = pl.program_id(0)
     count, chans, lanes = x_ref.shape
     blocks = halo.shape[0]
@@ -356,7 +416,6 @@
 
     @pl.when(step == 0)
     def _():
-        halo_conv(left_ref, right_ref, band_ref, True, xe, halo)
         up_t[...] = transposed(up_ref[1])
         dn_t[...] = halved(dn_ref[1])
         gain[...] = spread(g_ref[1:2], lanes)
@@ -364,6 +423,7 @@
         if near:
             flux[...] = old_ref[...]
         else:
+            halo_conv(left_ref, right_ref, band_ref, True, xe, halo)
             flux[0:HALO] = jnp.zeros((HALO,) + flux.shape[1:], BF)
             flux[tall - HALO : tall] = jnp.zeros((HALO,) + flux.shape[1:], BF)
 
@@ -386,61 +446,82 @@
         share = (tall - 2 * HALO) // members
         for k in range(half):
             dst = rank ^ (k if near else half + k)
-            chunk_refs[k][...] = flux[pl.ds(dst * share, share + 2 * HALO)]
-
-
-def second_block(near, members, at, x, a, left, right, band, gain, up, down, scale, flux_weight, earlier, step, steps):
+            chunk = flux[pl.ds(dst * share, share + 2 * HALO)]
+            if k % 2:
+                give_ref[k // 2] = chunk
+            else:
+                keep_ref[k // 2] = chunk
+
+
+def second_block(near, members, at, x, a, weights, others, step, steps):
     rows, chans, lanes = x.shape
     blocks = rows // SLOTS
+    gain, up, down, scale, flux_weight = weights
     hid = up.shape[2]
     flux = flux_weight.shape[0]
-    half = members // 2
     share = rows // members
     part = pl.BlockSpec((step, chans, lanes), lambda i, s: (s[0] + i, 0, 0))
-    args = [at, x, a, left, right, band, gain, up, down, scale, flux_weight]
-    in_specs = [part, part] + [VMEM] * 8
-    alias = {}
-    if near:
-        alias = {len(args): 0}
-        args += earlier
-        in_specs += [ANY, VMEM]
-    outs = [jax.ShapeDtypeStruct(x.shape, BF)]
-    outs += [jax.ShapeDtypeStruct((share + 2 * HALO, flux, lanes), BF)] * half
-    out_specs = [part] + [VMEM] * half
+    chunks = jax.ShapeDtypeStruct((members // 4, share + 2 * HALO, flux, lanes), BF)
+    field = jax.ShapeDtypeStruct((rows + 2 * HALO, flux, lanes), BF)
+    halo = jax.ShapeDtypeStruct((blocks, chans, lanes), F32)
+    args = [at, x, a, gain, up, down, scale, flux_weight, *others]
+    outs = [jax.ShapeDtypeStruct(x.shape, BF), chunks, chunks]
     scratch = [
-        pltpu.VMEM((TAPS - 1, SPAN, chans, lanes), BF),
-        pltpu.VMEM((blocks, chans, lanes), F32),
         pltpu.VMEM((hid, chans), BF),
         pltpu.VMEM((chans, hid), BF),
         pltpu.VMEM((chans, lanes), F32),
         pltpu.VMEM((chans, lanes), F32),
     ]
-    field = (rows + 2 * HALO, flux, lanes)
     if near:
-        scratch = [pltpu.VMEM(field, BF)] + scratch
+        scratch = [pltpu.VMEM(field.shape, BF)] + scratch
+        other_specs = [ANY, VMEM, VMEM]
     else:
-        outs.append(jax.ShapeDtypeStruct(field, BF))
-        out_specs.append(VMEM)
+        scratch = [pltpu.VMEM((TAPS - 1, SPAN, chans, lanes), BF)] + scratch
+        outs += [field, halo]
+        other_specs = [VMEM] * 3
     return pl.pallas_call(
         functools.partial(second_kernel, near, members),
         out_shape=outs,
         grid_spec=pltpu.PrefetchScalarGridSpec(
             num_scalar_prefetch=1,
             grid=(steps,),
-            in_specs=in_specs,
-            out_specs=out_specs,
+            in_specs=[part, part] + [VMEM] * 5 + other_specs,
+            out_specs=[part] + [VMEM] * (len(outs) - 1),
             scratch_shapes=scratch,
         ),
-        input_output_aliases=alias,
+        input_output_aliases={8: 0} if near else {},
         compiler_params=params(24),
         cost_estimate=cost(8 * steps * step / rows),
         name="second_block",
     )(*args)
 
 
+def add_kernel(keep_ref, got_ref, *out_refs):
+    for n, ref in enumerate(out_refs):
+        k = n + keep_ref.shape[0] - len(out_refs)
+        ref[...] = (keep_ref[k].astype(F32) + got_ref[k].astype(F32)).astype(BF)
+
+
+def add_pairs(keep, got, skip):
+    count = keep.shape[0] - skip
+    return pl.pallas_call(
+        add_kernel,
+        out_shape=[jax.ShapeDtypeStruct(keep.shape[1:], BF)] * count,
+        in_specs=[VMEM] * 2,
+        out_specs=[VMEM] * count,
+        compiler_params=params(24),
+        name="add_pairs",
+    )(keep, got)
+
+
+def send_xor(value, bits):
+    members = lax.axis_size("member")
+    return lax.ppermute(value, "member", [(i, i ^ bits) for i in range(members)])
+
+
 def force_kernel(members, *refs):
-    flux_refs = refs[:members]
-    ocean_ref, land_ref, ice_ref, lift_ref, mid_ref, p_ref, win, sem = refs[members:]
+    near_refs, flux_refs = refs[:2], refs[2 : members // 2 + 1]
+    ocean_ref, land_ref, ice_ref, lift_ref, mid_ref, p_ref, win, sem = refs[members // 2 + 1 :]
     span, flux, lanes = flux_refs[0].shape
     rows = land_ref.shape[0]
     chans = mid_ref.shape[1]
@@ -450,8 +531,8 @@
     start = jnp.clip(first, 0, rows - span)
     copy = pltpu.make_async_copy(ocean_ref.at[pl.ds(start, span)], win, sem)
     copy.start()
-    total = flux_refs[0][...].astype(F32)
-    for ref in flux_refs[1:]:
+    total = near_refs[0][0].astype(F32) + near_refs[1][0].astype(F32)
+    for ref in flux_refs:
         total = total + ref[...].astype(F32)
     low = (total / members).astype(BF)
     lift = jnp.concatenate([transposed(lift_ref[0]), transposed(lift_ref[1])], axis=0)
@@ -482,7 +563,7 @@
 
 
 def force(members, chunks, ocean, land, ice, lift):
-    span, _, lanes = chunks[0].shape
+    span, _, lanes = chunks[-1].shape
     rows, chans, _ = ocean.shape
     return pl.pallas_call(
         functools.partial(force_kernel, members),
@@ -490,7 +571,7 @@
             jax.ShapeDtypeStruct((span, chans, lanes), BF),
             jax.ShapeDtypeStruct((OCEAN_BLOCKS, chans, lanes), BF),
         ],
-        in_specs=[VMEM] * members + [ANY, VMEM, VMEM, VMEM],
+        in_specs=[VMEM] * len(chunks) + [HBM, VMEM, VMEM, VMEM],
         out_specs=[VMEM] * 2,
         scratch_shapes=[pltpu.VMEM((span, chans, lanes), BF), pltpu.SemaphoreType.DMA(())],
         compiler_params=params(24),
@@ -601,33 +682,38 @@
     atm = (atm_gain, atm_up, atm_down.transpose(0, 2, 1), atm_scale)
     taps = atm_kernel.transpose(1, 2, 0, 3)
 
-    left, right = neighbours(pack(state, big))
-    a, band = convolve(0, state, taps, HALO, blocks)
+    state, packed = pack(state, big)
+    left, right = neighbours(packed)
+    a, band = convolve(0, state, taps, blocks)
     state, packed = first_block(state, a, left, right, band, *atm, big)
 
     left, right = neighbours(packed)
-    a, band = convolve(1, state, taps, HALO, blocks)
+    a, band = convolve(1, state, taps, blocks)
     near_steps = (rows // 2 - small) // small
     far_steps = rows // small - near_steps
     upper = rank >= half
     far_at = jnp.where(upper, 0, near_steps).astype(jnp.int32)[None]
     near_at = jnp.where(upper, far_steps, 0).astype(jnp.int32)[None]
-    shared = (state, a, left, right, band, *atm, flux_weight.T)
-    partly, *chunks, flux = second_block(False, members, far_at, *shared, [], small, far_steps)
-    sent = [
-        lax.ppermute(chunk, "member", [(i, i ^ (half + k)) for i in range(members)])
-        for k, chunk in enumerate(chunks)
-    ]
-    state, *chunks = second_block(True, members, near_at, *shared, [partly, flux], small, near_steps)
-    sent += [
-        lax.ppermute(chunks[k], "member", [(i, i ^ k) for i in range(members)])
-        for k in range(half - 1, 0, -1)
-    ]
-    sent.append(chunks[0])
+    weights = (*atm, flux_weight.T)
+    partly, keep, give, flux, halo = second_block(
+        False, members, far_at, state, a, weights, [left, right, band], small, far_steps
+    )
+    got = send_xor(give, 1)
+    state, near_keep, near_give = second_block(
+        True, members, near_at, state, a, weights, [partly, flux, halo], small, near_steps
+    )
+    near_got = send_xor(near_give, 1)
+    got, near_keep, taps = lax.optimization_barrier((got, near_keep, ocn_kernel))
+    sums = add_pairs(keep, got, 0)
+    sent = [send_xor(part, half + 2 * k) for k, part in enumerate(sums)]
+    sums = add_pairs(near_keep, near_got, 1)
+    sent += [send_xor(part, 2 * k + 2) for k, part in enumerate(sums)]
+    sent = [near_keep, near_got] + sent
+    band = ocean_band(taps)
 
     mid, packed = force(members, sent, ocean, land_mask, ice_mask, flux_lift)
     left, right = neighbours(packed)
-    a, band = convolve(None, mid, ocn_kernel, 0, OCEAN_BLOCKS)
+    a = ocean_conv(mid, band)
     ocean_rows, surface = ocean_block(
         mid, a, left, right, band, land_mask, ocn_gain, ocn_up, ocn_down.T, ocn_scale, surf_weight.T
     )

time: 104 us -> 97.4 us (0.937)
  Pallas kernels: 53.5 us -> 49.9 us
  starting transfers between devices: 20.2 us -> 17.2 us
    ppermute x7 -> x5, starting transfers between devices: 7.35 us -> 4.29 us  [send_xor(): lax.ppermute(value, 'member', [(i, i ^ bits) for i in range(members)])]
    ppermute x3, waiting for transfers between devices: 1.57 us -> 3.95 us  [neighbours(): lax.ppermute(packed, 'lon', [(i, (i + 1) % count) for i in range(count)])]
    ppermute x7 -> x5, waiting for transfers between devices: 9.18 us -> 6.91 us  [send_xor(): lax.ppermute(value, 'member', [(i, i ^ bits) for i in range(members)])]
    pallas_call x4 -> x7, Pallas kernels: 25.2 us -> 23 us  [the longest x2 18.4 us: convolve(): pl.pallas_call(functools.partial(conv_kernel, layer), grid=(groups,), out...]
    pallas_call x2, Pallas kernels: 11.6 us -> 10.1 us  [second_block(): pl.pallas_call(functools.partial(second_kernel, near, members), out_shape...]
    unnamed x46 -> x44, local copies, waits for them, and re-layouts: 9.1 us -> 9.08 us
  transfers between devices with their start and end apart: 13 -> 11, of which waited for: 5 -> 4; matrix products, arithmetic and copies ran while one was open for 0% -> 0% of each run, Pallas kernels for 22% -> 26%
where the time goes in v4:
time: 97.4 us; the launch traced here: 97.2 us
  Pallas kernels  49.9 us (51%)
  starting transfers between devices  17.2 us (18%)
  waiting for transfers between devices  10.9 us (11%)
  blocking collectives  9.27 us (10%)
  local copies, waits for them, and re-layouts  9.08 us (9%)
    pallas_call x2, Pallas kernels, convolve(): pl.pallas_call(functools.partial(conv_kernel, layer), grid=(groups,), out...  18.4 us
    ppermute x3, starting transfers between devices, neighbours(): lax.ppermute(packed, 'lon', [((i + 1) % count, i) for i in range(count)])  12.9 us
    pallas_call x2, Pallas kernels, second_block(): pl.pallas_call(functools.partial(second_kernel, near, members), out_shape...  10.1 us
    all_gather x1, blocking collectives, local(): surface = lax.all_gather(surface, 'member')  9.27 us
    unnamed x44, local copies, waits for them, and re-layouts  9.08 us
    pallas_call x1, Pallas kernels, first_block(): pl.pallas_call(first_kernel, grid=(rows // step,), out_shape=[jax.ShapeDt...  8.61 us
    ppermute x5, waiting for transfers between devices, send_xor(): lax.ppermute(value, 'member', [(i, i ^ bits) for i in range(members)])  6.91 us
    ppermute x5, starting transfers between devices, send_xor(): lax.ppermute(value, 'member', [(i, i ^ bits) for i in range(members)])  4.29 us
  transfers between devices with their start and end apart: 11, of which 4 were waited for; matrix products, arithmetic and copies ran while one was open for 0% of the time, Pallas kernels for 26%

profile of v4, /device:TPU:0, one launch (start us, length us, event | category | flops | bytes accessed | tf_op | source)
XLA Modules:
  0.0 97.2 jit_solution(11471925744523516868)
XLA Ops:
  0.6 0.0 copy-start
  0.6 1.7 %copy-done = bf16[1,96,96,128]{3,2,1,0:T(8,128)(2,1)S(1)} copy-done((bf16[1,96,96,128]{3,2,1,0:T(8,128)(2,1)S(1)}, bf16[1,96,96,128]{3,2,1,0:T(8,128)(2,1)}, u32[]{:S(2)}) %copy-start) | copy-done | bytes 2359320
  2.3 1.4 %pack_edges.1 = (bf16[96,96,128]{2,1,0:T(8,128)(2,1)S(1)}, bf16[6,96,128]{2,1,0:T(8,128)(2,1)S(1)}) custom-call(bf16[96,96,128]{2,1,0:T(8,128)(2,1)S(1)} %bitcast.12), custom_call_target="tpu_custom_call" | custom-call | tf_op jit(solution)/shard_map/pack_edges/pallas_call | solution.py:81
  3.7 5.1 %collective-permute-start.1 = (bf16[6,96,128]{2,1,0:T(8,128)(2,1)S(1)}, bf16[6,96,128]{2,1,0:T(8,128)(2,1)S(1)}, u32[]{:S(2)}, u32[]{:S(2)}) collective-permute-start(bf16[6,96,128]{2,1,0:T(8,128)(2,1)S(1)} %get-tuple-element.29), channel_id=1, source_target_pairs={{1,0},{2,1},{3,2},{0,3},{5,4},{6,5},{7,6},{4,7},{9,8},{10,9},{11,1... | collective-permute-start | bytes 442376 | tf_op jit(solution)/shard_map/ppermute | solution.py:98
  8.8 0.0 collective-permute-start
  8.8 0.0 copy-done.13
  8.8 0.0 copy-start.16
  8.8 0.0 copy-start.17
  8.8 9.2 %conv.2 = (f32[96,96,128]{2,1,0:T(8,128)S(1)}, bf16[6,96,1792]{2,1,0:T(8,128)(2,1)S(1)}) custom-call(bf16[96,96,128]{2,1,0:T(8,128)(2,1)S(1)} %get-tuple-element.27.x_ref, f32[7,7,2,96]{3,2,1,0:T(2,128)S(1)} %bitcast.21), custom_call_target="tpu_custom_call" | custom-call | flops 8000000000 | tf_op jit(solution)/shard_map/conv/pallas_call | solution.py:201
  18.1 0.0 copy-start.18
  18.1 2.1 %copy-done.18 = f32[96,96,128]{2,1,0:T(8,128)} copy-done((f32[96,96,128]{2,1,0:T(8,128)}, f32[96,96,128]{2,1,0:T(8,128)S(1)}, u32[]{:S(2)}) %copy-start.18) | copy-done | bytes 4718616
  20.2 1.3 %copy-done.20 = bf16[6,96,1792]{2,1,0:T(8,128)(2,1)} copy-done((bf16[6,96,1792]{2,1,0:T(8,128)(2,1)}, bf16[6,96,1792]{2,1,0:T(8,128)(2,1)S(1)}, u32[]{:S(2)}) %copy-start.20) | copy-done | bytes 2064408
  21.5 0.0 collective-permute-done.1.right_ref
  21.5 0.0 collective-permute-done.left_ref
  21.5 0.0 copy-done.11
  21.5 0.0 copy-done.12
  21.5 0.0 copy-done.16
  21.5 0.0 copy-done.17
  21.5 0.0 copy-start.19
  21.5 2.3 %copy-done.19 = f32[96,96,128]{2,1,0:T(8,128)S(1)} copy-done((f32[96,96,128]{2,1,0:T(8,128)S(1)}, f32[96,96,128]{2,1,0:T(8,128)}, u32[]{:S(2)}) %copy-start.19) | copy-done | bytes 4718616
  23.9 1.6 %copy-done.21 = bf16[6,96,1792]{2,1,0:T(8,128)(2,1)S(1)} copy-done((bf16[6,96,1792]{2,1,0:T(8,128)(2,1)S(1)}, bf16[6,96,1792]{2,1,0:T(8,128)(2,1)}, u32[]{:S(2)}) %copy-start.21) | copy-done | bytes 2064408
  25.5 8.6 %first_block.1 = (bf16[96,96,128]{2,1,0:T(8,128)(2,1)S(1)}, bf16[6,96,128]{2,1,0:T(8,128)(2,1)S(1)}) custom-call(bf16[96,96,128]{2,1,0:T(8,128)(2,1)S(1)} %get-tuple-element.27.x_ref, f32[96,96,128]{2,1,0:T(8,128)S(1)} %copy-done.19, bf16[6,96,128]{2,1,0:T(8,128)(2,1)S(1)} %collective-permute-done.left_ref, ...), custom_call_target="tpu_custom_call" | custom-call | flops 8000000000 | tf_op jit(solution)/shard_map/first_block/pallas_call | solution.py:374
  34.1 3.9 %collective-permute-start.3 = (bf16[6,96,128]{2,1,0:T(8,128)(2,1)S(1)}, bf16[6,96,128]{2,1,0:T(8,128)(2,1)S(1)}, u32[]{:S(2)}, u32[]{:S(2)}) collective-permute-start(bf16[6,96,128]{2,1,0:T(8,128)(2,1)S(1)} %get-tuple-element.33), channel_id=1, source_target_pairs={{1,0},{2,1},{3,2},{0,3},{5,4},{6,5},{7,6},{4,7},{9,8},{10,9},{11,1... | collective-permute-start | bytes 442376 | tf_op jit(solution)/shard_map/ppermute | solution.py:98
  37.9 0.0 collective-permute-start.2
  37.9 9.2 %conv.3 = (f32[96,96,128]{2,1,0:T(8,128)S(1)}, bf16[6,96,1792]{2,1,0:T(8,128)(2,1)S(1)}) custom-call(bf16[96,96,128]{2,1,0:T(8,128)(2,1)S(1)} %get-tuple-element.31.x_ref.refs_0_, f32[7,7,2,96]{3,2,1,0:T(2,128)S(1)} %bitcast.22), custom_call_target="tpu_custom_call" | custom-call | flops 8000000000 | tf_op jit(solution)/shard_map/conv/pallas_call | solution.py:201
  47.2 0.0 collective-permute-done.3.refs_8_
  47.2 0.0 collective-permute-done.2.refs_7_
  47.2 0.0 copy-done.15
  47.2 6.8 %second_block.2 = (bf16[96,96,128]{2,1,0:T(8,128)(2,1)S(1)}, bf16[2,18,32,128]{3,2,1,0:T(8,128)(2,1)S(1)}, bf16[2,18,32,128]{3,2,1,0:T(8,128)(2,1)S(1)}, bf16[10...) custom-call(s32[1]{0:T(128)} %bitcast.5.at_ref, bf16[96,96,128]{2,1,0:T(8,128)(2,1)S(1)} %get-tuple-element.31.x_ref.refs_0_, ...), custom_call_target="tpu_custom_call" | custom-call | flops 5000000000 | tf_op jit(solution)/shard_map/second_block/pallas_call | solution.py:482
  54.0 0.1 collective-permute-start.4
  54.1 0.0 copy-start.14
  54.1 3.3 %second_block.3 = (bf16[96,96,128]{2,1,0:T(8,128)(2,1)S(1)}, bf16[2,18,32,128]{3,2,1,0:T(8,128)(2,1)S(1)}, bf16[2,18,32,128]{3,2,1,0:T(8,128)(2,1)S(1)}) custom-call(s32[1]{0:T(128)} %bitcast.at_ref, bf16[96,96,128]{2,1,0:T(8,128)(2,1)S(1)} %get-tuple-element.31.x_ref.refs_0_, ...), custom_call_target="tpu_custom_call", output_to_operand_aliasing={{0}: (8, {})} | custom-call | flops 3000000000 | tf_op jit(solution)/shard_map/second_block/pallas_call | solution.py:482
  57.5 0.5 collective-permute-start.5
  58.0 0.0 collective-permute-done.4.got_ref
  58.0 1.2 %collective-permute-done.5.got_ref.refs_1_ = bf16[2,18,32,128]{3,2,1,0:T(8,128)(2,1)S(1)} collective-permute-done((bf16[2,18,32,128]{3,2,1,0:T(8,128)(2,1)S(1)}, bf16[2,18,32,128]{3,2,1,0:T(8,128)(2,1)S(1)}, u32[]{:S(2)}, u32[]{:S(2)}) %collective-permute-start.5) | collective-permute-done | bytes 294944 | tf_op jit(solution)/shard_map/ppermute | solution.py:519
  59.2 1.5 %collective-permute-start.8 = (bf16[18,32,128]{2,1,0:T(8,128)(2,1)S(1)}, bf16[18,32,128]{2,1,0:T(8,128)(2,1)S(1)}, u32[]{:S(2)}, u32[]{:S(2)}) collective-permute-start(bf16[18,32,128]{2,1,0:T(8,128)(2,1)S(1)} %add_pairs.3), channel_id=1, source_target_pairs={{0,8},{4,12},{8,0},{12,4},{16,24},{20,28},{24,16},{28,20},{1,9},{5... | collective-permute-start | bytes 442376 | tf_op jit(solution)/shard_map/ppermute | solution.py:519
  60.8 0.1 add_pairs.2
  60.8 1.6 %collective-permute-start.6 = (bf16[18,32,128]{2,1,0:T(8,128)(2,1)S(1)}, bf16[18,32,128]{2,1,0:T(8,128)(2,1)S(1)}, u32[]{:S(2)}, u32[]{:S(2)}) collective-permute-start(bf16[18,32,128]{2,1,0:T(8,128)(2,1)S(1)} %get-tuple-element.45), channel_id=1, source_target_pairs={{0,16},{4,20},{8,24},{12,28},{16,0},{20,4},{24,8},{28,12},{1,17},{... | collective-permute-start | bytes 442376 | tf_op jit(solution)/shard_map/ppermute | solution.py:519
  62.4 0.6 collective-permute-start.7
  63.0 0.0 copy-done.14
  63.0 1.2 %ocean_band.1.band_ref = bf16[6,160,1792]{2,1,0:T(8,128)(2,1)S(1)} custom-call(f32[7,7,96]{2,1,0:T(8,128)S(1)} %copy-done.14), custom_call_target="tpu_custom_call" | custom-call | flops 3000000000 | tf_op jit(solution)/shard_map/ocean_band/pallas_call | solution.py:231
  64.2 1.8 %collective-permute-done.8.refs_4_ = bf16[18,32,128]{2,1,0:T(8,128)(2,1)S(1)} collective-permute-done((bf16[18,32,128]{2,1,0:T(8,128)(2,1)S(1)}, bf16[18,32,128]{2,1,0:T(8,128)(2,1)S(1)}, u32[]{:S(2)}, u32[]{:S(2)}) %collective-permute-start.8) | collective-permute-done | bytes 147488 | tf_op jit(solution)/shard_map/ppermute | solution.py:519
  66.0 3.9 %collective-permute-done.6.refs_2_ = bf16[18,32,128]{2,1,0:T(8,128)(2,1)S(1)} collective-permute-done((bf16[18,32,128]{2,1,0:T(8,128)(2,1)S(1)}, bf16[18,32,128]{2,1,0:T(8,128)(2,1)S(1)}, u32[]{:S(2)}, u32[]{:S(2)}) %collective-permute-start.6) | collective-permute-done | bytes 147488 | tf_op jit(solution)/shard_map/ppermute | solution.py:519
  69.9 0.0 collective-permute-done.7.refs_3_
  69.9 0.0 copy-done.1
  69.9 0.0 copy-done.2
  69.9 0.0 copy-done.5
  69.9 0.0 copy-done.6
  69.9 1.0 %ocean_forcing.1 = (bf16[18,96,128]{2,1,0:T(8,128)(2,1)S(1)}, bf16[2,96,128]{2,1,0:T(8,128)(2,1)S(1)}) custom-call(bf16[2,18,32,128]{3,2,1,0:T(8,128)(2,1)S(1)} %get-tuple-element.41.keep_ref.refs_0_, bf16[2,18,32,128]{3,2,1,0:T(8,128)(2,1)S(1)} %collective-permute-done.5.got_ref.refs_1_, bf16[18,32,128]{2,1,0:T(8,128)(2,1)S(1)} %collective-permute-done.6.refs_2_, ...), custom_call_target="tpu_custom_call" | custom-call | tf_op jit(solution)/shard_map/ocean_forcing/pallas_call | solution.py:568
  71.0 3.9 %collective-permute-start.10 = (bf16[2,96,128]{2,1,0:T(8,128)(2,1)S(1)}, bf16[2,96,128]{2,1,0:T(8,128)(2,1)S(1)}, u32[]{:S(2)}, u32[]{:S(2)}) collective-permute-start(bf16[2,96,128]{2,1,0:T(8,128)(2,1)S(1)} %get-tuple-element.49), channel_id=1, source_target_pairs={{1,0},{2,1},{3,2},{0,3},{5,4},{6,5},{7,6},{4,7},{9,8},{10,9},{11,1... | collective-permute-start | bytes 147464 | tf_op jit(solution)/shard_map/ppermute | solution.py:98
  74.9 0.0 collective-permute-start.9
  74.9 0.0 copy-start.9
  74.9 0.0 copy-start.10
  74.9 1.9 %ocean_conv.1.a_ref = f32[12,96,128]{2,1,0:T(8,128)S(1)} custom-call(bf16[18,96,128]{2,1,0:T(8,128)(2,1)S(1)} %get-tuple-element.47.x_ref.mid_ref, bf16[6,160,1792]{2,1,0:T(8,128)(2,1)S(1)} %ocean_band.1.band_ref), custom_call_target="tpu_custom_call" | custom-call | flops 2000000000 | tf_op jit(solution)/shard_map/ocean_conv/pallas_call | solution.py:255
  76.8 0.0 collective-permute-done.10.right_ref
  76.8 3.9 %collective-permute-done.9.left_ref = bf16[2,96,128]{2,1,0:T(8,128)(2,1)S(1)} collective-permute-done((bf16[2,96,128]{2,1,0:T(8,128)(2,1)S(1)}, bf16[2,96,128]{2,1,0:T(8,128)(2,1)S(1)}, u32[]{:S(2)}, u32[]{:S(2)}) %collective-permute-start.9) | collective-permute-done | bytes 49184 | tf_op jit(solution)/shard_map/ppermute | solution.py:97
  80.8 0.0 copy-done.3
  80.8 0.0 copy-done.4
  80.8 0.0 copy-done.9
  80.8 0.0 copy-done.10
  80.8 0.0 copy-start.8
  80.8 2.8 %ocean_block.1 = (bf16[12,96,128]{2,1,0:T(8,128)(2,1)}, bf16[12,8,128]{2,1,0:T(8,128)(2,1)S(1)}) custom-call(bf16[18,96,128]{2,1,0:T(8,128)(2,1)S(1)} %get-tuple-element.47.x_ref.mid_ref, f32[12,96,128]{2,1,0:T(8,128)S(1)} %ocean_conv.1.a_ref, bf16[2,96,128]{2,1,0:T(8,128)(2,1)S(1)} %collective-permute-done.9.left_ref, ...), custom_call_target="tpu_custom_call" | custom-call | tf_op jit(solution)/shard_map/ocean_block/pallas_call | solution.py:607
  83.6 9.3 %all-gather = bf16[96,8,128]{2,1,0:T(8,128)(2,1)S(1)} all-gather(bf16[12,8,128]{2,1,0:T(8,128)(2,1)S(1)} %get-tuple-element.50), channel_id=2, replica_groups=mesh['member'=8,'lon'=4] {'member'}, dimensions={0}, use_global_device_ids=true | all-gather | bytes 221184 | tf_op jit(solution)/shard_map/all_gather | solution.py:720
  92.9 4.3 %couple.1 = bf16[96,96,128]{2,1,0:T(8,128)(2,1)} custom-call(bf16[96,96,128]{2,1,0:T(8,128)(2,1)S(1)} %get-tuple-element.38.y_ref, bf16[8,12,8,128]{3,2,1,0:T(8,128)(2,1)S(1)} %bitcast.13, s32[96,128]{1,0:T(8,128)S(1)} %copy-done.2, bf16[8,96]{1,0:T(8,128)(2,1)S(1)} %copy-done.8), custom_call_target="tpu_custom_call" | custom-call | tf_op jit(solution)/shard_map/couple/pallas_call | solution.py:639
  (16 shorter events, 0.1 us)
Async XLA Ops:
  0.6 1.7 %copy-start = (bf16[1,96,96,128]{3,2,1,0:T(8,128)(2,1)S(1)}, bf16[1,96,96,128]{3,2,1,0:T(8,128)(2,1)}, u32[]{:S(2)}) copy-start(bf16[1,96,96,128]{3,2,1,0:T(8,128)(2,1)} %param.18) | copy-start | bytes 7077892
  2.3 6.5 %copy-start.13 = (f32[2,7,7,96]{3,0,2,1:T(2,128)S(1)}, f32[2,7,7,96]{3,0,2,1:T(2,128)}, u32[]{:S(2)}) copy-start(f32[2,7,7,96]{3,0,2,1:T(2,128)} %param.22) | copy-start | bytes 112900
  3.7 17.8 %collective-permute-start.1 = (bf16[6,96,128]{2,1,0:T(8,128)(2,1)S(1)}, bf16[6,96,128]{2,1,0:T(8,128)(2,1)S(1)}, u32[]{:S(2)}, u32[]{:S(2)}) collective-permute-start(bf16[6,96,128]{2,1,0:T(8,128)(2,1)S(1)} %get-tuple-element.29), channel_id=1, source_target_pairs={{1,0},{2,1},{3,2},{0,3},{5,4},{6,5},{7,6},{4,7},{9,8},{10,9},{11,1... | collective-permute-start | bytes 442376 | tf_op jit(solution)/shard_map/ppermute | solution.py:98
  8.8 12.7 %collective-permute-start = (bf16[6,96,128]{2,1,0:T(8,128)(2,1)S(1)}, bf16[6,96,128]{2,1,0:T(8,128)(2,1)S(1)}, u32[]{:S(2)}, u32[]{:S(2)}) collective-permute-start(bf16[6,96,128]{2,1,0:T(8,128)(2,1)S(1)} %get-tuple-element.29), channel_id=1, source_target_pairs={{0,1},{1,2},{2,3},{3,0},{4,5},{5,6},{6,7},{7,4},{8,9},{9,10},{10,1... | collective-permute-start | bytes 442376 | tf_op jit(solution)/shard_map/ppermute | solution.py:97
  8.8 12.7 %copy-start.11 = (bf16[2,96,384]{2,1,0:T(8,128)(2,1)S(1)}, bf16[2,96,384]{2,1,0:T(8,128)(2,1)}, u32[]{:S(2)}) copy-start(bf16[2,96,384]{2,1,0:T(8,128)(2,1)} %refs_3_.3) | copy-start | bytes 442372
  8.8 12.7 %copy-start.12 = (bf16[2,384,96]{1,2,0:T(8,128)(2,1)S(1)}, bf16[2,384,96]{1,2,0:T(8,128)(2,1)}, u32[]{:S(2)}) copy-start(bf16[2,384,96]{1,2,0:T(8,128)(2,1)} %param.25) | copy-start | bytes 442372
  8.8 12.7 %copy-start.16 = (f32[2,96]{1,0:T(2,128)S(1)}, f32[2,96]{1,0:T(2,128)}, u32[]{:S(2)}) copy-start(f32[2,96]{1,0:T(2,128)} %refs_2_.3) | copy-start | bytes 2308
  8.8 12.7 %copy-start.17 = (f32[2,96]{1,0:T(2,128)S(1)}, f32[2,96]{1,0:T(2,128)}, u32[]{:S(2)}) copy-start(f32[2,96]{1,0:T(2,128)} %refs_5_.4) | copy-start | bytes 2308
  18.1 2.1 %copy-start.18 = (f32[96,96,128]{2,1,0:T(8,128)}, f32[96,96,128]{2,1,0:T(8,128)S(1)}, u32[]{:S(2)}) copy-start(f32[96,96,128]{2,1,0:T(8,128)S(1)} %get-tuple-element.28.a_ref) | copy-start | bytes 14155780
  20.2 1.3 %copy-start.20 = (bf16[6,96,1792]{2,1,0:T(8,128)(2,1)}, bf16[6,96,1792]{2,1,0:T(8,128)(2,1)S(1)}, u32[]{:S(2)}) copy-start(bf16[6,96,1792]{2,1,0:T(8,128)(2,1)S(1)} %get-tuple-element.30.band_ref) | copy-start | bytes 6193156
  21.5 2.3 %copy-start.19 = (f32[96,96,128]{2,1,0:T(8,128)S(1)}, f32[96,96,128]{2,1,0:T(8,128)}, u32[]{:S(2)}) copy-start(f32[96,96,128]{2,1,0:T(8,128)} %copy-done.18) | copy-start | bytes 14155780
  23.9 1.6 %copy-start.21 = (bf16[6,96,1792]{2,1,0:T(8,128)(2,1)S(1)}, bf16[6,96,1792]{2,1,0:T(8,128)(2,1)}, u32[]{:S(2)}) copy-start(bf16[6,96,1792]{2,1,0:T(8,128)(2,1)} %copy-done.20) | copy-start | bytes 6193156
  34.1 13.1 %collective-permute-start.3 = (bf16[6,96,128]{2,1,0:T(8,128)(2,1)S(1)}, bf16[6,96,128]{2,1,0:T(8,128)(2,1)S(1)}, u32[]{:S(2)}, u32[]{:S(2)}) collective-permute-start(bf16[6,96,128]{2,1,0:T(8,128)(2,1)S(1)} %get-tuple-element.33), channel_id=1, source_target_pairs={{1,0},{2,1},{3,2},{0,3},{5,4},{6,5},{7,6},{4,7},{9,8},{10,9},{11,1... | collective-permute-start | bytes 442376 | tf_op jit(solution)/shard_map/ppermute | solution.py:98
  37.9 9.2 %collective-permute-start.2 = (bf16[6,96,128]{2,1,0:T(8,128)(2,1)S(1)}, bf16[6,96,128]{2,1,0:T(8,128)(2,1)S(1)}, u32[]{:S(2)}, u32[]{:S(2)}) collective-permute-start(bf16[6,96,128]{2,1,0:T(8,128)(2,1)S(1)} %get-tuple-element.33), channel_id=1, source_target_pairs={{0,1},{1,2},{2,3},{3,0},{4,5},{5,6},{6,7},{7,4},{8,9},{9,10},{10,1... | collective-permute-start | bytes 442376 | tf_op jit(solution)/shard_map/ppermute | solution.py:97
  37.9 9.3 %copy-start.15 = (bf16[96,32]{0,1:T(8,128)(2,1)S(1)}, bf16[96,32]{0,1:T(8,128)(2,1)}, u32[]{:S(2)}) copy-start(bf16[96,32]{0,1:T(8,128)(2,1)} %param.27) | copy-start | bytes 18436
  54.0 4.0 %collective-permute-start.4 = (bf16[2,18,32,128]{3,2,1,0:T(8,128)(2,1)S(1)}, bf16[2,18,32,128]{3,2,1,0:T(8,128)(2,1)S(1)}, u32[]{:S(2)}, u32[]{:S(2)}) collective-permute-start(bf16[2,18,32,128]{3,2,1,0:T(8,128)(2,1)S(1)} %get-tuple-element.39), channel_id=1, source_target_pairs={{0,4},{4,0},{8,12},{12,8},{16,20},{20,16},{24,28},{28,24},{1,5},{5... | collective-permute-start | bytes 884744 | tf_op jit(solution)/shard_map/ppermute | solution.py:519
  54.1 8.9 %copy-start.14 = (f32[7,7,96]{2,1,0:T(8,128)S(1)}, f32[7,7,96]{2,1,0:T(8,128)}, u32[]{:S(2)}) copy-start(f32[7,7,96]{2,1,0:T(8,128)} %k_ref) | copy-start | bytes 56452
  57.5 1.7 %collective-permute-start.5 = (bf16[2,18,32,128]{3,2,1,0:T(8,128)(2,1)S(1)}, bf16[2,18,32,128]{3,2,1,0:T(8,128)(2,1)S(1)}, u32[]{:S(2)}, u32[]{:S(2)}) collective-permute-start(bf16[2,18,32,128]{3,2,1,0:T(8,128)(2,1)S(1)} %get-tuple-element.42), channel_id=1, source_target_pairs={{0,4},{4,0},{8,12},{12,8},{16,20},{20,16},{24,28},{28,24},{1,5},{5... | collective-permute-start | bytes 884744 | tf_op jit(solution)/shard_map/ppermute | solution.py:519
  59.2 6.7 %collective-permute-start.8 = (bf16[18,32,128]{2,1,0:T(8,128)(2,1)S(1)}, bf16[18,32,128]{2,1,0:T(8,128)(2,1)S(1)}, u32[]{:S(2)}, u32[]{:S(2)}) collective-permute-start(bf16[18,32,128]{2,1,0:T(8,128)(2,1)S(1)} %add_pairs.3), channel_id=1, source_target_pairs={{0,8},{4,12},{8,0},{12,4},{16,24},{20,28},{24,16},{28,20},{1,9},{5... | collective-permute-start | bytes 442376 | tf_op jit(solution)/shard_map/ppermute | solution.py:519
  60.8 9.1 %collective-permute-start.6 = (bf16[18,32,128]{2,1,0:T(8,128)(2,1)S(1)}, bf16[18,32,128]{2,1,0:T(8,128)(2,1)S(1)}, u32[]{:S(2)}, u32[]{:S(2)}) collective-permute-start(bf16[18,32,128]{2,1,0:T(8,128)(2,1)S(1)} %get-tuple-element.45), channel_id=1, source_target_pairs={{0,16},{4,20},{8,24},{12,28},{16,0},{20,4},{24,8},{28,12},{1,17},{... | collective-permute-start | bytes 442376 | tf_op jit(solution)/shard_map/ppermute | solution.py:519
  62.4 7.5 %copy-start.1 = (bf16[96,96,128]{2,1,0:T(8,128)(2,1)S(1)}, bf16[96,96,128]{2,1,0:T(8,128)(2,1)}, u32[]{:S(2)}) copy-start(bf16[96,96,128]{2,1,0:T(8,128)(2,1)} %refs_5_.5) | copy-start | bytes 7077892
  62.4 7.5 %copy-start.2 = (s32[96,128]{1,0:T(8,128)S(1)}, s32[96,128]{1,0:T(8,128)}, u32[]{:S(2)}) copy-start(s32[96,128]{1,0:T(8,128)} %land_ref.3) | copy-start | bytes 147460
  62.4 7.5 %copy-start.5 = (s32[96,128]{1,0:T(8,128)S(1)}, s32[96,128]{1,0:T(8,128)}, u32[]{:S(2)}) copy-start(s32[96,128]{1,0:T(8,128)} %refs_7_.1) | copy-start | bytes 147460
  62.4 7.5 %copy-start.6 = (bf16[2,32,96]{2,1,0:T(8,128)(2,1)S(1)}, bf16[2,32,96]{2,1,0:T(8,128)(2,1)}, u32[]{:S(2)}) copy-start(bf16[2,32,96]{2,1,0:T(8,128)(2,1)} %refs_8_.1) | copy-start | bytes 36868
  62.4 7.5 %collective-permute-start.7 = (bf16[18,32,128]{2,1,0:T(8,128)(2,1)S(1)}, bf16[18,32,128]{2,1,0:T(8,128)(2,1)S(1)}, u32[]{:S(2)}, u32[]{:S(2)}) collective-permute-start(bf16[18,32,128]{2,1,0:T(8,128)(2,1)S(1)} %get-tuple-element.46), channel_id=1, source_target_pairs={{0,24},{4,28},{8,16},{12,20},{16,8},{20,12},{24,0},{28,4},{1,25},{... | collective-permute-start | bytes 442376 | tf_op jit(solution)/shard_map/ppermute | solution.py:519
  71.0 5.8 %collective-permute-start.10 = (bf16[2,96,128]{2,1,0:T(8,128)(2,1)S(1)}, bf16[2,96,128]{2,1,0:T(8,128)(2,1)S(1)}, u32[]{:S(2)}, u32[]{:S(2)}) collective-permute-start(bf16[2,96,128]{2,1,0:T(8,128)(2,1)S(1)} %get-tuple-element.49), channel_id=1, source_target_pairs={{1,0},{2,1},{3,2},{0,3},{5,4},{6,5},{7,6},{4,7},{9,8},{10,9},{11,1... | collective-permute-start | bytes 147464 | tf_op jit(solution)/shard_map/ppermute | solution.py:98
  74.9 5.9 %collective-permute-start.9 = (bf16[2,96,128]{2,1,0:T(8,128)(2,1)S(1)}, bf16[2,96,128]{2,1,0:T(8,128)(2,1)S(1)}, u32[]{:S(2)}, u32[]{:S(2)}) collective-permute-start(bf16[2,96,128]{2,1,0:T(8,128)(2,1)S(1)} %get-tuple-element.49), channel_id=1, source_target_pairs={{0,1},{1,2},{2,3},{3,0},{4,5},{5,6},{6,7},{7,4},{8,9},{9,10},{10,1... | collective-permute-start | bytes 147464 | tf_op jit(solution)/shard_map/ppermute | solution.py:97
  74.9 5.9 %copy-start.3 = (bf16[96,384]{1,0:T(8,128)(2,1)S(1)}, bf16[96,384]{1,0:T(8,128)(2,1)}, u32[]{:S(2)}) copy-start(bf16[96,384]{1,0:T(8,128)(2,1)} %up_ref.3) | copy-start | bytes 221188
  74.9 5.9 %copy-start.4 = (bf16[384,96]{0,1:T(8,128)(2,1)S(1)}, bf16[384,96]{0,1:T(8,128)(2,1)}, u32[]{:S(2)}) copy-start(bf16[384,96]{0,1:T(8,128)(2,1)} %param.32) | copy-start | bytes 221188
  74.9 5.9 %copy-start.7 = (bf16[96,8]{0,1:T(8,128)(2,1)S(1)}, bf16[96,8]{0,1:T(8,128)(2,1)}, u32[]{:S(2)}) copy-start(bf16[96,8]{0,1:T(8,128)(2,1)} %param.34) | copy-start | bytes 4612
  74.9 5.9 %copy-start.9 = (f32[96]{0:T(128)S(1)}, f32[96]{0:T(128)}, u32[]{:S(2)}) copy-start(f32[96]{0:T(128)} %param.30) | copy-start | bytes 1156
  74.9 5.9 %copy-start.10 = (f32[96]{0:T(128)S(1)}, f32[96]{0:T(128)}, u32[]{:S(2)}) copy-start(f32[96]{0:T(128)} %param.33) | copy-start | bytes 1156
  80.8 12.1 %copy-start.8 = (bf16[8,96]{1,0:T(8,128)(2,1)S(1)}, bf16[8,96]{1,0:T(8,128)(2,1)}, u32[]{:S(2)}) copy-start(bf16[8,96]{1,0:T(8,128)(2,1)} %bw_ref.1) | copy-start | bytes 4612

commit v5 on v4

--- a/solution.py
+++ b/solution.py
@@ -20,6 +20,7 @@
 SLOT = 8
 SLOTS = 16
 OCEAN_BLOCKS = 2
+BIG = 32
 BY_DOT = (0, 1, 5, 6)
 VMEM = pl.BlockSpec(memory_space=pltpu.VMEM)
 ANY = pl.BlockSpec(memory_space=pl.ANY)
@@ -177,43 +178,41 @@
         a_ref[s : s + take] = part.reshape(take, GROUP, lanes)
 
 
-def conv_kernel(layer, x_ref, k_ref, a_ref, band_ref, base, smat, xj, band):
-    g = pl.program_id(0)
-    count, _, lanes = x_ref.shape
-
-    @pl.when(g == 0)
-    def _():
-        fill_base(lambda i: k_ref[i, :, layer, :], base)
-        smat[...] = shift_matrix(lanes)
-        clear_pads(HALO, count, xj)
-
-    fill_band(base, g, band)
-    band_ref[0] = band[: band_ref.shape[1]]
-    fill_shifts(x_ref[...], HALO, smat[...], xj)
-    apply_band(band[...], xj, a_ref)
+def conv_kernel(layer, x_ref, k_ref, a_ref, band_ref, base, xj, band):
+    rows, chans, lanes = x_ref.shape
+    fill_base(lambda i: k_ref[i, :, layer, :], base)
+    smat = shift_matrix(lanes)
+    clear_pads(HALO, rows, xj)
+
+    def group(g, carry):
+        at = pl.ds(pl.multiple_of(GROUP * g, GROUP), GROUP)
+        fill_band(base, g, band)
+        band_ref[g] = band[: band_ref.shape[1]]
+        fill_shifts(x_ref[:, at, :], HALO, smat, xj)
+        apply_band(band[...], xj, a_ref.at[:, at, :])
+        return carry
+
+    lax.fori_loop(0, chans // GROUP, group, 0)
 
 
 def convolve(layer, x, taps, blocks):
     rows, chans, lanes = x.shape
     groups = chans // GROUP
     wide = TAPS * DEPTH
-    part = pl.BlockSpec((rows, GROUP, lanes), lambda g: (0, g, 0))
     return pl.pallas_call(
         functools.partial(conv_kernel, layer),
-        grid=(groups,),
         out_shape=[
             jax.ShapeDtypeStruct((rows, chans, lanes), F32),
             jax.ShapeDtypeStruct((groups, blocks * GROUP, wide), BF),
         ],
-        in_specs=[part, VMEM],
-        out_specs=[part, pl.BlockSpec((1, blocks * GROUP, wide), lambda g: (g, 0, 0))],
+        in_specs=[VMEM, VMEM],
+        out_specs=[VMEM, VMEM],
         scratch_shapes=[
             pltpu.VMEM((groups, GROUP, wide), F32),
-            pltpu.VMEM((lanes, len(BY_DOT) * lanes), BF),
             pltpu.VMEM((TAPS, rows + 2 * HALO, GROUP, lanes), BF),
             pltpu.VMEM((GROUP * OUT, wide), BF),
         ],
-        compiler_params=params(24),
+        compiler_params=params(BIG),
         cost_estimate=cost(8),
         name="conv",
     )(x, taps)
@@ -325,14 +324,14 @@
         halo[:, at, :] = out.reshape(blocks, GROUP, lanes)
 
 
-def branch_of(a_ref, halo, slot0, gain, up_t, down_t):
-    count, chans, lanes = a_ref.shape
+def branch_of(a_ref, row0, count, halo, slot0, gain, up_t, down_t):
+    _, chans, lanes = a_ref.shape
     blocks = halo.shape[0]
     edge = edge_lanes((chans, lanes))
     normed = []
     for r in range(count):
         shift = lax.rem(lanes - SLOT * (slot0 + r // blocks), lanes)
-        a = a_ref[r] + jnp.where(edge, pltpu.roll(halo[r % blocks], shift, 1), 0.0)
+        a = a_ref[row0 + r] + jnp.where(edge, pltpu.roll(halo[r % blocks], shift, 1), 0.0)
         center = a - jnp.mean(a, axis=0, keepdims=True)
         var = jnp.mean(center * center, axis=0, keepdims=True)
         normed.append((center * lax.rsqrt(var + 1e-06) * gain).astype(BF))
@@ -341,156 +340,126 @@
     return jnp.dot(down_t, h, preferred_element_type=F32)
 
 
-def first_kernel(x_ref, a_ref, left_ref, right_ref, band_ref, g_ref, up_ref, dn_ref, s_ref, y_ref, p_ref, xe, halo, up_t, dn_t, gain, scale):
-    step = pl.program_id(0)
-    count, chans, lanes = x_ref.shape
+def first_kernel(count, x_ref, a_ref, left_ref, right_ref, band_ref, g_ref, up_ref, dn_ref, s_ref, y_ref, p_ref, xe, halo):
+    rows, chans, lanes = x_ref.shape
     blocks = halo.shape[0]
-
-    @pl.when(step == 0)
-    def _():
-        halo_conv(left_ref, right_ref, band_ref, True, xe, halo)
-        up_t[...] = transposed(up_ref[0])
-        dn_t[...] = halved(dn_ref[0])
-        gain[...] = spread(g_ref[0:1], lanes)
-        scale[...] = spread(s_ref[0:1], lanes)
-        p_ref[...] = jnp.zeros(p_ref.shape, BF)
-
-    slot0 = step * (count // blocks)
-    branch = branch_of(a_ref, halo, slot0, gain[...], up_t[...], dn_t[...])
+    halo_conv(left_ref, right_ref, band_ref, True, xe, halo)
+    up_t = transposed(up_ref[0])
+    dn_t = halved(dn_ref[0])
+    gain = spread(g_ref[0:1], lanes)
+    scale = spread(s_ref[0:1], lanes)
     keep = edge_lanes((chans, lanes)).astype(F32).astype(BF)
-    for r in range(count):
-        y = x_ref[r].astype(F32) + scale[...] * branch[:, r * lanes : (r + 1) * lanes]
-        y = y.astype(BF)
-        y_ref[r] = y
-        moved = pltpu.roll(y * keep, SLOT * (slot0 + r // blocks), 1)
-        p_ref[r % blocks] = p_ref[r % blocks] + moved
+    p_ref[...] = jnp.zeros(p_ref.shape, BF)
+
+    def part(step, carry):
+        row0 = step * count
+        slot0 = step * (count // blocks)
+        branch = branch_of(a_ref, row0, count, halo, slot0, gain, up_t, dn_t)
+        for r in range(count):
+            y = x_ref[row0 + r].astype(F32) + scale * branch[:, r * lanes : (r + 1) * lanes]
+            y = y.astype(BF)
+            y_ref[row0 + r] = y
+            moved = pltpu.roll(y * keep, SLOT * (slot0 + r // blocks), 1)
+            p_ref[r % blocks] = p_ref[r % blocks] + moved
+        return carry
+
+    lax.fori_loop(0, rows // count, part, 0)
 
 
 def first_block(x, a, left, right, band, gain, up, down, scale, step):
     rows, chans, lanes = x.shape
     blocks = rows // SLOTS
-    hid = up.shape[2]
-    part = pl.BlockSpec((step, chans, lanes), lambda i: (i, 0, 0))
-    return pl.pallas_call(
-        first_kernel,
-        grid=(rows // step,),
+    return pl.pallas_call(
+        functools.partial(first_kernel, step),
         out_shape=[
             jax.ShapeDtypeStruct(x.shape, BF),
             jax.ShapeDtypeStruct((blocks, chans, lanes), BF),
         ],
-        in_specs=[part, part] + [VMEM] * 7,
-        out_specs=[part, pl.BlockSpec((blocks, chans, lanes), lambda i: (0, 0, 0))],
+        in_specs=[VMEM] * 9,
+        out_specs=[VMEM] * 2,
         scratch_shapes=[
             pltpu.VMEM((TAPS - 1, SPAN, chans, lanes), BF),
             pltpu.VMEM((blocks, chans, lanes), F32),
-            pltpu.VMEM((hid, chans), BF),
-            pltpu.VMEM((chans, hid), BF),
-            pltpu.VMEM((chans, lanes), F32),
-            pltpu.VMEM((chans, lanes), F32),
-        ],
-        compiler_params=params(24),
+        ],
+        compiler_params=params(BIG),
         cost_estimate=cost(8),
         name="first_block",
     )(x, a, left, right, band, gain, up, down, scale)
 
 
-def second_kernel(near, members, at_ref, *refs):
-    x_ref, a_ref, g_ref, up_ref, dn_ref, s_ref, fw_ref = refs[:7]
-    refs = refs[7:]
+def second_kernel(near, members, count, steps, x_ref, a_ref, g_ref, up_ref, dn_ref, s_ref, fw_ref, *refs):
     if near:
-        _, old_ref, halo = refs[:3]
-        refs = refs[3:]
+        _, old_ref, halo, y_ref, keep_ref, give_ref, flux = refs
     else:
-        left_ref, right_ref, band_ref = refs[:3]
-        refs = refs[3:]
-    y_ref, keep_ref, give_ref = refs[:3]
+        left_ref, right_ref, band_ref, y_ref, keep_ref, give_ref, flux, halo, xe = refs
+    half = members // 2
+    rows, chans, lanes = x_ref.shape
+    blocks = halo.shape[0]
+    rank = lax.axis_index("member")
+    at = jnp.where(rank >= half, rows // count - steps, 0)
+    if not near:
+        at = rows // count - steps - at
     if near:
-        flux, up_t, dn_t, gain, scale = refs[3:]
+        flux[...] = old_ref[...]
     else:
-        flux, halo, xe, up_t, dn_t, gain, scale = refs[3:]
-    half = members // 2
-    step = pl.program_id(0)
-    count, chans, lanes = x_ref.shape
-    blocks = halo.shape[0]
-    tall = flux.shape[0]
-
-    @pl.when(step == 0)
-    def _():
-        up_t[...] = transposed(up_ref[1])
-        dn_t[...] = halved(dn_ref[1])
-        gain[...] = spread(g_ref[1:2], lanes)
-        scale[...] = spread(s_ref[1:2], lanes)
-        if near:
-            flux[...] = old_ref[...]
+        halo_conv(left_ref, right_ref, band_ref, True, xe, halo)
+        blank = jnp.zeros((HALO,) + flux.shape[1:], BF)
+        flux[0:HALO] = blank
+        flux[rows + HALO : rows + 2 * HALO] = blank
+    up_t = transposed(up_ref[1])
+    dn_t = halved(dn_ref[1])
+    gain = spread(g_ref[1:2], lanes)
+    scale = spread(s_ref[1:2], lanes)
+
+    def part(step, carry):
+        row0 = (at + step) * count
+        slot0 = (at + step) * (count // blocks)
+        branch = branch_of(a_ref, row0, count, halo, slot0, gain, up_t, dn_t)
+        made = []
+        for r in range(count):
+            y = x_ref[row0 + r].astype(F32) + scale * branch[:, r * lanes : (r + 1) * lanes]
+            made.append(y.astype(BF))
+            y_ref[row0 + r] = made[r]
+        z = jnp.dot(fw_ref[...], jnp.concatenate(made, axis=1), preferred_element_type=F32)
+        f = (0.5 * twice_gelu(z)).astype(BF)
+        for r in range(count):
+            flux[row0 + HALO + r] = f[:, r * lanes : (r + 1) * lanes]
+        return carry
+
+    lax.fori_loop(0, steps, part, 0)
+    share = rows // members
+    for k in range(half):
+        dst = rank ^ (k if near else half + k)
+        chunk = flux[pl.ds(dst * share, share + 2 * HALO)]
+        if k % 2:
+            give_ref[k // 2] = chunk
         else:
-            halo_conv(left_ref, right_ref, band_ref, True, xe, halo)
-            flux[0:HALO] = jnp.zeros((HALO,) + flux.shape[1:], BF)
-            flux[tall - HALO : tall] = jnp.zeros((HALO,) + flux.shape[1:], BF)
-
-    row0 = (at_ref[0] + step) * count
-    slot0 = (at_ref[0] + step) * (count // blocks)
-    branch = branch_of(a_ref, halo, slot0, gain[...], up_t[...], dn_t[...])
-    made = []
-    for r in range(count):
-        y = x_ref[r].astype(F32) + scale[...] * branch[:, r * lanes : (r + 1) * lanes]
-        made.append(y.astype(BF))
-        y_ref[r] = made[r]
-    z = jnp.dot(fw_ref[...], jnp.concatenate(made, axis=1), preferred_element_type=F32)
-    f = (0.5 * twice_gelu(z)).astype(BF)
-    for r in range(count):
-        flux[row0 + HALO + r] = f[:, r * lanes : (r + 1) * lanes]
-
-    @pl.when(step == pl.num_programs(0) - 1)
-    def _():
-        rank = lax.axis_index("member")
-        share = (tall - 2 * HALO) // members
-        for k in range(half):
-            dst = rank ^ (k if near else half + k)
-            chunk = flux[pl.ds(dst * share, share + 2 * HALO)]
-            if k % 2:
-                give_ref[k // 2] = chunk
-            else:
-                keep_ref[k // 2] = chunk
-
-
-def second_block(near, members, at, x, a, weights, others, step, steps):
+            keep_ref[k // 2] = chunk
+
+
+def second_block(near, members, x, a, weights, others, step, steps):
     rows, chans, lanes = x.shape
     blocks = rows // SLOTS
-    gain, up, down, scale, flux_weight = weights
-    hid = up.shape[2]
-    flux = flux_weight.shape[0]
+    flux = weights[-1].shape[0]
     share = rows // members
-    part = pl.BlockSpec((step, chans, lanes), lambda i, s: (s[0] + i, 0, 0))
     chunks = jax.ShapeDtypeStruct((members // 4, share + 2 * HALO, flux, lanes), BF)
     field = jax.ShapeDtypeStruct((rows + 2 * HALO, flux, lanes), BF)
     halo = jax.ShapeDtypeStruct((blocks, chans, lanes), F32)
-    args = [at, x, a, gain, up, down, scale, flux_weight, *others]
+    args = [x, a, *weights, *others]
     outs = [jax.ShapeDtypeStruct(x.shape, BF), chunks, chunks]
-    scratch = [
-        pltpu.VMEM((hid, chans), BF),
-        pltpu.VMEM((chans, hid), BF),
-        pltpu.VMEM((chans, lanes), F32),
-        pltpu.VMEM((chans, lanes), F32),
-    ]
     if near:
-        scratch = [pltpu.VMEM(field.shape, BF)] + scratch
-        other_specs = [ANY, VMEM, VMEM]
+        scratch = [pltpu.VMEM(field.shape, BF)]
     else:
-        scratch = [pltpu.VMEM((TAPS - 1, SPAN, chans, lanes), BF)] + scratch
+        scratch = [pltpu.VMEM((TAPS - 1, SPAN, chans, lanes), BF)]
         outs += [field, halo]
-        other_specs = [VMEM] * 3
-    return pl.pallas_call(
-        functools.partial(second_kernel, near, members),
+    return pl.pallas_call(
+        functools.partial(second_kernel, near, members, step, steps),
         out_shape=outs,
-        grid_spec=pltpu.PrefetchScalarGridSpec(
-            num_scalar_prefetch=1,
-            grid=(steps,),
-            in_specs=[part, part] + [VMEM] * 5 + other_specs,
-            out_specs=[part] + [VMEM] * (len(outs) - 1),
-            scratch_shapes=scratch,
-        ),
-        input_output_aliases={8: 0} if near else {},
-        compiler_params=params(24),
+        in_specs=[VMEM] * len(args),
+        out_specs=[VMEM] * len(outs),
+        scratch_shapes=scratch,
+        input_output_aliases={7: 0} if near else {},
+        compiler_params=params(BIG),
         cost_estimate=cost(8 * steps * step / rows),
         name="second_block",
     )(*args)
@@ -585,7 +554,7 @@
     gain = spread(g_ref[...], lanes)
     scale = spread(s_ref[...], lanes)
     branch = branch_of(
-        a_ref, halo, 0, gain, transposed(up_ref[...]), halved(dn_ref[...])
+        a_ref, 0, share, halo, 0, gain, transposed(up_ref[...]), halved(dn_ref[...])
     )
     first = lax.axis_index("member") * share
     made = []
@@ -621,32 +590,27 @@
     )(mid, a, left, right, band, land, gain[None], up, down, scale[None], surf_weight)
 
 
-def couple_kernel(y_ref, surf_ref, land_ref, bw_ref, o_ref):
-    share, chans, lanes = y_ref.shape
-    surf = jnp.concatenate([surf_ref[0, r] for r in range(share)], axis=1)
-    back = jnp.dot(transposed(bw_ref[...]), surf, preferred_element_type=F32)
-    first = pl.program_id(0) * share
-    for r in range(share):
-        sea = (1 - land_ref[pl.ds(first + r, 1), :]).astype(F32)
-        out = y_ref[r].astype(F32) + sea * back[:, r * lanes : (r + 1) * lanes]
+def couple_kernel(count, y_ref, surf_ref, land_ref, bw_ref, o_ref):
+    rows, chans, lanes = y_ref.shape
+    share = surf_ref.shape[1]
+    first = pl.program_id(0) * count
+    owner = pl.program_id(0) * (count // share)
+    surf = [surf_ref[owner + r // share, r % share] for r in range(count)]
+    back = jnp.dot(bw_ref[...], jnp.concatenate(surf, axis=1), preferred_element_type=F32)
+    sea = (1 - land_ref[pl.ds(pl.multiple_of(first, SLOT), count), :]).astype(F32)
+    for r in range(count):
+        out = y_ref[first + r].astype(F32) + sea[r : r + 1] * back[:, r * lanes : (r + 1) * lanes]
         o_ref[r] = out.astype(BF)
 
 
-def couple(y, surface, land, back_weight):
-    members, share, surf, lanes = surface.shape
-    chans = y.shape[1]
-    rows = pl.BlockSpec((share, chans, lanes), lambda i: (i, 0, 0))
-    return pl.pallas_call(
-        couple_kernel,
-        grid=(members,),
+def couple(y, surface, land, back_weight, count):
+    rows, chans, lanes = y.shape
+    return pl.pallas_call(
+        functools.partial(couple_kernel, count),
+        grid=(rows // count,),
         out_shape=jax.ShapeDtypeStruct(y.shape, BF),
-        in_specs=[
-            rows,
-            pl.BlockSpec((1, share, surf, lanes), lambda i: (i, 0, 0, 0)),
-            VMEM,
-            VMEM,
-        ],
-        out_specs=rows,
+        in_specs=[VMEM] * 4,
+        out_specs=pl.BlockSpec((count, chans, lanes), lambda i: (i, 0, 0)),
         compiler_params=params(24),
         name="couple",
     )(y, surface, land, back_weight)
@@ -673,7 +637,6 @@
     back_weight,
 ):
     members = lax.axis_size("member")
-    rank = lax.axis_index("member")
     half = members // 2
     state = atmos[0]
     rows = state.shape[0]
@@ -691,16 +654,13 @@
     a, band = convolve(1, state, taps, blocks)
     near_steps = (rows // 2 - small) // small
     far_steps = rows // small - near_steps
-    upper = rank >= half
-    far_at = jnp.where(upper, 0, near_steps).astype(jnp.int32)[None]
-    near_at = jnp.where(upper, far_steps, 0).astype(jnp.int32)[None]
     weights = (*atm, flux_weight.T)
     partly, keep, give, flux, halo = second_block(
-        False, members, far_at, state, a, weights, [left, right, band], small, far_steps
+        False, members, state, a, weights, [left, right, band], small, far_steps
     )
     got = send_xor(give, 1)
     state, near_keep, near_give = second_block(
-        True, members, near_at, state, a, weights, [partly, flux, halo], small, near_steps
+        True, members, state, a, weights, [partly, flux, halo], small, near_steps
     )
     near_got = send_xor(near_give, 1)
     got, near_keep, taps = lax.optimization_barrier((got, near_keep, ocn_kernel))
@@ -718,7 +678,7 @@
         mid, a, left, right, band, land_mask, ocn_gain, ocn_up, ocn_down.T, ocn_scale, surf_weight.T
     )
     surface = lax.all_gather(surface, "member")
-    out = couple(state, surface, land_mask, back_weight)
+    out = couple(state, surface, land_mask, back_weight.T, big)
     return (out[None], ocean_rows)
 
 

time: 97.4 us -> 85 us (0.87)
  local copies, waits for them, and re-layouts: 9.08 us -> 3.36 us
  waiting for transfers between devices: 10.9 us -> 7.7 us
  starting transfers between devices: 17.2 us -> 15.3 us
  Pallas kernels: 49.9 us -> 48.3 us
    ppermute x3, starting transfers between devices: 12.9 us -> 5.96 us  [neighbours(): lax.ppermute(packed, 'lon', [((i + 1) % count, i) for i in range(count)])]
    unnamed x44 -> x39, local copies, waits for them, and re-layouts: 9.08 us -> 3.36 us
    ppermute x3, starting transfers between devices: 0.01 us -> 5.15 us  [neighbours(): lax.ppermute(packed, 'lon', [(i, (i + 1) % count) for i in range(count)])]
    ppermute x3, waiting for transfers between devices: 3.95 us -> 1.34 us  [neighbours(): lax.ppermute(packed, 'lon', [(i, (i + 1) % count) for i in range(count)])]
    pallas_call x6, Pallas kernels: 41.5 us -> 39.9 us  [the longest x2 17.4 us: convolve(): pl.pallas_call(functools.partial(conv_kernel, layer), out_shape=[jax.Shap...]
    ppermute x5, waiting for transfers between devices: 6.91 us -> 5.67 us  [send_xor(): lax.ppermute(value, 'member', [(i, i ^ bits) for i in range(members)])]
  transfers between devices with their start and end apart: 11 -> 11, of which waited for: 4 -> 5; matrix products, arithmetic and copies ran while one was open for 0% -> 1% of each run, Pallas kernels for 26% -> 29%
where the time goes in v5:
time: 85 us; the launch traced here: 84.8 us
  Pallas kernels  48.3 us (57%)
  starting transfers between devices  15.3 us (18%)
  blocking collectives  9.26 us (11%)
  waiting for transfers between devices  7.7 us (9%)
  local copies, waits for them, and re-layouts  3.36 us (4%)
  between operations  0.87 us (1%)
    pallas_call x2, Pallas kernels, convolve(): pl.pallas_call(functools.partial(conv_kernel, layer), out_shape=[jax.Shap...  17.4 us
    pallas_call x2, Pallas kernels, second_block(): pl.pallas_call(functools.partial(second_kernel, near, members, step, step...  11.3 us
    all_gather x1, blocking collectives, local(): surface = lax.all_gather(surface, 'member')  9.26 us
    pallas_call x1, Pallas kernels, first_block(): pl.pallas_call(functools.partial(first_kernel, step), out_shape=[jax.Shap...  8.68 us
    ppermute x3, starting transfers between devices, neighbours(): lax.ppermute(packed, 'lon', [((i + 1) % count, i) for i in range(count)])  5.96 us
    ppermute x5, waiting for transfers between devices, send_xor(): lax.ppermute(value, 'member', [(i, i ^ bits) for i in range(members)])  5.67 us
    ppermute x3, starting transfers between devices, neighbours(): lax.ppermute(packed, 'lon', [(i, (i + 1) % count) for i in range(count)])  5.15 us
    ppermute x5, starting transfers between devices, send_xor(): lax.ppermute(value, 'member', [(i, i ^ bits) for i in range(members)])  4.21 us
  transfers between devices with their start and end apart: 11, of which 5 were waited for; matrix products, arithmetic and copies ran while one was open for 1% of the time, Pallas kernels for 29%

profile of v5, /device:TPU:0, one launch (start us, length us, event | category | flops | bytes accessed | tf_op | source)
XLA Modules:
  0.0 84.8 jit_solution(2441454369236386779)
XLA Ops:
  0.6 0.0 copy-start
  0.6 1.7 %copy-done = bf16[1,96,96,128]{3,2,1,0:T(8,128)(2,1)S(1)} copy-done((bf16[1,96,96,128]{3,2,1,0:T(8,128)(2,1)S(1)}, bf16[1,96,96,128]{3,2,1,0:T(8,128)(2,1)}, u32[]{:S(2)}) %copy-start) | copy-done | bytes 2359320
  2.3 0.0 copy-start.13
  2.3 1.4 %pack_edges.1 = (bf16[96,96,128]{2,1,0:T(8,128)(2,1)S(1)}, bf16[6,96,128]{2,1,0:T(8,128)(2,1)S(1)}) custom-call(bf16[96,96,128]{2,1,0:T(8,128)(2,1)S(1)} %bitcast.11), custom_call_target="tpu_custom_call" | custom-call | tf_op jit(solution)/shard_map/pack_edges/pallas_call | solution.py:82
  3.7 3.1 %collective-permute-start = (bf16[6,96,128]{2,1,0:T(8,128)(2,1)S(1)}, bf16[6,96,128]{2,1,0:T(8,128)(2,1)S(1)}, u32[]{:S(2)}, u32[]{:S(2)}) collective-permute-start(bf16[6,96,128]{2,1,0:T(8,128)(2,1)S(1)} %get-tuple-element.29), channel_id=1, source_target_pairs={{0,1},{1,2},{2,3},{3,0},{4,5},{5,6},{6,7},{7,4},{8,9},{9,10},{10,1... | collective-permute-start | bytes 442376 | tf_op jit(solution)/shard_map/ppermute | solution.py:98
  6.8 2.1 %collective-permute-start.1 = (bf16[6,96,128]{2,1,0:T(8,128)(2,1)S(1)}, bf16[6,96,128]{2,1,0:T(8,128)(2,1)S(1)}, u32[]{:S(2)}, u32[]{:S(2)}) collective-permute-start(bf16[6,96,128]{2,1,0:T(8,128)(2,1)S(1)} %get-tuple-element.29), channel_id=1, source_target_pairs={{1,0},{2,1},{3,2},{0,3},{5,4},{6,5},{7,6},{4,7},{9,8},{10,9},{11,1... | collective-permute-start | bytes 442376 | tf_op jit(solution)/shard_map/ppermute | solution.py:99
  8.8 0.0 copy-done.13
  8.9 0.0 copy-start.11
  8.9 0.0 copy-start.12
  8.9 0.0 copy-start.16
  8.9 0.0 copy-start.17
  8.9 8.7 %conv.2 = (f32[96,96,128]{2,1,0:T(8,128)S(1)}, bf16[6,96,1792]{2,1,0:T(8,128)(2,1)S(1)}) custom-call(bf16[96,96,128]{2,1,0:T(8,128)(2,1)S(1)} %get-tuple-element.27.x_ref, f32[7,7,2,96]{3,2,1,0:T(2,128)S(1)} %bitcast.21), custom_call_target="tpu_custom_call" | custom-call | flops 8000000000 | tf_op jit(solution)/shard_map/conv/pallas_call | solution.py:202
  17.6 0.0 collective-permute-done.left_ref
  17.6 0.0 collective-permute-done.1.right_ref
  17.6 0.0 copy-done.11
  17.6 0.0 copy-done.12
  17.6 0.0 copy-done.16
  17.6 0.0 copy-done.17
  17.6 8.7 %first_block.1 = (bf16[96,96,128]{2,1,0:T(8,128)(2,1)S(1)}, bf16[6,96,128]{2,1,0:T(8,128)(2,1)S(1)}) custom-call(bf16[96,96,128]{2,1,0:T(8,128)(2,1)S(1)} %get-tuple-element.27.x_ref, f32[96,96,128]{2,1,0:T(8,128)S(1)} %get-tuple-element.28.a_ref, bf16[6,96,128]{2,1,0:T(8,128)(2,1)S(1)} %collective-permute-done.left_ref, ...), custom_call_target="tpu_custom_call" | custom-call | flops 8000000000 | tf_op jit(solution)/shard_map/first_block/pallas_call | solution.py:372
  26.3 0.1 collective-permute-start.2
  26.4 3.8 %collective-permute-start.3 = (bf16[6,96,128]{2,1,0:T(8,128)(2,1)S(1)}, bf16[6,96,128]{2,1,0:T(8,128)(2,1)S(1)}, u32[]{:S(2)}, u32[]{:S(2)}) collective-permute-start(bf16[6,96,128]{2,1,0:T(8,128)(2,1)S(1)} %get-tuple-element.33), channel_id=1, source_target_pairs={{1,0},{2,1},{3,2},{0,3},{5,4},{6,5},{7,6},{4,7},{9,8},{10,9},{11,1... | collective-permute-start | bytes 442376 | tf_op jit(solution)/shard_map/ppermute | solution.py:99
  30.2 0.0 copy-start.15
  30.2 8.7 %conv.3 = (f32[96,96,128]{2,1,0:T(8,128)S(1)}, bf16[6,96,1792]{2,1,0:T(8,128)(2,1)S(1)}) custom-call(bf16[96,96,128]{2,1,0:T(8,128)(2,1)S(1)} %get-tuple-element.31.x_ref, f32[7,7,2,96]{3,2,1,0:T(2,128)S(1)} %bitcast.22), custom_call_target="tpu_custom_call" | custom-call | flops 8000000000 | tf_op jit(solution)/shard_map/conv/pallas_call | solution.py:202
  38.9 0.0 collective-permute-done.2.refs_0_
  38.9 0.0 collective-permute-done.3.refs_1_
  38.9 0.0 copy-done.15
  39.0 7.3 %second_block.2 = (bf16[96,96,128]{2,1,0:T(8,128)(2,1)S(1)}, bf16[2,18,32,128]{3,2,1,0:T(8,128)(2,1)S(1)}, bf16[2,18,32,128]{3,2,1,0:T(8,128)(2,1)}, bf16[102,32,128]{2,1,0:T(8,128)(2,1)S(1)}, f32[6,96,128]{2,1,0:T(8,128)S(1)}) custom-call(bf16[96,96,128]{2,1,0:T(8,128)(2,1)S(1)} %get-tuple-element.31.x_ref, f32[96,96,128]{2,1,0:T(8,128)S(1)} %get-tuple-element.32.a_ref, ...), custom_call_target="tpu_custom_call" | custom-call | flops 5000000000 | tf_op jit(solution)/shard_map/second_block/pallas_call | solution.py:455
  46.3 0.0 collective-permute-start.4
  46.3 4.0 %second_block.3 = (bf16[96,96,128]{2,1,0:T(8,128)(2,1)S(1)}, bf16[2,18,32,128]{3,2,1,0:T(8,128)(2,1)S(1)}, bf16[2,18,32,128]{3,2,1,0:T(8,128)(2,1)}) custom-call(bf16[96,96,128]{2,1,0:T(8,128)(2,1)S(1)} %get-tuple-element.31.x_ref, f32[96,96,128]{2,1,0:T(8,128)S(1)} %get-tuple-element.32.a_ref, ...), custom_call_target="tpu_custom_call", output_to_operand_aliasing={{0}: (7, {})} | custom-call | flops 3000000000 | tf_op jit(solution)/shard_map/second_block/pallas_call | solution.py:455
  50.3 0.5 collective-permute-start.5
  50.8 0.0 copy-done.18
  50.8 0.7 copy.22
  51.5 0.0 collective-permute-done.4.got_ref
  51.5 0.7 collective-permute-done.5.got_ref.refs_1_
  52.2 1.7 %collective-permute-start.8 = (bf16[18,32,128]{2,1,0:T(8,128)(2,1)S(1)}, bf16[18,32,128]{2,1,0:T(8,128)(2,1)S(1)}, u32[]{:S(2)}, u32[]{:S(2)}) collective-permute-start(bf16[18,32,128]{2,1,0:T(8,128)(2,1)S(1)} %add_pairs.3), channel_id=1, source_target_pairs={{0,8},{4,12},{8,0},{12,4},{16,24},{20,28},{24,16},{28,20},{1,9},{5... | collective-permute-start | bytes 442376 | tf_op jit(solution)/shard_map/ppermute | solution.py:488
  54.0 0.1 add_pairs.2
  54.0 1.6 %collective-permute-start.6 = (bf16[18,32,128]{2,1,0:T(8,128)(2,1)S(1)}, bf16[18,32,128]{2,1,0:T(8,128)(2,1)S(1)}, u32[]{:S(2)}, u32[]{:S(2)}) collective-permute-start(bf16[18,32,128]{2,1,0:T(8,128)(2,1)S(1)} %get-tuple-element.45), channel_id=1, source_target_pairs={{0,16},{4,20},{8,24},{12,28},{16,0},{20,4},{24,8},{28,12},{1,17},{... | collective-permute-start | bytes 442376 | tf_op jit(solution)/shard_map/ppermute | solution.py:488
  55.6 0.4 collective-permute-start.7
  56.0 0.9 %copy-done.14 = f32[7,7,96]{2,1,0:T(8,128)S(1)} copy-done((f32[7,7,96]{2,1,0:T(8,128)S(1)}, f32[7,7,96]{2,1,0:T(8,128)}, u32[]{:S(2)}) %copy-start.14) | copy-done | bytes 18840
  57.0 1.2 %ocean_band.1.band_ref = bf16[6,160,1792]{2,1,0:T(8,128)(2,1)S(1)} custom-call(f32[7,7,96]{2,1,0:T(8,128)S(1)} %copy-done.14), custom_call_target="tpu_custom_call" | custom-call | flops 3000000000 | tf_op jit(solution)/shard_map/ocean_band/pallas_call | solution.py:230
  58.1 0.6 collective-permute-done.8.refs_4_
  58.8 4.3 %collective-permute-done.6.refs_2_ = bf16[18,32,128]{2,1,0:T(8,128)(2,1)S(1)} collective-permute-done((bf16[18,32,128]{2,1,0:T(8,128)(2,1)S(1)}, bf16[18,32,128]{2,1,0:T(8,128)(2,1)S(1)}, u32[]{:S(2)}, u32[]{:S(2)}) %collective-permute-start.6) | collective-permute-done | bytes 147488 | tf_op jit(solution)/shard_map/ppermute | solution.py:488
  63.1 0.0 collective-permute-done.7.refs_3_
  63.1 0.0 copy-done.1
  63.1 0.0 copy-done.2
  63.1 0.0 copy-done.6
  63.1 0.0 copy-done.7
  63.1 1.0 %ocean_forcing.1 = (bf16[18,96,128]{2,1,0:T(8,128)(2,1)S(1)}, bf16[2,96,128]{2,1,0:T(8,128)(2,1)S(1)}) custom-call(bf16[2,18,32,128]{3,2,1,0:T(8,128)(2,1)S(1)} %get-tuple-element.41.keep_ref.refs_0_, bf16[2,18,32,128]{3,2,1,0:T(8,128)(2,1)S(1)} %collective-permute-done.5.got_ref.refs_1_, bf16[18,32,128]{2,1,0:T(8,128)(2,1)S(1)} %collective-permute-done.6.refs_2_, ...), custom_call_target="tpu_custom_call" | custom-call | tf_op jit(solution)/shard_map/ocean_forcing/pallas_call | solution.py:537
  64.2 0.1 collective-permute-start.10
  64.2 2.0 %collective-permute-start.9 = (bf16[2,96,128]{2,1,0:T(8,128)(2,1)S(1)}, bf16[2,96,128]{2,1,0:T(8,128)(2,1)S(1)}, u32[]{:S(2)}, u32[]{:S(2)}) collective-permute-start(bf16[2,96,128]{2,1,0:T(8,128)(2,1)S(1)} %get-tuple-element.49), channel_id=1, source_target_pairs={{0,1},{1,2},{2,3},{3,0},{4,5},{5,6},{6,7},{7,4},{8,9},{9,10},{10,1... | collective-permute-start | bytes 147464 | tf_op jit(solution)/shard_map/ppermute | solution.py:98
  66.3 0.0 copy-start.10
  66.3 1.9 %ocean_conv.1.a_ref = f32[12,96,128]{2,1,0:T(8,128)S(1)} custom-call(bf16[18,96,128]{2,1,0:T(8,128)(2,1)S(1)} %get-tuple-element.47.x_ref.mid_ref, bf16[6,160,1792]{2,1,0:T(8,128)(2,1)S(1)} %ocean_band.1.band_ref), custom_call_target="tpu_custom_call" | custom-call | flops 2000000000 | tf_op jit(solution)/shard_map/ocean_conv/pallas_call | solution.py:254
  68.2 0.7 collective-permute-done.10.right_ref
  68.9 1.3 %collective-permute-done.9.left_ref = bf16[2,96,128]{2,1,0:T(8,128)(2,1)S(1)} collective-permute-done((bf16[2,96,128]{2,1,0:T(8,128)(2,1)S(1)}, bf16[2,96,128]{2,1,0:T(8,128)(2,1)S(1)}, u32[]{:S(2)}, u32[]{:S(2)}) %collective-permute-start.9) | collective-permute-done | bytes 49184 | tf_op jit(solution)/shard_map/ppermute | solution.py:98
  70.2 0.0 copy-done.4
  70.2 0.0 copy-done.5
  70.2 0.0 copy-done.8
  70.2 0.0 copy-done.9
  70.2 0.0 copy-done.10
  70.2 0.0 copy-start.3
  70.2 2.8 %ocean_block.1 = (bf16[12,96,128]{2,1,0:T(8,128)(2,1)}, bf16[12,8,128]{2,1,0:T(8,128)(2,1)S(1)}) custom-call(bf16[18,96,128]{2,1,0:T(8,128)(2,1)S(1)} %get-tuple-element.47.x_ref.mid_ref, f32[12,96,128]{2,1,0:T(8,128)S(1)} %ocean_conv.1.a_ref, bf16[2,96,128]{2,1,0:T(8,128)(2,1)S(1)} %collective-permute-done.9.left_ref, ...), custom_call_target="tpu_custom_call" | custom-call | tf_op jit(solution)/shard_map/ocean_block/pallas_call | solution.py:576
  73.1 9.3 %all-gather = bf16[96,8,128]{2,1,0:T(8,128)(2,1)S(1)} all-gather(bf16[12,8,128]{2,1,0:T(8,128)(2,1)S(1)} %get-tuple-element.50), channel_id=2, replica_groups=mesh['member'=8,'lon'=4] {'member'}, dimensions={0}, use_global_device_ids=true | all-gather | bytes 221184 | tf_op jit(solution)/shard_map/all_gather | solution.py:680
  82.3 0.0 copy-done.3
  82.3 2.5 %couple.1 = bf16[96,96,128]{2,1,0:T(8,128)(2,1)} custom-call(bf16[96,96,128]{2,1,0:T(8,128)(2,1)S(1)} %get-tuple-element.38.y_ref, bf16[8,12,8,128]{3,2,1,0:T(8,128)(2,1)S(1)} %bitcast.12, s32[96,128]{1,0:T(8,128)S(1)} %copy-done.2, bf16[96,8]{1,0:T(8,128)(2,1)S(1)} %bitcast.13), custom_call_target="tpu_custom_call" | custom-call | tf_op jit(solution)/shard_map/couple/pallas_call | solution.py:608
  (11 shorter events, 0.1 us)
Async XLA Ops:
  0.6 1.7 %copy-start = (bf16[1,96,96,128]{3,2,1,0:T(8,128)(2,1)S(1)}, bf16[1,96,96,128]{3,2,1,0:T(8,128)(2,1)}, u32[]{:S(2)}) copy-start(bf16[1,96,96,128]{3,2,1,0:T(8,128)(2,1)} %param.18) | copy-start | bytes 7077892
  2.3 6.6 %copy-start.13 = (f32[2,7,7,96]{3,0,2,1:T(2,128)S(1)}, f32[2,7,7,96]{3,0,2,1:T(2,128)}, u32[]{:S(2)}) copy-start(f32[2,7,7,96]{3,0,2,1:T(2,128)} %param.22) | copy-start | bytes 112900
  3.7 13.9 %collective-permute-start = (bf16[6,96,128]{2,1,0:T(8,128)(2,1)S(1)}, bf16[6,96,128]{2,1,0:T(8,128)(2,1)S(1)}, u32[]{:S(2)}, u32[]{:S(2)}) collective-permute-start(bf16[6,96,128]{2,1,0:T(8,128)(2,1)S(1)} %get-tuple-element.29), channel_id=1, source_target_pairs={{0,1},{1,2},{2,3},{3,0},{4,5},{5,6},{6,7},{7,4},{8,9},{9,10},{10,1... | collective-permute-start | bytes 442376 | tf_op jit(solution)/shard_map/ppermute | solution.py:98
  6.8 10.8 %collective-permute-start.1 = (bf16[6,96,128]{2,1,0:T(8,128)(2,1)S(1)}, bf16[6,96,128]{2,1,0:T(8,128)(2,1)S(1)}, u32[]{:S(2)}, u32[]{:S(2)}) collective-permute-start(bf16[6,96,128]{2,1,0:T(8,128)(2,1)S(1)} %get-tuple-element.29), channel_id=1, source_target_pairs={{1,0},{2,1},{3,2},{0,3},{5,4},{6,5},{7,6},{4,7},{9,8},{10,9},{11,1... | collective-permute-start | bytes 442376 | tf_op jit(solution)/shard_map/ppermute | solution.py:99
  8.9 8.8 %copy-start.11 = (bf16[2,96,384]{2,1,0:T(8,128)(2,1)S(1)}, bf16[2,96,384]{2,1,0:T(8,128)(2,1)}, u32[]{:S(2)}) copy-start(bf16[2,96,384]{2,1,0:T(8,128)(2,1)} %up_ref.6) | copy-start | bytes 442372
  8.9 8.8 %copy-start.12 = (bf16[2,384,96]{1,2,0:T(8,128)(2,1)S(1)}, bf16[2,384,96]{1,2,0:T(8,128)(2,1)}, u32[]{:S(2)}) copy-start(bf16[2,384,96]{1,2,0:T(8,128)(2,1)} %param.25) | copy-start | bytes 442372
  8.9 8.8 %copy-start.16 = (f32[2,96]{1,0:T(2,128)S(1)}, f32[2,96]{1,0:T(2,128)}, u32[]{:S(2)}) copy-start(f32[2,96]{1,0:T(2,128)} %g_ref.5) | copy-start | bytes 2308
  8.9 8.8 %copy-start.17 = (f32[2,96]{1,0:T(2,128)S(1)}, f32[2,96]{1,0:T(2,128)}, u32[]{:S(2)}) copy-start(f32[2,96]{1,0:T(2,128)} %s_ref.5) | copy-start | bytes 2308
  26.3 12.6 %collective-permute-start.2 = (bf16[6,96,128]{2,1,0:T(8,128)(2,1)S(1)}, bf16[6,96,128]{2,1,0:T(8,128)(2,1)S(1)}, u32[]{:S(2)}, u32[]{:S(2)}) collective-permute-start(bf16[6,96,128]{2,1,0:T(8,128)(2,1)S(1)} %get-tuple-element.33), channel_id=1, source_target_pairs={{0,1},{1,2},{2,3},{3,0},{4,5},{5,6},{6,7},{7,4},{8,9},{9,10},{10,1... | collective-permute-start | bytes 442376 | tf_op jit(solution)/shard_map/ppermute | solution.py:98
  26.4 12.5 %collective-permute-start.3 = (bf16[6,96,128]{2,1,0:T(8,128)(2,1)S(1)}, bf16[6,96,128]{2,1,0:T(8,128)(2,1)S(1)}, u32[]{:S(2)}, u32[]{:S(2)}) collective-permute-start(bf16[6,96,128]{2,1,0:T(8,128)(2,1)S(1)} %get-tuple-element.33), channel_id=1, source_target_pairs={{1,0},{2,1},{3,2},{0,3},{5,4},{6,5},{7,6},{4,7},{9,8},{10,9},{11,1... | collective-permute-start | bytes 442376 | tf_op jit(solution)/shard_map/ppermute | solution.py:99
  30.2 8.7 %copy-start.15 = (bf16[96,32]{0,1:T(8,128)(2,1)S(1)}, bf16[96,32]{0,1:T(8,128)(2,1)}, u32[]{:S(2)}) copy-start(bf16[96,32]{0,1:T(8,128)(2,1)} %param.27) | copy-start | bytes 18436
  46.3 5.2 %collective-permute-start.4 = (bf16[2,18,32,128]{3,2,1,0:T(8,128)(2,1)}, bf16[2,18,32,128]{3,2,1,0:T(8,128)(2,1)S(1)}, u32[]{:S(2)}, u32[]{:S(2)}) collective-permute-start(bf16[2,18,32,128]{3,2,1,0:T(8,128)(2,1)} %get-tuple-element.39), channel_id=1, source_target_pairs={{0,4},{4,0},{8,12},{12,8},{16,20},{20,16},{24,28},{28,24},{1,5},{5... | collective-permute-start | bytes 884744 | tf_op jit(solution)/shard_map/ppermute | solution.py:488
  46.3 4.5 %copy-start.18 = (bf16[8,96]{1,0:T(8,128)(2,1)S(1)}, bf16[8,96]{1,0:T(8,128)(2,1)}, u32[]{:S(2)}) copy-start(bf16[8,96]{1,0:T(8,128)(2,1)} %param.35) | copy-start | bytes 4612
  50.3 1.9 %collective-permute-start.5 = (bf16[2,18,32,128]{3,2,1,0:T(8,128)(2,1)}, bf16[2,18,32,128]{3,2,1,0:T(8,128)(2,1)S(1)}, u32[]{:S(2)}, u32[]{:S(2)}) collective-permute-start(bf16[2,18,32,128]{3,2,1,0:T(8,128)(2,1)} %get-tuple-element.42), channel_id=1, source_target_pairs={{0,4},{4,0},{8,12},{12,8},{16,20},{20,16},{24,28},{28,24},{1,5},{5... | collective-permute-start | bytes 884744 | tf_op jit(solution)/shard_map/ppermute | solution.py:488
  52.2 6.5 %collective-permute-start.8 = (bf16[18,32,128]{2,1,0:T(8,128)(2,1)S(1)}, bf16[18,32,128]{2,1,0:T(8,128)(2,1)S(1)}, u32[]{:S(2)}, u32[]{:S(2)}) collective-permute-start(bf16[18,32,128]{2,1,0:T(8,128)(2,1)S(1)} %add_pairs.3), channel_id=1, source_target_pairs={{0,8},{4,12},{8,0},{12,4},{16,24},{20,28},{24,16},{28,20},{1,9},{5... | collective-permute-start | bytes 442376 | tf_op jit(solution)/shard_map/ppermute | solution.py:488
  54.0 9.1 %collective-permute-start.6 = (bf16[18,32,128]{2,1,0:T(8,128)(2,1)S(1)}, bf16[18,32,128]{2,1,0:T(8,128)(2,1)S(1)}, u32[]{:S(2)}, u32[]{:S(2)}) collective-permute-start(bf16[18,32,128]{2,1,0:T(8,128)(2,1)S(1)} %get-tuple-element.45), channel_id=1, source_target_pairs={{0,16},{4,20},{8,24},{12,28},{16,0},{20,4},{24,8},{28,12},{1,17},{... | collective-permute-start | bytes 442376 | tf_op jit(solution)/shard_map/ppermute | solution.py:488
  55.6 7.5 %copy-start.1 = (bf16[96,96,128]{2,1,0:T(8,128)(2,1)S(1)}, bf16[96,96,128]{2,1,0:T(8,128)(2,1)}, u32[]{:S(2)}) copy-start(bf16[96,96,128]{2,1,0:T(8,128)(2,1)} %refs_5_.1) | copy-start | bytes 7077892
  55.6 7.5 %copy-start.2 = (s32[96,128]{1,0:T(8,128)S(1)}, s32[96,128]{1,0:T(8,128)}, u32[]{:S(2)}) copy-start(s32[96,128]{1,0:T(8,128)} %land_ref.3) | copy-start | bytes 147460
  55.6 7.5 %copy-start.6 = (s32[96,128]{1,0:T(8,128)S(1)}, s32[96,128]{1,0:T(8,128)}, u32[]{:S(2)}) copy-start(s32[96,128]{1,0:T(8,128)} %refs_7_.1) | copy-start | bytes 147460
  55.6 7.5 %copy-start.7 = (bf16[2,32,96]{2,1,0:T(8,128)(2,1)S(1)}, bf16[2,32,96]{2,1,0:T(8,128)(2,1)}, u32[]{:S(2)}) copy-start(bf16[2,32,96]{2,1,0:T(8,128)(2,1)} %refs_8_.1) | copy-start | bytes 36868
  55.6 7.5 %collective-permute-start.7 = (bf16[18,32,128]{2,1,0:T(8,128)(2,1)S(1)}, bf16[18,32,128]{2,1,0:T(8,128)(2,1)S(1)}, u32[]{:S(2)}, u32[]{:S(2)}) collective-permute-start(bf16[18,32,128]{2,1,0:T(8,128)(2,1)S(1)} %get-tuple-element.46), channel_id=1, source_target_pairs={{0,24},{4,28},{8,16},{12,20},{16,8},{20,12},{24,0},{28,4},{1,25},{... | collective-permute-start | bytes 442376 | tf_op jit(solution)/shard_map/ppermute | solution.py:488
  56.0 0.9 %copy-start.14 = (f32[7,7,96]{2,1,0:T(8,128)S(1)}, f32[7,7,96]{2,1,0:T(8,128)}, u32[]{:S(2)}) copy-start(f32[7,7,96]{2,1,0:T(8,128)} %k_ref) | copy-start | bytes 56452
  64.2 4.7 %collective-permute-start.10 = (bf16[2,96,128]{2,1,0:T(8,128)(2,1)S(1)}, bf16[2,96,128]{2,1,0:T(8,128)(2,1)S(1)}, u32[]{:S(2)}, u32[]{:S(2)}) collective-permute-start(bf16[2,96,128]{2,1,0:T(8,128)(2,1)S(1)} %get-tuple-element.49), channel_id=1, source_target_pairs={{1,0},{2,1},{3,2},{0,3},{5,4},{6,5},{7,6},{4,7},{9,8},{10,9},{11,1... | collective-permute-start | bytes 147464 | tf_op jit(solution)/shard_map/ppermute | solution.py:99
  64.2 5.9 %collective-permute-start.9 = (bf16[2,96,128]{2,1,0:T(8,128)(2,1)S(1)}, bf16[2,96,128]{2,1,0:T(8,128)(2,1)S(1)}, u32[]{:S(2)}, u32[]{:S(2)}) collective-permute-start(bf16[2,96,128]{2,1,0:T(8,128)(2,1)S(1)} %get-tuple-element.49), channel_id=1, source_target_pairs={{0,1},{1,2},{2,3},{3,0},{4,5},{5,6},{6,7},{7,4},{8,9},{9,10},{10,1... | collective-permute-start | bytes 147464 | tf_op jit(solution)/shard_map/ppermute | solution.py:98
  66.3 3.9 %copy-start.4 = (bf16[96,384]{1,0:T(8,128)(2,1)S(1)}, bf16[96,384]{1,0:T(8,128)(2,1)}, u32[]{:S(2)}) copy-start(bf16[96,384]{1,0:T(8,128)(2,1)} %up_ref.7) | copy-start | bytes 221188
  66.3 3.9 %copy-start.5 = (bf16[384,96]{0,1:T(8,128)(2,1)S(1)}, bf16[384,96]{0,1:T(8,128)(2,1)}, u32[]{:S(2)}) copy-start(bf16[384,96]{0,1:T(8,128)(2,1)} %param.32) | copy-start | bytes 221188
  66.3 3.9 %copy-start.8 = (bf16[96,8]{0,1:T(8,128)(2,1)S(1)}, bf16[96,8]{0,1:T(8,128)(2,1)}, u32[]{:S(2)}) copy-start(bf16[96,8]{0,1:T(8,128)(2,1)} %param.34) | copy-start | bytes 4612
  66.3 3.9 %copy-start.9 = (f32[96]{0:T(128)S(1)}, f32[96]{0:T(128)}, u32[]{:S(2)}) copy-start(f32[96]{0:T(128)} %param.30) | copy-start | bytes 1156
  66.3 3.9 %copy-start.10 = (f32[96]{0:T(128)S(1)}, f32[96]{0:T(128)}, u32[]{:S(2)}) copy-start(f32[96]{0:T(128)} %param.33) | copy-start | bytes 1156
  70.2 12.1 %copy-start.3 = (bf16[8,96]{0,1:T(8,128)(2,1)S(1)}, bf16[8,96]{0,1:T(8,128)(2,1)}, u32[]{:S(2)}) copy-start(bf16[8,96]{0,1:T(8,128)(2,1)} %copy.22) | copy-start | bytes 4612

commit v6 on v5

--- a/solution.py
+++ b/solution.py
@@ -21,7 +21,6 @@
 SLOTS = 16
 OCEAN_BLOCKS = 2
 BIG = 32
-BY_DOT = (0, 1, 5, 6)
 VMEM = pl.BlockSpec(memory_space=pltpu.VMEM)
 ANY = pl.BlockSpec(memory_space=pl.ANY)
 HBM = pl.BlockSpec(memory_space=pltpu.HBM)
@@ -56,7 +55,7 @@
     return (lane < HALO) | (lane >= shape[-1] - HALO)
 
 
-def pack_kernel(step, src_ref, x_ref, p_ref, sems):
+def pack_kernel(step, src_ref, p_ref, x_ref, sems):
     rows, chans, lanes = x_ref.shape
     blocks = p_ref.shape[0]
     copies = []
@@ -81,14 +80,11 @@
     rows, chans, lanes = x.shape
     return pl.pallas_call(
         functools.partial(pack_kernel, step),
-        out_shape=[
-            jax.ShapeDtypeStruct(x.shape, BF),
-            jax.ShapeDtypeStruct((rows // SLOTS, chans, lanes), BF),
-        ],
+        out_shape=jax.ShapeDtypeStruct((rows // SLOTS, chans, lanes), BF),
         in_specs=[HBM],
-        out_specs=[VMEM, VMEM],
-        scratch_shapes=[pltpu.SemaphoreType.DMA((rows // step,))],
-        compiler_params=params(24),
+        out_specs=VMEM,
+        scratch_shapes=[pltpu.VMEM(x.shape, BF), pltpu.SemaphoreType.DMA((rows // step,))],
+        compiler_params=params(60),
         name="pack_edges",
     )(x)
 
@@ -98,16 +94,6 @@
     left = lax.ppermute(packed, "lon", [(i, (i + 1) % count) for i in range(count)])
     right = lax.ppermute(packed, "lon", [((i + 1) % count, i) for i in range(count)])
     return left, right
-
-
-def shift_matrix(lanes):
-    shape = (lanes, len(BY_DOT) * lanes)
-    src = lax.broadcasted_iota(jnp.int32, shape, 0)
-    dst = lax.broadcasted_iota(jnp.int32, shape, 1)
-    hit = jnp.zeros(shape, jnp.bool_)
-    for a, j in enumerate(BY_DOT):
-        hit = hit | ((dst >= a * lanes) & (dst < (a + 1) * lanes) & (src == dst - a * lanes + j - HALO))
-    return hit.astype(F32).astype(BF)
 
 
 def fill_base(taps, base):
@@ -134,22 +120,16 @@
             band[GROUP * r : GROUP * (r + 1), j * DEPTH : (j + 1) * DEPTH] = moved.astype(BF)
 
 
-def fill_shifts(x, pad, smat, xj):
+def fill_shifts(x, pad, xj):
     count, _, lanes = x.shape
-    moved = jnp.dot(x.reshape(count * GROUP, lanes), smat, preferred_element_type=F32)
-    for a, j in enumerate(BY_DOT):
-        part = moved[:, a * lanes : (a + 1) * lanes].astype(BF)
-        xj[j, pad : pad + count] = part.reshape(count, GROUP, lanes)
     lane = lax.broadcasted_iota(jnp.int32, (GROUP, lanes), 1)
     for j in range(TAPS):
         d = j - HALO
-        if j in BY_DOT:
-            continue
-        if d == 0:
-            xj[j, pad : pad + count] = x
-        else:
+        if d:
             keep = ((lane < lanes - d) if d > 0 else (lane >= -d)).astype(F32).astype(BF)
             xj[j, pad : pad + count] = pltpu.roll(x, (-d) % lanes, 2) * keep[None]
+        else:
+            xj[j, pad : pad + count] = x
 
 
 def clear_pads(pad, count, xj):
@@ -178,21 +158,31 @@
         a_ref[s : s + take] = part.reshape(take, GROUP, lanes)
 
 
-def conv_kernel(layer, x_ref, k_ref, a_ref, band_ref, base, xj, band):
+def conv_kernel(layer, x_ref, k_ref, a_ref, band_ref, base, even_xj, odd_xj, even_band, odd_band):
     rows, chans, lanes = x_ref.shape
+    groups = chans // GROUP
     fill_base(lambda i: k_ref[i, :, layer, :], base)
-    smat = shift_matrix(lanes)
-    clear_pads(HALO, rows, xj)
-
-    def group(g, carry):
-        at = pl.ds(pl.multiple_of(GROUP * g, GROUP), GROUP)
+    clear_pads(HALO, rows, even_xj)
+    clear_pads(HALO, rows, odd_xj)
+
+    def at(g):
+        return pl.ds(pl.multiple_of(GROUP * g, GROUP), GROUP)
+
+    def prepare(g, xj, band):
         fill_band(base, g, band)
         band_ref[g] = band[: band_ref.shape[1]]
-        fill_shifts(x_ref[:, at, :], HALO, smat, xj)
-        apply_band(band[...], xj, a_ref.at[:, at, :])
+        fill_shifts(x_ref[:, at(g), :], HALO, xj)
+
+    prepare(0, even_xj, even_band)
+
+    def pair(i, carry):
+        prepare(2 * i + 1, odd_xj, odd_band)
+        apply_band(even_band[...], even_xj, a_ref.at[:, at(2 * i), :])
+        prepare(jnp.minimum(2 * i + 2, groups - 1), even_xj, even_band)
+        apply_band(odd_band[...], odd_xj, a_ref.at[:, at(2 * i + 1), :])
         return carry
 
-    lax.fori_loop(0, chans // GROUP, group, 0)
+    lax.fori_loop(0, groups // 2, pair, 0)
 
 
 def convolve(layer, x, taps, blocks):
@@ -209,44 +199,43 @@
         out_specs=[VMEM, VMEM],
         scratch_shapes=[
             pltpu.VMEM((groups, GROUP, wide), F32),
-            pltpu.VMEM((TAPS, rows + 2 * HALO, GROUP, lanes), BF),
-            pltpu.VMEM((GROUP * OUT, wide), BF),
-        ],
+        ]
+        + [pltpu.VMEM((TAPS, rows + 2 * HALO, GROUP, lanes), BF)] * 2
+        + [pltpu.VMEM((GROUP * OUT, wide), BF)] * 2,
         compiler_params=params(BIG),
         cost_estimate=cost(8),
         name="conv",
     )(x, taps)
 
 
-def band_kernel(k_ref, band_ref, base):
+def band_kernel(k_ref, _, band_ref, base):
     fill_base(lambda i: k_ref[i], base)
     for g in range(base.shape[0]):
         fill_band(base, g, band_ref.at[g])
 
 
-def ocean_band(taps):
+def ocean_band(taps, after):
     groups = taps.shape[2] // GROUP
     wide = TAPS * DEPTH
     return pl.pallas_call(
         band_kernel,
         out_shape=jax.ShapeDtypeStruct((groups, GROUP * OUT, wide), BF),
-        in_specs=[VMEM],
+        in_specs=[VMEM, ANY],
         out_specs=VMEM,
         scratch_shapes=[pltpu.VMEM((groups, GROUP, wide), F32)],
         compiler_params=params(24),
         cost_estimate=cost(3),
         name="ocean_band",
-    )(taps)
+    )(taps, after)
 
 
 def ocean_conv_kernel(x_ref, band_ref, a_ref, xj):
     count, chans, lanes = x_ref.shape
-    smat = shift_matrix(lanes)
-    clear_pads(0, count, xj)
     for g in range(chans // GROUP):
         at = slice(GROUP * g, GROUP * (g + 1))
-        fill_shifts(x_ref[:, at, :], 0, smat, xj)
-        apply_band(band_ref[g], xj, a_ref.at[:, at, :])
+        clear_pads(0, count, xj.at[g])
+        fill_shifts(x_ref[:, at, :], 0, xj.at[g])
+        apply_band(band_ref[g], xj.at[g], a_ref.at[:, at, :])
 
 
 def ocean_conv(x, band):
@@ -256,7 +245,7 @@
         out_shape=jax.ShapeDtypeStruct((count - 2 * HALO, chans, lanes), F32),
         in_specs=[VMEM, VMEM],
         out_specs=VMEM,
-        scratch_shapes=[pltpu.VMEM((TAPS, max(count, SPAN), GROUP, lanes), BF)],
+        scratch_shapes=[pltpu.VMEM((chans // GROUP, TAPS, max(count, SPAN), GROUP, lanes), BF)],
         compiler_params=params(24),
         cost_estimate=cost(2),
         name="ocean_conv",
@@ -324,144 +313,116 @@
         halo[:, at, :] = out.reshape(blocks, GROUP, lanes)
 
 
-def branch_of(a_ref, row0, count, halo, slot0, gain, up_t, down_t):
+def norm_rows(a_ref, row0, count, halo, gain, out):
     _, chans, lanes = a_ref.shape
     blocks = halo.shape[0]
     edge = edge_lanes((chans, lanes))
-    normed = []
     for r in range(count):
-        shift = lax.rem(lanes - SLOT * (slot0 + r // blocks), lanes)
-        a = a_ref[row0 + r] + jnp.where(edge, pltpu.roll(halo[r % blocks], shift, 1), 0.0)
+        q, slot = (row0 + r) % blocks, (row0 + r) // blocks
+        extra = pltpu.roll(halo[q], lanes - SLOT * slot, 1) if slot else halo[q]
+        a = a_ref[row0 + r] + jnp.where(edge, extra, 0.0)
         center = a - jnp.mean(a, axis=0, keepdims=True)
         var = jnp.mean(center * center, axis=0, keepdims=True)
-        normed.append((center * lax.rsqrt(var + 1e-06) * gain).astype(BF))
-    z = jnp.dot(up_t, jnp.concatenate(normed, axis=1), preferred_element_type=F32)
+        normed = (center * lax.rsqrt(var + 1e-06) * gain).astype(BF)
+        out[:, r * lanes : (r + 1) * lanes] = normed
+
+
+def branch_of(normed, up_t, down_t):
+    z = jnp.dot(up_t, normed, preferred_element_type=F32)
     h = twice_gelu(z.astype(BF))
     return jnp.dot(down_t, h, preferred_element_type=F32)
 
 
-def first_kernel(count, x_ref, a_ref, left_ref, right_ref, band_ref, g_ref, up_ref, dn_ref, s_ref, y_ref, p_ref, xe, halo):
+def atmos_kernel(layer, members, count, *refs):
+    x_ref, a_ref, left_ref, right_ref, band_ref, g_ref, up_ref, dn_ref, s_ref = refs[:9]
+    if layer == 0:
+        y_ref, p_ref = refs[9:11]
+    else:
+        fw_ref, y_ref, keep_ref, give_ref, flux = refs[9:14]
+    xe, halo, even, odd = refs[-4:]
     rows, chans, lanes = x_ref.shape
     blocks = halo.shape[0]
     halo_conv(left_ref, right_ref, band_ref, True, xe, halo)
-    up_t = transposed(up_ref[0])
-    dn_t = halved(dn_ref[0])
-    gain = spread(g_ref[0:1], lanes)
-    scale = spread(s_ref[0:1], lanes)
+    up_t = transposed(up_ref[layer])
+    dn_t = halved(dn_ref[layer])
+    gain = spread(g_ref[layer : layer + 1], lanes)
+    scale = spread(s_ref[layer : layer + 1], lanes)
     keep = edge_lanes((chans, lanes)).astype(F32).astype(BF)
-    p_ref[...] = jnp.zeros(p_ref.shape, BF)
-
-    def part(step, carry):
-        row0 = step * count
-        slot0 = step * (count // blocks)
-        branch = branch_of(a_ref, row0, count, halo, slot0, gain, up_t, dn_t)
-        for r in range(count):
-            y = x_ref[row0 + r].astype(F32) + scale * branch[:, r * lanes : (r + 1) * lanes]
-            y = y.astype(BF)
-            y_ref[row0 + r] = y
-            moved = pltpu.roll(y * keep, SLOT * (slot0 + r // blocks), 1)
-            p_ref[r % blocks] = p_ref[r % blocks] + moved
-        return carry
-
-    lax.fori_loop(0, rows // count, part, 0)
-
-
-def first_block(x, a, left, right, band, gain, up, down, scale, step):
-    rows, chans, lanes = x.shape
-    blocks = rows // SLOTS
-    return pl.pallas_call(
-        functools.partial(first_kernel, step),
-        out_shape=[
-            jax.ShapeDtypeStruct(x.shape, BF),
-            jax.ShapeDtypeStruct((blocks, chans, lanes), BF),
-        ],
-        in_specs=[VMEM] * 9,
-        out_specs=[VMEM] * 2,
-        scratch_shapes=[
-            pltpu.VMEM((TAPS - 1, SPAN, chans, lanes), BF),
-            pltpu.VMEM((blocks, chans, lanes), F32),
-        ],
-        compiler_params=params(BIG),
-        cost_estimate=cost(8),
-        name="first_block",
-    )(x, a, left, right, band, gain, up, down, scale)
-
-
-def second_kernel(near, members, count, steps, x_ref, a_ref, g_ref, up_ref, dn_ref, s_ref, fw_ref, *refs):
-    if near:
-        _, old_ref, halo, y_ref, keep_ref, give_ref, flux = refs
-    else:
-        left_ref, right_ref, band_ref, y_ref, keep_ref, give_ref, flux, halo, xe = refs
-    half = members // 2
-    rows, chans, lanes = x_ref.shape
-    blocks = halo.shape[0]
-    rank = lax.axis_index("member")
-    at = jnp.where(rank >= half, rows // count - steps, 0)
-    if not near:
-        at = rows // count - steps - at
-    if near:
-        flux[...] = old_ref[...]
-    else:
-        halo_conv(left_ref, right_ref, band_ref, True, xe, halo)
+    packed = [None] * blocks
+    if layer == 1:
         blank = jnp.zeros((HALO,) + flux.shape[1:], BF)
         flux[0:HALO] = blank
         flux[rows + HALO : rows + 2 * HALO] = blank
-    up_t = transposed(up_ref[1])
-    dn_t = halved(dn_ref[1])
-    gain = spread(g_ref[1:2], lanes)
-    scale = spread(s_ref[1:2], lanes)
-
-    def part(step, carry):
-        row0 = (at + step) * count
-        slot0 = (at + step) * (count // blocks)
-        branch = branch_of(a_ref, row0, count, halo, slot0, gain, up_t, dn_t)
+    norm_rows(a_ref, 0, count, halo, gain, even)
+    for step in range(rows // count):
+        row0 = step * count
+        now, later = (even, odd) if step % 2 == 0 else (odd, even)
+        if row0 + count < rows:
+            norm_rows(a_ref, row0 + count, count, halo, gain, later)
+        branch = branch_of(now[...], up_t, dn_t)
         made = []
         for r in range(count):
             y = x_ref[row0 + r].astype(F32) + scale * branch[:, r * lanes : (r + 1) * lanes]
             made.append(y.astype(BF))
             y_ref[row0 + r] = made[r]
-        z = jnp.dot(fw_ref[...], jnp.concatenate(made, axis=1), preferred_element_type=F32)
-        f = (0.5 * twice_gelu(z)).astype(BF)
-        for r in range(count):
-            flux[row0 + HALO + r] = f[:, r * lanes : (r + 1) * lanes]
-        return carry
-
-    lax.fori_loop(0, steps, part, 0)
-    share = rows // members
-    for k in range(half):
-        dst = rank ^ (k if near else half + k)
-        chunk = flux[pl.ds(dst * share, share + 2 * HALO)]
-        if k % 2:
-            give_ref[k // 2] = chunk
+        if layer == 0:
+            for r in range(count):
+                q, slot = (row0 + r) % blocks, (row0 + r) // blocks
+                moved = made[r] * keep
+                if slot:
+                    moved = pltpu.roll(moved, SLOT * slot, 1)
+                packed[q] = moved if packed[q] is None else packed[q] + moved
+            if row0 % (4 * count) == 3 * count or row0 + count == rows:
+                for q in range(blocks):
+                    if row0 < 4 * count:
+                        p_ref[q] = packed[q]
+                    else:
+                        p_ref[q] = p_ref[q] + packed[q]
+                packed = [None] * blocks
         else:
-            keep_ref[k // 2] = chunk
-
-
-def second_block(near, members, x, a, weights, others, step, steps):
+            z = jnp.dot(fw_ref[...], jnp.concatenate(made, axis=1), preferred_element_type=F32)
+            f = (0.5 * twice_gelu(z)).astype(BF)
+            for r in range(count):
+                flux[row0 + HALO + r] = f[:, r * lanes : (r + 1) * lanes]
+    if layer == 1:
+        rank = lax.axis_index("member")
+        share = rows // members
+        for k in range(members):
+            chunk = flux[pl.ds((rank ^ k) * share, share + 2 * HALO)]
+            if k % 2:
+                give_ref[k // 2] = chunk
+            else:
+                keep_ref[k // 2] = chunk
+
+
+def atmos_block(layer, members, x, a, edges, band, weights, count):
     rows, chans, lanes = x.shape
     blocks = rows // SLOTS
-    flux = weights[-1].shape[0]
-    share = rows // members
-    chunks = jax.ShapeDtypeStruct((members // 4, share + 2 * HALO, flux, lanes), BF)
-    field = jax.ShapeDtypeStruct((rows + 2 * HALO, flux, lanes), BF)
-    halo = jax.ShapeDtypeStruct((blocks, chans, lanes), F32)
-    args = [x, a, *weights, *others]
-    outs = [jax.ShapeDtypeStruct(x.shape, BF), chunks, chunks]
-    if near:
-        scratch = [pltpu.VMEM(field.shape, BF)]
+    args = [x, a, *edges, band, *weights]
+    outs = [jax.ShapeDtypeStruct(x.shape, BF)]
+    scratch = []
+    if layer == 0:
+        outs.append(jax.ShapeDtypeStruct((blocks, chans, lanes), BF))
     else:
-        scratch = [pltpu.VMEM((TAPS - 1, SPAN, chans, lanes), BF)]
-        outs += [field, halo]
-    return pl.pallas_call(
-        functools.partial(second_kernel, near, members, step, steps),
+        flux = weights[-1].shape[0]
+        share = rows // members
+        outs += [jax.ShapeDtypeStruct((members // 2, share + 2 * HALO, flux, lanes), BF)] * 2
+        scratch.append(pltpu.VMEM((rows + 2 * HALO, flux, lanes), BF))
+    return pl.pallas_call(
+        functools.partial(atmos_kernel, layer, members, count),
         out_shape=outs,
         in_specs=[VMEM] * len(args),
         out_specs=[VMEM] * len(outs),
-        scratch_shapes=scratch,
-        input_output_aliases={7: 0} if near else {},
+        scratch_shapes=scratch
+        + [
+            pltpu.VMEM((TAPS - 1, SPAN, chans, lanes), BF),
+            pltpu.VMEM((blocks, chans, lanes), F32),
+            pltpu.VMEM((chans, count * lanes), BF),
+            pltpu.VMEM((chans, count * lanes), BF),
+        ],
         compiler_params=params(BIG),
-        cost_estimate=cost(8 * steps * step / rows),
-        name="second_block",
+        cost_estimate=cost(8),
+        name="atmos_block",
     )(*args)
 
 
@@ -548,14 +509,13 @@
     )(*chunks, ocean, land, ice, lift)
 
 
-def ocean_kernel(mid_ref, a_ref, left_ref, right_ref, band_ref, land_ref, g_ref, up_ref, dn_ref, s_ref, sw_ref, new_ref, surf_ref, xe, halo):
+def ocean_kernel(mid_ref, a_ref, left_ref, right_ref, band_ref, land_ref, g_ref, up_ref, dn_ref, s_ref, sw_ref, new_ref, surf_ref, xe, halo, normed):
     share, chans, lanes = new_ref.shape
     halo_conv(left_ref, right_ref, band_ref, False, xe, halo)
     gain = spread(g_ref[...], lanes)
     scale = spread(s_ref[...], lanes)
-    branch = branch_of(
-        a_ref, 0, share, halo, 0, gain, transposed(up_ref[...]), halved(dn_ref[...])
-    )
+    norm_rows(a_ref, 0, share, halo, gain, normed)
+    branch = branch_of(normed[...], transposed(up_ref[...]), halved(dn_ref[...]))
     first = lax.axis_index("member") * share
     made = []
     for r in range(share):
@@ -584,36 +544,64 @@
         scratch_shapes=[
             pltpu.VMEM((TAPS - 1, SPAN, chans, lanes), BF),
             pltpu.VMEM((blocks, chans, lanes), F32),
+            pltpu.VMEM((chans, share * lanes), BF),
         ],
         compiler_params=params(24),
         name="ocean_block",
     )(mid, a, left, right, band, land, gain[None], up, down, scale[None], surf_weight)
 
 
-def couple_kernel(count, y_ref, surf_ref, land_ref, bw_ref, o_ref):
-    rows, chans, lanes = y_ref.shape
-    share = surf_ref.shape[1]
-    first = pl.program_id(0) * count
-    owner = pl.program_id(0) * (count // share)
-    surf = [surf_ref[owner + r // share, r % share] for r in range(count)]
+def pair_kernel(own_ref, got_ref, out_ref):
+    out_ref[0] = own_ref[...]
+    out_ref[1] = got_ref[...]
+
+
+def make_pair(own, got):
+    return pl.pallas_call(
+        pair_kernel,
+        out_shape=jax.ShapeDtypeStruct((2,) + own.shape, BF),
+        in_specs=[VMEM] * 2,
+        out_specs=VMEM,
+        compiler_params=params(24),
+        name="surface_pair",
+    )(own, got)
+
+
+def couple_kernel(y_ref, land_ref, bw_ref, *refs):
+    pair_refs, o_ref = refs[:-1], refs[-1]
+    chans, lanes = y_ref.shape[1:]
+    share = pair_refs[0].shape[1]
+    rank = lax.axis_index("member")
+    pair = pl.program_id(0)
+    parity = rank % 2
+    mine = pair ^ (rank // 2)
+    surf = [None] * (2 * share)
+    for side in range(2):
+        for r in range(share):
+            value = pair_refs[0][side ^ parity, r]
+            for k, ref in enumerate(pair_refs[1:]):
+                value = jnp.where(mine == k + 1, ref[side ^ parity, r], value)
+            surf[side * share + r] = value
     back = jnp.dot(bw_ref[...], jnp.concatenate(surf, axis=1), preferred_element_type=F32)
-    sea = (1 - land_ref[pl.ds(pl.multiple_of(first, SLOT), count), :]).astype(F32)
-    for r in range(count):
-        out = y_ref[first + r].astype(F32) + sea[r : r + 1] * back[:, r * lanes : (r + 1) * lanes]
+    first = pair * 2 * share
+    for r in range(2 * share):
+        sea = (1 - land_ref[pl.ds(first + r, 1), :]).astype(F32)
+        out = y_ref[first + r].astype(F32) + sea * back[:, r * lanes : (r + 1) * lanes]
         o_ref[r] = out.astype(BF)
 
 
-def couple(y, surface, land, back_weight, count):
+def couple(y, land, back_weight, pairs):
     rows, chans, lanes = y.shape
-    return pl.pallas_call(
-        functools.partial(couple_kernel, count),
+    count = 2 * pairs[0].shape[1]
+    return pl.pallas_call(
+        couple_kernel,
         grid=(rows // count,),
         out_shape=jax.ShapeDtypeStruct(y.shape, BF),
-        in_specs=[VMEM] * 4,
+        in_specs=[VMEM] * (3 + len(pairs)),
         out_specs=pl.BlockSpec((count, chans, lanes), lambda i: (i, 0, 0)),
         compiler_params=params(24),
         name="couple",
-    )(y, surface, land, back_weight)
+    )(y, land, back_weight, *pairs)
 
 
 def local(
@@ -645,31 +633,20 @@
     atm = (atm_gain, atm_up, atm_down.transpose(0, 2, 1), atm_scale)
     taps = atm_kernel.transpose(1, 2, 0, 3)
 
-    state, packed = pack(state, big)
-    left, right = neighbours(packed)
+    edges = neighbours(pack(state, big))
     a, band = convolve(0, state, taps, blocks)
-    state, packed = first_block(state, a, left, right, band, *atm, big)
-
-    left, right = neighbours(packed)
+    state, packed = atmos_block(0, members, state, a, edges, band, atm, small)
+
+    edges = neighbours(packed)
     a, band = convolve(1, state, taps, blocks)
-    near_steps = (rows // 2 - small) // small
-    far_steps = rows // small - near_steps
-    weights = (*atm, flux_weight.T)
-    partly, keep, give, flux, halo = second_block(
-        False, members, state, a, weights, [left, right, band], small, far_steps
+    state, keep, give = atmos_block(
+        1, members, state, a, edges, band, (*atm, flux_weight.T), small
     )
     got = send_xor(give, 1)
-    state, near_keep, near_give = second_block(
-        True, members, state, a, weights, [partly, flux, halo], small, near_steps
-    )
-    near_got = send_xor(near_give, 1)
-    got, near_keep, taps = lax.optimization_barrier((got, near_keep, ocn_kernel))
-    sums = add_pairs(keep, got, 0)
-    sent = [send_xor(part, half + 2 * k) for k, part in enumerate(sums)]
-    sums = add_pairs(near_keep, near_got, 1)
-    sent += [send_xor(part, 2 * k + 2) for k, part in enumerate(sums)]
-    sent = [near_keep, near_got] + sent
-    band = ocean_band(taps)
+    sums = add_pairs(keep, got, 1)
+    sent = [send_xor(sums[k - 1], 2 * k) for k in range(half - 1, 0, -1)]
+    band = ocean_band(ocn_kernel, sums[0])
+    sent = [keep, got] + sent
 
     mid, packed = force(members, sent, ocean, land_mask, ice_mask, flux_lift)
     left, right = neighbours(packed)
@@ -677,8 +654,9 @@
     ocean_rows, surface = ocean_block(
         mid, a, left, right, band, land_mask, ocn_gain, ocn_up, ocn_down.T, ocn_scale, surf_weight.T
     )
-    surface = lax.all_gather(surface, "member")
-    out = couple(state, surface, land_mask, back_weight.T, big)
+    own = make_pair(surface, send_xor(surface, 1))
+    pairs = [own] + [send_xor(own, 2 * k) for k in range(1, half)]
+    out = couple(state, land_mask, back_weight.T, pairs)
     return (out[None], ocean_rows)
 
 

time: 85 us -> 75.3 us (0.89)
  blocking collectives: 9.26 us -> 0 us
  Pallas kernels: 48.3 us -> 40.8 us
  waiting for transfers between devices: 7.7 us -> 13 us
  starting transfers between devices: 15.3 us -> 20.3 us
  local copies, waits for them, and re-layouts: 3.36 us -> 0.19 us
    all_gather x1 -> x0, blocking collectives: 9.26 us -> none  [local(): surface = lax.all_gather(surface, 'member')]
    ppermute x5 -> x8, waiting for transfers between devices: 5.67 us -> 12.1 us  [send_xor(): lax.ppermute(value, 'member', [(i, i ^ bits) for i in range(members)])]
    pallas_call x2, Pallas kernels: 17.4 us -> 12.7 us  [convolve(): pl.pallas_call(functools.partial(conv_kernel, layer), out_shape=[jax.Shap...]
    unnamed x39 -> x37, local copies, waits for them, and re-layouts: 3.36 us -> 0.19 us
    ppermute x5 -> x8, starting transfers between devices: 4.21 us -> 7.18 us  [send_xor(): lax.ppermute(value, 'member', [(i, i ^ bits) for i in range(members)])]
    ppermute x3, starting transfers between devices: 5.96 us -> 8.6 us  [neighbours(): lax.ppermute(packed, 'lon', [((i + 1) % count, i) for i in range(count)])]
    pallas_call x5, Pallas kernels: 23.8 us -> 21.5 us  [the longest x2 16.2 us: atmos_block(): pl.pallas_call(functools.partial(atmos_kernel, layer, members, count), ou...]
  transfers between devices with their start and end apart: 11 -> 14, of which waited for: 5 -> 10; matrix products, arithmetic and copies ran while one was open for 1% -> 0% of each run, Pallas kernels for 29% -> 20%
where the time goes in v6:
time: 75.3 us; the launch traced here: 75.2 us
  Pallas kernels  40.8 us (54%)
  starting transfers between devices  20.3 us (27%)
  waiting for transfers between devices  13 us (17%)
  between operations  0.88 us (1%)
    pallas_call x2, Pallas kernels, atmos_block(): pl.pallas_call(functools.partial(atmos_kernel, layer, members, count), ou...  16.2 us
    pallas_call x2, Pallas kernels, convolve(): pl.pallas_call(functools.partial(conv_kernel, layer), out_shape=[jax.Shap...  12.7 us
    ppermute x8, waiting for transfers between devices, send_xor(): lax.ppermute(value, 'member', [(i, i ^ bits) for i in range(members)])  12.1 us
    ppermute x3, starting transfers between devices, neighbours(): lax.ppermute(packed, 'lon', [((i + 1) % count, i) for i in range(count)])  8.6 us
    ppermute x8, starting transfers between devices, send_xor(): lax.ppermute(value, 'member', [(i, i ^ bits) for i in range(members)])  7.18 us
    ppermute x3, starting transfers between devices, neighbours(): lax.ppermute(packed, 'lon', [(i, (i + 1) % count) for i in range(count)])  4.53 us
    pallas_call x1, Pallas kernels, ocean_block(): pl.pallas_call(ocean_kernel, out_shape=[jax.ShapeDtypeStruct((share, chan...  2.88 us
    pallas_call x1, Pallas kernels, pack(): pl.pallas_call(functools.partial(pack_kernel, step), out_shape=jax.ShapeD...  2.77 us
  transfers between devices with their start and end apart: 14, of which 10 were waited for; matrix products, arithmetic and copies ran while one was open for 0% of the time, Pallas kernels for 20%

profile of v6, /device:TPU:0, one launch (start us, length us, event | category | flops | bytes accessed | tf_op | source)
XLA Modules:
  0.0 75.2 jit_solution(14724603178265149490)
XLA Ops:
  0.6 0.0 copy-start
  0.6 0.0 copy-start.12
  0.6 2.8 %pack_edges.1 = bf16[6,96,128]{2,1,0:T(8,128)(2,1)} custom-call(bf16[96,96,128]{2,1,0:T(8,128)(2,1)} %bitcast.10), custom_call_target="tpu_custom_call" | custom-call | tf_op jit(solution)/shard_map/pack_edges/pallas_call | solution.py:81
  3.4 3.1 %collective-permute-start = (bf16[6,96,128]{2,1,0:T(8,128)(2,1)}, bf16[6,96,128]{2,1,0:T(8,128)(2,1)S(1)}, u32[]{:S(2)}, u32[]{:S(2)}) collective-permute-start(bf16[6,96,128]{2,1,0:T(8,128)(2,1)} %pack_edges.1), channel_id=1, source_target_pairs={{0,1},{1,2},{2,3},{3,0},{4,5},{5,6},{6,7},{7,4},{8,9},{9,10},{10,1... | collective-permute-start | bytes 442376 | tf_op jit(solution)/shard_map/ppermute | solution.py:94
  6.5 2.1 %collective-permute-start.1 = (bf16[6,96,128]{2,1,0:T(8,128)(2,1)}, bf16[6,96,128]{2,1,0:T(8,128)(2,1)S(1)}, u32[]{:S(2)}, u32[]{:S(2)}) collective-permute-start(bf16[6,96,128]{2,1,0:T(8,128)(2,1)} %pack_edges.1), channel_id=1, source_target_pairs={{1,0},{2,1},{3,2},{0,3},{5,4},{6,5},{7,6},{4,7},{9,8},{10,9},{11,1... | collective-permute-start | bytes 442376 | tf_op jit(solution)/shard_map/ppermute | solution.py:95
  8.6 0.0 copy-done
  8.6 0.0 copy-done.12
  8.6 0.0 copy-start.15
  8.6 0.0 copy-start.16
  8.6 6.3 %conv.2 = (f32[96,96,128]{2,1,0:T(8,128)S(1)}, bf16[6,96,1792]{2,1,0:T(8,128)(2,1)S(1)}) custom-call(bf16[96,96,128]{2,1,0:T(8,128)(2,1)S(1)} %bitcast.11, f32[7,7,2,96]{3,2,1,0:T(2,128)S(1)} %bitcast.20), custom_call_target="tpu_custom_call" | custom-call | flops 8000000000 | tf_op jit(solution)/shard_map/conv/pallas_call | solution.py:192
  14.9 0.0 collective-permute-done.refs_2_
  14.9 0.3 collective-permute-done.1.refs_3_
  15.2 0.0 copy-done.10
  15.2 0.0 copy-done.11
  15.2 0.0 copy-done.15
  15.2 0.0 copy-done.16
  15.2 7.7 %atmos_block.2 = (bf16[96,96,128]{2,1,0:T(8,128)(2,1)S(1)}, bf16[6,96,128]{2,1,0:T(8,128)(2,1)S(1)}) custom-call(bf16[96,96,128]{2,1,0:T(8,128)(2,1)S(1)} %bitcast.12, f32[96,96,128]{2,1,0:T(8,128)S(1)} %get-tuple-element.18.refs_1_, bf16[6,96,128]{2,1,0:T(8,128)(2,1)S(1)} %collective-permute-done.refs_2_, ...), custom_call_target="tpu_custom_call" | custom-call | flops 8000000000 | tf_op jit(solution)/shard_map/atmos_block/pallas_call | solution.py:411
  22.9 1.2 %collective-permute-start.2 = (bf16[6,96,128]{2,1,0:T(8,128)(2,1)S(1)}, bf16[6,96,128]{2,1,0:T(8,128)(2,1)S(1)}, u32[]{:S(2)}, u32[]{:S(2)}) collective-permute-start(bf16[6,96,128]{2,1,0:T(8,128)(2,1)S(1)} %get-tuple-element.22), channel_id=1, source_target_pairs={{0,1},{1,2},{2,3},{3,0},{4,5},{5,6},{6,7},{7,4},{8,9},{9,10},{10,1... | collective-permute-start | bytes 442376 | tf_op jit(solution)/shard_map/ppermute | solution.py:94
  24.1 2.7 %collective-permute-start.3 = (bf16[6,96,128]{2,1,0:T(8,128)(2,1)S(1)}, bf16[6,96,128]{2,1,0:T(8,128)(2,1)S(1)}, u32[]{:S(2)}, u32[]{:S(2)}) collective-permute-start(bf16[6,96,128]{2,1,0:T(8,128)(2,1)S(1)} %get-tuple-element.22), channel_id=1, source_target_pairs={{1,0},{2,1},{3,2},{0,3},{5,4},{6,5},{7,6},{4,7},{9,8},{10,9},{11,1... | collective-permute-start | bytes 442376 | tf_op jit(solution)/shard_map/ppermute | solution.py:95
  26.8 6.4 %conv.3 = (f32[96,96,128]{2,1,0:T(8,128)S(1)}, bf16[6,96,1792]{2,1,0:T(8,128)(2,1)S(1)}) custom-call(bf16[96,96,128]{2,1,0:T(8,128)(2,1)S(1)} %get-tuple-element.20.x_ref.refs_0_, f32[7,7,2,96]{3,2,1,0:T(2,128)S(1)} %bitcast.21), custom_call_target="tpu_custom_call" | custom-call | flops 8000000000 | tf_op jit(solution)/shard_map/conv/pallas_call | solution.py:192
  33.2 0.0 collective-permute-done.2.refs_2_
  33.2 0.0 collective-permute-done.3.refs_3_
  33.2 0.0 copy-done.14
  33.3 0.0 copy-start.13
  33.3 8.5 %atmos_block.3 = (bf16[96,96,128]{2,1,0:T(8,128)(2,1)S(1)}, bf16[4,18,32,128]{3,2,1,0:T(8,128)(2,1)S(1)}, bf16[4,18,32,128]{3,2,1,0:T(8,128)(2,1)S(1)}) custom-call(bf16[96,96,128]{2,1,0:T(8,128)(2,1)S(1)} %get-tuple-element.20.x_ref.refs_0_, f32[96,96,128]{2,1,0:T(8,128)S(1)} %get-tuple-element.21.refs_1_, ...), custom_call_target="tpu_custom_call" | custom-call | flops 8000000000 | tf_op jit(solution)/shard_map/atmos_block/pallas_call | solution.py:411
  41.8 0.1 collective-permute-start.4
  41.8 2.0 %collective-permute-done.4.got_ref.refs_1_ = bf16[4,18,32,128]{3,2,1,0:T(8,128)(2,1)S(1)} collective-permute-done((bf16[4,18,32,128]{3,2,1,0:T(8,128)(2,1)S(1)}, bf16[4,18,32,128]{3,2,1,0:T(8,128)(2,1)S(1)}, u32[]{:S(2)}, u32[]{:S(2)}) %collective-permute-start.4) | collective-permute-done | bytes 589856 | tf_op jit(solution)/shard_map/ppermute | solution.py:449
  43.8 0.1 add_pairs.1
  44.0 2.5 %collective-permute-start.5 = (bf16[18,32,128]{2,1,0:T(8,128)(2,1)S(1)}, bf16[18,32,128]{2,1,0:T(8,128)(2,1)S(1)}, u32[]{:S(2)}, u32[]{:S(2)}) collective-permute-start(bf16[18,32,128]{2,1,0:T(8,128)(2,1)S(1)} %get-tuple-element.27), channel_id=1, source_target_pairs={{0,24},{4,28},{8,16},{12,20},{16,8},{20,12},{24,0},{28,4},{1,25},{... | collective-permute-start | bytes 442376 | tf_op jit(solution)/shard_map/ppermute | solution.py:449
  46.5 0.5 collective-permute-start.6
  47.0 0.6 collective-permute-start.7
  47.6 0.0 copy-done.13
  47.6 1.2 %ocean_band.1.band_ref = bf16[6,160,1792]{2,1,0:T(8,128)(2,1)S(1)} custom-call(f32[7,7,96]{2,1,0:T(8,128)S(1)} %copy-done.13, bf16[18,32,128]{2,1,0:T(8,128)(2,1)S(1)} %get-tuple-element.29._), custom_call_target="tpu_custom_call" | custom-call | flops 3000000000 | tf_op jit(solution)/shard_map/ocean_band/pallas_call | solution.py:220
  48.8 2.6 %collective-permute-done.5.refs_2_ = bf16[18,32,128]{2,1,0:T(8,128)(2,1)S(1)} collective-permute-done((bf16[18,32,128]{2,1,0:T(8,128)(2,1)S(1)}, bf16[18,32,128]{2,1,0:T(8,128)(2,1)S(1)}, u32[]{:S(2)}, u32[]{:S(2)}) %collective-permute-start.5) | collective-permute-done | bytes 147488 | tf_op jit(solution)/shard_map/ppermute | solution.py:449
  51.4 2.6 %collective-permute-done.6.refs_3_ = bf16[18,32,128]{2,1,0:T(8,128)(2,1)S(1)} collective-permute-done((bf16[18,32,128]{2,1,0:T(8,128)(2,1)S(1)}, bf16[18,32,128]{2,1,0:T(8,128)(2,1)S(1)}, u32[]{:S(2)}, u32[]{:S(2)}) %collective-permute-start.6) | collective-permute-done | bytes 147488 | tf_op jit(solution)/shard_map/ppermute | solution.py:449
  54.0 0.1 collective-permute-done.7.refs_4_
  54.1 0.0 copy-done.1
  54.1 0.0 copy-done.2
  54.1 0.0 copy-done.5
  54.1 0.0 copy-done.6
  54.1 1.0 %ocean_forcing.1 = (bf16[18,96,128]{2,1,0:T(8,128)(2,1)S(1)}, bf16[2,96,128]{2,1,0:T(8,128)(2,1)S(1)}) custom-call(bf16[4,18,32,128]{3,2,1,0:T(8,128)(2,1)S(1)} %get-tuple-element.25.keep_ref.refs_0_, bf16[4,18,32,128]{3,2,1,0:T(8,128)(2,1)S(1)} %collective-permute-done.4.got_ref.refs_1_, bf16[18,32,128]{2,1,0:T(8,128)(2,1)S(1)} %collective-permute-done.5.refs_2_, ...), custom_call_target="tpu_custom_call" | custom-call | tf_op jit(solution)/shard_map/ocean_forcing/pallas_call | solution.py:498
  55.1 0.3 collective-permute-start.8
  55.4 3.8 %collective-permute-start.9 = (bf16[2,96,128]{2,1,0:T(8,128)(2,1)S(1)}, bf16[2,96,128]{2,1,0:T(8,128)(2,1)S(1)}, u32[]{:S(2)}, u32[]{:S(2)}) collective-permute-start(bf16[2,96,128]{2,1,0:T(8,128)(2,1)S(1)} %get-tuple-element.31), channel_id=1, source_target_pairs={{1,0},{2,1},{3,2},{0,3},{5,4},{6,5},{7,6},{4,7},{9,8},{10,9},{11,1... | collective-permute-start | bytes 147464 | tf_op jit(solution)/shard_map/ppermute | solution.py:95
  59.3 0.0 copy-start.9
  59.3 1.4 %ocean_conv.1.a_ref = f32[12,96,128]{2,1,0:T(8,128)S(1)} custom-call(bf16[18,96,128]{2,1,0:T(8,128)(2,1)S(1)} %get-tuple-element.30.x_ref.mid_ref, bf16[6,160,1792]{2,1,0:T(8,128)(2,1)S(1)} %ocean_band.1.band_ref), custom_call_target="tpu_custom_call" | custom-call | flops 2000000000 | tf_op jit(solution)/shard_map/ocean_conv/pallas_call | solution.py:243
  60.7 0.7 collective-permute-done.8.left_ref
  61.3 0.0 collective-permute-done.9.right_ref
  61.3 0.0 copy-done.3
  61.3 0.0 copy-done.4
  61.3 0.0 copy-done.7
  61.3 0.0 copy-done.8
  61.4 0.0 copy-done.9
  61.4 0.0 copy-start.17
  61.4 2.9 %ocean_block.1 = (bf16[12,96,128]{2,1,0:T(8,128)(2,1)}, bf16[12,8,128]{2,1,0:T(8,128)(2,1)S(1)}) custom-call(bf16[18,96,128]{2,1,0:T(8,128)(2,1)S(1)} %get-tuple-element.30.x_ref.mid_ref, f32[12,96,128]{2,1,0:T(8,128)S(1)} %ocean_conv.1.a_ref, bf16[2,96,128]{2,1,0:T(8,128)(2,1)S(1)} %collective-permute-done.8.left_ref, ...), custom_call_target="tpu_custom_call" | custom-call | tf_op jit(solution)/shard_map/ocean_block/pallas_call | solution.py:536
  64.3 0.0 collective-permute-start.10
  64.3 1.2 %collective-permute-done.10.got_ref = bf16[12,8,128]{2,1,0:T(8,128)(2,1)S(1)} collective-permute-done((bf16[12,8,128]{2,1,0:T(8,128)(2,1)S(1)}, bf16[12,8,128]{2,1,0:T(8,128)(2,1)S(1)}, u32[]{:S(2)}, u32[]{:S(2)}) %collective-permute-start.10) | collective-permute-done | bytes 24608 | tf_op jit(solution)/shard_map/ppermute | solution.py:449
  65.5 1.5 %collective-permute-start.11 = (bf16[2,12,8,128]{3,2,1,0:T(8,128)(2,1)S(1)}, bf16[2,12,8,128]{3,2,1,0:T(8,128)(2,1)S(1)}, u32[]{:S(2)}, u32[]{:S(2)}) collective-permute-start(bf16[2,12,8,128]{3,2,1,0:T(8,128)(2,1)S(1)} %surface_pair.1.refs_0_), channel_id=1, source_target_pairs={{0,8},{4,12},{8,0},{12,4},{16,24},{20,28},{24,16},{28,20},{1,9},{5... | collective-permute-start | bytes 147464 | tf_op jit(solution)/shard_map/ppermute | solution.py:449
  66.9 0.7 collective-permute-start.12
  67.7 1.3 %collective-permute-start.13 = (bf16[2,12,8,128]{3,2,1,0:T(8,128)(2,1)S(1)}, bf16[2,12,8,128]{3,2,1,0:T(8,128)(2,1)S(1)}, u32[]{:S(2)}, u32[]{:S(2)}) collective-permute-start(bf16[2,12,8,128]{3,2,1,0:T(8,128)(2,1)S(1)} %surface_pair.1.refs_0_), channel_id=1, source_target_pairs={{0,24},{4,28},{8,16},{12,20},{16,8},{20,12},{24,0},{28,4},{1,25},{... | collective-permute-start | bytes 147464 | tf_op jit(solution)/shard_map/ppermute | solution.py:449
  69.0 0.1 copy.20
  69.1 0.5 collective-permute-done.11.refs_1_
  69.6 2.0 %collective-permute-done.12.refs_2_ = bf16[2,12,8,128]{3,2,1,0:T(8,128)(2,1)S(1)} collective-permute-done((bf16[2,12,8,128]{3,2,1,0:T(8,128)(2,1)S(1)}, bf16[2,12,8,128]{3,2,1,0:T(8,128)(2,1)S(1)}, u32[]{:S(2)}, u32[]{:S(2)}) %collective-permute-start.12) | collective-permute-done | bytes 49184 | tf_op jit(solution)/shard_map/ppermute | solution.py:449
  71.6 1.1 %collective-permute-done.13.refs_3_ = bf16[2,12,8,128]{3,2,1,0:T(8,128)(2,1)S(1)} collective-permute-done((bf16[2,12,8,128]{3,2,1,0:T(8,128)(2,1)S(1)}, bf16[2,12,8,128]{3,2,1,0:T(8,128)(2,1)S(1)}, u32[]{:S(2)}, u32[]{:S(2)}) %collective-permute-start.13) | collective-permute-done | bytes 49184 | tf_op jit(solution)/shard_map/ppermute | solution.py:449
  72.7 2.5 %couple.1 = bf16[96,96,128]{2,1,0:T(8,128)(2,1)} custom-call(bf16[96,96,128]{2,1,0:T(8,128)(2,1)S(1)} %get-tuple-element.24.y_ref, s32[96,128]{1,0:T(8,128)S(1)} %copy-done.2, bf16[96,8]{1,0:T(8,128)(2,1)S(1)} %bitcast.13, bf16[2,12,8,128]{3,2,1,0:T(8,128)(2,1)S(1)} %surface_pair.1.refs_0_, bf16[2,12,8,128]{3,2,1,0:T(8,128)(2,1)S(1)} %collective-permute-done.11.refs_1_, ...), custom_call_target="tpu_custom_call" | custom-call | tf_op jit(solution)/shard_map/couple/pallas_call | solution.py:596
  (13 shorter events, 0.0 us)
Async XLA Ops:
  0.6 8.0 %copy-start = (bf16[1,96,96,128]{3,2,1,0:T(8,128)(2,1)S(1)}, bf16[1,96,96,128]{3,2,1,0:T(8,128)(2,1)}, u32[]{:S(2)}) copy-start(bf16[1,96,96,128]{3,2,1,0:T(8,128)(2,1)} %param.18) | copy-start | bytes 7077892
  0.6 8.0 %copy-start.12 = (f32[2,7,7,96]{3,0,2,1:T(2,128)S(1)}, f32[2,7,7,96]{3,0,2,1:T(2,128)}, u32[]{:S(2)}) copy-start(f32[2,7,7,96]{3,0,2,1:T(2,128)} %param.22) | copy-start | bytes 112900
  3.4 11.5 %collective-permute-start = (bf16[6,96,128]{2,1,0:T(8,128)(2,1)}, bf16[6,96,128]{2,1,0:T(8,128)(2,1)S(1)}, u32[]{:S(2)}, u32[]{:S(2)}) collective-permute-start(bf16[6,96,128]{2,1,0:T(8,128)(2,1)} %pack_edges.1), channel_id=1, source_target_pairs={{0,1},{1,2},{2,3},{3,0},{4,5},{5,6},{6,7},{7,4},{8,9},{9,10},{10,1... | collective-permute-start | bytes 442376 | tf_op jit(solution)/shard_map/ppermute | solution.py:94
  6.5 8.7 %collective-permute-start.1 = (bf16[6,96,128]{2,1,0:T(8,128)(2,1)}, bf16[6,96,128]{2,1,0:T(8,128)(2,1)S(1)}, u32[]{:S(2)}, u32[]{:S(2)}) collective-permute-start(bf16[6,96,128]{2,1,0:T(8,128)(2,1)} %pack_edges.1), channel_id=1, source_target_pairs={{1,0},{2,1},{3,2},{0,3},{5,4},{6,5},{7,6},{4,7},{9,8},{10,9},{11,1... | collective-permute-start | bytes 442376 | tf_op jit(solution)/shard_map/ppermute | solution.py:95
  8.6 6.6 %copy-start.10 = (bf16[2,96,384]{2,1,0:T(8,128)(2,1)S(1)}, bf16[2,96,384]{2,1,0:T(8,128)(2,1)}, u32[]{:S(2)}) copy-start(bf16[2,96,384]{2,1,0:T(8,128)(2,1)} %refs_6_.4) | copy-start | bytes 442372
  8.6 6.6 %copy-start.11 = (bf16[2,384,96]{1,2,0:T(8,128)(2,1)S(1)}, bf16[2,384,96]{1,2,0:T(8,128)(2,1)}, u32[]{:S(2)}) copy-start(bf16[2,384,96]{1,2,0:T(8,128)(2,1)} %param.25) | copy-start | bytes 442372
  8.6 6.6 %copy-start.15 = (f32[2,96]{1,0:T(2,128)S(1)}, f32[2,96]{1,0:T(2,128)}, u32[]{:S(2)}) copy-start(f32[2,96]{1,0:T(2,128)} %refs_5_.4) | copy-start | bytes 2308
  8.6 6.6 %copy-start.16 = (f32[2,96]{1,0:T(2,128)S(1)}, f32[2,96]{1,0:T(2,128)}, u32[]{:S(2)}) copy-start(f32[2,96]{1,0:T(2,128)} %refs_8_.4) | copy-start | bytes 2308
  22.9 10.3 %collective-permute-start.2 = (bf16[6,96,128]{2,1,0:T(8,128)(2,1)S(1)}, bf16[6,96,128]{2,1,0:T(8,128)(2,1)S(1)}, u32[]{:S(2)}, u32[]{:S(2)}) collective-permute-start(bf16[6,96,128]{2,1,0:T(8,128)(2,1)S(1)} %get-tuple-element.22), channel_id=1, source_target_pairs={{0,1},{1,2},{2,3},{3,0},{4,5},{5,6},{6,7},{7,4},{8,9},{9,10},{10,1... | collective-permute-start | bytes 442376 | tf_op jit(solution)/shard_map/ppermute | solution.py:94
  24.1 9.2 %collective-permute-start.3 = (bf16[6,96,128]{2,1,0:T(8,128)(2,1)S(1)}, bf16[6,96,128]{2,1,0:T(8,128)(2,1)S(1)}, u32[]{:S(2)}, u32[]{:S(2)}) collective-permute-start(bf16[6,96,128]{2,1,0:T(8,128)(2,1)S(1)} %get-tuple-element.22), channel_id=1, source_target_pairs={{1,0},{2,1},{3,2},{0,3},{5,4},{6,5},{7,6},{4,7},{9,8},{10,9},{11,1... | collective-permute-start | bytes 442376 | tf_op jit(solution)/shard_map/ppermute | solution.py:95
  26.8 6.5 %copy-start.14 = (bf16[96,32]{0,1:T(8,128)(2,1)S(1)}, bf16[96,32]{0,1:T(8,128)(2,1)}, u32[]{:S(2)}) copy-start(bf16[96,32]{0,1:T(8,128)(2,1)} %param.27) | copy-start | bytes 18436
  33.3 14.3 %copy-start.13 = (f32[7,7,96]{2,1,0:T(8,128)S(1)}, f32[7,7,96]{2,1,0:T(8,128)}, u32[]{:S(2)}) copy-start(f32[7,7,96]{2,1,0:T(8,128)} %k_ref.1) | copy-start | bytes 56452
  41.8 2.1 %collective-permute-start.4 = (bf16[4,18,32,128]{3,2,1,0:T(8,128)(2,1)S(1)}, bf16[4,18,32,128]{3,2,1,0:T(8,128)(2,1)S(1)}, u32[]{:S(2)}, u32[]{:S(2)}) collective-permute-start(bf16[4,18,32,128]{3,2,1,0:T(8,128)(2,1)S(1)} %get-tuple-element.26), channel_id=1, source_target_pairs={{0,4},{4,0},{8,12},{12,8},{16,20},{20,16},{24,28},{28,24},{1,5},{5... | collective-permute-start | bytes 1769480 | tf_op jit(solution)/shard_map/ppermute | solution.py:449
  44.0 7.4 %collective-permute-start.5 = (bf16[18,32,128]{2,1,0:T(8,128)(2,1)S(1)}, bf16[18,32,128]{2,1,0:T(8,128)(2,1)S(1)}, u32[]{:S(2)}, u32[]{:S(2)}) collective-permute-start(bf16[18,32,128]{2,1,0:T(8,128)(2,1)S(1)} %get-tuple-element.27), channel_id=1, source_target_pairs={{0,24},{4,28},{8,16},{12,20},{16,8},{20,12},{24,0},{28,4},{1,25},{... | collective-permute-start | bytes 442376 | tf_op jit(solution)/shard_map/ppermute | solution.py:449
  46.5 7.5 %collective-permute-start.6 = (bf16[18,32,128]{2,1,0:T(8,128)(2,1)S(1)}, bf16[18,32,128]{2,1,0:T(8,128)(2,1)S(1)}, u32[]{:S(2)}, u32[]{:S(2)}) collective-permute-start(bf16[18,32,128]{2,1,0:T(8,128)(2,1)S(1)} %get-tuple-element.28), channel_id=1, source_target_pairs={{0,16},{4,20},{8,24},{12,28},{16,0},{20,4},{24,8},{28,12},{1,17},{... | collective-permute-start | bytes 442376 | tf_op jit(solution)/shard_map/ppermute | solution.py:449
  47.0 7.1 %copy-start.1 = (bf16[96,96,128]{2,1,0:T(8,128)(2,1)S(1)}, bf16[96,96,128]{2,1,0:T(8,128)(2,1)}, u32[]{:S(2)}) copy-start(bf16[96,96,128]{2,1,0:T(8,128)(2,1)} %refs_5_.5) | copy-start | bytes 7077892
  47.0 7.1 %copy-start.2 = (s32[96,128]{1,0:T(8,128)S(1)}, s32[96,128]{1,0:T(8,128)}, u32[]{:S(2)}) copy-start(s32[96,128]{1,0:T(8,128)} %land_ref.3) | copy-start | bytes 147460
  47.0 7.1 %copy-start.5 = (s32[96,128]{1,0:T(8,128)S(1)}, s32[96,128]{1,0:T(8,128)}, u32[]{:S(2)}) copy-start(s32[96,128]{1,0:T(8,128)} %refs_7_.1) | copy-start | bytes 147460
  47.0 7.1 %copy-start.6 = (bf16[2,32,96]{2,1,0:T(8,128)(2,1)S(1)}, bf16[2,32,96]{2,1,0:T(8,128)(2,1)}, u32[]{:S(2)}) copy-start(bf16[2,32,96]{2,1,0:T(8,128)(2,1)} %refs_8_.5) | copy-start | bytes 36868
  47.0 7.1 %collective-permute-start.7 = (bf16[18,32,128]{2,1,0:T(8,128)(2,1)S(1)}, bf16[18,32,128]{2,1,0:T(8,128)(2,1)S(1)}, u32[]{:S(2)}, u32[]{:S(2)}) collective-permute-start(bf16[18,32,128]{2,1,0:T(8,128)(2,1)S(1)} %get-tuple-element.29._), channel_id=1, source_target_pairs={{0,8},{4,12},{8,0},{12,4},{16,24},{20,28},{24,16},{28,20},{1,9},{5... | collective-permute-start | bytes 442376 | tf_op jit(solution)/shard_map/ppermute | solution.py:449
  55.1 6.2 %collective-permute-start.8 = (bf16[2,96,128]{2,1,0:T(8,128)(2,1)S(1)}, bf16[2,96,128]{2,1,0:T(8,128)(2,1)S(1)}, u32[]{:S(2)}, u32[]{:S(2)}) collective-permute-start(bf16[2,96,128]{2,1,0:T(8,128)(2,1)S(1)} %get-tuple-element.31), channel_id=1, source_target_pairs={{0,1},{1,2},{2,3},{3,0},{4,5},{5,6},{6,7},{7,4},{8,9},{9,10},{10,1... | collective-permute-start | bytes 147464 | tf_op jit(solution)/shard_map/ppermute | solution.py:94
  55.4 5.9 %collective-permute-start.9 = (bf16[2,96,128]{2,1,0:T(8,128)(2,1)S(1)}, bf16[2,96,128]{2,1,0:T(8,128)(2,1)S(1)}, u32[]{:S(2)}, u32[]{:S(2)}) collective-permute-start(bf16[2,96,128]{2,1,0:T(8,128)(2,1)S(1)} %get-tuple-element.31), channel_id=1, source_target_pairs={{1,0},{2,1},{3,2},{0,3},{5,4},{6,5},{7,6},{4,7},{9,8},{10,9},{11,1... | collective-permute-start | bytes 147464 | tf_op jit(solution)/shard_map/ppermute | solution.py:95
  59.2 2.1 %copy-start.3 = (bf16[96,384]{1,0:T(8,128)(2,1)S(1)}, bf16[96,384]{1,0:T(8,128)(2,1)}, u32[]{:S(2)}) copy-start(bf16[96,384]{1,0:T(8,128)(2,1)} %up_ref.1) | copy-start | bytes 221188
  59.2 2.1 %copy-start.4 = (bf16[384,96]{0,1:T(8,128)(2,1)S(1)}, bf16[384,96]{0,1:T(8,128)(2,1)}, u32[]{:S(2)}) copy-start(bf16[384,96]{0,1:T(8,128)(2,1)} %param.32) | copy-start | bytes 221188
  59.2 2.1 %copy-start.7 = (bf16[96,8]{0,1:T(8,128)(2,1)S(1)}, bf16[96,8]{0,1:T(8,128)(2,1)}, u32[]{:S(2)}) copy-start(bf16[96,8]{0,1:T(8,128)(2,1)} %param.34) | copy-start | bytes 4612
  59.3 2.1 %copy-start.8 = (f32[96]{0:T(128)S(1)}, f32[96]{0:T(128)}, u32[]{:S(2)}) copy-start(f32[96]{0:T(128)} %param.30) | copy-start | bytes 1156
  59.3 2.1 %copy-start.9 = (f32[96]{0:T(128)S(1)}, f32[96]{0:T(128)}, u32[]{:S(2)}) copy-start(f32[96]{0:T(128)} %param.33) | copy-start | bytes 1156
  61.4 7.6 %copy-start.17 = (bf16[8,96]{1,0:T(8,128)(2,1)S(1)}, bf16[8,96]{1,0:T(8,128)(2,1)}, u32[]{:S(2)}) copy-start(bf16[8,96]{1,0:T(8,128)(2,1)} %param.35) | copy-start | bytes 4612
  64.3 1.2 %collective-permute-start.10 = (bf16[12,8,128]{2,1,0:T(8,128)(2,1)S(1)}, bf16[12,8,128]{2,1,0:T(8,128)(2,1)S(1)}, u32[]{:S(2)}, u32[]{:S(2)}) collective-permute-start(bf16[12,8,128]{2,1,0:T(8,128)(2,1)S(1)} %get-tuple-element.32.own_ref), channel_id=1, source_target_pairs={{0,4},{4,0},{8,12},{12,8},{16,20},{20,16},{24,28},{28,24},{1,5},{5... | collective-permute-start | bytes 73736 | tf_op jit(solution)/shard_map/ppermute | solution.py:449
  65.5 4.1 %collective-permute-start.11 = (bf16[2,12,8,128]{3,2,1,0:T(8,128)(2,1)S(1)}, bf16[2,12,8,128]{3,2,1,0:T(8,128)(2,1)S(1)}, u32[]{:S(2)}, u32[]{:S(2)}) collective-permute-start(bf16[2,12,8,128]{3,2,1,0:T(8,128)(2,1)S(1)} %surface_pair.1.refs_0_), channel_id=1, source_target_pairs={{0,8},{4,12},{8,0},{12,4},{16,24},{20,28},{24,16},{28,20},{1,9},{5... | collective-permute-start | bytes 147464 | tf_op jit(solution)/shard_map/ppermute | solution.py:449
  66.9 4.6 %collective-permute-start.12 = (bf16[2,12,8,128]{3,2,1,0:T(8,128)(2,1)S(1)}, bf16[2,12,8,128]{3,2,1,0:T(8,128)(2,1)S(1)}, u32[]{:S(2)}, u32[]{:S(2)}) collective-permute-start(bf16[2,12,8,128]{3,2,1,0:T(8,128)(2,1)S(1)} %surface_pair.1.refs_0_), channel_id=1, source_target_pairs={{0,16},{4,20},{8,24},{12,28},{16,0},{20,4},{24,8},{28,12},{1,17},{... | collective-permute-start | bytes 147464 | tf_op jit(solution)/shard_map/ppermute | solution.py:449
  67.7 5.0 %collective-permute-start.13 = (bf16[2,12,8,128]{3,2,1,0:T(8,128)(2,1)S(1)}, bf16[2,12,8,128]{3,2,1,0:T(8,128)(2,1)S(1)}, u32[]{:S(2)}, u32[]{:S(2)}) collective-permute-start(bf16[2,12,8,128]{3,2,1,0:T(8,128)(2,1)S(1)} %surface_pair.1.refs_0_), channel_id=1, source_target_pairs={{0,24},{4,28},{8,16},{12,20},{16,8},{20,12},{24,0},{28,4},{1,25},{... | collective-permute-start | bytes 147464 | tf_op jit(solution)/shard_map/ppermute | solution.py:449

commit v7 on v6

--- a/solution.py
+++ b/solution.py
@@ -99,17 +99,21 @@
 def fill_base(taps, base):
     groups, _, wide = base.shape
     chans = groups * GROUP
-    t = lax.broadcasted_iota(jnp.int32, (TAPS, wide), 0)
-    n = lax.broadcasted_iota(jnp.int32, (TAPS, wide), 1)
-    total = jnp.zeros((chans, wide), F32)
+    tall = TAPS * SLOT
+    t = lax.broadcasted_iota(jnp.int32, (tall, wide), 0)
+    n = lax.broadcasted_iota(jnp.int32, (tall, wide), 1)
+    hit = (t % SLOT == n // DEPTH) & (t // SLOT == (n % DEPTH) // GROUP)
+    columns = []
     for i in range(TAPS):
-        put = ((t == n // DEPTH) & ((n % DEPTH) // GROUP == i)).astype(F32).astype(BF)
-        total = total + jnp.dot(taps(i).T.astype(BF), put, preferred_element_type=F32)
-    r = lax.broadcasted_iota(jnp.int32, (chans, wide), 0)
-    c = lax.broadcasted_iota(jnp.int32, (chans, wide), 1)
-    total = jnp.where(r % GROUP == c % GROUP, total, 0.0)
+        columns.append(taps(i).T)
+        columns.append(jnp.zeros((chans, SLOT - TAPS), F32))
+    columns = jnp.concatenate(columns, axis=1).astype(BF)
+    total = jnp.dot(columns, hit.astype(F32).astype(BF), preferred_element_type=F32)
+    r = lax.broadcasted_iota(jnp.int32, (GROUP, wide), 0)
+    c = lax.broadcasted_iota(jnp.int32, (GROUP, wide), 1)
+    same = r == c % GROUP
     for g in range(groups):
-        base[g] = total[GROUP * g : GROUP * (g + 1)]
+        base[g] = jnp.where(same, total[GROUP * g : GROUP * (g + 1)], 0.0)
 
 
 def fill_band(base, g, band):
@@ -208,25 +212,38 @@
     )(x, taps)
 
 
-def band_kernel(k_ref, _, band_ref, base):
+def prepare_kernel(k_ref, g_ref, up_ref, s_ref, _, band_ref, mat_ref, upt_ref, gain_ref, scale_ref, base):
+    lanes = gain_ref.shape[1]
+    mat_ref[...] = halo_matrix(lanes)
+    upt_ref[...] = transposed(up_ref[...])
+    gain_ref[...] = spread(g_ref[...], lanes)
+    scale_ref[...] = spread(s_ref[...], lanes)
     fill_base(lambda i: k_ref[i], base)
     for g in range(base.shape[0]):
         fill_band(base, g, band_ref.at[g])
 
 
-def ocean_band(taps, after):
-    groups = taps.shape[2] // GROUP
+def prepare_ocean(taps, gain, up, scale, after):
+    chans, hid = up.shape
+    lanes = after.shape[-1]
+    groups = chans // GROUP
     wide = TAPS * DEPTH
     return pl.pallas_call(
-        band_kernel,
-        out_shape=jax.ShapeDtypeStruct((groups, GROUP * OUT, wide), BF),
-        in_specs=[VMEM, ANY],
-        out_specs=VMEM,
+        prepare_kernel,
+        out_shape=[
+            jax.ShapeDtypeStruct((groups, GROUP * OUT, wide), BF),
+            jax.ShapeDtypeStruct((2 * lanes, (TAPS - 1) * lanes), BF),
+            jax.ShapeDtypeStruct((hid, chans), BF),
+            jax.ShapeDtypeStruct((chans, lanes), F32),
+            jax.ShapeDtypeStruct((chans, lanes), F32),
+        ],
+        in_specs=[VMEM] * 4 + [ANY],
+        out_specs=[VMEM] * 5,
         scratch_shapes=[pltpu.VMEM((groups, GROUP, wide), F32)],
         compiler_params=params(24),
         cost_estimate=cost(3),
-        name="ocean_band",
-    )(taps, after)
+        name="prepare_ocean",
+    )(taps, gain[None], up, scale[None], after)
 
 
 def ocean_conv_kernel(x_ref, band_ref, a_ref, xj):
@@ -253,25 +270,30 @@
 
 
 def halo_matrix(lanes):
-    side = [j for j in range(TAPS) if j != HALO]
-    shape = (2 * lanes, len(side) * lanes)
+    shape = (lanes, lanes)
     src = lax.broadcasted_iota(jnp.int32, shape, 0)
     dst = lax.broadcasted_iota(jnp.int32, shape, 1)
-    hit = jnp.zeros(shape, jnp.bool_)
-    to = dst % lanes
-    for a, j in enumerate(side):
+    ahead = (src - dst + lanes) % lanes
+    right = (src % SLOT < HALO) & (dst % SLOT >= SLOT - HALO)
+    left = (src % SLOT >= SLOT - HALO) & (dst % SLOT < HALO)
+    right = jnp.where(right, ahead, -1)
+    left = jnp.where(left, ahead, -1)
+    none = jnp.zeros(shape, BF)
+    upper, lower = [], []
+    for j in range(TAPS):
         d = j - HALO
-        here = (dst >= a * lanes) & (dst < (a + 1) * lanes)
-        from_ = (to + d + lanes) % lanes
         if d > 0:
-            ok = (src == from_) & (src % SLOT < HALO) & (to % SLOT >= SLOT - HALO)
-        else:
-            ok = (src == from_ + lanes) & (src % SLOT >= SLOT - HALO) & (to % SLOT < HALO)
-        hit = hit | (here & ok)
-    return hit.astype(F32).astype(BF)
-
-
-def halo_conv(left, right, band, wrapped, xe, halo):
+            upper.append((right == d).astype(F32).astype(BF))
+            lower.append(none)
+        elif d < 0:
+            upper.append(none)
+            lower.append((left == lanes + d).astype(F32).astype(BF))
+    return jnp.concatenate(
+        [jnp.concatenate(upper, axis=1), jnp.concatenate(lower, axis=1)], axis=0
+    )
+
+
+def halo_conv(left, right, band, wrapped, matrix, xe, halo):
     blocks, chans, lanes = halo.shape
     wide = TAPS * DEPTH
     both = [jnp.concatenate([right[q], left[q]], axis=1) for q in range(blocks)]
@@ -297,7 +319,7 @@
             for e in range(blocks, blocks + 2 * HALO)
         ]
     field = jnp.concatenate(tall, axis=0)
-    moved = jnp.dot(field, halo_matrix(lanes), preferred_element_type=F32)
+    moved = jnp.dot(field, matrix, preferred_element_type=F32)
     count = len(tall)
     for a in range(TAPS - 1):
         part = moved[:, a * lanes : (a + 1) * lanes].astype(BF)
@@ -342,7 +364,7 @@
     xe, halo, even, odd = refs[-4:]
     rows, chans, lanes = x_ref.shape
     blocks = halo.shape[0]
-    halo_conv(left_ref, right_ref, band_ref, True, xe, halo)
+    halo_conv(left_ref, right_ref, band_ref, True, halo_matrix(lanes), xe, halo)
     up_t = transposed(up_ref[layer])
     dn_t = halved(dn_ref[layer])
     gain = spread(g_ref[layer : layer + 1], lanes)
@@ -509,13 +531,12 @@
     )(*chunks, ocean, land, ice, lift)
 
 
-def ocean_kernel(mid_ref, a_ref, left_ref, right_ref, band_ref, land_ref, g_ref, up_ref, dn_ref, s_ref, sw_ref, new_ref, surf_ref, xe, halo, normed):
+def ocean_kernel(mid_ref, a_ref, left_ref, right_ref, band_ref, land_ref, mat_ref, upt_ref, gain_ref, scale_ref, dn_ref, sw_ref, new_ref, surf_ref, xe, halo, normed):
     share, chans, lanes = new_ref.shape
-    halo_conv(left_ref, right_ref, band_ref, False, xe, halo)
-    gain = spread(g_ref[...], lanes)
-    scale = spread(s_ref[...], lanes)
-    norm_rows(a_ref, 0, share, halo, gain, normed)
-    branch = branch_of(normed[...], transposed(up_ref[...]), halved(dn_ref[...]))
+    halo_conv(left_ref, right_ref, band_ref, False, mat_ref[...], xe, halo)
+    scale = scale_ref[...]
+    norm_rows(a_ref, 0, share, halo, gain_ref[...], normed)
+    branch = branch_of(normed[...], upt_ref[...], halved(dn_ref[...]))
     first = lax.axis_index("member") * share
     made = []
     for r in range(share):
@@ -530,7 +551,7 @@
         surf_ref[r] = surf[:, r * lanes : (r + 1) * lanes].astype(BF)
 
 
-def ocean_block(mid, a, left, right, band, land, gain, up, down, scale, surf_weight):
+def ocean_block(mid, a, left, right, band, land, ready, down, surf_weight):
     share, chans, lanes = a.shape
     blocks = left.shape[0]
     return pl.pallas_call(
@@ -539,7 +560,7 @@
             jax.ShapeDtypeStruct((share, chans, lanes), BF),
             jax.ShapeDtypeStruct((share, surf_weight.shape[0], lanes), BF),
         ],
-        in_specs=[VMEM] * 11,
+        in_specs=[VMEM] * 12,
         out_specs=[VMEM] * 2,
         scratch_shapes=[
             pltpu.VMEM((TAPS - 1, SPAN, chans, lanes), BF),
@@ -548,7 +569,7 @@
         ],
         compiler_params=params(24),
         name="ocean_block",
-    )(mid, a, left, right, band, land, gain[None], up, down, scale[None], surf_weight)
+    )(mid, a, left, right, band, land, *ready, down, surf_weight)
 
 
 def pair_kernel(own_ref, got_ref, out_ref):
@@ -645,14 +666,14 @@
     got = send_xor(give, 1)
     sums = add_pairs(keep, got, 1)
     sent = [send_xor(sums[k - 1], 2 * k) for k in range(half - 1, 0, -1)]
-    band = ocean_band(ocn_kernel, sums[0])
+    band, *ready = prepare_ocean(ocn_kernel, ocn_gain, ocn_up, ocn_scale, sums[0])
     sent = [keep, got] + sent
 
     mid, packed = force(members, sent, ocean, land_mask, ice_mask, flux_lift)
     left, right = neighbours(packed)
     a = ocean_conv(mid, band)
     ocean_rows, surface = ocean_block(
-        mid, a, left, right, band, land_mask, ocn_gain, ocn_up, ocn_down.T, ocn_scale, surf_weight.T
+        mid, a, left, right, band, land_mask, ready, ocn_down.T, surf_weight.T
     )
     own = make_pair(surface, send_xor(surface, 1))
     pairs = [own] + [send_xor(own, 2 * k) for k in range(1, half)]

time: 75.3 us -> 75.2 us (level)
  transfers between devices with their start and end apart: 14 -> 14, of which waited for: 10 -> 10; matrix products, arithmetic and copies ran while one was open for 0% -> 0% of each run, Pallas kernels for 20% -> 21%
where the time goes in v7:
time: 75.2 us; the launch traced here: 75.1 us
  Pallas kernels  40.8 us (54%)
  starting transfers between devices  20.2 us (27%)
  waiting for transfers between devices  12.9 us (17%)
  between operations  0.9 us (1%)
    pallas_call x2, Pallas kernels, atmos_block(): pl.pallas_call(functools.partial(atmos_kernel, layer, members, count), ou...  16.1 us
    pallas_call x2, Pallas kernels, convolve(): pl.pallas_call(functools.partial(conv_kernel, layer), out_shape=[jax.Shap...  12.9 us
    ppermute x8, waiting for transfers between devices, send_xor(): lax.ppermute(value, 'member', [(i, i ^ bits) for i in range(members)])  12.1 us
    ppermute x3, starting transfers between devices, neighbours(): lax.ppermute(packed, 'lon', [((i + 1) % count, i) for i in range(count)])  8.59 us
    ppermute x8, starting transfers between devices, send_xor(): lax.ppermute(value, 'member', [(i, i ^ bits) for i in range(members)])  7.12 us
    ppermute x3, starting transfers between devices, neighbours(): lax.ppermute(packed, 'lon', [(i, (i + 1) % count) for i in range(count)])  4.54 us
    pallas_call x1, Pallas kernels, pack(): pl.pallas_call(functools.partial(pack_kernel, step), out_shape=jax.ShapeD...  2.77 us
    pallas_call x1, Pallas kernels, ocean_block(): pl.pallas_call(ocean_kernel, out_shape=[jax.ShapeDtypeStruct((share, chan...  2.7 us
  transfers between devices with their start and end apart: 14, of which 10 were waited for; matrix products, arithmetic and copies ran while one was open for 0% of the time, Pallas kernels for 21%

profile of v7, /device:TPU:0, one launch (start us, length us, event | category | flops | bytes accessed | tf_op | source)
XLA Modules:
  0.0 75.1 jit_solution(12901910852634493247)
XLA Ops:
  0.6 0.0 copy-start
  0.6 0.0 copy-start.10
  0.6 2.8 %pack_edges.1 = bf16[6,96,128]{2,1,0:T(8,128)(2,1)} custom-call(bf16[96,96,128]{2,1,0:T(8,128)(2,1)} %bitcast.10), custom_call_target="tpu_custom_call" | custom-call | tf_op jit(solution)/shard_map/pack_edges/pallas_call | solution.py:81
  3.4 3.1 %collective-permute-start = (bf16[6,96,128]{2,1,0:T(8,128)(2,1)}, bf16[6,96,128]{2,1,0:T(8,128)(2,1)S(1)}, u32[]{:S(2)}, u32[]{:S(2)}) collective-permute-start(bf16[6,96,128]{2,1,0:T(8,128)(2,1)} %pack_edges.1), channel_id=1, source_target_pairs={{0,1},{1,2},{2,3},{3,0},{4,5},{5,6},{6,7},{7,4},{8,9},{9,10},{10,1... | collective-permute-start | bytes 442376 | tf_op jit(solution)/shard_map/ppermute | solution.py:94
  6.5 2.1 %collective-permute-start.1 = (bf16[6,96,128]{2,1,0:T(8,128)(2,1)}, bf16[6,96,128]{2,1,0:T(8,128)(2,1)S(1)}, u32[]{:S(2)}, u32[]{:S(2)}) collective-permute-start(bf16[6,96,128]{2,1,0:T(8,128)(2,1)} %pack_edges.1), channel_id=1, source_target_pairs={{1,0},{2,1},{3,2},{0,3},{5,4},{6,5},{7,6},{4,7},{9,8},{10,9},{11,1... | collective-permute-start | bytes 442376 | tf_op jit(solution)/shard_map/ppermute | solution.py:95
  8.6 0.0 copy-done
  8.6 0.0 copy-done.10
  8.6 0.0 copy-start.13
  8.6 0.0 copy-start.14
  8.6 6.4 %conv.2 = (f32[96,96,128]{2,1,0:T(8,128)S(1)}, bf16[6,96,1792]{2,1,0:T(8,128)(2,1)S(1)}) custom-call(bf16[96,96,128]{2,1,0:T(8,128)(2,1)S(1)} %bitcast.11, f32[7,7,2,96]{3,2,1,0:T(2,128)S(1)} %bitcast.18), custom_call_target="tpu_custom_call" | custom-call | flops 8000000000 | tf_op jit(solution)/shard_map/conv/pallas_call | solution.py:196
  15.0 0.0 collective-permute-done.refs_2_
  15.0 0.2 collective-permute-done.1.refs_3_
  15.2 0.0 copy-done.7
  15.2 0.0 copy-done.8
  15.2 0.0 copy-done.13
  15.2 0.0 copy-done.14
  15.2 7.6 %atmos_block.2 = (bf16[96,96,128]{2,1,0:T(8,128)(2,1)S(1)}, bf16[6,96,128]{2,1,0:T(8,128)(2,1)S(1)}) custom-call(bf16[96,96,128]{2,1,0:T(8,128)(2,1)S(1)} %bitcast.12, f32[96,96,128]{2,1,0:T(8,128)S(1)} %get-tuple-element.23.refs_1_, bf16[6,96,128]{2,1,0:T(8,128)(2,1)S(1)} %collective-permute-done.refs_2_, ...), custom_call_target="tpu_custom_call" | custom-call | flops 8000000000 | tf_op jit(solution)/shard_map/atmos_block/pallas_call | solution.py:433
  22.8 1.2 %collective-permute-start.2 = (bf16[6,96,128]{2,1,0:T(8,128)(2,1)S(1)}, bf16[6,96,128]{2,1,0:T(8,128)(2,1)S(1)}, u32[]{:S(2)}, u32[]{:S(2)}) collective-permute-start(bf16[6,96,128]{2,1,0:T(8,128)(2,1)S(1)} %get-tuple-element.27), channel_id=1, source_target_pairs={{0,1},{1,2},{2,3},{3,0},{4,5},{5,6},{6,7},{7,4},{8,9},{9,10},{10,1... | collective-permute-start | bytes 442376 | tf_op jit(solution)/shard_map/ppermute | solution.py:94
  24.0 2.7 %collective-permute-start.3 = (bf16[6,96,128]{2,1,0:T(8,128)(2,1)S(1)}, bf16[6,96,128]{2,1,0:T(8,128)(2,1)S(1)}, u32[]{:S(2)}, u32[]{:S(2)}) collective-permute-start(bf16[6,96,128]{2,1,0:T(8,128)(2,1)S(1)} %get-tuple-element.27), channel_id=1, source_target_pairs={{1,0},{2,1},{3,2},{0,3},{5,4},{6,5},{7,6},{4,7},{9,8},{10,9},{11,1... | collective-permute-start | bytes 442376 | tf_op jit(solution)/shard_map/ppermute | solution.py:95
  26.7 6.6 %conv.3 = (f32[96,96,128]{2,1,0:T(8,128)S(1)}, bf16[6,96,1792]{2,1,0:T(8,128)(2,1)S(1)}) custom-call(bf16[96,96,128]{2,1,0:T(8,128)(2,1)S(1)} %get-tuple-element.25.x_ref.refs_0_, f32[7,7,2,96]{3,2,1,0:T(2,128)S(1)} %bitcast.19), custom_call_target="tpu_custom_call" | custom-call | flops 8000000000 | tf_op jit(solution)/shard_map/conv/pallas_call | solution.py:196
  33.3 0.0 collective-permute-done.2.refs_2_
  33.3 0.0 collective-permute-done.3.refs_3_
  33.3 0.0 copy-start.9
  33.3 0.0 copy-start.11
  33.3 0.0 copy-start.15
  33.4 0.0 copy-start.16
  33.4 8.5 %atmos_block.3 = (bf16[96,96,128]{2,1,0:T(8,128)(2,1)S(1)}, bf16[4,18,32,128]{3,2,1,0:T(8,128)(2,1)S(1)}, bf16[4,18,32,128]{3,2,1,0:T(8,128)(2,1)S(1)}) custom-call(bf16[96,96,128]{2,1,0:T(8,128)(2,1)S(1)} %get-tuple-element.25.x_ref.refs_0_, f32[96,96,128]{2,1,0:T(8,128)S(1)} %get-tuple-element.26.refs_1_, ...), custom_call_target="tpu_custom_call" | custom-call | flops 8000000000 | tf_op jit(solution)/shard_map/atmos_block/pallas_call | solution.py:433
  41.8 0.1 collective-permute-start.4
  41.9 2.0 %collective-permute-done.4.got_ref.refs_1_ = bf16[4,18,32,128]{3,2,1,0:T(8,128)(2,1)S(1)} collective-permute-done((bf16[4,18,32,128]{3,2,1,0:T(8,128)(2,1)S(1)}, bf16[4,18,32,128]{3,2,1,0:T(8,128)(2,1)S(1)}, u32[]{:S(2)}, u32[]{:S(2)}) %collective-permute-start.4) | collective-permute-done | bytes 589856 | tf_op jit(solution)/shard_map/ppermute | solution.py:471
  43.9 0.1 add_pairs.1
  44.0 2.5 %collective-permute-start.5 = (bf16[18,32,128]{2,1,0:T(8,128)(2,1)S(1)}, bf16[18,32,128]{2,1,0:T(8,128)(2,1)S(1)}, u32[]{:S(2)}, u32[]{:S(2)}) collective-permute-start(bf16[18,32,128]{2,1,0:T(8,128)(2,1)S(1)} %get-tuple-element.32), channel_id=1, source_target_pairs={{0,24},{4,28},{8,16},{12,20},{16,8},{20,12},{24,0},{28,4},{1,25},{... | collective-permute-start | bytes 442376 | tf_op jit(solution)/shard_map/ppermute | solution.py:471
  46.6 0.5 collective-permute-start.6
  47.0 0.5 collective-permute-start.7
  47.6 0.0 copy-done.11
  47.6 0.0 copy-done.16
  47.6 0.0 copy-start.1
  47.6 0.0 copy-start.2
  47.6 0.0 copy-start.4
  47.6 0.0 copy-start.5
  47.6 1.2 %prepare_ocean.1 = (bf16[6,160,1792]{2,1,0:T(8,128)(2,1)S(1)}, bf16[256,768]{1,0:T(8,128)(2,1)S(1)}, bf16[384,96]{1,0:T(8,128)(2,1)S(1)}, f32[96,128]{1,0:T(8,128)S(1)}, f32[96,128]{1,0:T(8,128)S(1)}) custom-call(f32[7,7,96]{2,1,0:T(8,128)S(1)} %copy-done.11, f32[1,96]{1,0:T(1,128)S(1)} %bitcast.21, bf16[96,384]{1,0:T(8,128)(2,1)S(1)} %copy-done.9, ...), custom_call_target="tpu_custom_call" | custom-call | flops 3000000000 | tf_op jit(solution)/shard_map/prepare_ocean/pallas_call | solution.py:231
  48.8 2.7 %collective-permute-done.5.refs_2_ = bf16[18,32,128]{2,1,0:T(8,128)(2,1)S(1)} collective-permute-done((bf16[18,32,128]{2,1,0:T(8,128)(2,1)S(1)}, bf16[18,32,128]{2,1,0:T(8,128)(2,1)S(1)}, u32[]{:S(2)}, u32[]{:S(2)}) %collective-permute-start.5) | collective-permute-done | bytes 147488 | tf_op jit(solution)/shard_map/ppermute | solution.py:471
  51.5 2.6 %collective-permute-done.6.refs_3_ = bf16[18,32,128]{2,1,0:T(8,128)(2,1)S(1)} collective-permute-done((bf16[18,32,128]{2,1,0:T(8,128)(2,1)S(1)}, bf16[18,32,128]{2,1,0:T(8,128)(2,1)S(1)}, u32[]{:S(2)}, u32[]{:S(2)}) %collective-permute-start.6) | collective-permute-done | bytes 147488 | tf_op jit(solution)/shard_map/ppermute | solution.py:471
  54.0 0.1 collective-permute-done.7.refs_4_
  54.1 0.0 copy-done.2
  54.2 1.0 %ocean_forcing.1 = (bf16[18,96,128]{2,1,0:T(8,128)(2,1)S(1)}, bf16[2,96,128]{2,1,0:T(8,128)(2,1)S(1)}) custom-call(bf16[4,18,32,128]{3,2,1,0:T(8,128)(2,1)S(1)} %get-tuple-element.30.keep_ref.refs_0_, bf16[4,18,32,128]{3,2,1,0:T(8,128)(2,1)S(1)} %collective-permute-done.4.got_ref.refs_1_, bf16[18,32,128]{2,1,0:T(8,128)(2,1)S(1)} %collective-permute-done.5.refs_2_, ...), custom_call_target="tpu_custom_call" | custom-call | tf_op jit(solution)/shard_map/ocean_forcing/pallas_call | solution.py:520
  55.2 0.3 collective-permute-start.8
  55.5 3.8 %collective-permute-start.9 = (bf16[2,96,128]{2,1,0:T(8,128)(2,1)S(1)}, bf16[2,96,128]{2,1,0:T(8,128)(2,1)S(1)}, u32[]{:S(2)}, u32[]{:S(2)}) collective-permute-start(bf16[2,96,128]{2,1,0:T(8,128)(2,1)S(1)} %get-tuple-element.37), channel_id=1, source_target_pairs={{1,0},{2,1},{3,2},{0,3},{5,4},{6,5},{7,6},{4,7},{9,8},{10,9},{11,1... | collective-permute-start | bytes 147464 | tf_op jit(solution)/shard_map/ppermute | solution.py:95
  59.3 1.4 %ocean_conv.1.a_ref = f32[12,96,128]{2,1,0:T(8,128)S(1)} custom-call(bf16[18,96,128]{2,1,0:T(8,128)(2,1)S(1)} %get-tuple-element.35.x_ref.mid_ref, bf16[6,160,1792]{2,1,0:T(8,128)(2,1)S(1)} %get-tuple-element.36.band_ref), custom_call_target="tpu_custom_call" | custom-call | flops 2000000000 | tf_op jit(solution)/shard_map/ocean_conv/pallas_call | solution.py:260
  60.7 0.7 collective-permute-done.8.left_ref
  61.4 0.0 collective-permute-done.9.right_ref
  61.4 0.0 copy-done.3
  61.4 0.0 copy-start.17
  61.4 2.7 %ocean_block.1 = (bf16[12,96,128]{2,1,0:T(8,128)(2,1)}, bf16[12,8,128]{2,1,0:T(8,128)(2,1)S(1)}) custom-call(bf16[18,96,128]{2,1,0:T(8,128)(2,1)S(1)} %get-tuple-element.35.x_ref.mid_ref, f32[12,96,128]{2,1,0:T(8,128)S(1)} %ocean_conv.1.a_ref, bf16[2,96,128]{2,1,0:T(8,128)(2,1)S(1)} %collective-permute-done.8.left_ref, ...), custom_call_target="tpu_custom_call" | custom-call | tf_op jit(solution)/shard_map/ocean_block/pallas_call | solution.py:557
  64.1 0.0 collective-permute-start.10
  64.1 1.2 %collective-permute-done.10.got_ref = bf16[12,8,128]{2,1,0:T(8,128)(2,1)S(1)} collective-permute-done((bf16[12,8,128]{2,1,0:T(8,128)(2,1)S(1)}, bf16[12,8,128]{2,1,0:T(8,128)(2,1)S(1)}, u32[]{:S(2)}, u32[]{:S(2)}) %collective-permute-start.10) | collective-permute-done | bytes 24608 | tf_op jit(solution)/shard_map/ppermute | solution.py:471
  65.3 1.5 %collective-permute-start.11 = (bf16[2,12,8,128]{3,2,1,0:T(8,128)(2,1)S(1)}, bf16[2,12,8,128]{3,2,1,0:T(8,128)(2,1)S(1)}, u32[]{:S(2)}, u32[]{:S(2)}) collective-permute-start(bf16[2,12,8,128]{3,2,1,0:T(8,128)(2,1)S(1)} %surface_pair.1.refs_0_), channel_id=1, source_target_pairs={{0,8},{4,12},{8,0},{12,4},{16,24},{20,28},{24,16},{28,20},{1,9},{5... | collective-permute-start | bytes 147464 | tf_op jit(solution)/shard_map/ppermute | solution.py:471
  66.8 0.7 collective-permute-start.12
  67.5 1.3 %collective-permute-start.13 = (bf16[2,12,8,128]{3,2,1,0:T(8,128)(2,1)S(1)}, bf16[2,12,8,128]{3,2,1,0:T(8,128)(2,1)S(1)}, u32[]{:S(2)}, u32[]{:S(2)}) collective-permute-start(bf16[2,12,8,128]{3,2,1,0:T(8,128)(2,1)S(1)} %surface_pair.1.refs_0_), channel_id=1, source_target_pairs={{0,24},{4,28},{8,16},{12,20},{16,8},{20,12},{24,0},{28,4},{1,25},{... | collective-permute-start | bytes 147464 | tf_op jit(solution)/shard_map/ppermute | solution.py:471
  68.8 0.0 copy-done.17
  68.8 0.1 copy.20
  68.9 0.5 collective-permute-done.11.refs_1_
  69.4 2.0 %collective-permute-done.12.refs_2_ = bf16[2,12,8,128]{3,2,1,0:T(8,128)(2,1)S(1)} collective-permute-done((bf16[2,12,8,128]{3,2,1,0:T(8,128)(2,1)S(1)}, bf16[2,12,8,128]{3,2,1,0:T(8,128)(2,1)S(1)}, u32[]{:S(2)}, u32[]{:S(2)}) %collective-permute-start.12) | collective-permute-done | bytes 49184 | tf_op jit(solution)/shard_map/ppermute | solution.py:471
  71.4 1.1 %collective-permute-done.13.refs_3_ = bf16[2,12,8,128]{3,2,1,0:T(8,128)(2,1)S(1)} collective-permute-done((bf16[2,12,8,128]{3,2,1,0:T(8,128)(2,1)S(1)}, bf16[2,12,8,128]{3,2,1,0:T(8,128)(2,1)S(1)}, u32[]{:S(2)}, u32[]{:S(2)}) %collective-permute-start.13) | collective-permute-done | bytes 49184 | tf_op jit(solution)/shard_map/ppermute | solution.py:471
  72.5 2.5 %couple.1 = bf16[96,96,128]{2,1,0:T(8,128)(2,1)} custom-call(bf16[96,96,128]{2,1,0:T(8,128)(2,1)S(1)} %get-tuple-element.29.y_ref, s32[96,128]{1,0:T(8,128)S(1)} %copy-done.2, bf16[96,8]{1,0:T(8,128)(2,1)S(1)} %bitcast.13, bf16[2,12,8,128]{3,2,1,0:T(8,128)(2,1)S(1)} %surface_pair.1.refs_0_, bf16[2,12,8,128]{3,2,1,0:T(8,128)(2,1)S(1)} %collective-permute-done.11.refs_1_, ...), custom_call_target="tpu_custom_call" | custom-call | tf_op jit(solution)/shard_map/couple/pallas_call | solution.py:617
  (13 shorter events, 0.0 us)
Async XLA Ops:
  0.6 8.0 %copy-start = (bf16[1,96,96,128]{3,2,1,0:T(8,128)(2,1)S(1)}, bf16[1,96,96,128]{3,2,1,0:T(8,128)(2,1)}, u32[]{:S(2)}) copy-start(bf16[1,96,96,128]{3,2,1,0:T(8,128)(2,1)} %param.18) | copy-start | bytes 7077892
  0.6 8.0 %copy-start.10 = (f32[2,7,7,96]{3,0,2,1:T(2,128)S(1)}, f32[2,7,7,96]{3,0,2,1:T(2,128)}, u32[]{:S(2)}) copy-start(f32[2,7,7,96]{3,0,2,1:T(2,128)} %param.22) | copy-start | bytes 112900
  3.4 11.6 %collective-permute-start = (bf16[6,96,128]{2,1,0:T(8,128)(2,1)}, bf16[6,96,128]{2,1,0:T(8,128)(2,1)S(1)}, u32[]{:S(2)}, u32[]{:S(2)}) collective-permute-start(bf16[6,96,128]{2,1,0:T(8,128)(2,1)} %pack_edges.1), channel_id=1, source_target_pairs={{0,1},{1,2},{2,3},{3,0},{4,5},{5,6},{6,7},{7,4},{8,9},{9,10},{10,1... | collective-permute-start | bytes 442376 | tf_op jit(solution)/shard_map/ppermute | solution.py:94
  6.5 8.7 %collective-permute-start.1 = (bf16[6,96,128]{2,1,0:T(8,128)(2,1)}, bf16[6,96,128]{2,1,0:T(8,128)(2,1)S(1)}, u32[]{:S(2)}, u32[]{:S(2)}) collective-permute-start(bf16[6,96,128]{2,1,0:T(8,128)(2,1)} %pack_edges.1), channel_id=1, source_target_pairs={{1,0},{2,1},{3,2},{0,3},{5,4},{6,5},{7,6},{4,7},{9,8},{10,9},{11,1... | collective-permute-start | bytes 442376 | tf_op jit(solution)/shard_map/ppermute | solution.py:95
  8.6 6.6 %copy-start.7 = (bf16[2,96,384]{2,1,0:T(8,128)(2,1)S(1)}, bf16[2,96,384]{2,1,0:T(8,128)(2,1)}, u32[]{:S(2)}) copy-start(bf16[2,96,384]{2,1,0:T(8,128)(2,1)} %refs_6_.4) | copy-start | bytes 442372
  8.6 6.6 %copy-start.8 = (bf16[2,384,96]{1,2,0:T(8,128)(2,1)S(1)}, bf16[2,384,96]{1,2,0:T(8,128)(2,1)}, u32[]{:S(2)}) copy-start(bf16[2,384,96]{1,2,0:T(8,128)(2,1)} %param.25) | copy-start | bytes 442372
  8.6 6.6 %copy-start.13 = (f32[2,96]{1,0:T(2,128)S(1)}, f32[2,96]{1,0:T(2,128)}, u32[]{:S(2)}) copy-start(f32[2,96]{1,0:T(2,128)} %refs_5_.4) | copy-start | bytes 2308
  8.6 6.6 %copy-start.14 = (f32[2,96]{1,0:T(2,128)S(1)}, f32[2,96]{1,0:T(2,128)}, u32[]{:S(2)}) copy-start(f32[2,96]{1,0:T(2,128)} %refs_8_.4) | copy-start | bytes 2308
  22.8 10.4 %collective-permute-start.2 = (bf16[6,96,128]{2,1,0:T(8,128)(2,1)S(1)}, bf16[6,96,128]{2,1,0:T(8,128)(2,1)S(1)}, u32[]{:S(2)}, u32[]{:S(2)}) collective-permute-start(bf16[6,96,128]{2,1,0:T(8,128)(2,1)S(1)} %get-tuple-element.27), channel_id=1, source_target_pairs={{0,1},{1,2},{2,3},{3,0},{4,5},{5,6},{6,7},{7,4},{8,9},{9,10},{10,1... | collective-permute-start | bytes 442376 | tf_op jit(solution)/shard_map/ppermute | solution.py:94
  24.0 9.3 %collective-permute-start.3 = (bf16[6,96,128]{2,1,0:T(8,128)(2,1)S(1)}, bf16[6,96,128]{2,1,0:T(8,128)(2,1)S(1)}, u32[]{:S(2)}, u32[]{:S(2)}) collective-permute-start(bf16[6,96,128]{2,1,0:T(8,128)(2,1)S(1)} %get-tuple-element.27), channel_id=1, source_target_pairs={{1,0},{2,1},{3,2},{0,3},{5,4},{6,5},{7,6},{4,7},{9,8},{10,9},{11,1... | collective-permute-start | bytes 442376 | tf_op jit(solution)/shard_map/ppermute | solution.py:95
  26.7 6.6 %copy-start.12 = (bf16[96,32]{0,1:T(8,128)(2,1)S(1)}, bf16[96,32]{0,1:T(8,128)(2,1)}, u32[]{:S(2)}) copy-start(bf16[96,32]{0,1:T(8,128)(2,1)} %param.27) | copy-start | bytes 18436
  33.3 14.2 %copy-start.9 = (bf16[96,384]{1,0:T(8,128)(2,1)S(1)}, bf16[96,384]{1,0:T(8,128)(2,1)}, u32[]{:S(2)}) copy-start(bf16[96,384]{1,0:T(8,128)(2,1)} %up_ref.1) | copy-start | bytes 221188
  33.3 14.2 %copy-start.11 = (f32[7,7,96]{2,1,0:T(8,128)S(1)}, f32[7,7,96]{2,1,0:T(8,128)}, u32[]{:S(2)}) copy-start(f32[7,7,96]{2,1,0:T(8,128)} %k_ref.1) | copy-start | bytes 56452
  33.3 14.2 %copy-start.15 = (f32[96]{0:T(128)S(1)}, f32[96]{0:T(128)}, u32[]{:S(2)}) copy-start(f32[96]{0:T(128)} %param.30) | copy-start | bytes 1156
  33.4 14.2 %copy-start.16 = (f32[96]{0:T(128)S(1)}, f32[96]{0:T(128)}, u32[]{:S(2)}) copy-start(f32[96]{0:T(128)} %param.33) | copy-start | bytes 1156
  41.8 2.1 %collective-permute-start.4 = (bf16[4,18,32,128]{3,2,1,0:T(8,128)(2,1)S(1)}, bf16[4,18,32,128]{3,2,1,0:T(8,128)(2,1)S(1)}, u32[]{:S(2)}, u32[]{:S(2)}) collective-permute-start(bf16[4,18,32,128]{3,2,1,0:T(8,128)(2,1)S(1)} %get-tuple-element.31), channel_id=1, source_target_pairs={{0,4},{4,0},{8,12},{12,8},{16,20},{20,16},{24,28},{28,24},{1,5},{5... | collective-permute-start | bytes 1769480 | tf_op jit(solution)/shard_map/ppermute | solution.py:471
  44.0 7.5 %collective-permute-start.5 = (bf16[18,32,128]{2,1,0:T(8,128)(2,1)S(1)}, bf16[18,32,128]{2,1,0:T(8,128)(2,1)S(1)}, u32[]{:S(2)}, u32[]{:S(2)}) collective-permute-start(bf16[18,32,128]{2,1,0:T(8,128)(2,1)S(1)} %get-tuple-element.32), channel_id=1, source_target_pairs={{0,24},{4,28},{8,16},{12,20},{16,8},{20,12},{24,0},{28,4},{1,25},{... | collective-permute-start | bytes 442376 | tf_op jit(solution)/shard_map/ppermute | solution.py:471
  46.6 7.5 %collective-permute-start.6 = (bf16[18,32,128]{2,1,0:T(8,128)(2,1)S(1)}, bf16[18,32,128]{2,1,0:T(8,128)(2,1)S(1)}, u32[]{:S(2)}, u32[]{:S(2)}) collective-permute-start(bf16[18,32,128]{2,1,0:T(8,128)(2,1)S(1)} %get-tuple-element.33), channel_id=1, source_target_pairs={{0,16},{4,20},{8,24},{12,28},{16,0},{20,4},{24,8},{28,12},{1,17},{... | collective-permute-start | bytes 442376 | tf_op jit(solution)/shard_map/ppermute | solution.py:471
  47.0 7.1 %collective-permute-start.7 = (bf16[18,32,128]{2,1,0:T(8,128)(2,1)S(1)}, bf16[18,32,128]{2,1,0:T(8,128)(2,1)S(1)}, u32[]{:S(2)}, u32[]{:S(2)}) collective-permute-start(bf16[18,32,128]{2,1,0:T(8,128)(2,1)S(1)} %get-tuple-element.34._), channel_id=1, source_target_pairs={{0,8},{4,12},{8,0},{12,4},{16,24},{20,28},{24,16},{28,20},{1,9},{5... | collective-permute-start | bytes 442376 | tf_op jit(solution)/shard_map/ppermute | solution.py:471
  47.6 6.6 %copy-start.1 = (bf16[96,96,128]{2,1,0:T(8,128)(2,1)S(1)}, bf16[96,96,128]{2,1,0:T(8,128)(2,1)}, u32[]{:S(2)}) copy-start(bf16[96,96,128]{2,1,0:T(8,128)(2,1)} %refs_5_.5) | copy-start | bytes 7077892
  47.6 6.6 %copy-start.2 = (s32[96,128]{1,0:T(8,128)S(1)}, s32[96,128]{1,0:T(8,128)}, u32[]{:S(2)}) copy-start(s32[96,128]{1,0:T(8,128)} %land_ref.3) | copy-start | bytes 147460
  47.6 6.5 %copy-start.4 = (s32[96,128]{1,0:T(8,128)S(1)}, s32[96,128]{1,0:T(8,128)}, u32[]{:S(2)}) copy-start(s32[96,128]{1,0:T(8,128)} %refs_7_.1) | copy-start | bytes 147460
  47.6 6.5 %copy-start.5 = (bf16[2,32,96]{2,1,0:T(8,128)(2,1)S(1)}, bf16[2,32,96]{2,1,0:T(8,128)(2,1)}, u32[]{:S(2)}) copy-start(bf16[2,32,96]{2,1,0:T(8,128)(2,1)} %refs_8_.5) | copy-start | bytes 36868
  55.2 6.2 %collective-permute-start.8 = (bf16[2,96,128]{2,1,0:T(8,128)(2,1)S(1)}, bf16[2,96,128]{2,1,0:T(8,128)(2,1)S(1)}, u32[]{:S(2)}, u32[]{:S(2)}) collective-permute-start(bf16[2,96,128]{2,1,0:T(8,128)(2,1)S(1)} %get-tuple-element.37), channel_id=1, source_target_pairs={{0,1},{1,2},{2,3},{3,0},{4,5},{5,6},{6,7},{7,4},{8,9},{9,10},{10,1... | collective-permute-start | bytes 147464 | tf_op jit(solution)/shard_map/ppermute | solution.py:94
  55.5 5.9 %collective-permute-start.9 = (bf16[2,96,128]{2,1,0:T(8,128)(2,1)S(1)}, bf16[2,96,128]{2,1,0:T(8,128)(2,1)S(1)}, u32[]{:S(2)}, u32[]{:S(2)}) collective-permute-start(bf16[2,96,128]{2,1,0:T(8,128)(2,1)S(1)} %get-tuple-element.37), channel_id=1, source_target_pairs={{1,0},{2,1},{3,2},{0,3},{5,4},{6,5},{7,6},{4,7},{9,8},{10,9},{11,1... | collective-permute-start | bytes 147464 | tf_op jit(solution)/shard_map/ppermute | solution.py:95
  59.3 2.1 %copy-start.3 = (bf16[384,96]{0,1:T(8,128)(2,1)S(1)}, bf16[384,96]{0,1:T(8,128)(2,1)}, u32[]{:S(2)}) copy-start(bf16[384,96]{0,1:T(8,128)(2,1)} %param.32) | copy-start | bytes 221188
  59.3 2.1 %copy-start.6 = (bf16[96,8]{0,1:T(8,128)(2,1)S(1)}, bf16[96,8]{0,1:T(8,128)(2,1)}, u32[]{:S(2)}) copy-start(bf16[96,8]{0,1:T(8,128)(2,1)} %param.34) | copy-start | bytes 4612
  61.4 7.4 %copy-start.17 = (bf16[8,96]{1,0:T(8,128)(2,1)S(1)}, bf16[8,96]{1,0:T(8,128)(2,1)}, u32[]{:S(2)}) copy-start(bf16[8,96]{1,0:T(8,128)(2,1)} %param.35) | copy-start | bytes 4612
  64.1 1.2 %collective-permute-start.10 = (bf16[12,8,128]{2,1,0:T(8,128)(2,1)S(1)}, bf16[12,8,128]{2,1,0:T(8,128)(2,1)S(1)}, u32[]{:S(2)}, u32[]{:S(2)}) collective-permute-start(bf16[12,8,128]{2,1,0:T(8,128)(2,1)S(1)} %get-tuple-element.42.own_ref), channel_id=1, source_target_pairs={{0,4},{4,0},{8,12},{12,8},{16,20},{20,16},{24,28},{28,24},{1,5},{5... | collective-permute-start | bytes 73736 | tf_op jit(solution)/shard_map/ppermute | solution.py:471
  65.3 4.1 %collective-permute-start.11 = (bf16[2,12,8,128]{3,2,1,0:T(8,128)(2,1)S(1)}, bf16[2,12,8,128]{3,2,1,0:T(8,128)(2,1)S(1)}, u32[]{:S(2)}, u32[]{:S(2)}) collective-permute-start(bf16[2,12,8,128]{3,2,1,0:T(8,128)(2,1)S(1)} %surface_pair.1.refs_0_), channel_id=1, source_target_pairs={{0,8},{4,12},{8,0},{12,4},{16,24},{20,28},{24,16},{28,20},{1,9},{5... | collective-permute-start | bytes 147464 | tf_op jit(solution)/shard_map/ppermute | solution.py:471
  66.8 4.6 %collective-permute-start.12 = (bf16[2,12,8,128]{3,2,1,0:T(8,128)(2,1)S(1)}, bf16[2,12,8,128]{3,2,1,0:T(8,128)(2,1)S(1)}, u32[]{:S(2)}, u32[]{:S(2)}) collective-permute-start(bf16[2,12,8,128]{3,2,1,0:T(8,128)(2,1)S(1)} %surface_pair.1.refs_0_), channel_id=1, source_target_pairs={{0,16},{4,20},{8,24},{12,28},{16,0},{20,4},{24,8},{28,12},{1,17},{... | collective-permute-start | bytes 147464 | tf_op jit(solution)/shard_map/ppermute | solution.py:471
  67.5 5.0 %collective-permute-start.13 = (bf16[2,12,8,128]{3,2,1,0:T(8,128)(2,1)S(1)}, bf16[2,12,8,128]{3,2,1,0:T(8,128)(2,1)S(1)}, u32[]{:S(2)}, u32[]{:S(2)}) collective-permute-start(bf16[2,12,8,128]{3,2,1,0:T(8,128)(2,1)S(1)} %surface_pair.1.refs_0_), channel_id=1, source_target_pairs={{0,24},{4,28},{8,16},{12,20},{16,8},{20,12},{24,0},{28,4},{1,25},{... | collective-permute-start | bytes 147464 | tf_op jit(solution)/shard_map/ppermute | solution.py:471

commit v8 on v7

--- a/solution.py
+++ b/solution.py
@@ -91,9 +91,16 @@
 
 def neighbours(packed):
     count = lax.axis_size("lon")
-    left = lax.ppermute(packed, "lon", [(i, (i + 1) % count) for i in range(count)])
-    right = lax.ppermute(packed, "lon", [((i + 1) % count, i) for i in range(count)])
-    return left, right
+    first = lax.ppermute(packed, "lon", [(i, i ^ 1) for i in range(count)])
+    second = lax.ppermute(
+        packed, "lon", [(i, (i - 1) % count if i % 2 == 0 else (i + 1) % count) for i in range(count)]
+    )
+    return first, second
+
+
+def by_side(first, second):
+    even = lax.axis_index("lon") % 2 == 0
+    return jnp.where(even, second, first), jnp.where(even, first, second)
 
 
 def fill_base(taps, base):
@@ -293,10 +300,13 @@
     )
 
 
-def halo_conv(left, right, band, wrapped, matrix, xe, halo):
+def halo_conv(first, second, band, wrapped, matrix, xe, halo):
     blocks, chans, lanes = halo.shape
     wide = TAPS * DEPTH
-    both = [jnp.concatenate([right[q], left[q]], axis=1) for q in range(blocks)]
+    both = []
+    for q in range(blocks):
+        left, right = by_side(first[q], second[q])
+        both.append(jnp.concatenate([right, left], axis=1))
     lane = lax.broadcasted_iota(jnp.int32, (chans, lanes), 1)
     slot = (lane + HALO) // SLOT % SLOTS
 
@@ -588,41 +598,48 @@
     )(own, got)
 
 
-def couple_kernel(y_ref, land_ref, bw_ref, *refs):
-    pair_refs, o_ref = refs[:-1], refs[-1]
+def couple_kernel(k, y_ref, land_ref, bw_ref, pair_ref, *refs):
+    o_ref, buf, sems = refs[-3:]
     chans, lanes = y_ref.shape[1:]
-    share = pair_refs[0].shape[1]
+    share = pair_ref.shape[1]
     rank = lax.axis_index("member")
-    pair = pl.program_id(0)
     parity = rank % 2
-    mine = pair ^ (rank // 2)
-    surf = [None] * (2 * share)
+    first = ((rank // 2) ^ k) * 2 * share
+    surf = [pair_ref[side ^ parity, r] for side in range(2) for r in range(share)]
+    back = jnp.dot(bw_ref[...], jnp.concatenate(surf, axis=1), preferred_element_type=F32)
+    copies = []
     for side in range(2):
-        for r in range(share):
-            value = pair_refs[0][side ^ parity, r]
-            for k, ref in enumerate(pair_refs[1:]):
-                value = jnp.where(mine == k + 1, ref[side ^ parity, r], value)
-            surf[side * share + r] = value
-    back = jnp.dot(bw_ref[...], jnp.concatenate(surf, axis=1), preferred_element_type=F32)
-    first = pair * 2 * share
-    for r in range(2 * share):
-        sea = (1 - land_ref[pl.ds(first + r, 1), :]).astype(F32)
-        out = y_ref[first + r].astype(F32) + sea * back[:, r * lanes : (r + 1) * lanes]
-        o_ref[r] = out.astype(BF)
-
-
-def couple(y, land, back_weight, pairs):
-    rows, chans, lanes = y.shape
-    count = 2 * pairs[0].shape[1]
-    return pl.pallas_call(
-        couple_kernel,
-        grid=(rows // count,),
+        for r in range(side * share, (side + 1) * share):
+            sea = (1 - land_ref[pl.ds(first + r, 1), :]).astype(F32)
+            out = y_ref[first + r].astype(F32) + sea * back[:, r * lanes : (r + 1) * lanes]
+            buf[r] = out.astype(BF)
+        copies.append(
+            pltpu.make_async_copy(
+                buf.at[pl.ds(side * share, share)],
+                o_ref.at[pl.ds(first + side * share, share)],
+                sems.at[side],
+            )
+        )
+        copies[side].start()
+    for copy in copies:
+        copy.wait()
+
+
+def couple(k, y, land, back_weight, pair, earlier):
+    _, chans, lanes = y.shape
+    return pl.pallas_call(
+        functools.partial(couple_kernel, k),
         out_shape=jax.ShapeDtypeStruct(y.shape, BF),
-        in_specs=[VMEM] * (3 + len(pairs)),
-        out_specs=pl.BlockSpec((count, chans, lanes), lambda i: (i, 0, 0)),
+        in_specs=[VMEM] * 4 + [HBM] * len(earlier),
+        out_specs=HBM,
+        scratch_shapes=[
+            pltpu.VMEM((2 * pair.shape[1], chans, lanes), BF),
+            pltpu.SemaphoreType.DMA((2,)),
+        ],
+        input_output_aliases={4: 0} if earlier else {},
         compiler_params=params(24),
         name="couple",
-    )(y, land, back_weight, *pairs)
+    )(y, land, back_weight, pair, *earlier)
 
 
 def local(
@@ -677,7 +694,10 @@
     )
     own = make_pair(surface, send_xor(surface, 1))
     pairs = [own] + [send_xor(own, 2 * k) for k in range(1, half)]
-    out = couple(state, land_mask, back_weight.T, pairs)
+    out = []
+    for k, pair in enumerate(pairs):
+        out = [couple(k, state, land_mask, back_weight.T, pair, out)]
+    out = out[0]
     return (out[None], ocean_rows)
 
 

time: 75.2 us -> 74.2 us (0.987)
  starting transfers between devices: 20.2 us -> 17.9 us
  Pallas kernels: 40.8 us -> 42.5 us
    ppermute x8, waiting for transfers between devices: 12.1 us -> 8.94 us  [send_xor(): lax.ppermute(value, 'member', [(i, i ^ bits) for i in range(members)])]
    ppermute x6, waiting for transfers between devices: 0.84 us -> 3.44 us  [the longest x3 2.59 us: neighbours(): lax.ppermute(packed, 'lon', [(i, (i - 1) % count if i % 2 == 0 else (i +...]
    ppermute x6, starting transfers between devices: 13.1 us -> 10.8 us  [the longest x3 6.93 us: neighbours(): lax.ppermute(packed, 'lon', [(i, (i - 1) % count if i % 2 == 0 else (i +...]
    pallas_call x1 -> x4, Pallas kernels: 2.55 us -> 4.16 us  [couple(): pl.pallas_call(functools.partial(couple_kernel, k), out_shape=jax.ShapeDt...]
  transfers between devices with their start and end apart: 14 -> 14, of which waited for: 10 -> 10; matrix products, arithmetic and copies ran while one was open for 0% -> 0% of each run, Pallas kernels for 21% -> 25%
where the time goes in v8:
time: 74.2 us; the launch traced here: 74.1 us
  Pallas kernels  42.5 us (57%)
  starting transfers between devices  17.9 us (24%)
  waiting for transfers between devices  12.4 us (17%)
  between operations  1.1 us (1%)
    pallas_call x2, Pallas kernels, atmos_block(): pl.pallas_call(functools.partial(atmos_kernel, layer, members, count), ou...  16.1 us
    pallas_call x2, Pallas kernels, convolve(): pl.pallas_call(functools.partial(conv_kernel, layer), out_shape=[jax.Shap...  12.9 us
    ppermute x8, waiting for transfers between devices, send_xor(): lax.ppermute(value, 'member', [(i, i ^ bits) for i in range(members)])  8.94 us
    ppermute x8, starting transfers between devices, send_xor(): lax.ppermute(value, 'member', [(i, i ^ bits) for i in range(members)])  7.12 us
    ppermute x3, starting transfers between devices, neighbours(): lax.ppermute(packed, 'lon', [(i, (i - 1) % count if i % 2 == 0 else (i +...  6.93 us
    pallas_call x4, Pallas kernels, couple(): pl.pallas_call(functools.partial(couple_kernel, k), out_shape=jax.ShapeDt...  4.16 us
    ppermute x3, starting transfers between devices, neighbours(): first = lax.ppermute(packed, 'lon', [(i, i ^ 1) for i in range(count)])  3.83 us
    pallas_call x1, Pallas kernels, pack(): pl.pallas_call(functools.partial(pack_kernel, step), out_shape=jax.ShapeD...  2.77 us
  transfers between devices with their start and end apart: 14, of which 10 were waited for; matrix products, arithmetic and copies ran while one was open for 0% of the time, Pallas kernels for 25%

profile of v8, /device:TPU:0, one launch (start us, length us, event | category | flops | bytes accessed | tf_op | source)
XLA Modules:
  0.0 74.1 jit_solution(10798942490936099631)
XLA Ops:
  0.6 0.0 copy-start
  0.6 0.0 copy-start.10
  0.6 2.8 %pack_edges.1 = bf16[6,96,128]{2,1,0:T(8,128)(2,1)} custom-call(bf16[96,96,128]{2,1,0:T(8,128)(2,1)} %bitcast.10), custom_call_target="tpu_custom_call" | custom-call | tf_op jit(solution)/shard_map/pack_edges/pallas_call | solution.py:81
  3.4 3.1 %collective-permute-start = (bf16[6,96,128]{2,1,0:T(8,128)(2,1)}, bf16[6,96,128]{2,1,0:T(8,128)(2,1)S(1)}, u32[]{:S(2)}, u32[]{:S(2)}) collective-permute-start(bf16[6,96,128]{2,1,0:T(8,128)(2,1)} %pack_edges.1), channel_id=1, source_target_pairs={{0,1},{1,0},{2,3},{3,2},{4,5},{5,4},{6,7},{7,6},{8,9},{9,8},{10,11... | collective-permute-start | bytes 442376 | tf_op jit(solution)/shard_map/ppermute | solution.py:94
  6.5 2.5 %collective-permute-start.1 = (bf16[6,96,128]{2,1,0:T(8,128)(2,1)}, bf16[6,96,128]{2,1,0:T(8,128)(2,1)S(1)}, u32[]{:S(2)}, u32[]{:S(2)}) collective-permute-start(bf16[6,96,128]{2,1,0:T(8,128)(2,1)} %pack_edges.1), channel_id=1, source_target_pairs={{0,3},{1,2},{2,1},{3,0},{4,7},{5,6},{6,5},{7,4},{8,11},{9,10},{10,... | collective-permute-start | bytes 442376 | tf_op jit(solution)/shard_map/ppermute | solution.py:95
  9.0 0.0 copy-done
  9.0 0.0 copy-done.10
  9.0 0.0 copy-start.13
  9.0 0.0 copy-start.14
  9.0 6.4 %conv.2 = (f32[96,96,128]{2,1,0:T(8,128)S(1)}, bf16[6,96,1792]{2,1,0:T(8,128)(2,1)S(1)}) custom-call(bf16[96,96,128]{2,1,0:T(8,128)(2,1)S(1)} %bitcast.11, f32[7,7,2,96]{3,2,1,0:T(2,128)S(1)} %bitcast.21), custom_call_target="tpu_custom_call" | custom-call | flops 8000000000 | tf_op jit(solution)/shard_map/conv/pallas_call | solution.py:203
  15.4 0.0 collective-permute-done.refs_2_
  15.4 0.6 collective-permute-done.1.refs_3_
  16.0 0.0 copy-done.7
  16.0 0.0 copy-done.8
  16.0 0.0 copy-done.13
  16.0 0.0 copy-done.14
  16.1 7.6 %atmos_block.2 = (bf16[96,96,128]{2,1,0:T(8,128)(2,1)S(1)}, bf16[6,96,128]{2,1,0:T(8,128)(2,1)S(1)}) custom-call(bf16[96,96,128]{2,1,0:T(8,128)(2,1)S(1)} %bitcast.12, f32[96,96,128]{2,1,0:T(8,128)S(1)} %get-tuple-element.23.refs_1_, bf16[6,96,128]{2,1,0:T(8,128)(2,1)S(1)} %collective-permute-done.refs_2_, ...), custom_call_target="tpu_custom_call" | custom-call | flops 8000000000 | tf_op jit(solution)/shard_map/atmos_block/pallas_call | solution.py:443
  23.7 0.7 collective-permute-start.2
  24.4 2.6 %collective-permute-start.3 = (bf16[6,96,128]{2,1,0:T(8,128)(2,1)S(1)}, bf16[6,96,128]{2,1,0:T(8,128)(2,1)S(1)}, u32[]{:S(2)}, u32[]{:S(2)}) collective-permute-start(bf16[6,96,128]{2,1,0:T(8,128)(2,1)S(1)} %get-tuple-element.27), channel_id=1, source_target_pairs={{0,3},{1,2},{2,1},{3,0},{4,7},{5,6},{6,5},{7,4},{8,11},{9,10},{10,... | collective-permute-start | bytes 442376 | tf_op jit(solution)/shard_map/ppermute | solution.py:95
  27.0 6.6 %conv.3 = (f32[96,96,128]{2,1,0:T(8,128)S(1)}, bf16[6,96,1792]{2,1,0:T(8,128)(2,1)S(1)}) custom-call(bf16[96,96,128]{2,1,0:T(8,128)(2,1)S(1)} %get-tuple-element.25.x_ref.refs_0_, f32[7,7,2,96]{3,2,1,0:T(2,128)S(1)} %bitcast.22), custom_call_target="tpu_custom_call" | custom-call | flops 8000000000 | tf_op jit(solution)/shard_map/conv/pallas_call | solution.py:203
  33.5 0.0 collective-permute-done.2.refs_2_
  33.5 0.0 collective-permute-done.3.refs_3_
  33.6 0.0 copy-done.12
  33.6 0.0 copy-start.9
  33.6 0.0 copy-start.11
  33.6 0.0 copy-start.15
  33.6 0.0 copy-start.16
  33.6 8.5 %atmos_block.3 = (bf16[96,96,128]{2,1,0:T(8,128)(2,1)S(1)}, bf16[4,18,32,128]{3,2,1,0:T(8,128)(2,1)S(1)}, bf16[4,18,32,128]{3,2,1,0:T(8,128)(2,1)S(1)}) custom-call(bf16[96,96,128]{2,1,0:T(8,128)(2,1)S(1)} %get-tuple-element.25.x_ref.refs_0_, f32[96,96,128]{2,1,0:T(8,128)S(1)} %get-tuple-element.26.refs_1_, ...), custom_call_target="tpu_custom_call" | custom-call | flops 8000000000 | tf_op jit(solution)/shard_map/atmos_block/pallas_call | solution.py:443
  42.1 0.1 collective-permute-start.4
  42.2 2.0 %collective-permute-done.4.got_ref.refs_1_ = bf16[4,18,32,128]{3,2,1,0:T(8,128)(2,1)S(1)} collective-permute-done((bf16[4,18,32,128]{3,2,1,0:T(8,128)(2,1)S(1)}, bf16[4,18,32,128]{3,2,1,0:T(8,128)(2,1)S(1)}, u32[]{:S(2)}, u32[]{:S(2)}) %collective-permute-start.4) | collective-permute-done | bytes 589856 | tf_op jit(solution)/shard_map/ppermute | solution.py:481
  44.1 0.1 add_pairs.1
  44.3 2.5 %collective-permute-start.5 = (bf16[18,32,128]{2,1,0:T(8,128)(2,1)S(1)}, bf16[18,32,128]{2,1,0:T(8,128)(2,1)S(1)}, u32[]{:S(2)}, u32[]{:S(2)}) collective-permute-start(bf16[18,32,128]{2,1,0:T(8,128)(2,1)S(1)} %get-tuple-element.32), channel_id=1, source_target_pairs={{0,24},{4,28},{8,16},{12,20},{16,8},{20,12},{24,0},{28,4},{1,25},{... | collective-permute-start | bytes 442376 | tf_op jit(solution)/shard_map/ppermute | solution.py:481
  46.8 0.5 collective-permute-start.6
  47.3 0.5 collective-permute-start.7
  47.8 0.0 copy-start.1
  47.8 0.0 copy-start.2
  47.8 0.0 copy-start.4
  47.9 0.0 copy-start.5
  47.9 1.2 %prepare_ocean.1 = (bf16[6,160,1792]{2,1,0:T(8,128)(2,1)S(1)}, bf16[256,768]{1,0:T(8,128)(2,1)S(1)}, bf16[384,96]{1,0:T(8,128)(2,1)S(1)}, f32[96,128]{1,0:T(8,128)S(1)}, f32[96,128]{1,0:T(8,128)S(1)}) custom-call(f32[7,7,96]{2,1,0:T(8,128)S(1)} %copy-done.11, f32[1,96]{1,0:T(1,128)S(1)} %bitcast.24, bf16[96,384]{1,0:T(8,128)(2,1)S(1)} %copy-done.9, ...), custom_call_target="tpu_custom_call" | custom-call | flops 3000000000 | tf_op jit(solution)/shard_map/prepare_ocean/pallas_call | solution.py:238
  49.1 2.7 %collective-permute-done.5.refs_2_ = bf16[18,32,128]{2,1,0:T(8,128)(2,1)S(1)} collective-permute-done((bf16[18,32,128]{2,1,0:T(8,128)(2,1)S(1)}, bf16[18,32,128]{2,1,0:T(8,128)(2,1)S(1)}, u32[]{:S(2)}, u32[]{:S(2)}) %collective-permute-start.5) | collective-permute-done | bytes 147488 | tf_op jit(solution)/shard_map/ppermute | solution.py:481
  51.7 2.5 %collective-permute-done.6.refs_3_ = bf16[18,32,128]{2,1,0:T(8,128)(2,1)S(1)} collective-permute-done((bf16[18,32,128]{2,1,0:T(8,128)(2,1)S(1)}, bf16[18,32,128]{2,1,0:T(8,128)(2,1)S(1)}, u32[]{:S(2)}, u32[]{:S(2)}) %collective-permute-start.6) | collective-permute-done | bytes 147488 | tf_op jit(solution)/shard_map/ppermute | solution.py:481
  54.3 0.1 collective-permute-done.7.refs_4_
  54.4 0.0 copy-done.5
  54.4 1.3 %ocean_forcing.1 = (bf16[18,96,128]{2,1,0:T(8,128)(2,1)S(1)}, bf16[2,96,128]{2,1,0:T(8,128)(2,1)S(1)}) custom-call(bf16[4,18,32,128]{3,2,1,0:T(8,128)(2,1)S(1)} %get-tuple-element.30.keep_ref.refs_0_, bf16[4,18,32,128]{3,2,1,0:T(8,128)(2,1)S(1)} %collective-permute-done.4.got_ref.refs_1_, bf16[18,32,128]{2,1,0:T(8,128)(2,1)S(1)} %collective-permute-done.5.refs_2_, ...), custom_call_target="tpu_custom_call" | custom-call | tf_op jit(solution)/shard_map/ocean_forcing/pallas_call | solution.py:530
  55.7 0.1 collective-permute-start.8
  55.7 1.8 %collective-permute-start.9 = (bf16[2,96,128]{2,1,0:T(8,128)(2,1)S(1)}, bf16[2,96,128]{2,1,0:T(8,128)(2,1)S(1)}, u32[]{:S(2)}, u32[]{:S(2)}) collective-permute-start(bf16[2,96,128]{2,1,0:T(8,128)(2,1)S(1)} %get-tuple-element.37), channel_id=1, source_target_pairs={{0,3},{1,2},{2,1},{3,0},{4,7},{5,6},{6,5},{7,4},{8,11},{9,10},{10,... | collective-permute-start | bytes 147464 | tf_op jit(solution)/shard_map/ppermute | solution.py:95
  57.6 1.4 %ocean_conv.1.a_ref = f32[12,96,128]{2,1,0:T(8,128)S(1)} custom-call(bf16[18,96,128]{2,1,0:T(8,128)(2,1)S(1)} %get-tuple-element.35.x_ref.mid_ref, bf16[6,160,1792]{2,1,0:T(8,128)(2,1)S(1)} %get-tuple-element.36.band_ref), custom_call_target="tpu_custom_call" | custom-call | flops 2000000000 | tf_op jit(solution)/shard_map/ocean_conv/pallas_call | solution.py:267
  59.0 0.8 %collective-permute-done.8.left_ref = bf16[2,96,128]{2,1,0:T(8,128)(2,1)S(1)} collective-permute-done((bf16[2,96,128]{2,1,0:T(8,128)(2,1)S(1)}, bf16[2,96,128]{2,1,0:T(8,128)(2,1)S(1)}, u32[]{:S(2)}, u32[]{:S(2)}) %collective-permute-start.8) | collective-permute-done | bytes 49184 | tf_op jit(solution)/shard_map/ppermute | solution.py:94
  59.8 2.0 %collective-permute-done.9.right_ref = bf16[2,96,128]{2,1,0:T(8,128)(2,1)S(1)} collective-permute-done((bf16[2,96,128]{2,1,0:T(8,128)(2,1)S(1)}, bf16[2,96,128]{2,1,0:T(8,128)(2,1)S(1)}, u32[]{:S(2)}, u32[]{:S(2)}) %collective-permute-start.9) | collective-permute-done | bytes 49184 | tf_op jit(solution)/shard_map/ppermute | solution.py:95
  61.8 0.0 copy-done.3
  61.8 2.6 %ocean_block.1 = (bf16[12,96,128]{2,1,0:T(8,128)(2,1)}, bf16[12,8,128]{2,1,0:T(8,128)(2,1)S(1)}) custom-call(bf16[18,96,128]{2,1,0:T(8,128)(2,1)S(1)} %get-tuple-element.35.x_ref.mid_ref, f32[12,96,128]{2,1,0:T(8,128)S(1)} %ocean_conv.1.a_ref, bf16[2,96,128]{2,1,0:T(8,128)(2,1)S(1)} %collective-permute-done.8.left_ref, ...), custom_call_target="tpu_custom_call" | custom-call | tf_op jit(solution)/shard_map/ocean_block/pallas_call | solution.py:567
  64.5 0.0 collective-permute-start.10
  64.5 1.2 %collective-permute-done.10.got_ref = bf16[12,8,128]{2,1,0:T(8,128)(2,1)S(1)} collective-permute-done((bf16[12,8,128]{2,1,0:T(8,128)(2,1)S(1)}, bf16[12,8,128]{2,1,0:T(8,128)(2,1)S(1)}, u32[]{:S(2)}, u32[]{:S(2)}) %collective-permute-start.10) | collective-permute-done | bytes 24608 | tf_op jit(solution)/shard_map/ppermute | solution.py:481
  65.7 1.5 %collective-permute-start.13 = (bf16[2,12,8,128]{3,2,1,0:T(8,128)(2,1)S(1)}, bf16[2,12,8,128]{3,2,1,0:T(8,128)(2,1)S(1)}, u32[]{:S(2)}, u32[]{:S(2)}) collective-permute-start(bf16[2,12,8,128]{3,2,1,0:T(8,128)(2,1)S(1)} %surface_pair.1.pair_ref), channel_id=1, source_target_pairs={{0,8},{4,12},{8,0},{12,4},{16,24},{20,28},{24,16},{28,20},{1,9},{5... | collective-permute-start | bytes 147464 | tf_op jit(solution)/shard_map/ppermute | solution.py:481
  67.2 0.7 collective-permute-start.12
  67.9 1.3 %collective-permute-start.11 = (bf16[2,12,8,128]{3,2,1,0:T(8,128)(2,1)S(1)}, bf16[2,12,8,128]{3,2,1,0:T(8,128)(2,1)S(1)}, u32[]{:S(2)}, u32[]{:S(2)}) collective-permute-start(bf16[2,12,8,128]{3,2,1,0:T(8,128)(2,1)S(1)} %surface_pair.1.pair_ref), channel_id=1, source_target_pairs={{0,24},{4,28},{8,16},{12,20},{16,8},{20,12},{24,0},{28,4},{1,25},{... | collective-permute-start | bytes 147464 | tf_op jit(solution)/shard_map/ppermute | solution.py:481
  69.2 0.1 copy.23
  69.3 1.0 %couple.4.refs_0_ = bf16[96,96,128]{2,1,0:T(8,128)(2,1)} custom-call(bf16[96,96,128]{2,1,0:T(8,128)(2,1)S(1)} %get-tuple-element.29.y_ref, s32[96,128]{1,0:T(8,128)S(1)} %copy-done.2, bf16[96,8]{1,0:T(8,128)(2,1)S(1)} %bitcast.13, bf16[2,12,8,128]{3,2,1,0:T(8,128)(2,1)S(1)} %surface_pair.1.pair_ref), custom_call_target="tpu_custom_call" | custom-call | tf_op jit(solution)/shard_map/couple/pallas_call | solution.py:630
  70.3 0.0 collective-permute-done.13.pair_ref
  70.3 1.1 %couple.5.refs_0_ = bf16[96,96,128]{2,1,0:T(8,128)(2,1)} custom-call(bf16[96,96,128]{2,1,0:T(8,128)(2,1)S(1)} %get-tuple-element.29.y_ref, s32[96,128]{1,0:T(8,128)S(1)} %copy-done.2, bf16[96,8]{1,0:T(8,128)(2,1)S(1)} %bitcast.14, bf16[2,12,8,128]{3,2,1,0:T(8,128)(2,1)S(1)} %collective-permute-done.13.pair_ref, ...), custom_call_target="tpu_custom_call", output_to_operand_aliasing={{}: (4, {})} | custom-call | tf_op jit(solution)/shard_map/couple/pallas_call | solution.py:630
  71.4 0.4 collective-permute-done.12.pair_ref
  71.8 1.0 %couple.6.refs_0_ = bf16[96,96,128]{2,1,0:T(8,128)(2,1)} custom-call(bf16[96,96,128]{2,1,0:T(8,128)(2,1)S(1)} %get-tuple-element.29.y_ref, s32[96,128]{1,0:T(8,128)S(1)} %copy-done.2, bf16[96,8]{1,0:T(8,128)(2,1)S(1)} %bitcast.15, bf16[2,12,8,128]{3,2,1,0:T(8,128)(2,1)S(1)} %collective-permute-done.12.pair_ref, ...), custom_call_target="tpu_custom_call", output_to_operand_aliasing={{}: (4, {})} | custom-call | tf_op jit(solution)/shard_map/couple/pallas_call | solution.py:630
  72.8 0.1 collective-permute-done.11.pair_ref
  72.9 1.0 %couple.7 = bf16[96,96,128]{2,1,0:T(8,128)(2,1)} custom-call(bf16[96,96,128]{2,1,0:T(8,128)(2,1)S(1)} %get-tuple-element.29.y_ref, s32[96,128]{1,0:T(8,128)S(1)} %copy-done.2, bf16[96,8]{1,0:T(8,128)(2,1)S(1)} %bitcast.16, bf16[2,12,8,128]{3,2,1,0:T(8,128)(2,1)S(1)} %collective-permute-done.11.pair_ref, ...), custom_call_target="tpu_custom_call", output_to_operand_aliasing={{}: (4, {})} | custom-call | tf_op jit(solution)/shard_map/couple/pallas_call | solution.py:630
  (16 shorter events, 0.0 us)
Async XLA Ops:
  0.6 8.4 %copy-start = (bf16[1,96,96,128]{3,2,1,0:T(8,128)(2,1)S(1)}, bf16[1,96,96,128]{3,2,1,0:T(8,128)(2,1)}, u32[]{:S(2)}) copy-start(bf16[1,96,96,128]{3,2,1,0:T(8,128)(2,1)} %param.18) | copy-start | bytes 7077892
  0.6 8.4 %copy-start.10 = (f32[2,7,7,96]{3,0,2,1:T(2,128)S(1)}, f32[2,7,7,96]{3,0,2,1:T(2,128)}, u32[]{:S(2)}) copy-start(f32[2,7,7,96]{3,0,2,1:T(2,128)} %param.22) | copy-start | bytes 112900
  3.4 12.0 %collective-permute-start = (bf16[6,96,128]{2,1,0:T(8,128)(2,1)}, bf16[6,96,128]{2,1,0:T(8,128)(2,1)S(1)}, u32[]{:S(2)}, u32[]{:S(2)}) collective-permute-start(bf16[6,96,128]{2,1,0:T(8,128)(2,1)} %pack_edges.1), channel_id=1, source_target_pairs={{0,1},{1,0},{2,3},{3,2},{4,5},{5,4},{6,7},{7,6},{8,9},{9,8},{10,11... | collective-permute-start | bytes 442376 | tf_op jit(solution)/shard_map/ppermute | solution.py:94
  6.5 9.5 %collective-permute-start.1 = (bf16[6,96,128]{2,1,0:T(8,128)(2,1)}, bf16[6,96,128]{2,1,0:T(8,128)(2,1)S(1)}, u32[]{:S(2)}, u32[]{:S(2)}) collective-permute-start(bf16[6,96,128]{2,1,0:T(8,128)(2,1)} %pack_edges.1), channel_id=1, source_target_pairs={{0,3},{1,2},{2,1},{3,0},{4,7},{5,6},{6,5},{7,4},{8,11},{9,10},{10,... | collective-permute-start | bytes 442376 | tf_op jit(solution)/shard_map/ppermute | solution.py:95
  9.0 7.0 %copy-start.7 = (bf16[2,96,384]{2,1,0:T(8,128)(2,1)S(1)}, bf16[2,96,384]{2,1,0:T(8,128)(2,1)}, u32[]{:S(2)}) copy-start(bf16[2,96,384]{2,1,0:T(8,128)(2,1)} %refs_6_.4) | copy-start | bytes 442372
  9.0 7.0 %copy-start.8 = (bf16[2,384,96]{1,2,0:T(8,128)(2,1)S(1)}, bf16[2,384,96]{1,2,0:T(8,128)(2,1)}, u32[]{:S(2)}) copy-start(bf16[2,384,96]{1,2,0:T(8,128)(2,1)} %param.25) | copy-start | bytes 442372
  9.0 7.0 %copy-start.13 = (f32[2,96]{1,0:T(2,128)S(1)}, f32[2,96]{1,0:T(2,128)}, u32[]{:S(2)}) copy-start(f32[2,96]{1,0:T(2,128)} %refs_5_.4) | copy-start | bytes 2308
  9.0 7.0 %copy-start.14 = (f32[2,96]{1,0:T(2,128)S(1)}, f32[2,96]{1,0:T(2,128)}, u32[]{:S(2)}) copy-start(f32[2,96]{1,0:T(2,128)} %refs_8_.4) | copy-start | bytes 2308
  23.7 9.9 %collective-permute-start.2 = (bf16[6,96,128]{2,1,0:T(8,128)(2,1)S(1)}, bf16[6,96,128]{2,1,0:T(8,128)(2,1)S(1)}, u32[]{:S(2)}, u32[]{:S(2)}) collective-permute-start(bf16[6,96,128]{2,1,0:T(8,128)(2,1)S(1)} %get-tuple-element.27), channel_id=1, source_target_pairs={{0,1},{1,0},{2,3},{3,2},{4,5},{5,4},{6,7},{7,6},{8,9},{9,8},{10,11... | collective-permute-start | bytes 442376 | tf_op jit(solution)/shard_map/ppermute | solution.py:94
  24.4 9.2 %collective-permute-start.3 = (bf16[6,96,128]{2,1,0:T(8,128)(2,1)S(1)}, bf16[6,96,128]{2,1,0:T(8,128)(2,1)S(1)}, u32[]{:S(2)}, u32[]{:S(2)}) collective-permute-start(bf16[6,96,128]{2,1,0:T(8,128)(2,1)S(1)} %get-tuple-element.27), channel_id=1, source_target_pairs={{0,3},{1,2},{2,1},{3,0},{4,7},{5,6},{6,5},{7,4},{8,11},{9,10},{10,... | collective-permute-start | bytes 442376 | tf_op jit(solution)/shard_map/ppermute | solution.py:95
  27.0 6.6 %copy-start.12 = (bf16[96,32]{0,1:T(8,128)(2,1)S(1)}, bf16[96,32]{0,1:T(8,128)(2,1)}, u32[]{:S(2)}) copy-start(bf16[96,32]{0,1:T(8,128)(2,1)} %param.27) | copy-start | bytes 18436
  33.6 14.2 %copy-start.9 = (bf16[96,384]{1,0:T(8,128)(2,1)S(1)}, bf16[96,384]{1,0:T(8,128)(2,1)}, u32[]{:S(2)}) copy-start(bf16[96,384]{1,0:T(8,128)(2,1)} %up_ref.1) | copy-start | bytes 221188
  33.6 14.2 %copy-start.11 = (f32[7,7,96]{2,1,0:T(8,128)S(1)}, f32[7,7,96]{2,1,0:T(8,128)}, u32[]{:S(2)}) copy-start(f32[7,7,96]{2,1,0:T(8,128)} %k_ref.1) | copy-start | bytes 56452
  33.6 14.2 %copy-start.15 = (f32[96]{0:T(128)S(1)}, f32[96]{0:T(128)}, u32[]{:S(2)}) copy-start(f32[96]{0:T(128)} %param.30) | copy-start | bytes 1156
  33.6 14.2 %copy-start.16 = (f32[96]{0:T(128)S(1)}, f32[96]{0:T(128)}, u32[]{:S(2)}) copy-start(f32[96]{0:T(128)} %param.33) | copy-start | bytes 1156
  42.1 2.1 %collective-permute-start.4 = (bf16[4,18,32,128]{3,2,1,0:T(8,128)(2,1)S(1)}, bf16[4,18,32,128]{3,2,1,0:T(8,128)(2,1)S(1)}, u32[]{:S(2)}, u32[]{:S(2)}) collective-permute-start(bf16[4,18,32,128]{3,2,1,0:T(8,128)(2,1)S(1)} %get-tuple-element.31), channel_id=1, source_target_pairs={{0,4},{4,0},{8,12},{12,8},{16,20},{20,16},{24,28},{28,24},{1,5},{5... | collective-permute-start | bytes 1769480 | tf_op jit(solution)/shard_map/ppermute | solution.py:481
  44.3 7.5 %collective-permute-start.5 = (bf16[18,32,128]{2,1,0:T(8,128)(2,1)S(1)}, bf16[18,32,128]{2,1,0:T(8,128)(2,1)S(1)}, u32[]{:S(2)}, u32[]{:S(2)}) collective-permute-start(bf16[18,32,128]{2,1,0:T(8,128)(2,1)S(1)} %get-tuple-element.32), channel_id=1, source_target_pairs={{0,24},{4,28},{8,16},{12,20},{16,8},{20,12},{24,0},{28,4},{1,25},{... | collective-permute-start | bytes 442376 | tf_op jit(solution)/shard_map/ppermute | solution.py:481
  46.8 7.5 %collective-permute-start.6 = (bf16[18,32,128]{2,1,0:T(8,128)(2,1)S(1)}, bf16[18,32,128]{2,1,0:T(8,128)(2,1)S(1)}, u32[]{:S(2)}, u32[]{:S(2)}) collective-permute-start(bf16[18,32,128]{2,1,0:T(8,128)(2,1)S(1)} %get-tuple-element.33), channel_id=1, source_target_pairs={{0,16},{4,20},{8,24},{12,28},{16,0},{20,4},{24,8},{28,12},{1,17},{... | collective-permute-start | bytes 442376 | tf_op jit(solution)/shard_map/ppermute | solution.py:481
  47.3 7.1 %collective-permute-start.7 = (bf16[18,32,128]{2,1,0:T(8,128)(2,1)S(1)}, bf16[18,32,128]{2,1,0:T(8,128)(2,1)S(1)}, u32[]{:S(2)}, u32[]{:S(2)}) collective-permute-start(bf16[18,32,128]{2,1,0:T(8,128)(2,1)S(1)} %get-tuple-element.34._), channel_id=1, source_target_pairs={{0,8},{4,12},{8,0},{12,4},{16,24},{20,28},{24,16},{28,20},{1,9},{5... | collective-permute-start | bytes 442376 | tf_op jit(solution)/shard_map/ppermute | solution.py:481
  47.8 6.6 %copy-start.1 = (bf16[96,96,128]{2,1,0:T(8,128)(2,1)S(1)}, bf16[96,96,128]{2,1,0:T(8,128)(2,1)}, u32[]{:S(2)}) copy-start(bf16[96,96,128]{2,1,0:T(8,128)(2,1)} %refs_5_.5) | copy-start | bytes 7077892
  47.8 6.5 %copy-start.2 = (s32[96,128]{1,0:T(8,128)S(1)}, s32[96,128]{1,0:T(8,128)}, u32[]{:S(2)}) copy-start(s32[96,128]{1,0:T(8,128)} %land_ref.9) | copy-start | bytes 147460
  47.8 6.5 %copy-start.4 = (s32[96,128]{1,0:T(8,128)S(1)}, s32[96,128]{1,0:T(8,128)}, u32[]{:S(2)}) copy-start(s32[96,128]{1,0:T(8,128)} %refs_7_.1) | copy-start | bytes 147460
  47.9 6.5 %copy-start.5 = (bf16[2,32,96]{2,1,0:T(8,128)(2,1)S(1)}, bf16[2,32,96]{2,1,0:T(8,128)(2,1)}, u32[]{:S(2)}) copy-start(bf16[2,32,96]{2,1,0:T(8,128)(2,1)} %refs_8_.5) | copy-start | bytes 36868
  55.7 4.2 %collective-permute-start.8 = (bf16[2,96,128]{2,1,0:T(8,128)(2,1)S(1)}, bf16[2,96,128]{2,1,0:T(8,128)(2,1)S(1)}, u32[]{:S(2)}, u32[]{:S(2)}) collective-permute-start(bf16[2,96,128]{2,1,0:T(8,128)(2,1)S(1)} %get-tuple-element.37), channel_id=1, source_target_pairs={{0,1},{1,0},{2,3},{3,2},{4,5},{5,4},{6,7},{7,6},{8,9},{9,8},{10,11... | collective-permute-start | bytes 147464 | tf_op jit(solution)/shard_map/ppermute | solution.py:94
  55.7 6.1 %collective-permute-start.9 = (bf16[2,96,128]{2,1,0:T(8,128)(2,1)S(1)}, bf16[2,96,128]{2,1,0:T(8,128)(2,1)S(1)}, u32[]{:S(2)}, u32[]{:S(2)}) collective-permute-start(bf16[2,96,128]{2,1,0:T(8,128)(2,1)S(1)} %get-tuple-element.37), channel_id=1, source_target_pairs={{0,3},{1,2},{2,1},{3,0},{4,7},{5,6},{6,5},{7,4},{8,11},{9,10},{10,... | collective-permute-start | bytes 147464 | tf_op jit(solution)/shard_map/ppermute | solution.py:95
  57.6 4.2 %copy-start.3 = (bf16[384,96]{0,1:T(8,128)(2,1)S(1)}, bf16[384,96]{0,1:T(8,128)(2,1)}, u32[]{:S(2)}) copy-start(bf16[384,96]{0,1:T(8,128)(2,1)} %param.32) | copy-start | bytes 221188
  57.6 4.2 %copy-start.6 = (bf16[96,8]{0,1:T(8,128)(2,1)S(1)}, bf16[96,8]{0,1:T(8,128)(2,1)}, u32[]{:S(2)}) copy-start(bf16[96,8]{0,1:T(8,128)(2,1)} %param.34) | copy-start | bytes 4612
  61.8 7.3 %copy-start.17 = (bf16[8,96]{1,0:T(8,128)(2,1)S(1)}, bf16[8,96]{1,0:T(8,128)(2,1)}, u32[]{:S(2)}) copy-start(bf16[8,96]{1,0:T(8,128)(2,1)} %param.35) | copy-start | bytes 4612
  64.5 1.2 %collective-permute-start.10 = (bf16[12,8,128]{2,1,0:T(8,128)(2,1)S(1)}, bf16[12,8,128]{2,1,0:T(8,128)(2,1)S(1)}, u32[]{:S(2)}, u32[]{:S(2)}) collective-permute-start(bf16[12,8,128]{2,1,0:T(8,128)(2,1)S(1)} %get-tuple-element.42.own_ref), channel_id=1, source_target_pairs={{0,4},{4,0},{8,12},{12,8},{16,20},{20,16},{24,28},{28,24},{1,5},{5... | collective-permute-start | bytes 73736 | tf_op jit(solution)/shard_map/ppermute | solution.py:481
  65.7 4.7 %collective-permute-start.13 = (bf16[2,12,8,128]{3,2,1,0:T(8,128)(2,1)S(1)}, bf16[2,12,8,128]{3,2,1,0:T(8,128)(2,1)S(1)}, u32[]{:S(2)}, u32[]{:S(2)}) collective-permute-start(bf16[2,12,8,128]{3,2,1,0:T(8,128)(2,1)S(1)} %surface_pair.1.pair_ref), channel_id=1, source_target_pairs={{0,8},{4,12},{8,0},{12,4},{16,24},{20,28},{24,16},{28,20},{1,9},{5... | collective-permute-start | bytes 147464 | tf_op jit(solution)/shard_map/ppermute | solution.py:481
  67.2 4.6 %collective-permute-start.12 = (bf16[2,12,8,128]{3,2,1,0:T(8,128)(2,1)S(1)}, bf16[2,12,8,128]{3,2,1,0:T(8,128)(2,1)S(1)}, u32[]{:S(2)}, u32[]{:S(2)}) collective-permute-start(bf16[2,12,8,128]{3,2,1,0:T(8,128)(2,1)S(1)} %surface_pair.1.pair_ref), channel_id=1, source_target_pairs={{0,16},{4,20},{8,24},{12,28},{16,0},{20,4},{24,8},{28,12},{1,17},{... | collective-permute-start | bytes 147464 | tf_op jit(solution)/shard_map/ppermute | solution.py:481
  67.9 5.0 %collective-permute-start.11 = (bf16[2,12,8,128]{3,2,1,0:T(8,128)(2,1)S(1)}, bf16[2,12,8,128]{3,2,1,0:T(8,128)(2,1)S(1)}, u32[]{:S(2)}, u32[]{:S(2)}) collective-permute-start(bf16[2,12,8,128]{3,2,1,0:T(8,128)(2,1)S(1)} %surface_pair.1.pair_ref), channel_id=1, source_target_pairs={{0,24},{4,28},{8,16},{12,20},{16,8},{20,12},{24,0},{28,4},{1,25},{... | collective-permute-start | bytes 147464 | tf_op jit(solution)/shard_map/ppermute | solution.py:481

commit v9 on v8

--- a/solution.py
+++ b/solution.py
@@ -345,14 +345,21 @@
         halo[:, at, :] = out.reshape(blocks, GROUP, lanes)
 
 
-def norm_rows(a_ref, row0, count, halo, gain, out):
+def turned_by(value, slots):
+    lanes = value.shape[-1]
+    if isinstance(slots, int):
+        shift = SLOT * slots % lanes
+        return pltpu.roll(value, shift, 1) if shift else value
+    return pltpu.roll(value, lax.rem(SLOT * slots + lanes, lanes), 1)
+
+
+def norm_rows(a_ref, base, off, count, halo, gain, out):
     _, chans, lanes = a_ref.shape
     blocks = halo.shape[0]
     edge = edge_lanes((chans, lanes))
     for r in range(count):
-        q, slot = (row0 + r) % blocks, (row0 + r) // blocks
-        extra = pltpu.roll(halo[q], lanes - SLOT * slot, 1) if slot else halo[q]
-        a = a_ref[row0 + r] + jnp.where(edge, extra, 0.0)
+        extra = turned_by(halo[(off + r) % blocks], -(base // blocks + (off + r) // blocks))
+        a = a_ref[base + off + r] + jnp.where(edge, extra, 0.0)
         center = a - jnp.mean(a, axis=0, keepdims=True)
         var = jnp.mean(center * center, axis=0, keepdims=True)
         normed = (center * lax.rsqrt(var + 1e-06) * gain).astype(BF)
@@ -365,95 +372,105 @@
     return jnp.dot(down_t, h, preferred_element_type=F32)
 
 
-def atmos_kernel(layer, members, count, *refs):
-    x_ref, a_ref, left_ref, right_ref, band_ref, g_ref, up_ref, dn_ref, s_ref = refs[:9]
+def atmos_kernel(layer, near, members, count, steps, *refs):
+    x_ref, a_ref, g_ref, up_ref, dn_ref, s_ref = refs[:6]
+    refs = refs[6:]
+    even, odd = refs[-2:]
+    rows, chans, lanes = x_ref.shape
+    base = 0
     if layer == 0:
-        y_ref, p_ref = refs[9:11]
+        first_ref, second_ref, band_ref, y_ref, p_ref, xe, halo = refs[:-2]
+        blocks = halo.shape[0]
+        packed = [None] * blocks
+        keep = edge_lanes((chans, lanes)).astype(F32).astype(BF)
     else:
-        fw_ref, y_ref, keep_ref, give_ref, flux = refs[9:14]
-    xe, halo, even, odd = refs[-4:]
-    rows, chans, lanes = x_ref.shape
-    blocks = halo.shape[0]
-    halo_conv(left_ref, right_ref, band_ref, True, halo_matrix(lanes), xe, halo)
+        rank = lax.axis_index("member")
+        half = members // 2
+        upper = (rank >= half) if near else (rank < half)
+        base = jnp.where(upper, rows - steps * count, 0)
+        if near:
+            fw_ref, _, old_ref, halo, y_ref, keep_ref, give_ref, flux = refs[:-2]
+        else:
+            fw_ref, first_ref, second_ref, band_ref = refs[:4]
+            y_ref, keep_ref, give_ref, flux, halo, xe = refs[4:-2]
+    if near:
+        flux[...] = old_ref[...]
+    else:
+        halo_conv(first_ref, second_ref, band_ref, True, halo_matrix(lanes), xe, halo)
+        if layer == 1:
+            blank = jnp.zeros((HALO,) + flux.shape[1:], BF)
+            flux[0:HALO] = blank
+            flux[rows + HALO : rows + 2 * HALO] = blank
     up_t = transposed(up_ref[layer])
     dn_t = halved(dn_ref[layer])
     gain = spread(g_ref[layer : layer + 1], lanes)
     scale = spread(s_ref[layer : layer + 1], lanes)
-    keep = edge_lanes((chans, lanes)).astype(F32).astype(BF)
-    packed = [None] * blocks
-    if layer == 1:
-        blank = jnp.zeros((HALO,) + flux.shape[1:], BF)
-        flux[0:HALO] = blank
-        flux[rows + HALO : rows + 2 * HALO] = blank
-    norm_rows(a_ref, 0, count, halo, gain, even)
-    for step in range(rows // count):
-        row0 = step * count
+    norm_rows(a_ref, base, 0, count, halo, gain, even)
+    for step in range(steps):
+        off = step * count
         now, later = (even, odd) if step % 2 == 0 else (odd, even)
-        if row0 + count < rows:
-            norm_rows(a_ref, row0 + count, count, halo, gain, later)
+        if step + 1 < steps:
+            norm_rows(a_ref, base, off + count, count, halo, gain, later)
         branch = branch_of(now[...], up_t, dn_t)
         made = []
         for r in range(count):
-            y = x_ref[row0 + r].astype(F32) + scale * branch[:, r * lanes : (r + 1) * lanes]
+            y = x_ref[base + off + r].astype(F32) + scale * branch[:, r * lanes : (r + 1) * lanes]
             made.append(y.astype(BF))
-            y_ref[row0 + r] = made[r]
+            y_ref[base + off + r] = made[r]
         if layer == 0:
             for r in range(count):
-                q, slot = (row0 + r) % blocks, (row0 + r) // blocks
-                moved = made[r] * keep
-                if slot:
-                    moved = pltpu.roll(moved, SLOT * slot, 1)
+                q, slot = (off + r) % blocks, (off + r) // blocks
+                moved = turned_by(made[r] * keep, slot)
                 packed[q] = moved if packed[q] is None else packed[q] + moved
-            if row0 % (4 * count) == 3 * count or row0 + count == rows:
+            if step % 4 == 3 or step + 1 == steps:
                 for q in range(blocks):
-                    if row0 < 4 * count:
-                        p_ref[q] = packed[q]
-                    else:
-                        p_ref[q] = p_ref[q] + packed[q]
+                    p_ref[q] = packed[q] if step < 4 else p_ref[q] + packed[q]
                 packed = [None] * blocks
         else:
             z = jnp.dot(fw_ref[...], jnp.concatenate(made, axis=1), preferred_element_type=F32)
             f = (0.5 * twice_gelu(z)).astype(BF)
             for r in range(count):
-                flux[row0 + HALO + r] = f[:, r * lanes : (r + 1) * lanes]
+                flux[base + off + HALO + r] = f[:, r * lanes : (r + 1) * lanes]
     if layer == 1:
-        rank = lax.axis_index("member")
         share = rows // members
-        for k in range(members):
-            chunk = flux[pl.ds((rank ^ k) * share, share + 2 * HALO)]
+        for k in range(half):
+            dst = rank ^ (k if near else half + k)
+            chunk = flux[pl.ds(dst * share, share + 2 * HALO)]
             if k % 2:
                 give_ref[k // 2] = chunk
             else:
                 keep_ref[k // 2] = chunk
 
 
-def atmos_block(layer, members, x, a, edges, band, weights, count):
+def atmos_block(layer, near, members, x, a, weights, others, count, steps):
     rows, chans, lanes = x.shape
     blocks = rows // SLOTS
-    args = [x, a, *edges, band, *weights]
+    args = [x, a, *weights, *others]
     outs = [jax.ShapeDtypeStruct(x.shape, BF)]
-    scratch = []
+    halo = jax.ShapeDtypeStruct((blocks, chans, lanes), F32)
+    shifts = pltpu.VMEM((TAPS - 1, SPAN, chans, lanes), BF)
     if layer == 0:
         outs.append(jax.ShapeDtypeStruct((blocks, chans, lanes), BF))
+        scratch = [shifts, pltpu.VMEM(halo.shape, F32)]
     else:
         flux = weights[-1].shape[0]
         share = rows // members
-        outs += [jax.ShapeDtypeStruct((members // 2, share + 2 * HALO, flux, lanes), BF)] * 2
-        scratch.append(pltpu.VMEM((rows + 2 * HALO, flux, lanes), BF))
-    return pl.pallas_call(
-        functools.partial(atmos_kernel, layer, members, count),
+        field = (rows + 2 * HALO, flux, lanes)
+        outs += [jax.ShapeDtypeStruct((members // 4, share + 2 * HALO, flux, lanes), BF)] * 2
+        if near:
+            scratch = [pltpu.VMEM(field, BF)]
+        else:
+            outs += [jax.ShapeDtypeStruct(field, BF), halo]
+            scratch = [shifts]
+    return pl.pallas_call(
+        functools.partial(atmos_kernel, layer, near, members, count, steps),
         out_shape=outs,
         in_specs=[VMEM] * len(args),
         out_specs=[VMEM] * len(outs),
-        scratch_shapes=scratch
-        + [
-            pltpu.VMEM((TAPS - 1, SPAN, chans, lanes), BF),
-            pltpu.VMEM((blocks, chans, lanes), F32),
-            pltpu.VMEM((chans, count * lanes), BF),
-            pltpu.VMEM((chans, count * lanes), BF),
-        ],
+        scratch_shapes=scratch + [pltpu.VMEM((chans, count * lanes), BF)] * 2,
+        input_output_aliases={7: 0} if near else {},
         compiler_params=params(BIG),
-        cost_estimate=cost(8),
+        cost_estimate=cost(8 * steps * count / rows),
         name="atmos_block",
     )(*args)
 
@@ -545,7 +562,7 @@
     share, chans, lanes = new_ref.shape
     halo_conv(left_ref, right_ref, band_ref, False, mat_ref[...], xe, halo)
     scale = scale_ref[...]
-    norm_rows(a_ref, 0, share, halo, gain_ref[...], normed)
+    norm_rows(a_ref, 0, 0, share, halo, gain_ref[...], normed)
     branch = branch_of(normed[...], upt_ref[...], halved(dn_ref[...]))
     first = lax.axis_index("member") * share
     made = []
@@ -608,19 +625,20 @@
     surf = [pair_ref[side ^ parity, r] for side in range(2) for r in range(share)]
     back = jnp.dot(bw_ref[...], jnp.concatenate(surf, axis=1), preferred_element_type=F32)
     copies = []
-    for side in range(2):
-        for r in range(side * share, (side + 1) * share):
+    piece = share // 2
+    for n in range(4):
+        for r in range(n * piece, (n + 1) * piece):
             sea = (1 - land_ref[pl.ds(first + r, 1), :]).astype(F32)
             out = y_ref[first + r].astype(F32) + sea * back[:, r * lanes : (r + 1) * lanes]
             buf[r] = out.astype(BF)
         copies.append(
             pltpu.make_async_copy(
-                buf.at[pl.ds(side * share, share)],
-                o_ref.at[pl.ds(first + side * share, share)],
-                sems.at[side],
+                buf.at[pl.ds(n * piece, piece)],
+                o_ref.at[pl.ds(first + n * piece, piece)],
+                sems.at[n],
             )
         )
-        copies[side].start()
+        copies[n].start()
     for copy in copies:
         copy.wait()
 
@@ -634,7 +652,7 @@
         out_specs=HBM,
         scratch_shapes=[
             pltpu.VMEM((2 * pair.shape[1], chans, lanes), BF),
-            pltpu.SemaphoreType.DMA((2,)),
+            pltpu.SemaphoreType.DMA((4,)),
         ],
         input_output_aliases={4: 0} if earlier else {},
         compiler_params=params(24),
@@ -673,19 +691,29 @@
 
     edges = neighbours(pack(state, big))
     a, band = convolve(0, state, taps, blocks)
-    state, packed = atmos_block(0, members, state, a, edges, band, atm, small)
+    steps = rows // small
+    near_steps = (rows // 2) // small - 1
+    state, packed = atmos_block(0, False, members, state, a, atm, [*edges, band], small, steps)
 
     edges = neighbours(packed)
     a, band = convolve(1, state, taps, blocks)
+    weights = (*atm, flux_weight.T)
+    partly, far_keep, give, flux, halo = atmos_block(
+        1, False, members, state, a, weights, [*edges, band], small, steps - near_steps
+    )
+    far_got = send_xor(give, 1)
     state, keep, give = atmos_block(
-        1, members, state, a, edges, band, (*atm, flux_weight.T), small
+        1, True, members, state, a, weights, [partly, flux, halo], small, near_steps
     )
+    far_got, give = lax.optimization_barrier((far_got, give))
+    far_sums = add_pairs(far_keep, far_got, 0)
+    give, *far_sums = lax.optimization_barrier((give, *far_sums))
+    sent = [send_xor(far_sums[k], half + 2 * k) for k in reversed(range(len(far_sums)))]
     got = send_xor(give, 1)
     sums = add_pairs(keep, got, 1)
-    sent = [send_xor(sums[k - 1], 2 * k) for k in range(half - 1, 0, -1)]
+    sent += [send_xor(part, 2 * k + 2) for k, part in enumerate(sums)]
     band, *ready = prepare_ocean(ocn_kernel, ocn_gain, ocn_up, ocn_scale, sums[0])
     sent = [keep, got] + sent
-
     mid, packed = force(members, sent, ocean, land_mask, ice_mask, flux_lift)
     left, right = neighbours(packed)
     a = ocean_conv(mid, band)

time: 74.2 us -> 73.6 us (level)
  waiting for transfers between devices: 12.4 us -> 10.7 us
  Pallas kernels: 42.5 us -> 43.6 us
    ppermute x8 -> x9, waiting for transfers between devices: 8.94 us -> 6.81 us  [send_xor(): lax.ppermute(value, 'member', [(i, i ^ bits) for i in range(members)])]
    ppermute x3, waiting for transfers between devices: 2.59 us -> 3.93 us  [neighbours(): lax.ppermute(packed, 'lon', [(i, (i - 1) % count if i % 2 == 0 else (i +...]
    pallas_call x2 -> x3, Pallas kernels: 16.1 us -> 17.3 us  [atmos_block(): pl.pallas_call(functools.partial(atmos_kernel, layer, near, members, coun...]
    ppermute x3, waiting for transfers between devices: 0.85 us -> 0.01 us  [neighbours(): first = lax.ppermute(packed, 'lon', [(i, i ^ 1) for i in range(count)])]
    ppermute x8 -> x9, starting transfers between devices: 7.12 us -> 7.64 us  [send_xor(): lax.ppermute(value, 'member', [(i, i ^ bits) for i in range(members)])]
  transfers between devices with their start and end apart: 14 -> 15, of which waited for: 10 -> 8; matrix products, arithmetic and copies ran while one was open for 0% -> 0% of each run, Pallas kernels for 25% -> 29%
where the time goes in v9:
time: 73.6 us; the launch traced here: 73.5 us
  Pallas kernels  43.6 us (59%)
  starting transfers between devices  17.8 us (24%)
  waiting for transfers between devices  10.7 us (15%)
  between operations  1.13 us (2%)
    pallas_call x3, Pallas kernels, atmos_block(): pl.pallas_call(functools.partial(atmos_kernel, layer, near, members, coun...  17.3 us
    pallas_call x2, Pallas kernels, convolve(): pl.pallas_call(functools.partial(conv_kernel, layer), out_shape=[jax.Shap...  12.9 us
    ppermute x9, starting transfers between devices, send_xor(): lax.ppermute(value, 'member', [(i, i ^ bits) for i in range(members)])  7.64 us
    ppermute x9, waiting for transfers between devices, send_xor(): lax.ppermute(value, 'member', [(i, i ^ bits) for i in range(members)])  6.81 us
    ppermute x3, starting transfers between devices, neighbours(): lax.ppermute(packed, 'lon', [(i, (i - 1) % count if i % 2 == 0 else (i +...  6.37 us
    pallas_call x4, Pallas kernels, couple(): pl.pallas_call(functools.partial(couple_kernel, k), out_shape=jax.ShapeDt...  4.11 us
    ppermute x3, waiting for transfers between devices, neighbours(): lax.ppermute(packed, 'lon', [(i, (i - 1) % count if i % 2 == 0 else (i +...  3.93 us
    ppermute x3, starting transfers between devices, neighbours(): first = lax.ppermute(packed, 'lon', [(i, i ^ 1) for i in range(count)])  3.78 us
  transfers between devices with their start and end apart: 15, of which 8 were waited for; matrix products, arithmetic and copies ran while one was open for 0% of the time, Pallas kernels for 29%

profile of v9, /device:TPU:0, one launch (start us, length us, event | category | flops | bytes accessed | tf_op | source)
XLA Modules:
  0.0 73.5 jit_solution(4320333409791912522)
XLA Ops:
  0.6 2.8 %pack_edges.1 = bf16[6,96,128]{2,1,0:T(8,128)(2,1)} custom-call(bf16[96,96,128]{2,1,0:T(8,128)(2,1)} %bitcast.10), custom_call_target="tpu_custom_call" | custom-call | tf_op jit(solution)/shard_map/pack_edges/pallas_call | solution.py:81
  3.4 3.1 %collective-permute-start = (bf16[6,96,128]{2,1,0:T(8,128)(2,1)}, bf16[6,96,128]{2,1,0:T(8,128)(2,1)S(1)}, u32[]{:S(2)}, u32[]{:S(2)}) collective-permute-start(bf16[6,96,128]{2,1,0:T(8,128)(2,1)} %pack_edges.1), channel_id=1, source_target_pairs={{0,1},{1,0},{2,3},{3,2},{4,5},{5,4},{6,7},{7,6},{8,9},{9,8},{10,11... | collective-permute-start | bytes 442376 | tf_op jit(solution)/shard_map/ppermute | solution.py:94
  6.5 2.5 %collective-permute-start.1 = (bf16[6,96,128]{2,1,0:T(8,128)(2,1)}, bf16[6,96,128]{2,1,0:T(8,128)(2,1)S(1)}, u32[]{:S(2)}, u32[]{:S(2)}) collective-permute-start(bf16[6,96,128]{2,1,0:T(8,128)(2,1)} %pack_edges.1), channel_id=1, source_target_pairs={{0,3},{1,2},{2,1},{3,0},{4,7},{5,6},{6,5},{7,4},{8,11},{9,10},{10,... | collective-permute-start | bytes 442376 | tf_op jit(solution)/shard_map/ppermute | solution.py:95
  9.0 0.0 copy-done.10
  9.0 0.0 copy-start.13
  9.0 0.0 copy-start.14
  9.0 6.4 %conv.2 = (f32[96,96,128]{2,1,0:T(8,128)S(1)}, bf16[6,96,1792]{2,1,0:T(8,128)(2,1)S(1)}) custom-call(bf16[96,96,128]{2,1,0:T(8,128)(2,1)S(1)} %bitcast.11, f32[7,7,2,96]{3,2,1,0:T(2,128)S(1)} %bitcast.22), custom_call_target="tpu_custom_call" | custom-call | flops 8000000000 | tf_op jit(solution)/shard_map/conv/pallas_call | solution.py:203
  15.4 0.0 collective-permute-done.refs_6_
  15.4 0.6 collective-permute-done.1.refs_7_
  16.0 0.0 copy-done.14
  16.1 7.8 %atmos_block.3 = (bf16[96,96,128]{2,1,0:T(8,128)(2,1)S(1)}, bf16[6,96,128]{2,1,0:T(8,128)(2,1)S(1)}) custom-call(bf16[96,96,128]{2,1,0:T(8,128)(2,1)S(1)} %bitcast.12, f32[96,96,128]{2,1,0:T(8,128)S(1)} %get-tuple-element.32.refs_1_, f32[2,96]{1,0:T(2,128)S(1)} %copy-done.13, bf16[2,96,384]{2,1,0:T(8,128)(2,1)S(1)} %copy-done.7, ...), custom_call_target="tpu_custom_call" | custom-call | flops 8000000000 | tf_op jit(solution)/shard_map/atmos_block/pallas_call | solution.py:465
  23.9 0.7 collective-permute-start.2
  24.6 2.6 %collective-permute-start.3 = (bf16[6,96,128]{2,1,0:T(8,128)(2,1)S(1)}, bf16[6,96,128]{2,1,0:T(8,128)(2,1)S(1)}, u32[]{:S(2)}, u32[]{:S(2)}) collective-permute-start(bf16[6,96,128]{2,1,0:T(8,128)(2,1)S(1)} %get-tuple-element.36), channel_id=1, source_target_pairs={{0,3},{1,2},{2,1},{3,0},{4,7},{5,6},{6,5},{7,4},{8,11},{9,10},{10,... | collective-permute-start | bytes 442376 | tf_op jit(solution)/shard_map/ppermute | solution.py:95
  27.2 6.5 %conv.3 = (f32[96,96,128]{2,1,0:T(8,128)S(1)}, bf16[6,96,1792]{2,1,0:T(8,128)(2,1)S(1)}) custom-call(bf16[96,96,128]{2,1,0:T(8,128)(2,1)S(1)} %get-tuple-element.34.x_ref.refs_0_, f32[7,7,2,96]{3,2,1,0:T(2,128)S(1)} %bitcast.23), custom_call_target="tpu_custom_call" | custom-call | flops 8000000000 | tf_op jit(solution)/shard_map/conv/pallas_call | solution.py:203
  33.7 0.0 collective-permute-done.2.refs_7_
  33.7 0.0 collective-permute-done.3.refs_8_
  33.8 0.0 copy-done.12
  33.8 6.4 %atmos_block.4 = (bf16[96,96,128]{2,1,0:T(8,128)(2,1)S(1)}, bf16[2,18,32,128]{3,2,1,0:T(8,128)(2,1)S(1)}, bf16[2,18,32,128]{3,2,1,0:T(8,128)(2,1)S(1)}, bf16[102...) custom-call(bf16[96,96,128]{2,1,0:T(8,128)(2,1)S(1)} %get-tuple-element.34.x_ref.refs_0_, ...), custom_call_target="tpu_custom_call" | custom-call | flops 5000000000 | tf_op jit(solution)/shard_map/atmos_block/pallas_call | solution.py:465
  40.2 0.1 collective-permute-start.4
  40.3 0.0 copy-start.9
  40.3 0.0 copy-start.11
  40.3 0.0 copy-start.15
  40.3 0.0 copy-start.16
  40.3 3.0 %atmos_block.5 = (bf16[96,96,128]{2,1,0:T(8,128)(2,1)S(1)}, bf16[2,18,32,128]{3,2,1,0:T(8,128)(2,1)S(1)}, bf16[2,18,32,128]{3,2,1,0:T(8,128)(2,1)S(1)}) custom-call(bf16[96,96,128]{2,1,0:T(8,128)(2,1)S(1)} %get-tuple-element.34.x_ref.refs_0_, f32[96,96,128]{2,1,0:T(8,128)S(1)} %get-tuple-element.35.refs_1_, ...), custom_call_target="tpu_custom_call", output_to_operand_aliasing={{0}: (7, {})} | custom-call | flops 3000000000 | tf_op jit(solution)/shard_map/atmos_block/pallas_call | solution.py:465
  43.4 0.0 collective-permute-done.4.got_ref
  43.4 0.1 add_pairs.2
  43.4 0.5 collective-permute-start.5
  44.0 2.4 %collective-permute-start.6 = (bf16[18,32,128]{2,1,0:T(8,128)(2,1)S(1)}, bf16[18,32,128]{2,1,0:T(8,128)(2,1)S(1)}, u32[]{:S(2)}, u32[]{:S(2)}) collective-permute-start(bf16[18,32,128]{2,1,0:T(8,128)(2,1)S(1)} %get-tuple-element.51), channel_id=1, source_target_pairs={{0,24},{4,28},{8,16},{12,20},{16,8},{20,12},{24,0},{28,4},{1,25},{... | collective-permute-start | bytes 442376 | tf_op jit(solution)/shard_map/ppermute | solution.py:498
  46.4 0.5 collective-permute-start.7
  46.9 0.0 collective-permute-done.5.got_ref.refs_1_
  47.0 0.6 collective-permute-start.8
  47.6 0.0 copy-done.15
  47.6 0.0 copy-start.1
  47.6 0.0 copy-start.2
  47.6 0.0 copy-start.4
  47.6 0.0 copy-start.5
  47.6 1.2 %prepare_ocean.1 = (bf16[6,160,1792]{2,1,0:T(8,128)(2,1)S(1)}, bf16[256,768]{1,0:T(8,128)(2,1)S(1)}, bf16[384,96]{1,0:T(8,128)(2,1)S(1)}, f32[96,128]{1,0:T(8,128)S(1)}, f32[96,128]{1,0:T(8,128)S(1)}) custom-call(f32[7,7,96]{2,1,0:T(8,128)S(1)} %copy-done.11, f32[1,96]{1,0:T(1,128)S(1)} %bitcast.26, bf16[96,384]{1,0:T(8,128)(2,1)S(1)} %copy-done.9, ...), custom_call_target="tpu_custom_call" | custom-call | flops 3000000000 | tf_op jit(solution)/shard_map/prepare_ocean/pallas_call | solution.py:238
  48.8 2.4 %collective-permute-done.6.refs_2_ = bf16[18,32,128]{2,1,0:T(8,128)(2,1)S(1)} collective-permute-done((bf16[18,32,128]{2,1,0:T(8,128)(2,1)S(1)}, bf16[18,32,128]{2,1,0:T(8,128)(2,1)S(1)}, u32[]{:S(2)}, u32[]{:S(2)}) %collective-permute-start.6) | collective-permute-done | bytes 147488 | tf_op jit(solution)/shard_map/ppermute | solution.py:498
  51.3 2.6 %collective-permute-done.7.refs_3_ = bf16[18,32,128]{2,1,0:T(8,128)(2,1)S(1)} collective-permute-done((bf16[18,32,128]{2,1,0:T(8,128)(2,1)S(1)}, bf16[18,32,128]{2,1,0:T(8,128)(2,1)S(1)}, u32[]{:S(2)}, u32[]{:S(2)}) %collective-permute-start.7) | collective-permute-done | bytes 147488 | tf_op jit(solution)/shard_map/ppermute | solution.py:498
  53.9 0.1 collective-permute-done.8.refs_4_
  54.0 0.0 copy-done.4
  54.0 0.0 copy-done.5
  54.0 1.3 %ocean_forcing.1 = (bf16[18,96,128]{2,1,0:T(8,128)(2,1)S(1)}, bf16[2,96,128]{2,1,0:T(8,128)(2,1)S(1)}) custom-call(bf16[2,18,32,128]{3,2,1,0:T(8,128)(2,1)S(1)} %get-tuple-element.42.keep_ref.refs_0_, bf16[2,18,32,128]{3,2,1,0:T(8,128)(2,1)S(1)} %collective-permute-done.5.got_ref.refs_1_, bf16[18,32,128]{2,1,0:T(8,128)(2,1)S(1)} %collective-permute-done.6.refs_2_, ...), custom_call_target="tpu_custom_call" | custom-call | tf_op jit(solution)/shard_map/ocean_forcing/pallas_call | solution.py:547
  55.3 1.3 %collective-permute-start.10 = (bf16[2,96,128]{2,1,0:T(8,128)(2,1)S(1)}, bf16[2,96,128]{2,1,0:T(8,128)(2,1)S(1)}, u32[]{:S(2)}, u32[]{:S(2)}) collective-permute-start(bf16[2,96,128]{2,1,0:T(8,128)(2,1)S(1)} %get-tuple-element.55), channel_id=1, source_target_pairs={{0,3},{1,2},{2,1},{3,0},{4,7},{5,6},{6,5},{7,4},{8,11},{9,10},{10,... | collective-permute-start | bytes 147464 | tf_op jit(solution)/shard_map/ppermute | solution.py:95
  56.5 0.0 collective-permute-start.9
  56.5 1.3 %ocean_conv.1.a_ref = f32[12,96,128]{2,1,0:T(8,128)S(1)} custom-call(bf16[18,96,128]{2,1,0:T(8,128)(2,1)S(1)} %get-tuple-element.53.x_ref.mid_ref, bf16[6,160,1792]{2,1,0:T(8,128)(2,1)S(1)} %get-tuple-element.54.band_ref), custom_call_target="tpu_custom_call" | custom-call | flops 2000000000 | tf_op jit(solution)/shard_map/ocean_conv/pallas_call | solution.py:267
  57.9 3.3 %collective-permute-done.10.right_ref = bf16[2,96,128]{2,1,0:T(8,128)(2,1)S(1)} collective-permute-done((bf16[2,96,128]{2,1,0:T(8,128)(2,1)S(1)}, bf16[2,96,128]{2,1,0:T(8,128)(2,1)S(1)}, u32[]{:S(2)}, u32[]{:S(2)}) %collective-permute-start.10) | collective-permute-done | bytes 49184 | tf_op jit(solution)/shard_map/ppermute | solution.py:95
  61.2 0.0 collective-permute-done.9.left_ref
  61.2 0.0 copy-done.3
  61.2 0.0 copy-start.17
  61.2 2.6 %ocean_block.1 = (bf16[12,96,128]{2,1,0:T(8,128)(2,1)}, bf16[12,8,128]{2,1,0:T(8,128)(2,1)S(1)}) custom-call(bf16[18,96,128]{2,1,0:T(8,128)(2,1)S(1)} %get-tuple-element.53.x_ref.mid_ref, f32[12,96,128]{2,1,0:T(8,128)S(1)} %ocean_conv.1.a_ref, bf16[2,96,128]{2,1,0:T(8,128)(2,1)S(1)} %collective-permute-done.9.left_ref, ...), custom_call_target="tpu_custom_call" | custom-call | tf_op jit(solution)/shard_map/ocean_block/pallas_call | solution.py:584
  63.9 0.0 collective-permute-start.11
  63.9 1.2 %collective-permute-done.11.got_ref = bf16[12,8,128]{2,1,0:T(8,128)(2,1)S(1)} collective-permute-done((bf16[12,8,128]{2,1,0:T(8,128)(2,1)S(1)}, bf16[12,8,128]{2,1,0:T(8,128)(2,1)S(1)}, u32[]{:S(2)}, u32[]{:S(2)}) %collective-permute-start.11) | collective-permute-done | bytes 24608 | tf_op jit(solution)/shard_map/ppermute | solution.py:498
  65.1 1.5 %collective-permute-start.14 = (bf16[2,12,8,128]{3,2,1,0:T(8,128)(2,1)S(1)}, bf16[2,12,8,128]{3,2,1,0:T(8,128)(2,1)S(1)}, u32[]{:S(2)}, u32[]{:S(2)}) collective-permute-start(bf16[2,12,8,128]{3,2,1,0:T(8,128)(2,1)S(1)} %surface_pair.1.pair_ref), channel_id=1, source_target_pairs={{0,8},{4,12},{8,0},{12,4},{16,24},{20,28},{24,16},{28,20},{1,9},{5... | collective-permute-start | bytes 147464 | tf_op jit(solution)/shard_map/ppermute | solution.py:498
  66.6 0.7 collective-permute-start.13
  67.3 1.3 %collective-permute-start.12 = (bf16[2,12,8,128]{3,2,1,0:T(8,128)(2,1)S(1)}, bf16[2,12,8,128]{3,2,1,0:T(8,128)(2,1)S(1)}, u32[]{:S(2)}, u32[]{:S(2)}) collective-permute-start(bf16[2,12,8,128]{3,2,1,0:T(8,128)(2,1)S(1)} %surface_pair.1.pair_ref), channel_id=1, source_target_pairs={{0,24},{4,28},{8,16},{12,20},{16,8},{20,12},{24,0},{28,4},{1,25},{... | collective-permute-start | bytes 147464 | tf_op jit(solution)/shard_map/ppermute | solution.py:498
  68.6 0.1 copy.24
  68.7 1.0 %couple.4.refs_0_ = bf16[96,96,128]{2,1,0:T(8,128)(2,1)} custom-call(bf16[96,96,128]{2,1,0:T(8,128)(2,1)S(1)} %get-tuple-element.41.y_ref, s32[96,128]{1,0:T(8,128)S(1)} %copy-done.2, bf16[96,8]{1,0:T(8,128)(2,1)S(1)} %bitcast.13, bf16[2,12,8,128]{3,2,1,0:T(8,128)(2,1)S(1)} %surface_pair.1.pair_ref), custom_call_target="tpu_custom_call" | custom-call | tf_op jit(solution)/shard_map/couple/pallas_call | solution.py:648
  69.7 0.0 collective-permute-done.14.pair_ref
  69.7 1.0 %couple.5.refs_0_ = bf16[96,96,128]{2,1,0:T(8,128)(2,1)} custom-call(bf16[96,96,128]{2,1,0:T(8,128)(2,1)S(1)} %get-tuple-element.41.y_ref, s32[96,128]{1,0:T(8,128)S(1)} %copy-done.2, bf16[96,8]{1,0:T(8,128)(2,1)S(1)} %bitcast.14, bf16[2,12,8,128]{3,2,1,0:T(8,128)(2,1)S(1)} %collective-permute-done.14.pair_ref, ...), custom_call_target="tpu_custom_call", output_to_operand_aliasing={{}: (4, {})} | custom-call | tf_op jit(solution)/shard_map/couple/pallas_call | solution.py:648
  70.8 0.4 collective-permute-done.13.pair_ref
  71.2 1.0 %couple.6.refs_0_ = bf16[96,96,128]{2,1,0:T(8,128)(2,1)} custom-call(bf16[96,96,128]{2,1,0:T(8,128)(2,1)S(1)} %get-tuple-element.41.y_ref, s32[96,128]{1,0:T(8,128)S(1)} %copy-done.2, bf16[96,8]{1,0:T(8,128)(2,1)S(1)} %bitcast.15, bf16[2,12,8,128]{3,2,1,0:T(8,128)(2,1)S(1)} %collective-permute-done.13.pair_ref, ...), custom_call_target="tpu_custom_call", output_to_operand_aliasing={{}: (4, {})} | custom-call | tf_op jit(solution)/shard_map/couple/pallas_call | solution.py:648
  72.2 0.1 collective-permute-done.12.pair_ref
  72.3 1.0 %couple.7 = bf16[96,96,128]{2,1,0:T(8,128)(2,1)} custom-call(bf16[96,96,128]{2,1,0:T(8,128)(2,1)S(1)} %get-tuple-element.41.y_ref, s32[96,128]{1,0:T(8,128)S(1)} %copy-done.2, bf16[96,8]{1,0:T(8,128)(2,1)S(1)} %bitcast.16, bf16[2,12,8,128]{3,2,1,0:T(8,128)(2,1)S(1)} %collective-permute-done.12.pair_ref, ...), custom_call_target="tpu_custom_call", output_to_operand_aliasing={{}: (4, {})} | custom-call | tf_op jit(solution)/shard_map/couple/pallas_call | solution.py:648
  (20 shorter events, 0.1 us)
Async XLA Ops:
  0.6 8.4 %copy-start = (bf16[1,96,96,128]{3,2,1,0:T(8,128)(2,1)S(1)}, bf16[1,96,96,128]{3,2,1,0:T(8,128)(2,1)}, u32[]{:S(2)}) copy-start(bf16[1,96,96,128]{3,2,1,0:T(8,128)(2,1)} %param.18) | copy-start | bytes 7077892
  0.6 8.4 %copy-start.10 = (f32[2,7,7,96]{3,0,2,1:T(2,128)S(1)}, f32[2,7,7,96]{3,0,2,1:T(2,128)}, u32[]{:S(2)}) copy-start(f32[2,7,7,96]{3,0,2,1:T(2,128)} %param.22) | copy-start | bytes 112900
  3.4 12.0 %collective-permute-start = (bf16[6,96,128]{2,1,0:T(8,128)(2,1)}, bf16[6,96,128]{2,1,0:T(8,128)(2,1)S(1)}, u32[]{:S(2)}, u32[]{:S(2)}) collective-permute-start(bf16[6,96,128]{2,1,0:T(8,128)(2,1)} %pack_edges.1), channel_id=1, source_target_pairs={{0,1},{1,0},{2,3},{3,2},{4,5},{5,4},{6,7},{7,6},{8,9},{9,8},{10,11... | collective-permute-start | bytes 442376 | tf_op jit(solution)/shard_map/ppermute | solution.py:94
  6.5 9.5 %collective-permute-start.1 = (bf16[6,96,128]{2,1,0:T(8,128)(2,1)}, bf16[6,96,128]{2,1,0:T(8,128)(2,1)S(1)}, u32[]{:S(2)}, u32[]{:S(2)}) collective-permute-start(bf16[6,96,128]{2,1,0:T(8,128)(2,1)} %pack_edges.1), channel_id=1, source_target_pairs={{0,3},{1,2},{2,1},{3,0},{4,7},{5,6},{6,5},{7,4},{8,11},{9,10},{10,... | collective-permute-start | bytes 442376 | tf_op jit(solution)/shard_map/ppermute | solution.py:95
  9.0 7.0 %copy-start.7 = (bf16[2,96,384]{2,1,0:T(8,128)(2,1)S(1)}, bf16[2,96,384]{2,1,0:T(8,128)(2,1)}, u32[]{:S(2)}) copy-start(bf16[2,96,384]{2,1,0:T(8,128)(2,1)} %refs_3_.5) | copy-start | bytes 442372
  9.0 7.0 %copy-start.8 = (bf16[2,384,96]{1,2,0:T(8,128)(2,1)S(1)}, bf16[2,384,96]{1,2,0:T(8,128)(2,1)}, u32[]{:S(2)}) copy-start(bf16[2,384,96]{1,2,0:T(8,128)(2,1)} %param.25) | copy-start | bytes 442372
  9.0 7.0 %copy-start.13 = (f32[2,96]{1,0:T(2,128)S(1)}, f32[2,96]{1,0:T(2,128)}, u32[]{:S(2)}) copy-start(f32[2,96]{1,0:T(2,128)} %refs_2_.5) | copy-start | bytes 2308
  9.0 7.0 %copy-start.14 = (f32[2,96]{1,0:T(2,128)S(1)}, f32[2,96]{1,0:T(2,128)}, u32[]{:S(2)}) copy-start(f32[2,96]{1,0:T(2,128)} %refs_5_.6) | copy-start | bytes 2308
  23.9 9.9 %collective-permute-start.2 = (bf16[6,96,128]{2,1,0:T(8,128)(2,1)S(1)}, bf16[6,96,128]{2,1,0:T(8,128)(2,1)S(1)}, u32[]{:S(2)}, u32[]{:S(2)}) collective-permute-start(bf16[6,96,128]{2,1,0:T(8,128)(2,1)S(1)} %get-tuple-element.36), channel_id=1, source_target_pairs={{0,1},{1,0},{2,3},{3,2},{4,5},{5,4},{6,7},{7,6},{8,9},{9,8},{10,11... | collective-permute-start | bytes 442376 | tf_op jit(solution)/shard_map/ppermute | solution.py:94
  24.6 9.2 %collective-permute-start.3 = (bf16[6,96,128]{2,1,0:T(8,128)(2,1)S(1)}, bf16[6,96,128]{2,1,0:T(8,128)(2,1)S(1)}, u32[]{:S(2)}, u32[]{:S(2)}) collective-permute-start(bf16[6,96,128]{2,1,0:T(8,128)(2,1)S(1)} %get-tuple-element.36), channel_id=1, source_target_pairs={{0,3},{1,2},{2,1},{3,0},{4,7},{5,6},{6,5},{7,4},{8,11},{9,10},{10,... | collective-permute-start | bytes 442376 | tf_op jit(solution)/shard_map/ppermute | solution.py:95
  27.2 6.6 %copy-start.12 = (bf16[96,32]{0,1:T(8,128)(2,1)S(1)}, bf16[96,32]{0,1:T(8,128)(2,1)}, u32[]{:S(2)}) copy-start(bf16[96,32]{0,1:T(8,128)(2,1)} %param.27) | copy-start | bytes 18436
  40.2 3.1 %collective-permute-start.4 = (bf16[2,18,32,128]{3,2,1,0:T(8,128)(2,1)S(1)}, bf16[2,18,32,128]{3,2,1,0:T(8,128)(2,1)S(1)}, u32[]{:S(2)}, u32[]{:S(2)}) collective-permute-start(bf16[2,18,32,128]{3,2,1,0:T(8,128)(2,1)S(1)} %get-tuple-element.43), channel_id=1, source_target_pairs={{0,4},{4,0},{8,12},{12,8},{16,20},{20,16},{24,28},{28,24},{1,5},{5... | collective-permute-start | bytes 884744 | tf_op jit(solution)/shard_map/ppermute | solution.py:498
  40.3 7.3 %copy-start.9 = (bf16[96,384]{1,0:T(8,128)(2,1)S(1)}, bf16[96,384]{1,0:T(8,128)(2,1)}, u32[]{:S(2)}) copy-start(bf16[96,384]{1,0:T(8,128)(2,1)} %up_ref.1) | copy-start | bytes 221188
  40.3 7.3 %copy-start.11 = (f32[7,7,96]{2,1,0:T(8,128)S(1)}, f32[7,7,96]{2,1,0:T(8,128)}, u32[]{:S(2)}) copy-start(f32[7,7,96]{2,1,0:T(8,128)} %k_ref.1) | copy-start | bytes 56452
  40.3 7.3 %copy-start.15 = (f32[96]{0:T(128)S(1)}, f32[96]{0:T(128)}, u32[]{:S(2)}) copy-start(f32[96]{0:T(128)} %param.30) | copy-start | bytes 1156
  40.3 7.3 %copy-start.16 = (f32[96]{0:T(128)S(1)}, f32[96]{0:T(128)}, u32[]{:S(2)}) copy-start(f32[96]{0:T(128)} %param.33) | copy-start | bytes 1156
  43.4 3.5 %collective-permute-start.5 = (bf16[2,18,32,128]{3,2,1,0:T(8,128)(2,1)S(1)}, bf16[2,18,32,128]{3,2,1,0:T(8,128)(2,1)S(1)}, u32[]{:S(2)}, u32[]{:S(2)}) collective-permute-start(bf16[2,18,32,128]{3,2,1,0:T(8,128)(2,1)S(1)} %get-tuple-element.50), channel_id=1, source_target_pairs={{0,4},{4,0},{8,12},{12,8},{16,20},{20,16},{24,28},{28,24},{1,5},{5... | collective-permute-start | bytes 884744 | tf_op jit(solution)/shard_map/ppermute | solution.py:498
  44.0 7.3 %collective-permute-start.6 = (bf16[18,32,128]{2,1,0:T(8,128)(2,1)S(1)}, bf16[18,32,128]{2,1,0:T(8,128)(2,1)S(1)}, u32[]{:S(2)}, u32[]{:S(2)}) collective-permute-start(bf16[18,32,128]{2,1,0:T(8,128)(2,1)S(1)} %get-tuple-element.51), channel_id=1, source_target_pairs={{0,24},{4,28},{8,16},{12,20},{16,8},{20,12},{24,0},{28,4},{1,25},{... | collective-permute-start | bytes 442376 | tf_op jit(solution)/shard_map/ppermute | solution.py:498
  46.4 7.5 %collective-permute-start.7 = (bf16[18,32,128]{2,1,0:T(8,128)(2,1)S(1)}, bf16[18,32,128]{2,1,0:T(8,128)(2,1)S(1)}, u32[]{:S(2)}, u32[]{:S(2)}) collective-permute-start(bf16[18,32,128]{2,1,0:T(8,128)(2,1)S(1)} %get-tuple-element.52), channel_id=1, source_target_pairs={{0,16},{4,20},{8,24},{12,28},{16,0},{20,4},{24,8},{28,12},{1,17},{... | collective-permute-start | bytes 442376 | tf_op jit(solution)/shard_map/ppermute | solution.py:498
  47.0 7.0 %collective-permute-start.8 = (bf16[18,32,128]{2,1,0:T(8,128)(2,1)S(1)}, bf16[18,32,128]{2,1,0:T(8,128)(2,1)S(1)}, u32[]{:S(2)}, u32[]{:S(2)}) collective-permute-start(bf16[18,32,128]{2,1,0:T(8,128)(2,1)S(1)} %add_pairs.3._), channel_id=1, source_target_pairs={{0,8},{4,12},{8,0},{12,4},{16,24},{20,28},{24,16},{28,20},{1,9},{5... | collective-permute-start | bytes 442376 | tf_op jit(solution)/shard_map/ppermute | solution.py:498
  47.6 6.4 %copy-start.1 = (bf16[96,96,128]{2,1,0:T(8,128)(2,1)S(1)}, bf16[96,96,128]{2,1,0:T(8,128)(2,1)}, u32[]{:S(2)}) copy-start(bf16[96,96,128]{2,1,0:T(8,128)(2,1)} %refs_5_.7) | copy-start | bytes 7077892
  47.6 6.4 %copy-start.2 = (s32[96,128]{1,0:T(8,128)S(1)}, s32[96,128]{1,0:T(8,128)}, u32[]{:S(2)}) copy-start(s32[96,128]{1,0:T(8,128)} %land_ref.9) | copy-start | bytes 147460
  47.6 6.4 %copy-start.4 = (s32[96,128]{1,0:T(8,128)S(1)}, s32[96,128]{1,0:T(8,128)}, u32[]{:S(2)}) copy-start(s32[96,128]{1,0:T(8,128)} %refs_7_.1) | copy-start | bytes 147460
  47.6 6.4 %copy-start.5 = (bf16[2,32,96]{2,1,0:T(8,128)(2,1)S(1)}, bf16[2,32,96]{2,1,0:T(8,128)(2,1)}, u32[]{:S(2)}) copy-start(bf16[2,32,96]{2,1,0:T(8,128)(2,1)} %refs_8_.1) | copy-start | bytes 36868
  55.3 6.0 %collective-permute-start.10 = (bf16[2,96,128]{2,1,0:T(8,128)(2,1)S(1)}, bf16[2,96,128]{2,1,0:T(8,128)(2,1)S(1)}, u32[]{:S(2)}, u32[]{:S(2)}) collective-permute-start(bf16[2,96,128]{2,1,0:T(8,128)(2,1)S(1)} %get-tuple-element.55), channel_id=1, source_target_pairs={{0,3},{1,2},{2,1},{3,0},{4,7},{5,6},{6,5},{7,4},{8,11},{9,10},{10,... | collective-permute-start | bytes 147464 | tf_op jit(solution)/shard_map/ppermute | solution.py:95
  56.5 4.7 %collective-permute-start.9 = (bf16[2,96,128]{2,1,0:T(8,128)(2,1)S(1)}, bf16[2,96,128]{2,1,0:T(8,128)(2,1)S(1)}, u32[]{:S(2)}, u32[]{:S(2)}) collective-permute-start(bf16[2,96,128]{2,1,0:T(8,128)(2,1)S(1)} %get-tuple-element.55), channel_id=1, source_target_pairs={{0,1},{1,0},{2,3},{3,2},{4,5},{5,4},{6,7},{7,6},{8,9},{9,8},{10,11... | collective-permute-start | bytes 147464 | tf_op jit(solution)/shard_map/ppermute | solution.py:94
  56.5 4.7 %copy-start.3 = (bf16[384,96]{0,1:T(8,128)(2,1)S(1)}, bf16[384,96]{0,1:T(8,128)(2,1)}, u32[]{:S(2)}) copy-start(bf16[384,96]{0,1:T(8,128)(2,1)} %param.32) | copy-start | bytes 221188
  56.5 4.7 %copy-start.6 = (bf16[96,8]{0,1:T(8,128)(2,1)S(1)}, bf16[96,8]{0,1:T(8,128)(2,1)}, u32[]{:S(2)}) copy-start(bf16[96,8]{0,1:T(8,128)(2,1)} %param.34) | copy-start | bytes 4612
  61.2 7.3 %copy-start.17 = (bf16[8,96]{1,0:T(8,128)(2,1)S(1)}, bf16[8,96]{1,0:T(8,128)(2,1)}, u32[]{:S(2)}) copy-start(bf16[8,96]{1,0:T(8,128)(2,1)} %param.35) | copy-start | bytes 4612
  63.9 1.2 %collective-permute-start.11 = (bf16[12,8,128]{2,1,0:T(8,128)(2,1)S(1)}, bf16[12,8,128]{2,1,0:T(8,128)(2,1)S(1)}, u32[]{:S(2)}, u32[]{:S(2)}) collective-permute-start(bf16[12,8,128]{2,1,0:T(8,128)(2,1)S(1)} %get-tuple-element.60.own_ref), channel_id=1, source_target_pairs={{0,4},{4,0},{8,12},{12,8},{16,20},{20,16},{24,28},{28,24},{1,5},{5... | collective-permute-start | bytes 73736 | tf_op jit(solution)/shard_map/ppermute | solution.py:498
  65.1 4.6 %collective-permute-start.14 = (bf16[2,12,8,128]{3,2,1,0:T(8,128)(2,1)S(1)}, bf16[2,12,8,128]{3,2,1,0:T(8,128)(2,1)S(1)}, u32[]{:S(2)}, u32[]{:S(2)}) collective-permute-start(bf16[2,12,8,128]{3,2,1,0:T(8,128)(2,1)S(1)} %surface_pair.1.pair_ref), channel_id=1, source_target_pairs={{0,8},{4,12},{8,0},{12,4},{16,24},{20,28},{24,16},{28,20},{1,9},{5... | collective-permute-start | bytes 147464 | tf_op jit(solution)/shard_map/ppermute | solution.py:498
  66.6 4.6 %collective-permute-start.13 = (bf16[2,12,8,128]{3,2,1,0:T(8,128)(2,1)S(1)}, bf16[2,12,8,128]{3,2,1,0:T(8,128)(2,1)S(1)}, u32[]{:S(2)}, u32[]{:S(2)}) collective-permute-start(bf16[2,12,8,128]{3,2,1,0:T(8,128)(2,1)S(1)} %surface_pair.1.pair_ref), channel_id=1, source_target_pairs={{0,16},{4,20},{8,24},{12,28},{16,0},{20,4},{24,8},{28,12},{1,17},{... | collective-permute-start | bytes 147464 | tf_op jit(solution)/shard_map/ppermute | solution.py:498
  67.3 5.0 %collective-permute-start.12 = (bf16[2,12,8,128]{3,2,1,0:T(8,128)(2,1)S(1)}, bf16[2,12,8,128]{3,2,1,0:T(8,128)(2,1)S(1)}, u32[]{:S(2)}, u32[]{:S(2)}) collective-permute-start(bf16[2,12,8,128]{3,2,1,0:T(8,128)(2,1)S(1)} %surface_pair.1.pair_ref), channel_id=1, source_target_pairs={{0,24},{4,28},{8,16},{12,20},{16,8},{20,12},{24,0},{28,4},{1,25},{... | collective-permute-start | bytes 147464 | tf_op jit(solution)/shard_map/ppermute | solution.py:498

commit v10 on v9

--- a/solution.py
+++ b/solution.py
@@ -219,38 +219,55 @@
     )(x, taps)
 
 
-def prepare_kernel(k_ref, g_ref, up_ref, s_ref, _, band_ref, mat_ref, upt_ref, gain_ref, scale_ref, base):
+def window(members, rows):
+    share = rows // members
+    span = share + 2 * HALO
+    first = lax.axis_index("member") * share - HALO
+    return span, first, jnp.clip(first, 0, rows - span)
+
+
+def prepare_kernel(members, k_ref, g_ref, up_ref, s_ref, lift_ref, ocean_ref, _, *refs):
+    band_ref, mat_ref, upt_ref, gain_ref, scale_ref, lift_out, win_ref, base, sem = refs
     lanes = gain_ref.shape[1]
+    span, _, start = window(members, ocean_ref.shape[0])
+    copy = pltpu.make_async_copy(ocean_ref.at[pl.ds(start, span)], win_ref, sem)
+    copy.start()
     mat_ref[...] = halo_matrix(lanes)
     upt_ref[...] = transposed(up_ref[...])
     gain_ref[...] = spread(g_ref[...], lanes)
     scale_ref[...] = spread(s_ref[...], lanes)
+    lift_out[...] = jnp.concatenate([transposed(lift_ref[0]), transposed(lift_ref[1])], axis=0)
     fill_base(lambda i: k_ref[i], base)
     for g in range(base.shape[0]):
         fill_band(base, g, band_ref.at[g])
-
-
-def prepare_ocean(taps, gain, up, scale, after):
+    copy.wait()
+
+
+def prepare_ocean(members, taps, gain, up, scale, lift, ocean, after):
     chans, hid = up.shape
-    lanes = after.shape[-1]
+    rows, _, lanes = ocean.shape
+    flux = lift.shape[1]
     groups = chans // GROUP
     wide = TAPS * DEPTH
-    return pl.pallas_call(
-        prepare_kernel,
+    span = rows // members + 2 * HALO
+    return pl.pallas_call(
+        functools.partial(prepare_kernel, members),
         out_shape=[
             jax.ShapeDtypeStruct((groups, GROUP * OUT, wide), BF),
             jax.ShapeDtypeStruct((2 * lanes, (TAPS - 1) * lanes), BF),
             jax.ShapeDtypeStruct((hid, chans), BF),
             jax.ShapeDtypeStruct((chans, lanes), F32),
             jax.ShapeDtypeStruct((chans, lanes), F32),
+            jax.ShapeDtypeStruct((2 * chans, flux), BF),
+            jax.ShapeDtypeStruct((span, chans, lanes), BF),
         ],
-        in_specs=[VMEM] * 4 + [ANY],
-        out_specs=[VMEM] * 5,
-        scratch_shapes=[pltpu.VMEM((groups, GROUP, wide), F32)],
+        in_specs=[VMEM] * 5 + [HBM, ANY],
+        out_specs=[VMEM] * 7,
+        scratch_shapes=[pltpu.VMEM((groups, GROUP, wide), F32), pltpu.SemaphoreType.DMA(())],
         compiler_params=params(24),
         cost_estimate=cost(3),
         name="prepare_ocean",
-    )(taps, gain[None], up, scale[None], after)
+    )(taps, gain[None], up, scale[None], lift, ocean, after)
 
 
 def ocean_conv_kernel(x_ref, band_ref, a_ref, xj):
@@ -302,7 +319,6 @@
 
 def halo_conv(first, second, band, wrapped, matrix, xe, halo):
     blocks, chans, lanes = halo.shape
-    wide = TAPS * DEPTH
     both = []
     for q in range(blocks):
         left, right = by_side(first[q], second[q])
@@ -331,16 +347,22 @@
     field = jnp.concatenate(tall, axis=0)
     moved = jnp.dot(field, matrix, preferred_element_type=F32)
     count = len(tall)
+    span = xe.shape[1]
     for a in range(TAPS - 1):
         part = moved[:, a * lanes : (a + 1) * lanes].astype(BF)
         xe[a, :count] = part.reshape(count, chans, lanes)
-        xe[a, count:] = jnp.zeros((SPAN - count, chans, lanes), BF)
-    low = HALO * DEPTH
+        if count < span:
+            xe[a, count:] = jnp.zeros((span - count, chans, lanes), BF)
+    tops = slice(0, blocks * GROUP)
+    side = [j for j in range(TAPS) if j != HALO]
     for g in range(chans // GROUP):
         at = slice(GROUP * g, GROUP * (g + 1))
-        rhs = jnp.concatenate([xe[a, :, at, :].reshape(DEPTH, lanes) for a in range(TAPS - 1)], axis=0)
-        tops = slice(0, blocks * GROUP)
-        lhs = jnp.concatenate([band[g, tops, :low], band[g, tops, low + DEPTH : wide]], axis=1)
+        rhs = jnp.concatenate(
+            [xe[a, :, at, :].reshape(span * GROUP, lanes) for a in range(TAPS - 1)], axis=0
+        )
+        lhs = jnp.concatenate(
+            [band[g, tops, j * DEPTH : j * DEPTH + span * GROUP] for j in side], axis=1
+        )
         out = jnp.dot(lhs, rhs, preferred_element_type=F32)
         halo[:, at, :] = out.reshape(blocks, GROUP, lanes)
 
@@ -500,27 +522,20 @@
 
 def force_kernel(members, *refs):
     near_refs, flux_refs = refs[:2], refs[2 : members // 2 + 1]
-    ocean_ref, land_ref, ice_ref, lift_ref, mid_ref, p_ref, win, sem = refs[members // 2 + 1 :]
-    span, flux, lanes = flux_refs[0].shape
+    win_ref, land_ref, ice_ref, lift_ref, mid_ref, p_ref = refs[members // 2 + 1 :]
+    lanes = land_ref.shape[1]
     rows = land_ref.shape[0]
     chans = mid_ref.shape[1]
-    share = rows // members
     blocks = p_ref.shape[0]
-    first = lax.axis_index("member") * share - HALO
-    start = jnp.clip(first, 0, rows - span)
-    copy = pltpu.make_async_copy(ocean_ref.at[pl.ds(start, span)], win, sem)
-    copy.start()
+    span, first, start = window(members, rows)
     total = near_refs[0][0].astype(F32) + near_refs[1][0].astype(F32)
     for ref in flux_refs:
         total = total + ref[...].astype(F32)
     low = (total / members).astype(BF)
-    lift = jnp.concatenate([transposed(lift_ref[0]), transposed(lift_ref[1])], axis=0)
-    terms = jnp.dot(
-        lift, jnp.concatenate([low[r] for r in range(span)], axis=1), preferred_element_type=F32
-    )
+    columns = jnp.concatenate([low[r] for r in range(span)], axis=1)
+    terms = jnp.dot(lift_ref[...], columns, preferred_element_type=F32)
     keep = edge_lanes((chans, lanes)).astype(F32).astype(BF)
     packed = [None] * blocks
-    copy.wait()
     for r in range(span):
         row = first + r
         safe = jnp.clip(row, 0, rows - 1)
@@ -528,7 +543,7 @@
         ice = ice_ref[pl.ds(safe, 1), :].astype(F32)
         at = slice(r * lanes, (r + 1) * lanes)
         forcing = sea * ((1.0 - ice) * terms[:chans, at] + ice * terms[chans:, at])
-        mid = win[jnp.clip(row - start, 0, span - 1)].astype(F32) + forcing
+        mid = win_ref[jnp.clip(row - start, 0, span - 1)].astype(F32) + forcing
         inside = (row >= 0) & (row < rows)
         mid = jnp.where(inside, mid, 0.0).astype(BF)
         mid_ref[r] = mid
@@ -541,21 +556,19 @@
         p_ref[q] = packed[q]
 
 
-def force(members, chunks, ocean, land, ice, lift):
-    span, _, lanes = chunks[-1].shape
-    rows, chans, _ = ocean.shape
+def force(members, chunks, win, land, ice, lift):
+    span, chans, lanes = win.shape
     return pl.pallas_call(
         functools.partial(force_kernel, members),
         out_shape=[
             jax.ShapeDtypeStruct((span, chans, lanes), BF),
             jax.ShapeDtypeStruct((OCEAN_BLOCKS, chans, lanes), BF),
         ],
-        in_specs=[VMEM] * len(chunks) + [HBM, VMEM, VMEM, VMEM],
+        in_specs=[VMEM] * (len(chunks) + 4),
         out_specs=[VMEM] * 2,
-        scratch_shapes=[pltpu.VMEM((span, chans, lanes), BF), pltpu.SemaphoreType.DMA(())],
         compiler_params=params(24),
         name="ocean_forcing",
-    )(*chunks, ocean, land, ice, lift)
+    )(*chunks, win, land, ice, lift)
 
 
 def ocean_kernel(mid_ref, a_ref, left_ref, right_ref, band_ref, land_ref, mat_ref, upt_ref, gain_ref, scale_ref, dn_ref, sw_ref, new_ref, surf_ref, xe, halo, normed):
@@ -590,7 +603,7 @@
         in_specs=[VMEM] * 12,
         out_specs=[VMEM] * 2,
         scratch_shapes=[
-            pltpu.VMEM((TAPS - 1, SPAN, chans, lanes), BF),
+            pltpu.VMEM((TAPS - 1, OCEAN_BLOCKS + 2 * HALO, chans, lanes), BF),
             pltpu.VMEM((blocks, chans, lanes), F32),
             pltpu.VMEM((chans, share * lanes), BF),
         ],
@@ -615,49 +628,46 @@
     )(own, got)
 
 
-def couple_kernel(k, y_ref, land_ref, bw_ref, pair_ref, *refs):
+def couple_kernel(ks, y_ref, land_ref, bw_ref, *refs):
+    pair_refs = refs[: len(ks)]
     o_ref, buf, sems = refs[-3:]
     chans, lanes = y_ref.shape[1:]
-    share = pair_ref.shape[1]
+    share = pair_refs[0].shape[1]
     rank = lax.axis_index("member")
     parity = rank % 2
-    first = ((rank // 2) ^ k) * 2 * share
-    surf = [pair_ref[side ^ parity, r] for side in range(2) for r in range(share)]
-    back = jnp.dot(bw_ref[...], jnp.concatenate(surf, axis=1), preferred_element_type=F32)
     copies = []
-    piece = share // 2
-    for n in range(4):
-        for r in range(n * piece, (n + 1) * piece):
+    for n, (k, pair_ref) in enumerate(zip(ks, pair_refs)):
+        first = ((rank // 2) ^ k) * 2 * share
+        surf = [pair_ref[side ^ parity, r] for side in range(2) for r in range(share)]
+        back = jnp.dot(bw_ref[...], jnp.concatenate(surf, axis=1), preferred_element_type=F32)
+        for r in range(2 * share):
             sea = (1 - land_ref[pl.ds(first + r, 1), :]).astype(F32)
             out = y_ref[first + r].astype(F32) + sea * back[:, r * lanes : (r + 1) * lanes]
-            buf[r] = out.astype(BF)
+            buf[n, r] = out.astype(BF)
         copies.append(
-            pltpu.make_async_copy(
-                buf.at[pl.ds(n * piece, piece)],
-                o_ref.at[pl.ds(first + n * piece, piece)],
-                sems.at[n],
-            )
+            pltpu.make_async_copy(buf.at[n], o_ref.at[pl.ds(first, 2 * share)], sems.at[n])
         )
         copies[n].start()
     for copy in copies:
         copy.wait()
 
 
-def couple(k, y, land, back_weight, pair, earlier):
+def couple(ks, y, land, back_weight, pairs, earlier):
     _, chans, lanes = y.shape
-    return pl.pallas_call(
-        functools.partial(couple_kernel, k),
+    count = len(ks)
+    return pl.pallas_call(
+        functools.partial(couple_kernel, ks),
         out_shape=jax.ShapeDtypeStruct(y.shape, BF),
-        in_specs=[VMEM] * 4 + [HBM] * len(earlier),
+        in_specs=[VMEM] * (3 + count) + [HBM] * len(earlier),
         out_specs=HBM,
         scratch_shapes=[
-            pltpu.VMEM((2 * pair.shape[1], chans, lanes), BF),
-            pltpu.SemaphoreType.DMA((4,)),
+            pltpu.VMEM((count, 2 * pairs[0].shape[1], chans, lanes), BF),
+            pltpu.SemaphoreType.DMA((count,)),
         ],
-        input_output_aliases={4: 0} if earlier else {},
+        input_output_aliases={3 + count: 0} if earlier else {},
         compiler_params=params(24),
         name="couple",
-    )(y, land, back_weight, pair, *earlier)
+    )(y, land, back_weight, *pairs, *earlier)
 
 
 def local(
@@ -685,11 +695,11 @@
     state = atmos[0]
     rows = state.shape[0]
     blocks = rows // SLOTS
-    big, small = 4 * blocks, 2 * blocks
+    small = 2 * blocks
     atm = (atm_gain, atm_up, atm_down.transpose(0, 2, 1), atm_scale)
     taps = atm_kernel.transpose(1, 2, 0, 3)
 
-    edges = neighbours(pack(state, big))
+    edges = neighbours(pack(state, small))
     a, band = convolve(0, state, taps, blocks)
     steps = rows // small
     near_steps = (rows // 2) // small - 1
@@ -712,9 +722,11 @@
     got = send_xor(give, 1)
     sums = add_pairs(keep, got, 1)
     sent += [send_xor(part, 2 * k + 2) for k, part in enumerate(sums)]
-    band, *ready = prepare_ocean(ocn_kernel, ocn_gain, ocn_up, ocn_scale, sums[0])
+    band, *ready, lift, win = prepare_ocean(
+        members, ocn_kernel, ocn_gain, ocn_up, ocn_scale, flux_lift, ocean, sums[0]
+    )
     sent = [keep, got] + sent
-    mid, packed = force(members, sent, ocean, land_mask, ice_mask, flux_lift)
+    mid, packed = force(members, sent, win, land_mask, ice_mask, lift)
     left, right = neighbours(packed)
     a = ocean_conv(mid, band)
     ocean_rows, surface = ocean_block(
@@ -722,10 +734,9 @@
     )
     own = make_pair(surface, send_xor(surface, 1))
     pairs = [own] + [send_xor(own, 2 * k) for k in range(1, half)]
-    out = []
-    for k, pair in enumerate(pairs):
-        out = [couple(k, state, land_mask, back_weight.T, pair, out)]
-    out = out[0]
+    out = couple((0,), state, land_mask, back_weight.T, pairs[:1], [])
+    rest = tuple(range(1, half))
+    out = couple(rest, state, land_mask, back_weight.T, pairs[1:], [out])
     return (out[None], ocean_rows)
 
 

time: 73.6 us -> 73.5 us (level)
  Pallas kernels: 43.6 us -> 42.2 us
  waiting for transfers between devices: 10.7 us -> 12 us
    ppermute x9, waiting for transfers between devices: 6.81 us -> 8.26 us  [send_xor(): lax.ppermute(value, 'member', [(i, i ^ bits) for i in range(members)])]
    pallas_call x5 -> x3, Pallas kernels: 5.3 us -> 4.37 us  [the longest x2 2.63 us: couple(): pl.pallas_call(functools.partial(couple_kernel, ks), out_shape=jax.ShapeD...]
    pallas_call x1, Pallas kernels: 1.27 us -> 0.52 us  [force(): pl.pallas_call(functools.partial(force_kernel, members), out_shape=[jax.S...]
  transfers between devices with their start and end apart: 15 -> 15, of which waited for: 8 -> 8; matrix products, arithmetic and copies ran while one was open for 0% -> 0% of each run, Pallas kernels for 29% -> 28%
where the time goes in v10:
time: 73.5 us; the launch traced here: 73.3 us
  Pallas kernels  42.2 us (57%)
  starting transfers between devices  17.7 us (24%)
  waiting for transfers between devices  12 us (16%)
  between operations  1.13 us (2%)
    pallas_call x3, Pallas kernels, atmos_block(): pl.pallas_call(functools.partial(atmos_kernel, layer, near, members, coun...  17.3 us
    pallas_call x2, Pallas kernels, convolve(): pl.pallas_call(functools.partial(conv_kernel, layer), out_shape=[jax.Shap...  13.1 us
    ppermute x9, waiting for transfers between devices, send_xor(): lax.ppermute(value, 'member', [(i, i ^ bits) for i in range(members)])  8.26 us
    ppermute x9, starting transfers between devices, send_xor(): lax.ppermute(value, 'member', [(i, i ^ bits) for i in range(members)])  7.64 us
    ppermute x3, starting transfers between devices, neighbours(): lax.ppermute(packed, 'lon', [(i, (i - 1) % count if i % 2 == 0 else (i +...  6.33 us
    ppermute x3, waiting for transfers between devices, neighbours(): lax.ppermute(packed, 'lon', [(i, (i - 1) % count if i % 2 == 0 else (i +...  3.76 us
    ppermute x3, starting transfers between devices, neighbours(): first = lax.ppermute(packed, 'lon', [(i, i ^ 1) for i in range(count)])  3.75 us
    pallas_call x1, Pallas kernels, pack(): pl.pallas_call(functools.partial(pack_kernel, step), out_shape=jax.ShapeD...  3 us
  transfers between devices with their start and end apart: 15, of which 8 were waited for; matrix products, arithmetic and copies ran while one was open for 0% of the time, Pallas kernels for 28%

profile of v10, /device:TPU:0, one launch (start us, length us, event | category | flops | bytes accessed | tf_op | source)
XLA Modules:
  0.0 73.3 jit_solution(15450017660932151496)
XLA Ops:
  0.6 0.0 copy-start
  0.6 0.0 copy-start.9
  0.6 3.0 %pack_edges.1 = bf16[6,96,128]{2,1,0:T(8,128)(2,1)} custom-call(bf16[96,96,128]{2,1,0:T(8,128)(2,1)} %bitcast.10), custom_call_target="tpu_custom_call" | custom-call | tf_op jit(solution)/shard_map/pack_edges/pallas_call | solution.py:81
  3.7 3.1 %collective-permute-start = (bf16[6,96,128]{2,1,0:T(8,128)(2,1)}, bf16[6,96,128]{2,1,0:T(8,128)(2,1)S(1)}, u32[]{:S(2)}, u32[]{:S(2)}) collective-permute-start(bf16[6,96,128]{2,1,0:T(8,128)(2,1)} %pack_edges.1), channel_id=1, source_target_pairs={{0,1},{1,0},{2,3},{3,2},{4,5},{5,4},{6,7},{7,6},{8,9},{9,8},{10,11... | collective-permute-start | bytes 442376 | tf_op jit(solution)/shard_map/ppermute | solution.py:94
  6.7 2.5 %collective-permute-start.1 = (bf16[6,96,128]{2,1,0:T(8,128)(2,1)}, bf16[6,96,128]{2,1,0:T(8,128)(2,1)S(1)}, u32[]{:S(2)}, u32[]{:S(2)}) collective-permute-start(bf16[6,96,128]{2,1,0:T(8,128)(2,1)} %pack_edges.1), channel_id=1, source_target_pairs={{0,3},{1,2},{2,1},{3,0},{4,7},{5,6},{6,5},{7,4},{8,11},{9,10},{10,... | collective-permute-start | bytes 442376 | tf_op jit(solution)/shard_map/ppermute | solution.py:95
  9.2 0.0 copy-done
  9.2 0.0 copy-done.9
  9.2 0.0 copy-start.13
  9.2 0.0 copy-start.14
  9.3 6.6 %conv.2 = (f32[96,96,128]{2,1,0:T(8,128)S(1)}, bf16[6,96,1792]{2,1,0:T(8,128)(2,1)S(1)}) custom-call(bf16[96,96,128]{2,1,0:T(8,128)(2,1)S(1)} %bitcast.11, f32[7,7,2,96]{3,2,1,0:T(2,128)S(1)} %bitcast.20), custom_call_target="tpu_custom_call" | custom-call | flops 8000000000 | tf_op jit(solution)/shard_map/conv/pallas_call | solution.py:203
  15.8 0.0 collective-permute-done.refs_6_
  15.8 0.4 collective-permute-done.1.refs_7_
  16.3 0.0 copy-done.7
  16.3 7.9 %atmos_block.3 = (bf16[96,96,128]{2,1,0:T(8,128)(2,1)S(1)}, bf16[6,96,128]{2,1,0:T(8,128)(2,1)S(1)}) custom-call(bf16[96,96,128]{2,1,0:T(8,128)(2,1)S(1)} %bitcast.12, f32[96,96,128]{2,1,0:T(8,128)S(1)} %get-tuple-element.34.refs_1_, f32[2,96]{1,0:T(2,128)S(1)} %copy-done.13, bf16[2,96,384]{2,1,0:T(8,128)(2,1)S(1)} %copy-done.6, ...), custom_call_target="tpu_custom_call" | custom-call | flops 8000000000 | tf_op jit(solution)/shard_map/atmos_block/pallas_call | solution.py:487
  24.1 0.7 collective-permute-start.2
  24.8 2.6 %collective-permute-start.3 = (bf16[6,96,128]{2,1,0:T(8,128)(2,1)S(1)}, bf16[6,96,128]{2,1,0:T(8,128)(2,1)S(1)}, u32[]{:S(2)}, u32[]{:S(2)}) collective-permute-start(bf16[6,96,128]{2,1,0:T(8,128)(2,1)S(1)} %get-tuple-element.38), channel_id=1, source_target_pairs={{0,3},{1,2},{2,1},{3,0},{4,7},{5,6},{6,5},{7,4},{8,11},{9,10},{10,... | collective-permute-start | bytes 442376 | tf_op jit(solution)/shard_map/ppermute | solution.py:95
  27.4 6.6 %conv.3 = (f32[96,96,128]{2,1,0:T(8,128)S(1)}, bf16[6,96,1792]{2,1,0:T(8,128)(2,1)S(1)}) custom-call(bf16[96,96,128]{2,1,0:T(8,128)(2,1)S(1)} %get-tuple-element.36.x_ref.refs_0_, f32[7,7,2,96]{3,2,1,0:T(2,128)S(1)} %bitcast.21), custom_call_target="tpu_custom_call" | custom-call | flops 8000000000 | tf_op jit(solution)/shard_map/conv/pallas_call | solution.py:203
  34.0 0.0 collective-permute-done.2.refs_7_
  34.0 0.0 collective-permute-done.3.refs_8_
  34.0 0.0 copy-done.12
  34.0 6.5 %atmos_block.4 = (bf16[96,96,128]{2,1,0:T(8,128)(2,1)S(1)}, bf16[2,18,32,128]{3,2,1,0:T(8,128)(2,1)S(1)}, bf16[2,18,32,128]{3,2,1,0:T(8,128)(2,1)S(1)}, bf16[102...) custom-call(bf16[96,96,128]{2,1,0:T(8,128)(2,1)S(1)} %get-tuple-element.36.x_ref.refs_0_, ...), custom_call_target="tpu_custom_call" | custom-call | flops 5000000000 | tf_op jit(solution)/shard_map/atmos_block/pallas_call | solution.py:487
  40.5 0.1 collective-permute-start.4
  40.6 0.0 copy-start.5
  40.6 0.0 copy-start.8
  40.6 0.0 copy-start.10
  40.6 0.0 copy-start.11
  40.6 0.0 copy-start.15
  40.6 0.0 copy-start.16
  40.6 3.0 %atmos_block.5 = (bf16[96,96,128]{2,1,0:T(8,128)(2,1)S(1)}, bf16[2,18,32,128]{3,2,1,0:T(8,128)(2,1)S(1)}, bf16[2,18,32,128]{3,2,1,0:T(8,128)(2,1)S(1)}) custom-call(bf16[96,96,128]{2,1,0:T(8,128)(2,1)S(1)} %get-tuple-element.36.x_ref.refs_0_, f32[96,96,128]{2,1,0:T(8,128)S(1)} %get-tuple-element.37.refs_1_, ...), custom_call_target="tpu_custom_call", output_to_operand_aliasing={{0}: (7, {})} | custom-call | flops 3000000000 | tf_op jit(solution)/shard_map/atmos_block/pallas_call | solution.py:487
  43.7 0.0 collective-permute-done.4.got_ref
  43.7 0.1 add_pairs.2
  43.7 0.5 collective-permute-start.5
  44.3 2.5 %collective-permute-start.6 = (bf16[18,32,128]{2,1,0:T(8,128)(2,1)S(1)}, bf16[18,32,128]{2,1,0:T(8,128)(2,1)S(1)}, u32[]{:S(2)}, u32[]{:S(2)}) collective-permute-start(bf16[18,32,128]{2,1,0:T(8,128)(2,1)S(1)} %get-tuple-element.53), channel_id=1, source_target_pairs={{0,24},{4,28},{8,16},{12,20},{16,8},{20,12},{24,0},{28,4},{1,25},{... | collective-permute-start | bytes 442376 | tf_op jit(solution)/shard_map/ppermute | solution.py:520
  46.7 0.5 collective-permute-start.7
  47.2 0.0 collective-permute-done.5.got_ref.refs_1_
  47.3 0.6 collective-permute-start.8
  47.9 0.0 copy-done.10
  47.9 0.0 copy-start.1
  47.9 0.0 copy-start.3
  47.9 1.7 %prepare_ocean.1 = (bf16[6,160,1792]{2,1,0:T(8,128)(2,1)S(1)}, bf16[256,768]{1,0:T(8,128)(2,1)S(1)}, bf16[384,96]{1,0:T(8,128)(2,1)S(1)}, f32[96,128]{1,0:T(8,12...) custom-call(f32[7,7,96]{2,1,0:T(8,128)S(1)} %copy-done.10, ...), custom_call_target="tpu_custom_call" | custom-call | flops 3000000000 | tf_op jit(solution)/shard_map/prepare_ocean/pallas_call | solution.py:253
  49.7 1.8 %collective-permute-done.6.refs_2_ = bf16[18,32,128]{2,1,0:T(8,128)(2,1)S(1)} collective-permute-done((bf16[18,32,128]{2,1,0:T(8,128)(2,1)S(1)}, bf16[18,32,128]{2,1,0:T(8,128)(2,1)S(1)}, u32[]{:S(2)}, u32[]{:S(2)}) %collective-permute-start.6) | collective-permute-done | bytes 147488 | tf_op jit(solution)/shard_map/ppermute | solution.py:520
  51.5 2.6 %collective-permute-done.7.refs_3_ = bf16[18,32,128]{2,1,0:T(8,128)(2,1)S(1)} collective-permute-done((bf16[18,32,128]{2,1,0:T(8,128)(2,1)S(1)}, bf16[18,32,128]{2,1,0:T(8,128)(2,1)S(1)}, u32[]{:S(2)}, u32[]{:S(2)}) %collective-permute-start.7) | collective-permute-done | bytes 147488 | tf_op jit(solution)/shard_map/ppermute | solution.py:520
  54.2 0.1 collective-permute-done.8.refs_4_
  54.3 0.5 ocean_forcing.1
  54.8 1.3 %collective-permute-start.10 = (bf16[2,96,128]{2,1,0:T(8,128)(2,1)S(1)}, bf16[2,96,128]{2,1,0:T(8,128)(2,1)S(1)}, u32[]{:S(2)}, u32[]{:S(2)}) collective-permute-start(bf16[2,96,128]{2,1,0:T(8,128)(2,1)S(1)} %get-tuple-element.59), channel_id=1, source_target_pairs={{0,3},{1,2},{2,1},{3,0},{4,7},{5,6},{6,5},{7,4},{8,11},{9,10},{10,... | collective-permute-start | bytes 147464 | tf_op jit(solution)/shard_map/ppermute | solution.py:95
  56.1 0.0 collective-permute-start.9
  56.1 1.4 %ocean_conv.1.a_ref = f32[12,96,128]{2,1,0:T(8,128)S(1)} custom-call(bf16[18,96,128]{2,1,0:T(8,128)(2,1)S(1)} %get-tuple-element.57.x_ref.mid_ref, bf16[6,160,1792]{2,1,0:T(8,128)(2,1)S(1)} %get-tuple-element.58.band_ref), custom_call_target="tpu_custom_call" | custom-call | flops 2000000000 | tf_op jit(solution)/shard_map/ocean_conv/pallas_call | solution.py:284
  57.4 3.3 %collective-permute-done.10.right_ref = bf16[2,96,128]{2,1,0:T(8,128)(2,1)S(1)} collective-permute-done((bf16[2,96,128]{2,1,0:T(8,128)(2,1)S(1)}, bf16[2,96,128]{2,1,0:T(8,128)(2,1)S(1)}, u32[]{:S(2)}, u32[]{:S(2)}) %collective-permute-start.10) | collective-permute-done | bytes 49184 | tf_op jit(solution)/shard_map/ppermute | solution.py:95
  60.8 0.0 collective-permute-done.9.left_ref
  60.8 0.0 copy-done.2
  60.8 0.0 copy-start.17
  60.8 2.4 %ocean_block.1 = (bf16[12,96,128]{2,1,0:T(8,128)(2,1)}, bf16[12,8,128]{2,1,0:T(8,128)(2,1)S(1)}) custom-call(bf16[18,96,128]{2,1,0:T(8,128)(2,1)S(1)} %get-tuple-element.57.x_ref.mid_ref, f32[12,96,128]{2,1,0:T(8,128)S(1)} %ocean_conv.1.a_ref, bf16[2,96,128]{2,1,0:T(8,128)(2,1)S(1)} %collective-permute-done.9.left_ref, ...), custom_call_target="tpu_custom_call" | custom-call | tf_op jit(solution)/shard_map/ocean_block/pallas_call | solution.py:597
  63.2 0.0 collective-permute-start.11
  63.2 1.2 %collective-permute-done.11.got_ref = bf16[12,8,128]{2,1,0:T(8,128)(2,1)S(1)} collective-permute-done((bf16[12,8,128]{2,1,0:T(8,128)(2,1)S(1)}, bf16[12,8,128]{2,1,0:T(8,128)(2,1)S(1)}, u32[]{:S(2)}, u32[]{:S(2)}) %collective-permute-start.11) | collective-permute-done | bytes 24608 | tf_op jit(solution)/shard_map/ppermute | solution.py:520
  64.4 1.5 %collective-permute-start.12 = (bf16[2,12,8,128]{3,2,1,0:T(8,128)(2,1)S(1)}, bf16[2,12,8,128]{3,2,1,0:T(8,128)(2,1)S(1)}, u32[]{:S(2)}, u32[]{:S(2)}) collective-permute-start(bf16[2,12,8,128]{3,2,1,0:T(8,128)(2,1)S(1)} %surface_pair.1.refs_0_), channel_id=1, source_target_pairs={{0,8},{4,12},{8,0},{12,4},{16,24},{20,28},{24,16},{28,20},{1,9},{5... | collective-permute-start | bytes 147464 | tf_op jit(solution)/shard_map/ppermute | solution.py:520
  65.9 0.7 collective-permute-start.13
  66.6 1.3 %collective-permute-start.14 = (bf16[2,12,8,128]{3,2,1,0:T(8,128)(2,1)S(1)}, bf16[2,12,8,128]{3,2,1,0:T(8,128)(2,1)S(1)}, u32[]{:S(2)}, u32[]{:S(2)}) collective-permute-start(bf16[2,12,8,128]{3,2,1,0:T(8,128)(2,1)S(1)} %surface_pair.1.refs_0_), channel_id=1, source_target_pairs={{0,24},{4,28},{8,16},{12,20},{16,8},{20,12},{24,0},{28,4},{1,25},{... | collective-permute-start | bytes 147464 | tf_op jit(solution)/shard_map/ppermute | solution.py:520
  67.9 0.0 copy-done.17
  67.9 0.1 copy.22
  68.0 1.1 %couple.2.refs_3_ = bf16[96,96,128]{2,1,0:T(8,128)(2,1)} custom-call(bf16[96,96,128]{2,1,0:T(8,128)(2,1)S(1)} %get-tuple-element.43.y_ref, s32[96,128]{1,0:T(8,128)S(1)} %copy-done.1, bf16[96,8]{1,0:T(8,128)(2,1)S(1)} %bitcast.13, bf16[2,12,8,128]{3,2,1,0:T(8,128)(2,1)S(1)} %surface_pair.1.refs_0_), custom_call_target="tpu_custom_call" | custom-call | tf_op jit(solution)/shard_map/couple/pallas_call | solution.py:658
  69.1 0.0 collective-permute-done.12.refs_0_
  69.2 1.4 %collective-permute-done.13.refs_1_ = bf16[2,12,8,128]{3,2,1,0:T(8,128)(2,1)S(1)} collective-permute-done((bf16[2,12,8,128]{3,2,1,0:T(8,128)(2,1)S(1)}, bf16[2,12,8,128]{3,2,1,0:T(8,128)(2,1)S(1)}, u32[]{:S(2)}, u32[]{:S(2)}) %collective-permute-start.13) | collective-permute-done | bytes 49184 | tf_op jit(solution)/shard_map/ppermute | solution.py:520
  70.5 1.1 %collective-permute-done.14.refs_2_ = bf16[2,12,8,128]{3,2,1,0:T(8,128)(2,1)S(1)} collective-permute-done((bf16[2,12,8,128]{3,2,1,0:T(8,128)(2,1)S(1)}, bf16[2,12,8,128]{3,2,1,0:T(8,128)(2,1)S(1)}, u32[]{:S(2)}, u32[]{:S(2)}) %collective-permute-start.14) | collective-permute-done | bytes 49184 | tf_op jit(solution)/shard_map/ppermute | solution.py:520
  71.6 1.5 %couple.3 = bf16[96,96,128]{2,1,0:T(8,128)(2,1)} custom-call(bf16[96,96,128]{2,1,0:T(8,128)(2,1)S(1)} %get-tuple-element.43.y_ref, s32[96,128]{1,0:T(8,128)S(1)} %copy-done.1, bf16[96,8]{1,0:T(8,128)(2,1)S(1)} %bitcast.14, bf16[2,12,8,128]{3,2,1,0:T(8,128)(2,1)S(1)} %collective-permute-done.12.refs_0_, ...), custom_call_target="tpu_custom_call", output_to_operand_aliasing={{}: (6, {})} | custom-call | tf_op jit(solution)/shard_map/couple/pallas_call | solution.py:658
  (18 shorter events, 0.1 us)
Async XLA Ops:
  0.6 8.6 %copy-start = (bf16[1,96,96,128]{3,2,1,0:T(8,128)(2,1)S(1)}, bf16[1,96,96,128]{3,2,1,0:T(8,128)(2,1)}, u32[]{:S(2)}) copy-start(bf16[1,96,96,128]{3,2,1,0:T(8,128)(2,1)} %param.18) | copy-start | bytes 7077892
  0.6 8.6 %copy-start.9 = (f32[2,7,7,96]{3,0,2,1:T(2,128)S(1)}, f32[2,7,7,96]{3,0,2,1:T(2,128)}, u32[]{:S(2)}) copy-start(f32[2,7,7,96]{3,0,2,1:T(2,128)} %param.22) | copy-start | bytes 112900
  3.7 12.2 %collective-permute-start = (bf16[6,96,128]{2,1,0:T(8,128)(2,1)}, bf16[6,96,128]{2,1,0:T(8,128)(2,1)S(1)}, u32[]{:S(2)}, u32[]{:S(2)}) collective-permute-start(bf16[6,96,128]{2,1,0:T(8,128)(2,1)} %pack_edges.1), channel_id=1, source_target_pairs={{0,1},{1,0},{2,3},{3,2},{4,5},{5,4},{6,7},{7,6},{8,9},{9,8},{10,11... | collective-permute-start | bytes 442376 | tf_op jit(solution)/shard_map/ppermute | solution.py:94
  6.7 9.5 %collective-permute-start.1 = (bf16[6,96,128]{2,1,0:T(8,128)(2,1)}, bf16[6,96,128]{2,1,0:T(8,128)(2,1)S(1)}, u32[]{:S(2)}, u32[]{:S(2)}) collective-permute-start(bf16[6,96,128]{2,1,0:T(8,128)(2,1)} %pack_edges.1), channel_id=1, source_target_pairs={{0,3},{1,2},{2,1},{3,0},{4,7},{5,6},{6,5},{7,4},{8,11},{9,10},{10,... | collective-permute-start | bytes 442376 | tf_op jit(solution)/shard_map/ppermute | solution.py:95
  9.2 7.0 %copy-start.6 = (bf16[2,96,384]{2,1,0:T(8,128)(2,1)S(1)}, bf16[2,96,384]{2,1,0:T(8,128)(2,1)}, u32[]{:S(2)}) copy-start(bf16[2,96,384]{2,1,0:T(8,128)(2,1)} %refs_3_.5) | copy-start | bytes 442372
  9.2 7.0 %copy-start.7 = (bf16[2,384,96]{1,2,0:T(8,128)(2,1)S(1)}, bf16[2,384,96]{1,2,0:T(8,128)(2,1)}, u32[]{:S(2)}) copy-start(bf16[2,384,96]{1,2,0:T(8,128)(2,1)} %param.25) | copy-start | bytes 442372
  9.2 7.0 %copy-start.13 = (f32[2,96]{1,0:T(2,128)S(1)}, f32[2,96]{1,0:T(2,128)}, u32[]{:S(2)}) copy-start(f32[2,96]{1,0:T(2,128)} %refs_2_.5) | copy-start | bytes 2308
  9.2 7.0 %copy-start.14 = (f32[2,96]{1,0:T(2,128)S(1)}, f32[2,96]{1,0:T(2,128)}, u32[]{:S(2)}) copy-start(f32[2,96]{1,0:T(2,128)} %refs_5_.5) | copy-start | bytes 2308
  24.1 9.9 %collective-permute-start.2 = (bf16[6,96,128]{2,1,0:T(8,128)(2,1)S(1)}, bf16[6,96,128]{2,1,0:T(8,128)(2,1)S(1)}, u32[]{:S(2)}, u32[]{:S(2)}) collective-permute-start(bf16[6,96,128]{2,1,0:T(8,128)(2,1)S(1)} %get-tuple-element.38), channel_id=1, source_target_pairs={{0,1},{1,0},{2,3},{3,2},{4,5},{5,4},{6,7},{7,6},{8,9},{9,8},{10,11... | collective-permute-start | bytes 442376 | tf_op jit(solution)/shard_map/ppermute | solution.py:94
  24.8 9.2 %collective-permute-start.3 = (bf16[6,96,128]{2,1,0:T(8,128)(2,1)S(1)}, bf16[6,96,128]{2,1,0:T(8,128)(2,1)S(1)}, u32[]{:S(2)}, u32[]{:S(2)}) collective-permute-start(bf16[6,96,128]{2,1,0:T(8,128)(2,1)S(1)} %get-tuple-element.38), channel_id=1, source_target_pairs={{0,3},{1,2},{2,1},{3,0},{4,7},{5,6},{6,5},{7,4},{8,11},{9,10},{10,... | collective-permute-start | bytes 442376 | tf_op jit(solution)/shard_map/ppermute | solution.py:95
  27.4 6.6 %copy-start.12 = (bf16[96,32]{0,1:T(8,128)(2,1)S(1)}, bf16[96,32]{0,1:T(8,128)(2,1)}, u32[]{:S(2)}) copy-start(bf16[96,32]{0,1:T(8,128)(2,1)} %param.27) | copy-start | bytes 18436
  40.5 3.2 %collective-permute-start.4 = (bf16[2,18,32,128]{3,2,1,0:T(8,128)(2,1)S(1)}, bf16[2,18,32,128]{3,2,1,0:T(8,128)(2,1)S(1)}, u32[]{:S(2)}, u32[]{:S(2)}) collective-permute-start(bf16[2,18,32,128]{3,2,1,0:T(8,128)(2,1)S(1)} %get-tuple-element.45), channel_id=1, source_target_pairs={{0,4},{4,0},{8,12},{12,8},{16,20},{20,16},{24,28},{28,24},{1,5},{5... | collective-permute-start | bytes 884744 | tf_op jit(solution)/shard_map/ppermute | solution.py:520
  40.6 7.3 %copy-start.5 = (bf16[96,96,128]{2,1,0:T(8,128)(2,1)S(1)}, bf16[96,96,128]{2,1,0:T(8,128)(2,1)}, u32[]{:S(2)}) copy-start(bf16[96,96,128]{2,1,0:T(8,128)(2,1)} %ocean_ref.1) | copy-start | bytes 7077892
  40.6 7.3 %copy-start.8 = (bf16[96,384]{1,0:T(8,128)(2,1)S(1)}, bf16[96,384]{1,0:T(8,128)(2,1)}, u32[]{:S(2)}) copy-start(bf16[96,384]{1,0:T(8,128)(2,1)} %up_ref.1) | copy-start | bytes 221188
  40.6 7.3 %copy-start.10 = (f32[7,7,96]{2,1,0:T(8,128)S(1)}, f32[7,7,96]{2,1,0:T(8,128)}, u32[]{:S(2)}) copy-start(f32[7,7,96]{2,1,0:T(8,128)} %k_ref.1) | copy-start | bytes 56452
  40.6 7.3 %copy-start.11 = (bf16[2,32,96]{2,1,0:T(8,128)(2,1)S(1)}, bf16[2,32,96]{2,1,0:T(8,128)(2,1)}, u32[]{:S(2)}) copy-start(bf16[2,32,96]{2,1,0:T(8,128)(2,1)} %lift_ref.1) | copy-start | bytes 36868
  40.6 7.3 %copy-start.15 = (f32[96]{0:T(128)S(1)}, f32[96]{0:T(128)}, u32[]{:S(2)}) copy-start(f32[96]{0:T(128)} %param.30) | copy-start | bytes 1156
  40.6 7.3 %copy-start.16 = (f32[96]{0:T(128)S(1)}, f32[96]{0:T(128)}, u32[]{:S(2)}) copy-start(f32[96]{0:T(128)} %param.33) | copy-start | bytes 1156
  43.7 3.5 %collective-permute-start.5 = (bf16[2,18,32,128]{3,2,1,0:T(8,128)(2,1)S(1)}, bf16[2,18,32,128]{3,2,1,0:T(8,128)(2,1)S(1)}, u32[]{:S(2)}, u32[]{:S(2)}) collective-permute-start(bf16[2,18,32,128]{3,2,1,0:T(8,128)(2,1)S(1)} %get-tuple-element.52), channel_id=1, source_target_pairs={{0,4},{4,0},{8,12},{12,8},{16,20},{20,16},{24,28},{28,24},{1,5},{5... | collective-permute-start | bytes 884744 | tf_op jit(solution)/shard_map/ppermute | solution.py:520
  44.3 7.2 %collective-permute-start.6 = (bf16[18,32,128]{2,1,0:T(8,128)(2,1)S(1)}, bf16[18,32,128]{2,1,0:T(8,128)(2,1)S(1)}, u32[]{:S(2)}, u32[]{:S(2)}) collective-permute-start(bf16[18,32,128]{2,1,0:T(8,128)(2,1)S(1)} %get-tuple-element.53), channel_id=1, source_target_pairs={{0,24},{4,28},{8,16},{12,20},{16,8},{20,12},{24,0},{28,4},{1,25},{... | collective-permute-start | bytes 442376 | tf_op jit(solution)/shard_map/ppermute | solution.py:520
  46.7 7.4 %collective-permute-start.7 = (bf16[18,32,128]{2,1,0:T(8,128)(2,1)S(1)}, bf16[18,32,128]{2,1,0:T(8,128)(2,1)S(1)}, u32[]{:S(2)}, u32[]{:S(2)}) collective-permute-start(bf16[18,32,128]{2,1,0:T(8,128)(2,1)S(1)} %get-tuple-element.54), channel_id=1, source_target_pairs={{0,16},{4,20},{8,24},{12,28},{16,0},{20,4},{24,8},{28,12},{1,17},{... | collective-permute-start | bytes 442376 | tf_op jit(solution)/shard_map/ppermute | solution.py:520
  47.3 7.0 %collective-permute-start.8 = (bf16[18,32,128]{2,1,0:T(8,128)(2,1)S(1)}, bf16[18,32,128]{2,1,0:T(8,128)(2,1)S(1)}, u32[]{:S(2)}, u32[]{:S(2)}) collective-permute-start(bf16[18,32,128]{2,1,0:T(8,128)(2,1)S(1)} %add_pairs.3._), channel_id=1, source_target_pairs={{0,8},{4,12},{8,0},{12,4},{16,24},{20,28},{24,16},{28,20},{1,9},{5... | collective-permute-start | bytes 442376 | tf_op jit(solution)/shard_map/ppermute | solution.py:520
  47.9 6.4 %copy-start.1 = (s32[96,128]{1,0:T(8,128)S(1)}, s32[96,128]{1,0:T(8,128)}, u32[]{:S(2)}) copy-start(s32[96,128]{1,0:T(8,128)} %land_ref.5) | copy-start | bytes 147460
  47.9 6.4 %copy-start.3 = (s32[96,128]{1,0:T(8,128)S(1)}, s32[96,128]{1,0:T(8,128)}, u32[]{:S(2)}) copy-start(s32[96,128]{1,0:T(8,128)} %refs_7_.1) | copy-start | bytes 147460
  54.8 6.0 %collective-permute-start.10 = (bf16[2,96,128]{2,1,0:T(8,128)(2,1)S(1)}, bf16[2,96,128]{2,1,0:T(8,128)(2,1)S(1)}, u32[]{:S(2)}, u32[]{:S(2)}) collective-permute-start(bf16[2,96,128]{2,1,0:T(8,128)(2,1)S(1)} %get-tuple-element.59), channel_id=1, source_target_pairs={{0,3},{1,2},{2,1},{3,0},{4,7},{5,6},{6,5},{7,4},{8,11},{9,10},{10,... | collective-permute-start | bytes 147464 | tf_op jit(solution)/shard_map/ppermute | solution.py:95
  56.1 4.7 %collective-permute-start.9 = (bf16[2,96,128]{2,1,0:T(8,128)(2,1)S(1)}, bf16[2,96,128]{2,1,0:T(8,128)(2,1)S(1)}, u32[]{:S(2)}, u32[]{:S(2)}) collective-permute-start(bf16[2,96,128]{2,1,0:T(8,128)(2,1)S(1)} %get-tuple-element.59), channel_id=1, source_target_pairs={{0,1},{1,0},{2,3},{3,2},{4,5},{5,4},{6,7},{7,6},{8,9},{9,8},{10,11... | collective-permute-start | bytes 147464 | tf_op jit(solution)/shard_map/ppermute | solution.py:94
  56.1 4.7 %copy-start.2 = (bf16[384,96]{0,1:T(8,128)(2,1)S(1)}, bf16[384,96]{0,1:T(8,128)(2,1)}, u32[]{:S(2)}) copy-start(bf16[384,96]{0,1:T(8,128)(2,1)} %param.32) | copy-start | bytes 221188
  56.1 4.7 %copy-start.4 = (bf16[96,8]{0,1:T(8,128)(2,1)S(1)}, bf16[96,8]{0,1:T(8,128)(2,1)}, u32[]{:S(2)}) copy-start(bf16[96,8]{0,1:T(8,128)(2,1)} %param.34) | copy-start | bytes 4612
  60.8 7.1 %copy-start.17 = (bf16[8,96]{1,0:T(8,128)(2,1)S(1)}, bf16[8,96]{1,0:T(8,128)(2,1)}, u32[]{:S(2)}) copy-start(bf16[8,96]{1,0:T(8,128)(2,1)} %param.35) | copy-start | bytes 4612
  63.2 1.2 %collective-permute-start.11 = (bf16[12,8,128]{2,1,0:T(8,128)(2,1)S(1)}, bf16[12,8,128]{2,1,0:T(8,128)(2,1)S(1)}, u32[]{:S(2)}, u32[]{:S(2)}) collective-permute-start(bf16[12,8,128]{2,1,0:T(8,128)(2,1)S(1)} %get-tuple-element.64.own_ref), channel_id=1, source_target_pairs={{0,4},{4,0},{8,12},{12,8},{16,20},{20,16},{24,28},{28,24},{1,5},{5... | collective-permute-start | bytes 73736 | tf_op jit(solution)/shard_map/ppermute | solution.py:520
  64.4 4.7 %collective-permute-start.12 = (bf16[2,12,8,128]{3,2,1,0:T(8,128)(2,1)S(1)}, bf16[2,12,8,128]{3,2,1,0:T(8,128)(2,1)S(1)}, u32[]{:S(2)}, u32[]{:S(2)}) collective-permute-start(bf16[2,12,8,128]{3,2,1,0:T(8,128)(2,1)S(1)} %surface_pair.1.refs_0_), channel_id=1, source_target_pairs={{0,8},{4,12},{8,0},{12,4},{16,24},{20,28},{24,16},{28,20},{1,9},{5... | collective-permute-start | bytes 147464 | tf_op jit(solution)/shard_map/ppermute | solution.py:520
  65.9 4.6 %collective-permute-start.13 = (bf16[2,12,8,128]{3,2,1,0:T(8,128)(2,1)S(1)}, bf16[2,12,8,128]{3,2,1,0:T(8,128)(2,1)S(1)}, u32[]{:S(2)}, u32[]{:S(2)}) collective-permute-start(bf16[2,12,8,128]{3,2,1,0:T(8,128)(2,1)S(1)} %surface_pair.1.refs_0_), channel_id=1, source_target_pairs={{0,16},{4,20},{8,24},{12,28},{16,0},{20,4},{24,8},{28,12},{1,17},{... | collective-permute-start | bytes 147464 | tf_op jit(solution)/shard_map/ppermute | solution.py:520
  66.6 5.0 %collective-permute-start.14 = (bf16[2,12,8,128]{3,2,1,0:T(8,128)(2,1)S(1)}, bf16[2,12,8,128]{3,2,1,0:T(8,128)(2,1)S(1)}, u32[]{:S(2)}, u32[]{:S(2)}) collective-permute-start(bf16[2,12,8,128]{3,2,1,0:T(8,128)(2,1)S(1)} %surface_pair.1.refs_0_), channel_id=1, source_target_pairs={{0,24},{4,28},{8,16},{12,20},{16,8},{20,12},{24,0},{28,4},{1,25},{... | collective-permute-start | bytes 147464 | tf_op jit(solution)/shard_map/ppermute | solution.py:520

commit v11 on v10

--- a/solution.py
+++ b/solution.py
@@ -91,16 +91,16 @@
 
 def neighbours(packed):
     count = lax.axis_size("lon")
-    first = lax.ppermute(packed, "lon", [(i, i ^ 1) for i in range(count)])
-    second = lax.ppermute(
+    first = lax.ppermute(
         packed, "lon", [(i, (i - 1) % count if i % 2 == 0 else (i + 1) % count) for i in range(count)]
     )
+    second = lax.ppermute(packed, "lon", [(i, i ^ 1) for i in range(count)])
     return first, second
 
 
 def by_side(first, second):
     even = lax.axis_index("lon") % 2 == 0
-    return jnp.where(even, second, first), jnp.where(even, first, second)
+    return jnp.where(even, first, second), jnp.where(even, second, first)
 
 
 def fill_base(taps, base):
@@ -699,7 +699,7 @@
     atm = (atm_gain, atm_up, atm_down.transpose(0, 2, 1), atm_scale)
     taps = atm_kernel.transpose(1, 2, 0, 3)
 
-    edges = neighbours(pack(state, small))
+    edges = neighbours(pack(state, 2 * small))
     a, band = convolve(0, state, taps, blocks)
     steps = rows // small
     near_steps = (rows // 2) // small - 1
@@ -733,10 +733,10 @@
         mid, a, left, right, band, land_mask, ready, ocn_down.T, surf_weight.T
     )
     own = make_pair(surface, send_xor(surface, 1))
-    pairs = [own] + [send_xor(own, 2 * k) for k in range(1, half)]
-    out = couple((0,), state, land_mask, back_weight.T, pairs[:1], [])
-    rest = tuple(range(1, half))
-    out = couple(rest, state, land_mask, back_weight.T, pairs[1:], [out])
+    rest = tuple(range(half - 1, 0, -1))
+    pairs = [send_xor(own, 2 * k) for k in rest]
+    out = couple((0,), state, land_mask, back_weight.T, [own], [])
+    out = couple(rest, state, land_mask, back_weight.T, pairs, [out])
     return (out[None], ocean_rows)
 
 

time: 73.5 us -> 73.4 us (level)
    ppermute x3, starting transfers between devices: 6.33 us -> 9.16 us  [neighbours(): lax.ppermute(packed, 'lon', [(i, (i - 1) % count if i % 2 == 0 else (i +...]
    ppermute x3, starting transfers between devices: 3.75 us -> 1.38 us  [neighbours(): second = lax.ppermute(packed, 'lon', [(i, i ^ 1) for i in range(count)])]
    ppermute x3, waiting for transfers between devices: 0.01 us -> 1.39 us  [neighbours(): second = lax.ppermute(packed, 'lon', [(i, i ^ 1) for i in range(count)])]
    ppermute x3, waiting for transfers between devices: 3.76 us -> 2.49 us  [neighbours(): lax.ppermute(packed, 'lon', [(i, (i - 1) % count if i % 2 == 0 else (i +...]
  transfers between devices with their start and end apart: 15 -> 15, of which waited for: 8 -> 11; matrix products, arithmetic and copies ran while one was open for 0% -> 0% of each run, Pallas kernels for 28% -> 28%
where the time goes in v11:
time: 73.4 us; the launch traced here: 73.2 us
  Pallas kernels  41.7 us (57%)
  starting transfers between devices  18.2 us (25%)
  waiting for transfers between devices  12 us (16%)
  between operations  1.09 us (1%)
    pallas_call x3, Pallas kernels, atmos_block(): pl.pallas_call(functools.partial(atmos_kernel, layer, near, members, coun...  17.3 us
    pallas_call x2, Pallas kernels, convolve(): pl.pallas_call(functools.partial(conv_kernel, layer), out_shape=[jax.Shap...  12.9 us
    ppermute x3, starting transfers between devices, neighbours(): lax.ppermute(packed, 'lon', [(i, (i - 1) % count if i % 2 == 0 else (i +...  9.16 us
    ppermute x9, waiting for transfers between devices, send_xor(): lax.ppermute(value, 'member', [(i, i ^ bits) for i in range(members)])  8.11 us
    ppermute x9, starting transfers between devices, send_xor(): lax.ppermute(value, 'member', [(i, i ^ bits) for i in range(members)])  7.64 us
    pallas_call x1, Pallas kernels, pack(): pl.pallas_call(functools.partial(pack_kernel, step), out_shape=jax.ShapeD...  2.77 us
    pallas_call x2, Pallas kernels, couple(): pl.pallas_call(functools.partial(couple_kernel, ks), out_shape=jax.ShapeD...  2.62 us
    ppermute x3, waiting for transfers between devices, neighbours(): lax.ppermute(packed, 'lon', [(i, (i - 1) % count if i % 2 == 0 else (i +...  2.49 us
  transfers between devices with their start and end apart: 15, of which 11 were waited for; matrix products, arithmetic and copies ran while one was open for 0% of the time, Pallas kernels for 28%

profile of v11, /device:TPU:0, one launch (start us, length us, event | category | flops | bytes accessed | tf_op | source)
XLA Modules:
  0.0 73.2 jit_solution(11630781778506833144)
XLA Ops:
  0.6 0.0 copy-start
  0.6 0.0 copy-start.9
  0.6 2.8 %pack_edges.1 = bf16[6,96,128]{2,1,0:T(8,128)(2,1)} custom-call(bf16[96,96,128]{2,1,0:T(8,128)(2,1)} %bitcast.10), custom_call_target="tpu_custom_call" | custom-call | tf_op jit(solution)/shard_map/pack_edges/pallas_call | solution.py:81
  3.4 5.1 %collective-permute-start = (bf16[6,96,128]{2,1,0:T(8,128)(2,1)}, bf16[6,96,128]{2,1,0:T(8,128)(2,1)S(1)}, u32[]{:S(2)}, u32[]{:S(2)}) collective-permute-start(bf16[6,96,128]{2,1,0:T(8,128)(2,1)} %pack_edges.1), channel_id=1, source_target_pairs={{0,3},{1,2},{2,1},{3,0},{4,7},{5,6},{6,5},{7,4},{8,11},{9,10},{10,... | collective-permute-start | bytes 442376 | tf_op jit(solution)/shard_map/ppermute | solution.py:94
  8.5 0.0 collective-permute-start.1
  8.5 0.0 copy-done.9
  8.6 0.0 copy-start.6
  8.6 0.0 copy-start.7
  8.6 0.0 copy-start.13
  8.6 0.0 copy-start.14
  8.6 6.4 %conv.2 = (f32[96,96,128]{2,1,0:T(8,128)S(1)}, bf16[6,96,1792]{2,1,0:T(8,128)(2,1)S(1)}) custom-call(bf16[96,96,128]{2,1,0:T(8,128)(2,1)S(1)} %bitcast.11, f32[7,7,2,96]{3,2,1,0:T(2,128)S(1)} %bitcast.20), custom_call_target="tpu_custom_call" | custom-call | flops 8000000000 | tf_op jit(solution)/shard_map/conv/pallas_call | solution.py:203
  15.0 0.0 collective-permute-done.refs_6_
  15.0 0.9 %collective-permute-done.1.refs_7_ = bf16[6,96,128]{2,1,0:T(8,128)(2,1)S(1)} collective-permute-done((bf16[6,96,128]{2,1,0:T(8,128)(2,1)}, bf16[6,96,128]{2,1,0:T(8,128)(2,1)S(1)}, u32[]{:S(2)}, u32[]{:S(2)}) %collective-permute-start.1) | collective-permute-done | bytes 147488 | tf_op jit(solution)/shard_map/ppermute | solution.py:97
  15.9 0.0 copy-done.6
  15.9 0.0 copy-done.13
  15.9 7.8 %atmos_block.3 = (bf16[96,96,128]{2,1,0:T(8,128)(2,1)S(1)}, bf16[6,96,128]{2,1,0:T(8,128)(2,1)S(1)}) custom-call(bf16[96,96,128]{2,1,0:T(8,128)(2,1)S(1)} %bitcast.12, f32[96,96,128]{2,1,0:T(8,128)S(1)} %get-tuple-element.34.refs_1_, f32[2,96]{1,0:T(2,128)S(1)} %copy-done.13, bf16[2,96,384]{2,1,0:T(8,128)(2,1)S(1)} %copy-done.6, ...), custom_call_target="tpu_custom_call" | custom-call | flops 8000000000 | tf_op jit(solution)/shard_map/atmos_block/pallas_call | solution.py:487
  23.7 1.8 %collective-permute-start.2 = (bf16[6,96,128]{2,1,0:T(8,128)(2,1)S(1)}, bf16[6,96,128]{2,1,0:T(8,128)(2,1)S(1)}, u32[]{:S(2)}, u32[]{:S(2)}) collective-permute-start(bf16[6,96,128]{2,1,0:T(8,128)(2,1)S(1)} %get-tuple-element.38), channel_id=1, source_target_pairs={{0,3},{1,2},{2,1},{3,0},{4,7},{5,6},{6,5},{7,4},{8,11},{9,10},{10,... | collective-permute-start | bytes 442376 | tf_op jit(solution)/shard_map/ppermute | solution.py:94
  25.5 0.0 collective-permute-start.3
  25.6 6.5 %conv.3 = (f32[96,96,128]{2,1,0:T(8,128)S(1)}, bf16[6,96,1792]{2,1,0:T(8,128)(2,1)S(1)}) custom-call(bf16[96,96,128]{2,1,0:T(8,128)(2,1)S(1)} %get-tuple-element.36.x_ref.refs_0_, f32[7,7,2,96]{3,2,1,0:T(2,128)S(1)} %bitcast.21), custom_call_target="tpu_custom_call" | custom-call | flops 8000000000 | tf_op jit(solution)/shard_map/conv/pallas_call | solution.py:203
  32.1 0.2 collective-permute-done.2.refs_7_
  32.4 0.5 collective-permute-done.3.refs_8_
  32.9 6.4 %atmos_block.4 = (bf16[96,96,128]{2,1,0:T(8,128)(2,1)S(1)}, bf16[2,18,32,128]{3,2,1,0:T(8,128)(2,1)S(1)}, bf16[2,18,32,128]{3,2,1,0:T(8,128)(2,1)S(1)}, bf16[102...) custom-call(bf16[96,96,128]{2,1,0:T(8,128)(2,1)S(1)} %get-tuple-element.36.x_ref.refs_0_, ...), custom_call_target="tpu_custom_call" | custom-call | flops 5000000000 | tf_op jit(solution)/shard_map/atmos_block/pallas_call | solution.py:487
  39.3 0.1 collective-permute-start.4
  39.4 0.0 copy-start.5
  39.4 0.0 copy-start.8
  39.4 0.0 copy-start.10
  39.5 0.0 copy-start.11
  39.5 0.0 copy-start.15
  39.5 0.0 copy-start.16
  39.5 3.0 %atmos_block.5 = (bf16[96,96,128]{2,1,0:T(8,128)(2,1)S(1)}, bf16[2,18,32,128]{3,2,1,0:T(8,128)(2,1)S(1)}, bf16[2,18,32,128]{3,2,1,0:T(8,128)(2,1)S(1)}) custom-call(bf16[96,96,128]{2,1,0:T(8,128)(2,1)S(1)} %get-tuple-element.36.x_ref.refs_0_, f32[96,96,128]{2,1,0:T(8,128)S(1)} %get-tuple-element.37.refs_1_, ...), custom_call_target="tpu_custom_call", output_to_operand_aliasing={{0}: (7, {})} | custom-call | flops 3000000000 | tf_op jit(solution)/shard_map/atmos_block/pallas_call | solution.py:487
  42.5 0.0 collective-permute-done.4.got_ref
  42.5 0.1 add_pairs.2
  42.6 0.5 collective-permute-start.5
  43.1 2.4 %collective-permute-start.6 = (bf16[18,32,128]{2,1,0:T(8,128)(2,1)S(1)}, bf16[18,32,128]{2,1,0:T(8,128)(2,1)S(1)}, u32[]{:S(2)}, u32[]{:S(2)}) collective-permute-start(bf16[18,32,128]{2,1,0:T(8,128)(2,1)S(1)} %get-tuple-element.53), channel_id=1, source_target_pairs={{0,24},{4,28},{8,16},{12,20},{16,8},{20,12},{24,0},{28,4},{1,25},{... | collective-permute-start | bytes 442376 | tf_op jit(solution)/shard_map/ppermute | solution.py:520
  45.5 0.5 collective-permute-start.7
  46.0 0.0 collective-permute-done.5.got_ref.refs_1_
  46.1 0.6 collective-permute-start.8
  46.7 0.0 copy-done.11
  46.8 0.0 copy-start.1
  46.8 0.0 copy-start.3
  46.8 1.7 %prepare_ocean.1 = (bf16[6,160,1792]{2,1,0:T(8,128)(2,1)S(1)}, bf16[256,768]{1,0:T(8,128)(2,1)S(1)}, bf16[384,96]{1,0:T(8,128)(2,1)S(1)}, f32[96,128]{1,0:T(8,12...) custom-call(f32[7,7,96]{2,1,0:T(8,128)S(1)} %copy-done.10, ...), custom_call_target="tpu_custom_call" | custom-call | flops 3000000000 | tf_op jit(solution)/shard_map/prepare_ocean/pallas_call | solution.py:253
  48.5 1.9 %collective-permute-done.6.refs_2_ = bf16[18,32,128]{2,1,0:T(8,128)(2,1)S(1)} collective-permute-done((bf16[18,32,128]{2,1,0:T(8,128)(2,1)S(1)}, bf16[18,32,128]{2,1,0:T(8,128)(2,1)S(1)}, u32[]{:S(2)}, u32[]{:S(2)}) %collective-permute-start.6) | collective-permute-done | bytes 147488 | tf_op jit(solution)/shard_map/ppermute | solution.py:520
  50.4 2.6 %collective-permute-done.7.refs_3_ = bf16[18,32,128]{2,1,0:T(8,128)(2,1)S(1)} collective-permute-done((bf16[18,32,128]{2,1,0:T(8,128)(2,1)S(1)}, bf16[18,32,128]{2,1,0:T(8,128)(2,1)S(1)}, u32[]{:S(2)}, u32[]{:S(2)}) %collective-permute-start.7) | collective-permute-done | bytes 147488 | tf_op jit(solution)/shard_map/ppermute | solution.py:520
  53.0 0.1 collective-permute-done.8.refs_4_
  53.1 0.0 copy-done.3
  53.1 0.5 ocean_forcing.1
  53.6 1.3 %collective-permute-start.10 = (bf16[2,96,128]{2,1,0:T(8,128)(2,1)S(1)}, bf16[2,96,128]{2,1,0:T(8,128)(2,1)S(1)}, u32[]{:S(2)}, u32[]{:S(2)}) collective-permute-start(bf16[2,96,128]{2,1,0:T(8,128)(2,1)S(1)} %get-tuple-element.59), channel_id=1, source_target_pairs={{0,1},{1,0},{2,3},{3,2},{4,5},{5,4},{6,7},{7,6},{8,9},{9,8},{10,11... | collective-permute-start | bytes 147464 | tf_op jit(solution)/shard_map/ppermute | solution.py:97
  55.0 2.3 %collective-permute-start.9 = (bf16[2,96,128]{2,1,0:T(8,128)(2,1)S(1)}, bf16[2,96,128]{2,1,0:T(8,128)(2,1)S(1)}, u32[]{:S(2)}, u32[]{:S(2)}) collective-permute-start(bf16[2,96,128]{2,1,0:T(8,128)(2,1)S(1)} %get-tuple-element.59), channel_id=1, source_target_pairs={{0,3},{1,2},{2,1},{3,0},{4,7},{5,6},{6,5},{7,4},{8,11},{9,10},{10,... | collective-permute-start | bytes 147464 | tf_op jit(solution)/shard_map/ppermute | solution.py:94
  57.2 1.3 %ocean_conv.1.a_ref = f32[12,96,128]{2,1,0:T(8,128)S(1)} custom-call(bf16[18,96,128]{2,1,0:T(8,128)(2,1)S(1)} %get-tuple-element.57.x_ref.mid_ref, bf16[6,160,1792]{2,1,0:T(8,128)(2,1)S(1)} %get-tuple-element.58.band_ref), custom_call_target="tpu_custom_call" | custom-call | flops 2000000000 | tf_op jit(solution)/shard_map/ocean_conv/pallas_call | solution.py:284
  58.6 0.0 collective-permute-done.10.right_ref
  58.6 2.3 %collective-permute-done.9.left_ref = bf16[2,96,128]{2,1,0:T(8,128)(2,1)S(1)} collective-permute-done((bf16[2,96,128]{2,1,0:T(8,128)(2,1)S(1)}, bf16[2,96,128]{2,1,0:T(8,128)(2,1)S(1)}, u32[]{:S(2)}, u32[]{:S(2)}) %collective-permute-start.9) | collective-permute-done | bytes 49184 | tf_op jit(solution)/shard_map/ppermute | solution.py:94
  60.8 0.0 copy-done.2
  60.9 2.4 %ocean_block.1 = (bf16[12,96,128]{2,1,0:T(8,128)(2,1)}, bf16[12,8,128]{2,1,0:T(8,128)(2,1)S(1)}) custom-call(bf16[18,96,128]{2,1,0:T(8,128)(2,1)S(1)} %get-tuple-element.57.x_ref.mid_ref, f32[12,96,128]{2,1,0:T(8,128)S(1)} %ocean_conv.1.a_ref, bf16[2,96,128]{2,1,0:T(8,128)(2,1)S(1)} %collective-permute-done.9.left_ref, ...), custom_call_target="tpu_custom_call" | custom-call | tf_op jit(solution)/shard_map/ocean_block/pallas_call | solution.py:597
  63.3 0.0 collective-permute-start.11
  63.3 1.2 %collective-permute-done.11.got_ref = bf16[12,8,128]{2,1,0:T(8,128)(2,1)S(1)} collective-permute-done((bf16[12,8,128]{2,1,0:T(8,128)(2,1)S(1)}, bf16[12,8,128]{2,1,0:T(8,128)(2,1)S(1)}, u32[]{:S(2)}, u32[]{:S(2)}) %collective-permute-start.11) | collective-permute-done | bytes 24608 | tf_op jit(solution)/shard_map/ppermute | solution.py:520
  64.5 1.7 %collective-permute-start.12 = (bf16[2,12,8,128]{3,2,1,0:T(8,128)(2,1)S(1)}, bf16[2,12,8,128]{3,2,1,0:T(8,128)(2,1)S(1)}, u32[]{:S(2)}, u32[]{:S(2)}) collective-permute-start(bf16[2,12,8,128]{3,2,1,0:T(8,128)(2,1)S(1)} %surface_pair.1.refs_0_), channel_id=1, source_target_pairs={{0,24},{4,28},{8,16},{12,20},{16,8},{20,12},{24,0},{28,4},{1,25},{... | collective-permute-start | bytes 147464 | tf_op jit(solution)/shard_map/ppermute | solution.py:520
  66.1 1.3 %collective-permute-start.13 = (bf16[2,12,8,128]{3,2,1,0:T(8,128)(2,1)S(1)}, bf16[2,12,8,128]{3,2,1,0:T(8,128)(2,1)S(1)}, u32[]{:S(2)}, u32[]{:S(2)}) collective-permute-start(bf16[2,12,8,128]{3,2,1,0:T(8,128)(2,1)S(1)} %surface_pair.1.refs_0_), channel_id=1, source_target_pairs={{0,16},{4,20},{8,24},{12,28},{16,0},{20,4},{24,8},{28,12},{1,17},{... | collective-permute-start | bytes 147464 | tf_op jit(solution)/shard_map/ppermute | solution.py:520
  67.4 0.5 collective-permute-start.14
  68.0 0.1 copy.22
  68.1 1.1 %couple.2.refs_3_ = bf16[96,96,128]{2,1,0:T(8,128)(2,1)} custom-call(bf16[96,96,128]{2,1,0:T(8,128)(2,1)S(1)} %get-tuple-element.43.y_ref, s32[96,128]{1,0:T(8,128)S(1)} %copy-done.1, bf16[96,8]{1,0:T(8,128)(2,1)S(1)} %bitcast.13, bf16[2,12,8,128]{3,2,1,0:T(8,128)(2,1)S(1)} %surface_pair.1.refs_0_), custom_call_target="tpu_custom_call" | custom-call | tf_op jit(solution)/shard_map/couple/pallas_call | solution.py:658
  69.2 0.3 collective-permute-done.12.refs_0_
  69.5 0.7 collective-permute-done.13.refs_1_
  70.3 1.3 %collective-permute-done.14.refs_2_ = bf16[2,12,8,128]{3,2,1,0:T(8,128)(2,1)S(1)} collective-permute-done((bf16[2,12,8,128]{3,2,1,0:T(8,128)(2,1)S(1)}, bf16[2,12,8,128]{3,2,1,0:T(8,128)(2,1)S(1)}, u32[]{:S(2)}, u32[]{:S(2)}) %collective-permute-start.14) | collective-permute-done | bytes 49184 | tf_op jit(solution)/shard_map/ppermute | solution.py:520
  71.5 1.5 %couple.3 = bf16[96,96,128]{2,1,0:T(8,128)(2,1)} custom-call(bf16[96,96,128]{2,1,0:T(8,128)(2,1)S(1)} %get-tuple-element.43.y_ref, s32[96,128]{1,0:T(8,128)S(1)} %copy-done.1, bf16[96,8]{1,0:T(8,128)(2,1)S(1)} %bitcast.14, bf16[2,12,8,128]{3,2,1,0:T(8,128)(2,1)S(1)} %collective-permute-done.12.refs_0_, ...), custom_call_target="tpu_custom_call", output_to_operand_aliasing={{}: (6, {})} | custom-call | tf_op jit(solution)/shard_map/couple/pallas_call | solution.py:658
  (18 shorter events, 0.1 us)
Async XLA Ops:
  0.6 7.9 %copy-start = (bf16[1,96,96,128]{3,2,1,0:T(8,128)(2,1)S(1)}, bf16[1,96,96,128]{3,2,1,0:T(8,128)(2,1)}, u32[]{:S(2)}) copy-start(bf16[1,96,96,128]{3,2,1,0:T(8,128)(2,1)} %param.18) | copy-start | bytes 7077892
  0.6 7.9 %copy-start.9 = (f32[2,7,7,96]{3,0,2,1:T(2,128)S(1)}, f32[2,7,7,96]{3,0,2,1:T(2,128)}, u32[]{:S(2)}) copy-start(f32[2,7,7,96]{3,0,2,1:T(2,128)} %param.22) | copy-start | bytes 112900
  3.4 11.6 %collective-permute-start = (bf16[6,96,128]{2,1,0:T(8,128)(2,1)}, bf16[6,96,128]{2,1,0:T(8,128)(2,1)S(1)}, u32[]{:S(2)}, u32[]{:S(2)}) collective-permute-start(bf16[6,96,128]{2,1,0:T(8,128)(2,1)} %pack_edges.1), channel_id=1, source_target_pairs={{0,3},{1,2},{2,1},{3,0},{4,7},{5,6},{6,5},{7,4},{8,11},{9,10},{10,... | collective-permute-start | bytes 442376 | tf_op jit(solution)/shard_map/ppermute | solution.py:94
  8.5 7.3 %collective-permute-start.1 = (bf16[6,96,128]{2,1,0:T(8,128)(2,1)}, bf16[6,96,128]{2,1,0:T(8,128)(2,1)S(1)}, u32[]{:S(2)}, u32[]{:S(2)}) collective-permute-start(bf16[6,96,128]{2,1,0:T(8,128)(2,1)} %pack_edges.1), channel_id=1, source_target_pairs={{0,1},{1,0},{2,3},{3,2},{4,5},{5,4},{6,7},{7,6},{8,9},{9,8},{10,11... | collective-permute-start | bytes 442376 | tf_op jit(solution)/shard_map/ppermute | solution.py:97
  8.6 7.3 %copy-start.6 = (bf16[2,96,384]{2,1,0:T(8,128)(2,1)S(1)}, bf16[2,96,384]{2,1,0:T(8,128)(2,1)}, u32[]{:S(2)}) copy-start(bf16[2,96,384]{2,1,0:T(8,128)(2,1)} %refs_3_.5) | copy-start | bytes 442372
  8.6 7.3 %copy-start.7 = (bf16[2,384,96]{1,2,0:T(8,128)(2,1)S(1)}, bf16[2,384,96]{1,2,0:T(8,128)(2,1)}, u32[]{:S(2)}) copy-start(bf16[2,384,96]{1,2,0:T(8,128)(2,1)} %param.25) | copy-start | bytes 442372
  8.6 7.3 %copy-start.13 = (f32[2,96]{1,0:T(2,128)S(1)}, f32[2,96]{1,0:T(2,128)}, u32[]{:S(2)}) copy-start(f32[2,96]{1,0:T(2,128)} %refs_2_.5) | copy-start | bytes 2308
  8.6 7.3 %copy-start.14 = (f32[2,96]{1,0:T(2,128)S(1)}, f32[2,96]{1,0:T(2,128)}, u32[]{:S(2)}) copy-start(f32[2,96]{1,0:T(2,128)} %refs_5_.5) | copy-start | bytes 2308
  23.7 8.6 %collective-permute-start.2 = (bf16[6,96,128]{2,1,0:T(8,128)(2,1)S(1)}, bf16[6,96,128]{2,1,0:T(8,128)(2,1)S(1)}, u32[]{:S(2)}, u32[]{:S(2)}) collective-permute-start(bf16[6,96,128]{2,1,0:T(8,128)(2,1)S(1)} %get-tuple-element.38), channel_id=1, source_target_pairs={{0,3},{1,2},{2,1},{3,0},{4,7},{5,6},{6,5},{7,4},{8,11},{9,10},{10,... | collective-permute-start | bytes 442376 | tf_op jit(solution)/shard_map/ppermute | solution.py:94
  25.5 7.4 %collective-permute-start.3 = (bf16[6,96,128]{2,1,0:T(8,128)(2,1)S(1)}, bf16[6,96,128]{2,1,0:T(8,128)(2,1)S(1)}, u32[]{:S(2)}, u32[]{:S(2)}) collective-permute-start(bf16[6,96,128]{2,1,0:T(8,128)(2,1)S(1)} %get-tuple-element.38), channel_id=1, source_target_pairs={{0,1},{1,0},{2,3},{3,2},{4,5},{5,4},{6,7},{7,6},{8,9},{9,8},{10,11... | collective-permute-start | bytes 442376 | tf_op jit(solution)/shard_map/ppermute | solution.py:97
  25.6 7.3 %copy-start.12 = (bf16[96,32]{0,1:T(8,128)(2,1)S(1)}, bf16[96,32]{0,1:T(8,128)(2,1)}, u32[]{:S(2)}) copy-start(bf16[96,32]{0,1:T(8,128)(2,1)} %param.27) | copy-start | bytes 18436
  39.3 3.2 %collective-permute-start.4 = (bf16[2,18,32,128]{3,2,1,0:T(8,128)(2,1)S(1)}, bf16[2,18,32,128]{3,2,1,0:T(8,128)(2,1)S(1)}, u32[]{:S(2)}, u32[]{:S(2)}) collective-permute-start(bf16[2,18,32,128]{3,2,1,0:T(8,128)(2,1)S(1)} %get-tuple-element.45), channel_id=1, source_target_pairs={{0,4},{4,0},{8,12},{12,8},{16,20},{20,16},{24,28},{28,24},{1,5},{5... | collective-permute-start | bytes 884744 | tf_op jit(solution)/shard_map/ppermute | solution.py:520
  39.4 7.3 %copy-start.5 = (bf16[96,96,128]{2,1,0:T(8,128)(2,1)S(1)}, bf16[96,96,128]{2,1,0:T(8,128)(2,1)}, u32[]{:S(2)}) copy-start(bf16[96,96,128]{2,1,0:T(8,128)(2,1)} %ocean_ref.1) | copy-start | bytes 7077892
  39.4 7.3 %copy-start.8 = (bf16[96,384]{1,0:T(8,128)(2,1)S(1)}, bf16[96,384]{1,0:T(8,128)(2,1)}, u32[]{:S(2)}) copy-start(bf16[96,384]{1,0:T(8,128)(2,1)} %up_ref.1) | copy-start | bytes 221188
  39.4 7.3 %copy-start.10 = (f32[7,7,96]{2,1,0:T(8,128)S(1)}, f32[7,7,96]{2,1,0:T(8,128)}, u32[]{:S(2)}) copy-start(f32[7,7,96]{2,1,0:T(8,128)} %k_ref.1) | copy-start | bytes 56452
  39.5 7.3 %copy-start.11 = (bf16[2,32,96]{2,1,0:T(8,128)(2,1)S(1)}, bf16[2,32,96]{2,1,0:T(8,128)(2,1)}, u32[]{:S(2)}) copy-start(bf16[2,32,96]{2,1,0:T(8,128)(2,1)} %lift_ref.1) | copy-start | bytes 36868
  39.5 7.3 %copy-start.15 = (f32[96]{0:T(128)S(1)}, f32[96]{0:T(128)}, u32[]{:S(2)}) copy-start(f32[96]{0:T(128)} %param.30) | copy-start | bytes 1156
  39.5 7.3 %copy-start.16 = (f32[96]{0:T(128)S(1)}, f32[96]{0:T(128)}, u32[]{:S(2)}) copy-start(f32[96]{0:T(128)} %param.33) | copy-start | bytes 1156
  42.6 3.5 %collective-permute-start.5 = (bf16[2,18,32,128]{3,2,1,0:T(8,128)(2,1)S(1)}, bf16[2,18,32,128]{3,2,1,0:T(8,128)(2,1)S(1)}, u32[]{:S(2)}, u32[]{:S(2)}) collective-permute-start(bf16[2,18,32,128]{3,2,1,0:T(8,128)(2,1)S(1)} %get-tuple-element.52), channel_id=1, source_target_pairs={{0,4},{4,0},{8,12},{12,8},{16,20},{20,16},{24,28},{28,24},{1,5},{5... | collective-permute-start | bytes 884744 | tf_op jit(solution)/shard_map/ppermute | solution.py:520
  43.1 7.3 %collective-permute-start.6 = (bf16[18,32,128]{2,1,0:T(8,128)(2,1)S(1)}, bf16[18,32,128]{2,1,0:T(8,128)(2,1)S(1)}, u32[]{:S(2)}, u32[]{:S(2)}) collective-permute-start(bf16[18,32,128]{2,1,0:T(8,128)(2,1)S(1)} %get-tuple-element.53), channel_id=1, source_target_pairs={{0,24},{4,28},{8,16},{12,20},{16,8},{20,12},{24,0},{28,4},{1,25},{... | collective-permute-start | bytes 442376 | tf_op jit(solution)/shard_map/ppermute | solution.py:520
  45.5 7.5 %collective-permute-start.7 = (bf16[18,32,128]{2,1,0:T(8,128)(2,1)S(1)}, bf16[18,32,128]{2,1,0:T(8,128)(2,1)S(1)}, u32[]{:S(2)}, u32[]{:S(2)}) collective-permute-start(bf16[18,32,128]{2,1,0:T(8,128)(2,1)S(1)} %get-tuple-element.54), channel_id=1, source_target_pairs={{0,16},{4,20},{8,24},{12,28},{16,0},{20,4},{24,8},{28,12},{1,17},{... | collective-permute-start | bytes 442376 | tf_op jit(solution)/shard_map/ppermute | solution.py:520
  46.1 7.0 %collective-permute-start.8 = (bf16[18,32,128]{2,1,0:T(8,128)(2,1)S(1)}, bf16[18,32,128]{2,1,0:T(8,128)(2,1)S(1)}, u32[]{:S(2)}, u32[]{:S(2)}) collective-permute-start(bf16[18,32,128]{2,1,0:T(8,128)(2,1)S(1)} %add_pairs.3._), channel_id=1, source_target_pairs={{0,8},{4,12},{8,0},{12,4},{16,24},{20,28},{24,16},{28,20},{1,9},{5... | collective-permute-start | bytes 442376 | tf_op jit(solution)/shard_map/ppermute | solution.py:520
  46.8 6.3 %copy-start.1 = (s32[96,128]{1,0:T(8,128)S(1)}, s32[96,128]{1,0:T(8,128)}, u32[]{:S(2)}) copy-start(s32[96,128]{1,0:T(8,128)} %land_ref.5) | copy-start | bytes 147460
  46.8 6.3 %copy-start.3 = (s32[96,128]{1,0:T(8,128)S(1)}, s32[96,128]{1,0:T(8,128)}, u32[]{:S(2)}) copy-start(s32[96,128]{1,0:T(8,128)} %refs_7_.1) | copy-start | bytes 147460
  53.6 5.0 %collective-permute-start.10 = (bf16[2,96,128]{2,1,0:T(8,128)(2,1)S(1)}, bf16[2,96,128]{2,1,0:T(8,128)(2,1)S(1)}, u32[]{:S(2)}, u32[]{:S(2)}) collective-permute-start(bf16[2,96,128]{2,1,0:T(8,128)(2,1)S(1)} %get-tuple-element.59), channel_id=1, source_target_pairs={{0,1},{1,0},{2,3},{3,2},{4,5},{5,4},{6,7},{7,6},{8,9},{9,8},{10,11... | collective-permute-start | bytes 147464 | tf_op jit(solution)/shard_map/ppermute | solution.py:97
  55.0 5.9 %collective-permute-start.9 = (bf16[2,96,128]{2,1,0:T(8,128)(2,1)S(1)}, bf16[2,96,128]{2,1,0:T(8,128)(2,1)S(1)}, u32[]{:S(2)}, u32[]{:S(2)}) collective-permute-start(bf16[2,96,128]{2,1,0:T(8,128)(2,1)S(1)} %get-tuple-element.59), channel_id=1, source_target_pairs={{0,3},{1,2},{2,1},{3,0},{4,7},{5,6},{6,5},{7,4},{8,11},{9,10},{10,... | collective-permute-start | bytes 147464 | tf_op jit(solution)/shard_map/ppermute | solution.py:94
  57.2 3.6 %copy-start.2 = (bf16[384,96]{0,1:T(8,128)(2,1)S(1)}, bf16[384,96]{0,1:T(8,128)(2,1)}, u32[]{:S(2)}) copy-start(bf16[384,96]{0,1:T(8,128)(2,1)} %param.32) | copy-start | bytes 221188
  57.2 3.6 %copy-start.4 = (bf16[96,8]{0,1:T(8,128)(2,1)S(1)}, bf16[96,8]{0,1:T(8,128)(2,1)}, u32[]{:S(2)}) copy-start(bf16[96,8]{0,1:T(8,128)(2,1)} %param.34) | copy-start | bytes 4612
  60.9 7.1 %copy-start.17 = (bf16[8,96]{1,0:T(8,128)(2,1)S(1)}, bf16[8,96]{1,0:T(8,128)(2,1)}, u32[]{:S(2)}) copy-start(bf16[8,96]{1,0:T(8,128)(2,1)} %param.35) | copy-start | bytes 4612
  63.3 1.2 %collective-permute-start.11 = (bf16[12,8,128]{2,1,0:T(8,128)(2,1)S(1)}, bf16[12,8,128]{2,1,0:T(8,128)(2,1)S(1)}, u32[]{:S(2)}, u32[]{:S(2)}) collective-permute-start(bf16[12,8,128]{2,1,0:T(8,128)(2,1)S(1)} %get-tuple-element.64.own_ref), channel_id=1, source_target_pairs={{0,4},{4,0},{8,12},{12,8},{16,20},{20,16},{24,28},{28,24},{1,5},{5... | collective-permute-start | bytes 73736 | tf_op jit(solution)/shard_map/ppermute | solution.py:520
  64.5 5.0 %collective-permute-start.12 = (bf16[2,12,8,128]{3,2,1,0:T(8,128)(2,1)S(1)}, bf16[2,12,8,128]{3,2,1,0:T(8,128)(2,1)S(1)}, u32[]{:S(2)}, u32[]{:S(2)}) collective-permute-start(bf16[2,12,8,128]{3,2,1,0:T(8,128)(2,1)S(1)} %surface_pair.1.refs_0_), channel_id=1, source_target_pairs={{0,24},{4,28},{8,16},{12,20},{16,8},{20,12},{24,0},{28,4},{1,25},{... | collective-permute-start | bytes 147464 | tf_op jit(solution)/shard_map/ppermute | solution.py:520
  66.1 4.1 %collective-permute-start.13 = (bf16[2,12,8,128]{3,2,1,0:T(8,128)(2,1)S(1)}, bf16[2,12,8,128]{3,2,1,0:T(8,128)(2,1)S(1)}, u32[]{:S(2)}, u32[]{:S(2)}) collective-permute-start(bf16[2,12,8,128]{3,2,1,0:T(8,128)(2,1)S(1)} %surface_pair.1.refs_0_), channel_id=1, source_target_pairs={{0,16},{4,20},{8,24},{12,28},{16,0},{20,4},{24,8},{28,12},{1,17},{... | collective-permute-start | bytes 147464 | tf_op jit(solution)/shard_map/ppermute | solution.py:520
  67.4 4.1 %collective-permute-start.14 = (bf16[2,12,8,128]{3,2,1,0:T(8,128)(2,1)S(1)}, bf16[2,12,8,128]{3,2,1,0:T(8,128)(2,1)S(1)}, u32[]{:S(2)}, u32[]{:S(2)}) collective-permute-start(bf16[2,12,8,128]{3,2,1,0:T(8,128)(2,1)S(1)} %surface_pair.1.refs_0_), channel_id=1, source_target_pairs={{0,8},{4,12},{8,0},{12,4},{16,24},{20,28},{24,16},{28,20},{1,9},{5... | collective-permute-start | bytes 147464 | tf_op jit(solution)/shard_map/ppermute | solution.py:520

commit v12 on v11

--- a/solution.py
+++ b/solution.py
@@ -89,18 +89,19 @@
     )(x)
 
 
-def neighbours(packed):
+def neighbours(packed, wrap_first):
     count = lax.axis_size("lon")
-    first = lax.ppermute(
-        packed, "lon", [(i, (i - 1) % count if i % 2 == 0 else (i + 1) % count) for i in range(count)]
-    )
-    second = lax.ppermute(packed, "lon", [(i, i ^ 1) for i in range(count)])
-    return first, second
-
-
-def by_side(first, second):
-    even = lax.axis_index("lon") % 2 == 0
-    return jnp.where(even, first, second), jnp.where(even, second, first)
+    inner = [(i, i ^ 1) for i in range(count)]
+    outer = [(i, (i - 1) % count if i % 2 == 0 else (i + 1) % count) for i in range(count)]
+    return [
+        lax.ppermute(packed, "lon", pairs)
+        for pairs in ((outer, inner) if wrap_first else (inner, outer))
+    ]
+
+
+def by_side(first, second, wrap_first):
+    swap = (lax.axis_index("lon") % 2 == 0) != wrap_first
+    return jnp.where(swap, second, first), jnp.where(swap, first, second)
 
 
 def fill_base(taps, base):
@@ -321,7 +322,7 @@
     blocks, chans, lanes = halo.shape
     both = []
     for q in range(blocks):
-        left, right = by_side(first[q], second[q])
+        left, right = by_side(first[q], second[q], wrapped)
         both.append(jnp.concatenate([right, left], axis=1))
     lane = lax.broadcasted_iota(jnp.int32, (chans, lanes), 1)
     slot = (lane + HALO) // SLOT % SLOTS
@@ -571,9 +572,9 @@
     )(*chunks, win, land, ice, lift)
 
 
-def ocean_kernel(mid_ref, a_ref, left_ref, right_ref, band_ref, land_ref, mat_ref, upt_ref, gain_ref, scale_ref, dn_ref, sw_ref, new_ref, surf_ref, xe, halo, normed):
+def ocean_kernel(mid_ref, a_ref, first_ref, second_ref, band_ref, land_ref, mat_ref, upt_ref, gain_ref, scale_ref, dn_ref, sw_ref, new_ref, surf_ref, xe, halo, normed):
     share, chans, lanes = new_ref.shape
-    halo_conv(left_ref, right_ref, band_ref, False, mat_ref[...], xe, halo)
+    halo_conv(first_ref, second_ref, band_ref, False, mat_ref[...], xe, halo)
     scale = scale_ref[...]
     norm_rows(a_ref, 0, 0, share, halo, gain_ref[...], normed)
     branch = branch_of(normed[...], upt_ref[...], halved(dn_ref[...]))
@@ -591,9 +592,9 @@
         surf_ref[r] = surf[:, r * lanes : (r + 1) * lanes].astype(BF)
 
 
-def ocean_block(mid, a, left, right, band, land, ready, down, surf_weight):
+def ocean_block(mid, a, edges, band, land, ready, down, surf_weight):
     share, chans, lanes = a.shape
-    blocks = left.shape[0]
+    blocks = edges[0].shape[0]
     return pl.pallas_call(
         ocean_kernel,
         out_shape=[
@@ -609,7 +610,7 @@
         ],
         compiler_params=params(24),
         name="ocean_block",
-    )(mid, a, left, right, band, land, *ready, down, surf_weight)
+    )(mid, a, *edges, band, land, *ready, down, surf_weight)
 
 
 def pair_kernel(own_ref, got_ref, out_ref):
@@ -699,13 +700,13 @@
     atm = (atm_gain, atm_up, atm_down.transpose(0, 2, 1), atm_scale)
     taps = atm_kernel.transpose(1, 2, 0, 3)
 
-    edges = neighbours(pack(state, 2 * small))
+    edges = neighbours(pack(state, 2 * small), True)
     a, band = convolve(0, state, taps, blocks)
     steps = rows // small
     near_steps = (rows // 2) // small - 1
     state, packed = atmos_block(0, False, members, state, a, atm, [*edges, band], small, steps)
 
-    edges = neighbours(packed)
+    edges = neighbours(packed, True)
     a, band = convolve(1, state, taps, blocks)
     weights = (*atm, flux_weight.T)
     partly, far_keep, give, flux, halo = atmos_block(
@@ -727,10 +728,10 @@
     )
     sent = [keep, got] + sent
     mid, packed = force(members, sent, win, land_mask, ice_mask, lift)
-    left, right = neighbours(packed)
+    edges = neighbours(packed, False)
     a = ocean_conv(mid, band)
     ocean_rows, surface = ocean_block(
-        mid, a, left, right, band, land_mask, ready, ocn_down.T, surf_weight.T
+        mid, a, edges, band, land_mask, ready, ocn_down.T, surf_weight.T
     )
     own = make_pair(surface, send_xor(surface, 1))
     rest = tuple(range(half - 1, 0, -1))

time: 73.4 us -> 72.7 us (level)
  starting transfers between devices: 18.2 us -> 17.3 us
    ppermute x6, starting transfers between devices: 10.5 us -> 9.65 us  [neighbours(): lax.ppermute(packed, 'lon', pairs)]
  transfers between devices with their start and end apart: 15 -> 15, of which waited for: 11 -> 12; matrix products, arithmetic and copies ran while one was open for 0% -> 0% of each run, Pallas kernels for 28% -> 28%
where the time goes in v12:
time: 72.7 us; the launch traced here: 72.5 us
  Pallas kernels  41.7 us (57%)
  starting transfers between devices  17.3 us (24%)
  waiting for transfers between devices  12.2 us (17%)
  between operations  1.09 us (1%)
    pallas_call x3, Pallas kernels, atmos_block(): pl.pallas_call(functools.partial(atmos_kernel, layer, near, members, coun...  17.3 us
    pallas_call x2, Pallas kernels, convolve(): pl.pallas_call(functools.partial(conv_kernel, layer), out_shape=[jax.Shap...  12.9 us
    ppermute x6, starting transfers between devices, neighbours(): lax.ppermute(packed, 'lon', pairs)  9.65 us
    ppermute x9, waiting for transfers between devices, send_xor(): lax.ppermute(value, 'member', [(i, i ^ bits) for i in range(members)])  8.11 us
    ppermute x9, starting transfers between devices, send_xor(): lax.ppermute(value, 'member', [(i, i ^ bits) for i in range(members)])  7.64 us
    ppermute x6, waiting for transfers between devices, neighbours(): lax.ppermute(packed, 'lon', pairs)  4.1 us
    pallas_call x1, Pallas kernels, pack(): pl.pallas_call(functools.partial(pack_kernel, step), out_shape=jax.ShapeD...  2.77 us
    pallas_call x2, Pallas kernels, couple(): pl.pallas_call(functools.partial(couple_kernel, ks), out_shape=jax.ShapeD...  2.63 us
  transfers between devices with their start and end apart: 15, of which 12 were waited for; matrix products, arithmetic and copies ran while one was open for 0% of the time, Pallas kernels for 28%

profile of v12, /device:TPU:0, one launch (start us, length us, event | category | flops | bytes accessed | tf_op | source)
XLA Modules:
  0.0 72.5 jit_solution(13654362489363920466)
XLA Ops:
  0.6 0.0 copy-start
  0.6 0.0 copy-start.9
  0.6 2.8 %pack_edges.1 = bf16[6,96,128]{2,1,0:T(8,128)(2,1)} custom-call(bf16[96,96,128]{2,1,0:T(8,128)(2,1)} %bitcast.10), custom_call_target="tpu_custom_call" | custom-call | tf_op jit(solution)/shard_map/pack_edges/pallas_call | solution.py:81
  3.4 5.1 %collective-permute-start = (bf16[6,96,128]{2,1,0:T(8,128)(2,1)}, bf16[6,96,128]{2,1,0:T(8,128)(2,1)S(1)}, u32[]{:S(2)}, u32[]{:S(2)}) collective-permute-start(bf16[6,96,128]{2,1,0:T(8,128)(2,1)} %pack_edges.1), channel_id=1, source_target_pairs={{0,3},{1,2},{2,1},{3,0},{4,7},{5,6},{6,5},{7,4},{8,11},{9,10},{10,... | collective-permute-start | bytes 442376 | tf_op jit(solution)/shard_map/ppermute | solution.py:97
  8.5 0.0 collective-permute-start.1
  8.5 0.0 copy-done.9
  8.6 0.0 copy-start.6
  8.6 0.0 copy-start.7
  8.6 0.0 copy-start.13
  8.6 0.0 copy-start.14
  8.6 6.4 %conv.2 = (f32[96,96,128]{2,1,0:T(8,128)S(1)}, bf16[6,96,1792]{2,1,0:T(8,128)(2,1)S(1)}) custom-call(bf16[96,96,128]{2,1,0:T(8,128)(2,1)S(1)} %bitcast.11, f32[7,7,2,96]{3,2,1,0:T(2,128)S(1)} %bitcast.20), custom_call_target="tpu_custom_call" | custom-call | flops 8000000000 | tf_op jit(solution)/shard_map/conv/pallas_call | solution.py:204
  15.0 0.0 collective-permute-done.refs_6_
  15.0 0.9 %collective-permute-done.1.refs_7_ = bf16[6,96,128]{2,1,0:T(8,128)(2,1)S(1)} collective-permute-done((bf16[6,96,128]{2,1,0:T(8,128)(2,1)}, bf16[6,96,128]{2,1,0:T(8,128)(2,1)S(1)}, u32[]{:S(2)}, u32[]{:S(2)}) %collective-permute-start.1) | collective-permute-done | bytes 147488 | tf_op jit(solution)/shard_map/ppermute | solution.py:97
  15.9 0.0 copy-done.13
  15.9 0.0 copy-done.14
  15.9 7.8 %atmos_block.3 = (bf16[96,96,128]{2,1,0:T(8,128)(2,1)S(1)}, bf16[6,96,128]{2,1,0:T(8,128)(2,1)S(1)}) custom-call(bf16[96,96,128]{2,1,0:T(8,128)(2,1)S(1)} %bitcast.12, f32[96,96,128]{2,1,0:T(8,128)S(1)} %get-tuple-element.34.refs_1_, f32[2,96]{1,0:T(2,128)S(1)} %copy-done.13, bf16[2,96,384]{2,1,0:T(8,128)(2,1)S(1)} %copy-done.6, ...), custom_call_target="tpu_custom_call" | custom-call | flops 8000000000 | tf_op jit(solution)/shard_map/atmos_block/pallas_call | solution.py:488
  23.7 1.8 %collective-permute-start.2 = (bf16[6,96,128]{2,1,0:T(8,128)(2,1)S(1)}, bf16[6,96,128]{2,1,0:T(8,128)(2,1)S(1)}, u32[]{:S(2)}, u32[]{:S(2)}) collective-permute-start(bf16[6,96,128]{2,1,0:T(8,128)(2,1)S(1)} %get-tuple-element.38), channel_id=1, source_target_pairs={{0,3},{1,2},{2,1},{3,0},{4,7},{5,6},{6,5},{7,4},{8,11},{9,10},{10,... | collective-permute-start | bytes 442376 | tf_op jit(solution)/shard_map/ppermute | solution.py:97
  25.5 0.0 collective-permute-start.3
  25.6 6.5 %conv.3 = (f32[96,96,128]{2,1,0:T(8,128)S(1)}, bf16[6,96,1792]{2,1,0:T(8,128)(2,1)S(1)}) custom-call(bf16[96,96,128]{2,1,0:T(8,128)(2,1)S(1)} %get-tuple-element.36.x_ref.refs_0_, f32[7,7,2,96]{3,2,1,0:T(2,128)S(1)} %bitcast.21), custom_call_target="tpu_custom_call" | custom-call | flops 8000000000 | tf_op jit(solution)/shard_map/conv/pallas_call | solution.py:204
  32.1 0.2 collective-permute-done.2.refs_7_
  32.4 0.5 collective-permute-done.3.refs_8_
  32.9 6.4 %atmos_block.4 = (bf16[96,96,128]{2,1,0:T(8,128)(2,1)S(1)}, bf16[2,18,32,128]{3,2,1,0:T(8,128)(2,1)S(1)}, bf16[2,18,32,128]{3,2,1,0:T(8,128)(2,1)S(1)}, bf16[102...) custom-call(bf16[96,96,128]{2,1,0:T(8,128)(2,1)S(1)} %get-tuple-element.36.x_ref.refs_0_, ...), custom_call_target="tpu_custom_call" | custom-call | flops 5000000000 | tf_op jit(solution)/shard_map/atmos_block/pallas_call | solution.py:488
  39.3 0.1 collective-permute-start.4
  39.4 0.0 copy-start.5
  39.4 0.0 copy-start.8
  39.4 0.0 copy-start.10
  39.5 0.0 copy-start.11
  39.5 0.0 copy-start.15
  39.5 0.0 copy-start.16
  39.5 3.0 %atmos_block.5 = (bf16[96,96,128]{2,1,0:T(8,128)(2,1)S(1)}, bf16[2,18,32,128]{3,2,1,0:T(8,128)(2,1)S(1)}, bf16[2,18,32,128]{3,2,1,0:T(8,128)(2,1)S(1)}) custom-call(bf16[96,96,128]{2,1,0:T(8,128)(2,1)S(1)} %get-tuple-element.36.x_ref.refs_0_, f32[96,96,128]{2,1,0:T(8,128)S(1)} %get-tuple-element.37.refs_1_, ...), custom_call_target="tpu_custom_call", output_to_operand_aliasing={{0}: (7, {})} | custom-call | flops 3000000000 | tf_op jit(solution)/shard_map/atmos_block/pallas_call | solution.py:488
  42.5 0.0 collective-permute-done.4.got_ref
  42.5 0.1 add_pairs.2
  42.6 0.5 collective-permute-start.5
  43.1 2.4 %collective-permute-start.6 = (bf16[18,32,128]{2,1,0:T(8,128)(2,1)S(1)}, bf16[18,32,128]{2,1,0:T(8,128)(2,1)S(1)}, u32[]{:S(2)}, u32[]{:S(2)}) collective-permute-start(bf16[18,32,128]{2,1,0:T(8,128)(2,1)S(1)} %get-tuple-element.53), channel_id=1, source_target_pairs={{0,24},{4,28},{8,16},{12,20},{16,8},{20,12},{24,0},{28,4},{1,25},{... | collective-permute-start | bytes 442376 | tf_op jit(solution)/shard_map/ppermute | solution.py:521
  45.5 0.5 collective-permute-start.7
  46.0 0.0 collective-permute-done.5.got_ref.refs_1_
  46.1 0.6 collective-permute-start.8
  46.7 0.0 copy-done.11
  46.7 0.0 copy-done.15
  46.7 0.0 copy-done.16
  46.8 0.0 copy-start.1
  46.8 0.0 copy-start.3
  46.8 1.7 %prepare_ocean.1 = (bf16[6,160,1792]{2,1,0:T(8,128)(2,1)S(1)}, bf16[256,768]{1,0:T(8,128)(2,1)S(1)}, bf16[384,96]{1,0:T(8,128)(2,1)S(1)}, f32[96,128]{1,0:T(8,12...) custom-call(f32[7,7,96]{2,1,0:T(8,128)S(1)} %copy-done.10, ...), custom_call_target="tpu_custom_call" | custom-call | flops 3000000000 | tf_op jit(solution)/shard_map/prepare_ocean/pallas_call | solution.py:254
  48.5 1.9 %collective-permute-done.6.refs_2_ = bf16[18,32,128]{2,1,0:T(8,128)(2,1)S(1)} collective-permute-done((bf16[18,32,128]{2,1,0:T(8,128)(2,1)S(1)}, bf16[18,32,128]{2,1,0:T(8,128)(2,1)S(1)}, u32[]{:S(2)}, u32[]{:S(2)}) %collective-permute-start.6) | collective-permute-done | bytes 147488 | tf_op jit(solution)/shard_map/ppermute | solution.py:521
  50.4 2.6 %collective-permute-done.7.refs_3_ = bf16[18,32,128]{2,1,0:T(8,128)(2,1)S(1)} collective-permute-done((bf16[18,32,128]{2,1,0:T(8,128)(2,1)S(1)}, bf16[18,32,128]{2,1,0:T(8,128)(2,1)S(1)}, u32[]{:S(2)}, u32[]{:S(2)}) %collective-permute-start.7) | collective-permute-done | bytes 147488 | tf_op jit(solution)/shard_map/ppermute | solution.py:521
  53.0 0.1 collective-permute-done.8.refs_4_
  53.1 0.5 ocean_forcing.1
  53.6 2.2 %collective-permute-start.10 = (bf16[2,96,128]{2,1,0:T(8,128)(2,1)S(1)}, bf16[2,96,128]{2,1,0:T(8,128)(2,1)S(1)}, u32[]{:S(2)}, u32[]{:S(2)}) collective-permute-start(bf16[2,96,128]{2,1,0:T(8,128)(2,1)S(1)} %get-tuple-element.59), channel_id=1, source_target_pairs={{0,3},{1,2},{2,1},{3,0},{4,7},{5,6},{6,5},{7,4},{8,11},{9,10},{10,... | collective-permute-start | bytes 147464 | tf_op jit(solution)/shard_map/ppermute | solution.py:97
  55.8 0.5 collective-permute-start.9
  56.3 1.4 %ocean_conv.1.a_ref = f32[12,96,128]{2,1,0:T(8,128)S(1)} custom-call(bf16[18,96,128]{2,1,0:T(8,128)(2,1)S(1)} %get-tuple-element.57.x_ref.mid_ref, bf16[6,160,1792]{2,1,0:T(8,128)(2,1)S(1)} %get-tuple-element.58.band_ref), custom_call_target="tpu_custom_call" | custom-call | flops 2000000000 | tf_op jit(solution)/shard_map/ocean_conv/pallas_call | solution.py:285
  57.7 2.0 %collective-permute-done.10.second_ref = bf16[2,96,128]{2,1,0:T(8,128)(2,1)S(1)} collective-permute-done((bf16[2,96,128]{2,1,0:T(8,128)(2,1)S(1)}, bf16[2,96,128]{2,1,0:T(8,128)(2,1)S(1)}, u32[]{:S(2)}, u32[]{:S(2)}) %collective-permute-start.10) | collective-permute-done | bytes 49184 | tf_op jit(solution)/shard_map/ppermute | solution.py:97
  59.7 0.5 collective-permute-done.9.first_ref
  60.2 2.4 %ocean_block.1 = (bf16[12,96,128]{2,1,0:T(8,128)(2,1)}, bf16[12,8,128]{2,1,0:T(8,128)(2,1)S(1)}) custom-call(bf16[18,96,128]{2,1,0:T(8,128)(2,1)S(1)} %get-tuple-element.57.x_ref.mid_ref, f32[12,96,128]{2,1,0:T(8,128)S(1)} %ocean_conv.1.a_ref, bf16[2,96,128]{2,1,0:T(8,128)(2,1)S(1)} %collective-permute-done.9.first_ref, ...), custom_call_target="tpu_custom_call" | custom-call | tf_op jit(solution)/shard_map/ocean_block/pallas_call | solution.py:598
  62.6 0.0 collective-permute-start.11
  62.6 1.2 %collective-permute-done.11.got_ref = bf16[12,8,128]{2,1,0:T(8,128)(2,1)S(1)} collective-permute-done((bf16[12,8,128]{2,1,0:T(8,128)(2,1)S(1)}, bf16[12,8,128]{2,1,0:T(8,128)(2,1)S(1)}, u32[]{:S(2)}, u32[]{:S(2)}) %collective-permute-start.11) | collective-permute-done | bytes 24608 | tf_op jit(solution)/shard_map/ppermute | solution.py:521
  63.8 1.6 %collective-permute-start.12 = (bf16[2,12,8,128]{3,2,1,0:T(8,128)(2,1)S(1)}, bf16[2,12,8,128]{3,2,1,0:T(8,128)(2,1)S(1)}, u32[]{:S(2)}, u32[]{:S(2)}) collective-permute-start(bf16[2,12,8,128]{3,2,1,0:T(8,128)(2,1)S(1)} %surface_pair.1.refs_0_), channel_id=1, source_target_pairs={{0,24},{4,28},{8,16},{12,20},{16,8},{20,12},{24,0},{28,4},{1,25},{... | collective-permute-start | bytes 147464 | tf_op jit(solution)/shard_map/ppermute | solution.py:521
  65.4 1.3 %collective-permute-start.13 = (bf16[2,12,8,128]{3,2,1,0:T(8,128)(2,1)S(1)}, bf16[2,12,8,128]{3,2,1,0:T(8,128)(2,1)S(1)}, u32[]{:S(2)}, u32[]{:S(2)}) collective-permute-start(bf16[2,12,8,128]{3,2,1,0:T(8,128)(2,1)S(1)} %surface_pair.1.refs_0_), channel_id=1, source_target_pairs={{0,16},{4,20},{8,24},{12,28},{16,0},{20,4},{24,8},{28,12},{1,17},{... | collective-permute-start | bytes 147464 | tf_op jit(solution)/shard_map/ppermute | solution.py:521
  66.7 0.5 collective-permute-start.14
  67.3 0.1 copy.22
  67.4 1.1 %couple.2.refs_3_ = bf16[96,96,128]{2,1,0:T(8,128)(2,1)} custom-call(bf16[96,96,128]{2,1,0:T(8,128)(2,1)S(1)} %get-tuple-element.43.y_ref, s32[96,128]{1,0:T(8,128)S(1)} %copy-done.1, bf16[96,8]{1,0:T(8,128)(2,1)S(1)} %bitcast.13, bf16[2,12,8,128]{3,2,1,0:T(8,128)(2,1)S(1)} %surface_pair.1.refs_0_), custom_call_target="tpu_custom_call" | custom-call | tf_op jit(solution)/shard_map/couple/pallas_call | solution.py:659
  68.5 0.3 collective-permute-done.12.refs_0_
  68.8 0.7 collective-permute-done.13.refs_1_
  69.6 1.3 %collective-permute-done.14.refs_2_ = bf16[2,12,8,128]{3,2,1,0:T(8,128)(2,1)S(1)} collective-permute-done((bf16[2,12,8,128]{3,2,1,0:T(8,128)(2,1)S(1)}, bf16[2,12,8,128]{3,2,1,0:T(8,128)(2,1)S(1)}, u32[]{:S(2)}, u32[]{:S(2)}) %collective-permute-start.14) | collective-permute-done | bytes 49184 | tf_op jit(solution)/shard_map/ppermute | solution.py:521
  70.8 1.5 %couple.3 = bf16[96,96,128]{2,1,0:T(8,128)(2,1)} custom-call(bf16[96,96,128]{2,1,0:T(8,128)(2,1)S(1)} %get-tuple-element.43.y_ref, s32[96,128]{1,0:T(8,128)S(1)} %copy-done.1, bf16[96,8]{1,0:T(8,128)(2,1)S(1)} %bitcast.14, bf16[2,12,8,128]{3,2,1,0:T(8,128)(2,1)S(1)} %collective-permute-done.12.refs_0_, ...), custom_call_target="tpu_custom_call", output_to_operand_aliasing={{}: (6, {})} | custom-call | tf_op jit(solution)/shard_map/couple/pallas_call | solution.py:659
  (18 shorter events, 0.1 us)
Async XLA Ops:
  0.6 7.9 %copy-start = (bf16[1,96,96,128]{3,2,1,0:T(8,128)(2,1)S(1)}, bf16[1,96,96,128]{3,2,1,0:T(8,128)(2,1)}, u32[]{:S(2)}) copy-start(bf16[1,96,96,128]{3,2,1,0:T(8,128)(2,1)} %param.18) | copy-start | bytes 7077892
  0.6 7.9 %copy-start.9 = (f32[2,7,7,96]{3,0,2,1:T(2,128)S(1)}, f32[2,7,7,96]{3,0,2,1:T(2,128)}, u32[]{:S(2)}) copy-start(f32[2,7,7,96]{3,0,2,1:T(2,128)} %param.22) | copy-start | bytes 112900
  3.4 11.6 %collective-permute-start = (bf16[6,96,128]{2,1,0:T(8,128)(2,1)}, bf16[6,96,128]{2,1,0:T(8,128)(2,1)S(1)}, u32[]{:S(2)}, u32[]{:S(2)}) collective-permute-start(bf16[6,96,128]{2,1,0:T(8,128)(2,1)} %pack_edges.1), channel_id=1, source_target_pairs={{0,3},{1,2},{2,1},{3,0},{4,7},{5,6},{6,5},{7,4},{8,11},{9,10},{10,... | collective-permute-start | bytes 442376 | tf_op jit(solution)/shard_map/ppermute | solution.py:97
  8.5 7.3 %collective-permute-start.1 = (bf16[6,96,128]{2,1,0:T(8,128)(2,1)}, bf16[6,96,128]{2,1,0:T(8,128)(2,1)S(1)}, u32[]{:S(2)}, u32[]{:S(2)}) collective-permute-start(bf16[6,96,128]{2,1,0:T(8,128)(2,1)} %pack_edges.1), channel_id=1, source_target_pairs={{0,1},{1,0},{2,3},{3,2},{4,5},{5,4},{6,7},{7,6},{8,9},{9,8},{10,11... | collective-permute-start | bytes 442376 | tf_op jit(solution)/shard_map/ppermute | solution.py:97
  8.6 7.3 %copy-start.6 = (bf16[2,96,384]{2,1,0:T(8,128)(2,1)S(1)}, bf16[2,96,384]{2,1,0:T(8,128)(2,1)}, u32[]{:S(2)}) copy-start(bf16[2,96,384]{2,1,0:T(8,128)(2,1)} %refs_3_.5) | copy-start | bytes 442372
  8.6 7.3 %copy-start.7 = (bf16[2,384,96]{1,2,0:T(8,128)(2,1)S(1)}, bf16[2,384,96]{1,2,0:T(8,128)(2,1)}, u32[]{:S(2)}) copy-start(bf16[2,384,96]{1,2,0:T(8,128)(2,1)} %param.25) | copy-start | bytes 442372
  8.6 7.3 %copy-start.13 = (f32[2,96]{1,0:T(2,128)S(1)}, f32[2,96]{1,0:T(2,128)}, u32[]{:S(2)}) copy-start(f32[2,96]{1,0:T(2,128)} %refs_2_.5) | copy-start | bytes 2308
  8.6 7.3 %copy-start.14 = (f32[2,96]{1,0:T(2,128)S(1)}, f32[2,96]{1,0:T(2,128)}, u32[]{:S(2)}) copy-start(f32[2,96]{1,0:T(2,128)} %refs_5_.5) | copy-start | bytes 2308
  23.7 8.6 %collective-permute-start.2 = (bf16[6,96,128]{2,1,0:T(8,128)(2,1)S(1)}, bf16[6,96,128]{2,1,0:T(8,128)(2,1)S(1)}, u32[]{:S(2)}, u32[]{:S(2)}) collective-permute-start(bf16[6,96,128]{2,1,0:T(8,128)(2,1)S(1)} %get-tuple-element.38), channel_id=1, source_target_pairs={{0,3},{1,2},{2,1},{3,0},{4,7},{5,6},{6,5},{7,4},{8,11},{9,10},{10,... | collective-permute-start | bytes 442376 | tf_op jit(solution)/shard_map/ppermute | solution.py:97
  25.5 7.4 %collective-permute-start.3 = (bf16[6,96,128]{2,1,0:T(8,128)(2,1)S(1)}, bf16[6,96,128]{2,1,0:T(8,128)(2,1)S(1)}, u32[]{:S(2)}, u32[]{:S(2)}) collective-permute-start(bf16[6,96,128]{2,1,0:T(8,128)(2,1)S(1)} %get-tuple-element.38), channel_id=1, source_target_pairs={{0,1},{1,0},{2,3},{3,2},{4,5},{5,4},{6,7},{7,6},{8,9},{9,8},{10,11... | collective-permute-start | bytes 442376 | tf_op jit(solution)/shard_map/ppermute | solution.py:97
  25.6 7.3 %copy-start.12 = (bf16[96,32]{0,1:T(8,128)(2,1)S(1)}, bf16[96,32]{0,1:T(8,128)(2,1)}, u32[]{:S(2)}) copy-start(bf16[96,32]{0,1:T(8,128)(2,1)} %param.27) | copy-start | bytes 18436
  39.3 3.2 %collective-permute-start.4 = (bf16[2,18,32,128]{3,2,1,0:T(8,128)(2,1)S(1)}, bf16[2,18,32,128]{3,2,1,0:T(8,128)(2,1)S(1)}, u32[]{:S(2)}, u32[]{:S(2)}) collective-permute-start(bf16[2,18,32,128]{3,2,1,0:T(8,128)(2,1)S(1)} %get-tuple-element.45), channel_id=1, source_target_pairs={{0,4},{4,0},{8,12},{12,8},{16,20},{20,16},{24,28},{28,24},{1,5},{5... | collective-permute-start | bytes 884744 | tf_op jit(solution)/shard_map/ppermute | solution.py:521
  39.4 7.3 %copy-start.5 = (bf16[96,96,128]{2,1,0:T(8,128)(2,1)S(1)}, bf16[96,96,128]{2,1,0:T(8,128)(2,1)}, u32[]{:S(2)}) copy-start(bf16[96,96,128]{2,1,0:T(8,128)(2,1)} %ocean_ref.1) | copy-start | bytes 7077892
  39.4 7.3 %copy-start.8 = (bf16[96,384]{1,0:T(8,128)(2,1)S(1)}, bf16[96,384]{1,0:T(8,128)(2,1)}, u32[]{:S(2)}) copy-start(bf16[96,384]{1,0:T(8,128)(2,1)} %up_ref.1) | copy-start | bytes 221188
  39.4 7.3 %copy-start.10 = (f32[7,7,96]{2,1,0:T(8,128)S(1)}, f32[7,7,96]{2,1,0:T(8,128)}, u32[]{:S(2)}) copy-start(f32[7,7,96]{2,1,0:T(8,128)} %k_ref.1) | copy-start | bytes 56452
  39.5 7.3 %copy-start.11 = (bf16[2,32,96]{2,1,0:T(8,128)(2,1)S(1)}, bf16[2,32,96]{2,1,0:T(8,128)(2,1)}, u32[]{:S(2)}) copy-start(bf16[2,32,96]{2,1,0:T(8,128)(2,1)} %lift_ref.1) | copy-start | bytes 36868
  39.5 7.3 %copy-start.15 = (f32[96]{0:T(128)S(1)}, f32[96]{0:T(128)}, u32[]{:S(2)}) copy-start(f32[96]{0:T(128)} %param.30) | copy-start | bytes 1156
  39.5 7.3 %copy-start.16 = (f32[96]{0:T(128)S(1)}, f32[96]{0:T(128)}, u32[]{:S(2)}) copy-start(f32[96]{0:T(128)} %param.33) | copy-start | bytes 1156
  42.6 3.5 %collective-permute-start.5 = (bf16[2,18,32,128]{3,2,1,0:T(8,128)(2,1)S(1)}, bf16[2,18,32,128]{3,2,1,0:T(8,128)(2,1)S(1)}, u32[]{:S(2)}, u32[]{:S(2)}) collective-permute-start(bf16[2,18,32,128]{3,2,1,0:T(8,128)(2,1)S(1)} %get-tuple-element.52), channel_id=1, source_target_pairs={{0,4},{4,0},{8,12},{12,8},{16,20},{20,16},{24,28},{28,24},{1,5},{5... | collective-permute-start | bytes 884744 | tf_op jit(solution)/shard_map/ppermute | solution.py:521
  43.1 7.3 %collective-permute-start.6 = (bf16[18,32,128]{2,1,0:T(8,128)(2,1)S(1)}, bf16[18,32,128]{2,1,0:T(8,128)(2,1)S(1)}, u32[]{:S(2)}, u32[]{:S(2)}) collective-permute-start(bf16[18,32,128]{2,1,0:T(8,128)(2,1)S(1)} %get-tuple-element.53), channel_id=1, source_target_pairs={{0,24},{4,28},{8,16},{12,20},{16,8},{20,12},{24,0},{28,4},{1,25},{... | collective-permute-start | bytes 442376 | tf_op jit(solution)/shard_map/ppermute | solution.py:521
  45.5 7.5 %collective-permute-start.7 = (bf16[18,32,128]{2,1,0:T(8,128)(2,1)S(1)}, bf16[18,32,128]{2,1,0:T(8,128)(2,1)S(1)}, u32[]{:S(2)}, u32[]{:S(2)}) collective-permute-start(bf16[18,32,128]{2,1,0:T(8,128)(2,1)S(1)} %get-tuple-element.54), channel_id=1, source_target_pairs={{0,16},{4,20},{8,24},{12,28},{16,0},{20,4},{24,8},{28,12},{1,17},{... | collective-permute-start | bytes 442376 | tf_op jit(solution)/shard_map/ppermute | solution.py:521
  46.1 7.0 %collective-permute-start.8 = (bf16[18,32,128]{2,1,0:T(8,128)(2,1)S(1)}, bf16[18,32,128]{2,1,0:T(8,128)(2,1)S(1)}, u32[]{:S(2)}, u32[]{:S(2)}) collective-permute-start(bf16[18,32,128]{2,1,0:T(8,128)(2,1)S(1)} %add_pairs.3._), channel_id=1, source_target_pairs={{0,8},{4,12},{8,0},{12,4},{16,24},{20,28},{24,16},{28,20},{1,9},{5... | collective-permute-start | bytes 442376 | tf_op jit(solution)/shard_map/ppermute | solution.py:521
  46.8 6.3 %copy-start.1 = (s32[96,128]{1,0:T(8,128)S(1)}, s32[96,128]{1,0:T(8,128)}, u32[]{:S(2)}) copy-start(s32[96,128]{1,0:T(8,128)} %land_ref.5) | copy-start | bytes 147460
  46.8 6.3 %copy-start.3 = (s32[96,128]{1,0:T(8,128)S(1)}, s32[96,128]{1,0:T(8,128)}, u32[]{:S(2)}) copy-start(s32[96,128]{1,0:T(8,128)} %refs_7_.1) | copy-start | bytes 147460
  53.6 6.0 %collective-permute-start.10 = (bf16[2,96,128]{2,1,0:T(8,128)(2,1)S(1)}, bf16[2,96,128]{2,1,0:T(8,128)(2,1)S(1)}, u32[]{:S(2)}, u32[]{:S(2)}) collective-permute-start(bf16[2,96,128]{2,1,0:T(8,128)(2,1)S(1)} %get-tuple-element.59), channel_id=1, source_target_pairs={{0,3},{1,2},{2,1},{3,0},{4,7},{5,6},{6,5},{7,4},{8,11},{9,10},{10,... | collective-permute-start | bytes 147464 | tf_op jit(solution)/shard_map/ppermute | solution.py:97
  55.8 4.3 %collective-permute-start.9 = (bf16[2,96,128]{2,1,0:T(8,128)(2,1)S(1)}, bf16[2,96,128]{2,1,0:T(8,128)(2,1)S(1)}, u32[]{:S(2)}, u32[]{:S(2)}) collective-permute-start(bf16[2,96,128]{2,1,0:T(8,128)(2,1)S(1)} %get-tuple-element.59), channel_id=1, source_target_pairs={{0,1},{1,0},{2,3},{3,2},{4,5},{5,4},{6,7},{7,6},{8,9},{9,8},{10,11... | collective-permute-start | bytes 147464 | tf_op jit(solution)/shard_map/ppermute | solution.py:97
  56.3 3.8 %copy-start.2 = (bf16[384,96]{0,1:T(8,128)(2,1)S(1)}, bf16[384,96]{0,1:T(8,128)(2,1)}, u32[]{:S(2)}) copy-start(bf16[384,96]{0,1:T(8,128)(2,1)} %param.32) | copy-start | bytes 221188
  56.3 3.8 %copy-start.4 = (bf16[96,8]{0,1:T(8,128)(2,1)S(1)}, bf16[96,8]{0,1:T(8,128)(2,1)}, u32[]{:S(2)}) copy-start(bf16[96,8]{0,1:T(8,128)(2,1)} %param.34) | copy-start | bytes 4612
  60.2 7.1 %copy-start.17 = (bf16[8,96]{1,0:T(8,128)(2,1)S(1)}, bf16[8,96]{1,0:T(8,128)(2,1)}, u32[]{:S(2)}) copy-start(bf16[8,96]{1,0:T(8,128)(2,1)} %param.35) | copy-start | bytes 4612
  62.6 1.2 %collective-permute-start.11 = (bf16[12,8,128]{2,1,0:T(8,128)(2,1)S(1)}, bf16[12,8,128]{2,1,0:T(8,128)(2,1)S(1)}, u32[]{:S(2)}, u32[]{:S(2)}) collective-permute-start(bf16[12,8,128]{2,1,0:T(8,128)(2,1)S(1)} %get-tuple-element.64.own_ref), channel_id=1, source_target_pairs={{0,4},{4,0},{8,12},{12,8},{16,20},{20,16},{24,28},{28,24},{1,5},{5... | collective-permute-start | bytes 73736 | tf_op jit(solution)/shard_map/ppermute | solution.py:521
  63.8 5.0 %collective-permute-start.12 = (bf16[2,12,8,128]{3,2,1,0:T(8,128)(2,1)S(1)}, bf16[2,12,8,128]{3,2,1,0:T(8,128)(2,1)S(1)}, u32[]{:S(2)}, u32[]{:S(2)}) collective-permute-start(bf16[2,12,8,128]{3,2,1,0:T(8,128)(2,1)S(1)} %surface_pair.1.refs_0_), channel_id=1, source_target_pairs={{0,24},{4,28},{8,16},{12,20},{16,8},{20,12},{24,0},{28,4},{1,25},{... | collective-permute-start | bytes 147464 | tf_op jit(solution)/shard_map/ppermute | solution.py:521
  65.4 4.1 %collective-permute-start.13 = (bf16[2,12,8,128]{3,2,1,0:T(8,128)(2,1)S(1)}, bf16[2,12,8,128]{3,2,1,0:T(8,128)(2,1)S(1)}, u32[]{:S(2)}, u32[]{:S(2)}) collective-permute-start(bf16[2,12,8,128]{3,2,1,0:T(8,128)(2,1)S(1)} %surface_pair.1.refs_0_), channel_id=1, source_target_pairs={{0,16},{4,20},{8,24},{12,28},{16,0},{20,4},{24,8},{28,12},{1,17},{... | collective-permute-start | bytes 147464 | tf_op jit(solution)/shard_map/ppermute | solution.py:521
  66.7 4.1 %collective-permute-start.14 = (bf16[2,12,8,128]{3,2,1,0:T(8,128)(2,1)S(1)}, bf16[2,12,8,128]{3,2,1,0:T(8,128)(2,1)S(1)}, u32[]{:S(2)}, u32[]{:S(2)}) collective-permute-start(bf16[2,12,8,128]{3,2,1,0:T(8,128)(2,1)S(1)} %surface_pair.1.refs_0_), channel_id=1, source_target_pairs={{0,8},{4,12},{8,0},{12,4},{16,24},{20,28},{24,16},{28,20},{1,9},{5... | collective-permute-start | bytes 147464 | tf_op jit(solution)/shard_map/ppermute | solution.py:521

commit v13 on v12

--- a/solution.py
+++ b/solution.py
@@ -636,11 +636,12 @@
     share = pair_refs[0].shape[1]
     rank = lax.axis_index("member")
     parity = rank % 2
+    back_t = transposed(bw_ref[...])
     copies = []
     for n, (k, pair_ref) in enumerate(zip(ks, pair_refs)):
         first = ((rank // 2) ^ k) * 2 * share
         surf = [pair_ref[side ^ parity, r] for side in range(2) for r in range(share)]
-        back = jnp.dot(bw_ref[...], jnp.concatenate(surf, axis=1), preferred_element_type=F32)
+        back = jnp.dot(back_t, jnp.concatenate(surf, axis=1), preferred_element_type=F32)
         for r in range(2 * share):
             sea = (1 - land_ref[pl.ds(first + r, 1), :]).astype(F32)
             out = y_ref[first + r].astype(F32) + sea * back[:, r * lanes : (r + 1) * lanes]
@@ -736,8 +737,9 @@
     own = make_pair(surface, send_xor(surface, 1))
     rest = tuple(range(half - 1, 0, -1))
     pairs = [send_xor(own, 2 * k) for k in rest]
-    out = couple((0,), state, land_mask, back_weight.T, [own], [])
-    out = couple(rest, state, land_mask, back_weight.T, pairs, [out])
+    out = couple((0,), state, land_mask, back_weight, [own], [])
+    out = couple(rest[:1], state, land_mask, back_weight, pairs[:1], [out])
+    out = couple(rest[1:], state, land_mask, back_weight, pairs[1:], [out])
     return (out[None], ocean_rows)
 
 

time: 72.7 us -> 72.5 us (level)
  waiting for transfers between devices: 12.2 us -> 10.9 us
  Pallas kernels: 41.7 us -> 42.5 us
    pallas_call x2 -> x3, Pallas kernels: 2.63 us -> 3.74 us  [couple(): pl.pallas_call(functools.partial(couple_kernel, ks), out_shape=jax.ShapeD...]
    ppermute x9, waiting for transfers between devices: 8.11 us -> 7.02 us  [send_xor(): lax.ppermute(value, 'member', [(i, i ^ bits) for i in range(members)])]
  transfers between devices with their start and end apart: 15 -> 15, of which waited for: 12 -> 8; matrix products, arithmetic and copies ran while one was open for 0% -> 0% of each run, Pallas kernels for 28% -> 30%
where the time goes in v13:
time: 72.5 us; the launch traced here: 72.4 us
  Pallas kernels  42.5 us (59%)
  starting transfers between devices  17.8 us (25%)
  waiting for transfers between devices  10.9 us (15%)
  between operations  1.12 us (2%)
    pallas_call x3, Pallas kernels, atmos_block(): pl.pallas_call(functools.partial(atmos_kernel, layer, near, members, coun...  16.9 us
    pallas_call x2, Pallas kernels, convolve(): pl.pallas_call(functools.partial(conv_kernel, layer), out_shape=[jax.Shap...  12.9 us
    ppermute x6, starting transfers between devices, neighbours(): lax.ppermute(packed, 'lon', pairs)  10.1 us
    ppermute x9, starting transfers between devices, send_xor(): lax.ppermute(value, 'member', [(i, i ^ bits) for i in range(members)])  7.64 us
    ppermute x9, waiting for transfers between devices, send_xor(): lax.ppermute(value, 'member', [(i, i ^ bits) for i in range(members)])  7.02 us
    ppermute x6, waiting for transfers between devices, neighbours(): lax.ppermute(packed, 'lon', pairs)  3.87 us
    pallas_call x3, Pallas kernels, couple(): pl.pallas_call(functools.partial(couple_kernel, ks), out_shape=jax.ShapeD...  3.74 us
    pallas_call x1, Pallas kernels, pack(): pl.pallas_call(functools.partial(pack_kernel, step), out_shape=jax.ShapeD...  2.77 us
  transfers between devices with their start and end apart: 15, of which 8 were waited for; matrix products, arithmetic and copies ran while one was open for 0% of the time, Pallas kernels for 30%

profile of v13, /device:TPU:0, one launch (start us, length us, event | category | flops | bytes accessed | tf_op | source)
XLA Modules:
  0.0 72.4 jit_solution(18361127195231079786)
XLA Ops:
  0.6 0.0 copy-start
  0.6 0.0 copy-start.10
  0.6 2.8 %pack_edges.1 = bf16[6,96,128]{2,1,0:T(8,128)(2,1)} custom-call(bf16[96,96,128]{2,1,0:T(8,128)(2,1)} %bitcast.9), custom_call_target="tpu_custom_call" | custom-call | tf_op jit(solution)/shard_map/pack_edges/pallas_call | solution.py:81
  3.4 3.1 %collective-permute-start.1 = (bf16[6,96,128]{2,1,0:T(8,128)(2,1)}, bf16[6,96,128]{2,1,0:T(8,128)(2,1)S(1)}, u32[]{:S(2)}, u32[]{:S(2)}) collective-permute-start(bf16[6,96,128]{2,1,0:T(8,128)(2,1)} %pack_edges.1), channel_id=1, source_target_pairs={{0,1},{1,0},{2,3},{3,2},{4,5},{5,4},{6,7},{7,6},{8,9},{9,8},{10,11... | collective-permute-start | bytes 442376 | tf_op jit(solution)/shard_map/ppermute | solution.py:97
  6.5 2.5 %collective-permute-start = (bf16[6,96,128]{2,1,0:T(8,128)(2,1)}, bf16[6,96,128]{2,1,0:T(8,128)(2,1)S(1)}, u32[]{:S(2)}, u32[]{:S(2)}) collective-permute-start(bf16[6,96,128]{2,1,0:T(8,128)(2,1)} %pack_edges.1), channel_id=1, source_target_pairs={{0,3},{1,2},{2,1},{3,0},{4,7},{5,6},{6,5},{7,4},{8,11},{9,10},{10,... | collective-permute-start | bytes 442376 | tf_op jit(solution)/shard_map/ppermute | solution.py:97
  9.0 0.0 copy-done.10
  9.0 0.0 copy-start.14
  9.0 0.0 copy-start.15
  9.0 6.4 %conv.2 = (f32[96,96,128]{2,1,0:T(8,128)S(1)}, bf16[6,96,1792]{2,1,0:T(8,128)(2,1)S(1)}) custom-call(bf16[96,96,128]{2,1,0:T(8,128)(2,1)S(1)} %bitcast.10, f32[7,7,2,96]{3,2,1,0:T(2,128)S(1)} %bitcast.17), custom_call_target="tpu_custom_call" | custom-call | flops 8000000000 | tf_op jit(solution)/shard_map/conv/pallas_call | solution.py:204
  15.4 0.0 collective-permute-done.1.refs_7_
  15.4 0.6 collective-permute-done.refs_6_
  16.0 0.0 copy-done.15
  16.1 7.6 %atmos_block.3 = (bf16[96,96,128]{2,1,0:T(8,128)(2,1)S(1)}, bf16[6,96,128]{2,1,0:T(8,128)(2,1)S(1)}) custom-call(bf16[96,96,128]{2,1,0:T(8,128)(2,1)S(1)} %bitcast.11, f32[96,96,128]{2,1,0:T(8,128)S(1)} %get-tuple-element.34.refs_1_, f32[2,96]{1,0:T(2,128)S(1)} %copy-done.14, bf16[2,96,384]{2,1,0:T(8,128)(2,1)S(1)} %copy-done.7, ...), custom_call_target="tpu_custom_call" | custom-call | flops 8000000000 | tf_op jit(solution)/shard_map/atmos_block/pallas_call | solution.py:488
  23.7 0.7 collective-permute-start.3
  24.4 2.6 %collective-permute-start.2 = (bf16[6,96,128]{2,1,0:T(8,128)(2,1)S(1)}, bf16[6,96,128]{2,1,0:T(8,128)(2,1)S(1)}, u32[]{:S(2)}, u32[]{:S(2)}) collective-permute-start(bf16[6,96,128]{2,1,0:T(8,128)(2,1)S(1)} %get-tuple-element.38), channel_id=1, source_target_pairs={{0,3},{1,2},{2,1},{3,0},{4,7},{5,6},{6,5},{7,4},{8,11},{9,10},{10,... | collective-permute-start | bytes 442376 | tf_op jit(solution)/shard_map/ppermute | solution.py:97
  27.0 6.5 %conv.3 = (f32[96,96,128]{2,1,0:T(8,128)S(1)}, bf16[6,96,1792]{2,1,0:T(8,128)(2,1)S(1)}) custom-call(bf16[96,96,128]{2,1,0:T(8,128)(2,1)S(1)} %get-tuple-element.36.x_ref.refs_0_, f32[7,7,2,96]{3,2,1,0:T(2,128)S(1)} %bitcast.18), custom_call_target="tpu_custom_call" | custom-call | flops 8000000000 | tf_op jit(solution)/shard_map/conv/pallas_call | solution.py:204
  33.5 0.0 collective-permute-done.3.refs_8_
  33.6 0.0 collective-permute-done.2.refs_7_
  33.6 0.0 copy-done.13
  33.6 6.3 %atmos_block.4 = (bf16[96,96,128]{2,1,0:T(8,128)(2,1)S(1)}, bf16[2,18,32,128]{3,2,1,0:T(8,128)(2,1)S(1)}, bf16[2,18,32,128]{3,2,1,0:T(8,128)(2,1)S(1)}, bf16[102...) custom-call(bf16[96,96,128]{2,1,0:T(8,128)(2,1)S(1)} %get-tuple-element.36.x_ref.refs_0_, ...), custom_call_target="tpu_custom_call" | custom-call | flops 5000000000 | tf_op jit(solution)/shard_map/atmos_block/pallas_call | solution.py:488
  39.9 0.1 collective-permute-start.4
  40.0 0.0 copy-start.6
  40.0 0.0 copy-start.9
  40.0 0.0 copy-start.11
  40.0 0.0 copy-start.12
  40.0 0.0 copy-start.16
  40.0 0.0 copy-start.17
  40.0 2.9 %atmos_block.5 = (bf16[96,96,128]{2,1,0:T(8,128)(2,1)S(1)}, bf16[2,18,32,128]{3,2,1,0:T(8,128)(2,1)S(1)}, bf16[2,18,32,128]{3,2,1,0:T(8,128)(2,1)S(1)}) custom-call(bf16[96,96,128]{2,1,0:T(8,128)(2,1)S(1)} %get-tuple-element.36.x_ref.refs_0_, f32[96,96,128]{2,1,0:T(8,128)S(1)} %get-tuple-element.37.refs_1_, ...), custom_call_target="tpu_custom_call", output_to_operand_aliasing={{0}: (7, {})} | custom-call | flops 3000000000 | tf_op jit(solution)/shard_map/atmos_block/pallas_call | solution.py:488
  43.0 0.0 collective-permute-done.4.got_ref
  43.0 0.1 add_pairs.2
  43.1 0.5 collective-permute-start.5
  43.6 2.4 %collective-permute-start.6 = (bf16[18,32,128]{2,1,0:T(8,128)(2,1)S(1)}, bf16[18,32,128]{2,1,0:T(8,128)(2,1)S(1)}, u32[]{:S(2)}, u32[]{:S(2)}) collective-permute-start(bf16[18,32,128]{2,1,0:T(8,128)(2,1)S(1)} %get-tuple-element.53), channel_id=1, source_target_pairs={{0,24},{4,28},{8,16},{12,20},{16,8},{20,12},{24,0},{28,4},{1,25},{... | collective-permute-start | bytes 442376 | tf_op jit(solution)/shard_map/ppermute | solution.py:521
  46.0 0.5 collective-permute-start.7
  46.6 0.0 collective-permute-done.5.got_ref.refs_1_
  46.6 0.6 collective-permute-start.8
  47.2 0.0 copy-done.11
  47.2 0.0 copy-start.1
  47.2 0.0 copy-start.3
  47.3 1.7 %prepare_ocean.1 = (bf16[6,160,1792]{2,1,0:T(8,128)(2,1)S(1)}, bf16[256,768]{1,0:T(8,128)(2,1)S(1)}, bf16[384,96]{1,0:T(8,128)(2,1)S(1)}, f32[96,128]{1,0:T(8,12...) custom-call(f32[7,7,96]{2,1,0:T(8,128)S(1)} %copy-done.11, ...), custom_call_target="tpu_custom_call" | custom-call | flops 3000000000 | tf_op jit(solution)/shard_map/prepare_ocean/pallas_call | solution.py:254
  49.0 1.9 %collective-permute-done.6.refs_2_ = bf16[18,32,128]{2,1,0:T(8,128)(2,1)S(1)} collective-permute-done((bf16[18,32,128]{2,1,0:T(8,128)(2,1)S(1)}, bf16[18,32,128]{2,1,0:T(8,128)(2,1)S(1)}, u32[]{:S(2)}, u32[]{:S(2)}) %collective-permute-start.6) | collective-permute-done | bytes 147488 | tf_op jit(solution)/shard_map/ppermute | solution.py:521
  50.9 2.6 %collective-permute-done.7.refs_3_ = bf16[18,32,128]{2,1,0:T(8,128)(2,1)S(1)} collective-permute-done((bf16[18,32,128]{2,1,0:T(8,128)(2,1)S(1)}, bf16[18,32,128]{2,1,0:T(8,128)(2,1)S(1)}, u32[]{:S(2)}, u32[]{:S(2)}) %collective-permute-start.7) | collective-permute-done | bytes 147488 | tf_op jit(solution)/shard_map/ppermute | solution.py:521
  53.5 0.1 collective-permute-done.8.refs_4_
  53.6 0.0 copy-done.1
  53.6 0.5 ocean_forcing.1
  54.1 1.3 %collective-permute-start.10 = (bf16[2,96,128]{2,1,0:T(8,128)(2,1)S(1)}, bf16[2,96,128]{2,1,0:T(8,128)(2,1)S(1)}, u32[]{:S(2)}, u32[]{:S(2)}) collective-permute-start(bf16[2,96,128]{2,1,0:T(8,128)(2,1)S(1)} %get-tuple-element.59), channel_id=1, source_target_pairs={{0,3},{1,2},{2,1},{3,0},{4,7},{5,6},{6,5},{7,4},{8,11},{9,10},{10,... | collective-permute-start | bytes 147464 | tf_op jit(solution)/shard_map/ppermute | solution.py:97
  55.4 0.0 collective-permute-start.9
  55.4 1.4 %ocean_conv.1.a_ref = f32[12,96,128]{2,1,0:T(8,128)S(1)} custom-call(bf16[18,96,128]{2,1,0:T(8,128)(2,1)S(1)} %get-tuple-element.57.x_ref.mid_ref, bf16[6,160,1792]{2,1,0:T(8,128)(2,1)S(1)} %get-tuple-element.58.band_ref), custom_call_target="tpu_custom_call" | custom-call | flops 2000000000 | tf_op jit(solution)/shard_map/ocean_conv/pallas_call | solution.py:285
  56.8 3.3 %collective-permute-done.10.second_ref = bf16[2,96,128]{2,1,0:T(8,128)(2,1)S(1)} collective-permute-done((bf16[2,96,128]{2,1,0:T(8,128)(2,1)S(1)}, bf16[2,96,128]{2,1,0:T(8,128)(2,1)S(1)}, u32[]{:S(2)}, u32[]{:S(2)}) %collective-permute-start.10) | collective-permute-done | bytes 49184 | tf_op jit(solution)/shard_map/ppermute | solution.py:97
  60.1 0.0 collective-permute-done.9.first_ref
  60.1 0.0 copy-done.5
  60.1 0.0 copy-start.4
  60.1 2.4 %ocean_block.1 = (bf16[12,96,128]{2,1,0:T(8,128)(2,1)}, bf16[12,8,128]{2,1,0:T(8,128)(2,1)S(1)}) custom-call(bf16[18,96,128]{2,1,0:T(8,128)(2,1)S(1)} %get-tuple-element.57.x_ref.mid_ref, f32[12,96,128]{2,1,0:T(8,128)S(1)} %ocean_conv.1.a_ref, bf16[2,96,128]{2,1,0:T(8,128)(2,1)S(1)} %collective-permute-done.9.first_ref, ...), custom_call_target="tpu_custom_call" | custom-call | tf_op jit(solution)/shard_map/ocean_block/pallas_call | solution.py:598
  62.5 0.0 collective-permute-start.11
  62.5 1.2 %collective-permute-done.11.got_ref = bf16[12,8,128]{2,1,0:T(8,128)(2,1)S(1)} collective-permute-done((bf16[12,8,128]{2,1,0:T(8,128)(2,1)S(1)}, bf16[12,8,128]{2,1,0:T(8,128)(2,1)S(1)}, u32[]{:S(2)}, u32[]{:S(2)}) %collective-permute-start.11) | collective-permute-done | bytes 24608 | tf_op jit(solution)/shard_map/ppermute | solution.py:521
  63.7 1.6 %collective-permute-start.14 = (bf16[2,12,8,128]{3,2,1,0:T(8,128)(2,1)S(1)}, bf16[2,12,8,128]{3,2,1,0:T(8,128)(2,1)S(1)}, u32[]{:S(2)}, u32[]{:S(2)}) collective-permute-start(bf16[2,12,8,128]{3,2,1,0:T(8,128)(2,1)S(1)} %surface_pair.1.refs_0_), channel_id=1, source_target_pairs={{0,24},{4,28},{8,16},{12,20},{16,8},{20,12},{24,0},{28,4},{1,25},{... | collective-permute-start | bytes 147464 | tf_op jit(solution)/shard_map/ppermute | solution.py:521
  65.4 1.3 %collective-permute-start.13 = (bf16[2,12,8,128]{3,2,1,0:T(8,128)(2,1)S(1)}, bf16[2,12,8,128]{3,2,1,0:T(8,128)(2,1)S(1)}, u32[]{:S(2)}, u32[]{:S(2)}) collective-permute-start(bf16[2,12,8,128]{3,2,1,0:T(8,128)(2,1)S(1)} %surface_pair.1.refs_0_), channel_id=1, source_target_pairs={{0,8},{4,12},{8,0},{12,4},{16,24},{20,28},{24,16},{28,20},{1,9},{5... | collective-permute-start | bytes 147464 | tf_op jit(solution)/shard_map/ppermute | solution.py:521
  66.7 0.5 collective-permute-start.12
  67.2 0.0 copy-done.4
  67.2 1.2 %couple.3.refs_1_ = bf16[96,96,128]{2,1,0:T(8,128)(2,1)} custom-call(bf16[96,96,128]{2,1,0:T(8,128)(2,1)S(1)} %get-tuple-element.43.y_ref, s32[96,128]{1,0:T(8,128)S(1)} %copy-done.1, bf16[8,96]{1,0:T(8,128)(2,1)S(1)} %copy-done.4, bf16[2,12,8,128]{3,2,1,0:T(8,128)(2,1)S(1)} %surface_pair.1.refs_0_), custom_call_target="tpu_custom_call" | custom-call | tf_op jit(solution)/shard_map/couple/pallas_call | solution.py:660
  68.4 0.5 collective-permute-done.14.refs_0_
  68.9 1.2 %couple.4.refs_2_ = bf16[96,96,128]{2,1,0:T(8,128)(2,1)} custom-call(bf16[96,96,128]{2,1,0:T(8,128)(2,1)S(1)} %get-tuple-element.43.y_ref, s32[96,128]{1,0:T(8,128)S(1)} %copy-done.1, bf16[8,96]{1,0:T(8,128)(2,1)S(1)} %copy-done.4, bf16[2,12,8,128]{3,2,1,0:T(8,128)(2,1)S(1)} %collective-permute-done.14.refs_0_, ...), custom_call_target="tpu_custom_call", output_to_operand_aliasing={{}: (4, {})} | custom-call | tf_op jit(solution)/shard_map/couple/pallas_call | solution.py:660
  70.1 0.0 collective-permute-done.13.refs_1_
  70.1 0.7 collective-permute-done.12.refs_0_
  70.8 1.4 %couple.5 = bf16[96,96,128]{2,1,0:T(8,128)(2,1)} custom-call(bf16[96,96,128]{2,1,0:T(8,128)(2,1)S(1)} %get-tuple-element.43.y_ref, s32[96,128]{1,0:T(8,128)S(1)} %copy-done.1, bf16[8,96]{1,0:T(8,128)(2,1)S(1)} %copy-done.4, bf16[2,12,8,128]{3,2,1,0:T(8,128)(2,1)S(1)} %collective-permute-done.12.refs_0_, ...), custom_call_target="tpu_custom_call", output_to_operand_aliasing={{}: (5, {})} | custom-call | tf_op jit(solution)/shard_map/couple/pallas_call | solution.py:660
  (18 shorter events, 0.1 us)
Async XLA Ops:
  0.6 8.4 %copy-start = (bf16[1,96,96,128]{3,2,1,0:T(8,128)(2,1)S(1)}, bf16[1,96,96,128]{3,2,1,0:T(8,128)(2,1)}, u32[]{:S(2)}) copy-start(bf16[1,96,96,128]{3,2,1,0:T(8,128)(2,1)} %param.18) | copy-start | bytes 7077892
  0.6 8.4 %copy-start.10 = (f32[2,7,7,96]{3,0,2,1:T(2,128)S(1)}, f32[2,7,7,96]{3,0,2,1:T(2,128)}, u32[]{:S(2)}) copy-start(f32[2,7,7,96]{3,0,2,1:T(2,128)} %param.22) | copy-start | bytes 112900
  3.4 12.0 %collective-permute-start.1 = (bf16[6,96,128]{2,1,0:T(8,128)(2,1)}, bf16[6,96,128]{2,1,0:T(8,128)(2,1)S(1)}, u32[]{:S(2)}, u32[]{:S(2)}) collective-permute-start(bf16[6,96,128]{2,1,0:T(8,128)(2,1)} %pack_edges.1), channel_id=1, source_target_pairs={{0,1},{1,0},{2,3},{3,2},{4,5},{5,4},{6,7},{7,6},{8,9},{9,8},{10,11... | collective-permute-start | bytes 442376 | tf_op jit(solution)/shard_map/ppermute | solution.py:97
  6.5 9.5 %collective-permute-start = (bf16[6,96,128]{2,1,0:T(8,128)(2,1)}, bf16[6,96,128]{2,1,0:T(8,128)(2,1)S(1)}, u32[]{:S(2)}, u32[]{:S(2)}) collective-permute-start(bf16[6,96,128]{2,1,0:T(8,128)(2,1)} %pack_edges.1), channel_id=1, source_target_pairs={{0,3},{1,2},{2,1},{3,0},{4,7},{5,6},{6,5},{7,4},{8,11},{9,10},{10,... | collective-permute-start | bytes 442376 | tf_op jit(solution)/shard_map/ppermute | solution.py:97
  9.0 7.0 %copy-start.7 = (bf16[2,96,384]{2,1,0:T(8,128)(2,1)S(1)}, bf16[2,96,384]{2,1,0:T(8,128)(2,1)}, u32[]{:S(2)}) copy-start(bf16[2,96,384]{2,1,0:T(8,128)(2,1)} %refs_3_.5) | copy-start | bytes 442372
  9.0 7.0 %copy-start.8 = (bf16[2,384,96]{1,2,0:T(8,128)(2,1)S(1)}, bf16[2,384,96]{1,2,0:T(8,128)(2,1)}, u32[]{:S(2)}) copy-start(bf16[2,384,96]{1,2,0:T(8,128)(2,1)} %param.25) | copy-start | bytes 442372
  9.0 7.0 %copy-start.14 = (f32[2,96]{1,0:T(2,128)S(1)}, f32[2,96]{1,0:T(2,128)}, u32[]{:S(2)}) copy-start(f32[2,96]{1,0:T(2,128)} %refs_2_.5) | copy-start | bytes 2308
  9.0 7.0 %copy-start.15 = (f32[2,96]{1,0:T(2,128)S(1)}, f32[2,96]{1,0:T(2,128)}, u32[]{:S(2)}) copy-start(f32[2,96]{1,0:T(2,128)} %refs_5_.5) | copy-start | bytes 2308
  23.7 9.8 %collective-permute-start.3 = (bf16[6,96,128]{2,1,0:T(8,128)(2,1)S(1)}, bf16[6,96,128]{2,1,0:T(8,128)(2,1)S(1)}, u32[]{:S(2)}, u32[]{:S(2)}) collective-permute-start(bf16[6,96,128]{2,1,0:T(8,128)(2,1)S(1)} %get-tuple-element.38), channel_id=1, source_target_pairs={{0,1},{1,0},{2,3},{3,2},{4,5},{5,4},{6,7},{7,6},{8,9},{9,8},{10,11... | collective-permute-start | bytes 442376 | tf_op jit(solution)/shard_map/ppermute | solution.py:97
  24.4 9.2 %collective-permute-start.2 = (bf16[6,96,128]{2,1,0:T(8,128)(2,1)S(1)}, bf16[6,96,128]{2,1,0:T(8,128)(2,1)S(1)}, u32[]{:S(2)}, u32[]{:S(2)}) collective-permute-start(bf16[6,96,128]{2,1,0:T(8,128)(2,1)S(1)} %get-tuple-element.38), channel_id=1, source_target_pairs={{0,3},{1,2},{2,1},{3,0},{4,7},{5,6},{6,5},{7,4},{8,11},{9,10},{10,... | collective-permute-start | bytes 442376 | tf_op jit(solution)/shard_map/ppermute | solution.py:97
  27.0 6.6 %copy-start.13 = (bf16[96,32]{0,1:T(8,128)(2,1)S(1)}, bf16[96,32]{0,1:T(8,128)(2,1)}, u32[]{:S(2)}) copy-start(bf16[96,32]{0,1:T(8,128)(2,1)} %param.27) | copy-start | bytes 18436
  39.9 3.1 %collective-permute-start.4 = (bf16[2,18,32,128]{3,2,1,0:T(8,128)(2,1)S(1)}, bf16[2,18,32,128]{3,2,1,0:T(8,128)(2,1)S(1)}, u32[]{:S(2)}, u32[]{:S(2)}) collective-permute-start(bf16[2,18,32,128]{3,2,1,0:T(8,128)(2,1)S(1)} %get-tuple-element.45), channel_id=1, source_target_pairs={{0,4},{4,0},{8,12},{12,8},{16,20},{20,16},{24,28},{28,24},{1,5},{5... | collective-permute-start | bytes 884744 | tf_op jit(solution)/shard_map/ppermute | solution.py:521
  40.0 7.2 %copy-start.6 = (bf16[96,96,128]{2,1,0:T(8,128)(2,1)S(1)}, bf16[96,96,128]{2,1,0:T(8,128)(2,1)}, u32[]{:S(2)}) copy-start(bf16[96,96,128]{2,1,0:T(8,128)(2,1)} %ocean_ref.1) | copy-start | bytes 7077892
  40.0 7.2 %copy-start.9 = (bf16[96,384]{1,0:T(8,128)(2,1)S(1)}, bf16[96,384]{1,0:T(8,128)(2,1)}, u32[]{:S(2)}) copy-start(bf16[96,384]{1,0:T(8,128)(2,1)} %up_ref.1) | copy-start | bytes 221188
  40.0 7.2 %copy-start.11 = (f32[7,7,96]{2,1,0:T(8,128)S(1)}, f32[7,7,96]{2,1,0:T(8,128)}, u32[]{:S(2)}) copy-start(f32[7,7,96]{2,1,0:T(8,128)} %k_ref.1) | copy-start | bytes 56452
  40.0 7.2 %copy-start.12 = (bf16[2,32,96]{2,1,0:T(8,128)(2,1)S(1)}, bf16[2,32,96]{2,1,0:T(8,128)(2,1)}, u32[]{:S(2)}) copy-start(bf16[2,32,96]{2,1,0:T(8,128)(2,1)} %lift_ref.1) | copy-start | bytes 36868
  40.0 7.2 %copy-start.16 = (f32[96]{0:T(128)S(1)}, f32[96]{0:T(128)}, u32[]{:S(2)}) copy-start(f32[96]{0:T(128)} %param.30) | copy-start | bytes 1156
  40.0 7.2 %copy-start.17 = (f32[96]{0:T(128)S(1)}, f32[96]{0:T(128)}, u32[]{:S(2)}) copy-start(f32[96]{0:T(128)} %param.33) | copy-start | bytes 1156
  43.1 3.5 %collective-permute-start.5 = (bf16[2,18,32,128]{3,2,1,0:T(8,128)(2,1)S(1)}, bf16[2,18,32,128]{3,2,1,0:T(8,128)(2,1)S(1)}, u32[]{:S(2)}, u32[]{:S(2)}) collective-permute-start(bf16[2,18,32,128]{3,2,1,0:T(8,128)(2,1)S(1)} %get-tuple-element.52), channel_id=1, source_target_pairs={{0,4},{4,0},{8,12},{12,8},{16,20},{20,16},{24,28},{28,24},{1,5},{5... | collective-permute-start | bytes 884744 | tf_op jit(solution)/shard_map/ppermute | solution.py:521
  43.6 7.3 %collective-permute-start.6 = (bf16[18,32,128]{2,1,0:T(8,128)(2,1)S(1)}, bf16[18,32,128]{2,1,0:T(8,128)(2,1)S(1)}, u32[]{:S(2)}, u32[]{:S(2)}) collective-permute-start(bf16[18,32,128]{2,1,0:T(8,128)(2,1)S(1)} %get-tuple-element.53), channel_id=1, source_target_pairs={{0,24},{4,28},{8,16},{12,20},{16,8},{20,12},{24,0},{28,4},{1,25},{... | collective-permute-start | bytes 442376 | tf_op jit(solution)/shard_map/ppermute | solution.py:521
  46.0 7.4 %collective-permute-start.7 = (bf16[18,32,128]{2,1,0:T(8,128)(2,1)S(1)}, bf16[18,32,128]{2,1,0:T(8,128)(2,1)S(1)}, u32[]{:S(2)}, u32[]{:S(2)}) collective-permute-start(bf16[18,32,128]{2,1,0:T(8,128)(2,1)S(1)} %get-tuple-element.54), channel_id=1, source_target_pairs={{0,16},{4,20},{8,24},{12,28},{16,0},{20,4},{24,8},{28,12},{1,17},{... | collective-permute-start | bytes 442376 | tf_op jit(solution)/shard_map/ppermute | solution.py:521
  46.6 7.0 %collective-permute-start.8 = (bf16[18,32,128]{2,1,0:T(8,128)(2,1)S(1)}, bf16[18,32,128]{2,1,0:T(8,128)(2,1)S(1)}, u32[]{:S(2)}, u32[]{:S(2)}) collective-permute-start(bf16[18,32,128]{2,1,0:T(8,128)(2,1)S(1)} %add_pairs.3._), channel_id=1, source_target_pairs={{0,8},{4,12},{8,0},{12,4},{16,24},{20,28},{24,16},{28,20},{1,9},{5... | collective-permute-start | bytes 442376 | tf_op jit(solution)/shard_map/ppermute | solution.py:521
  47.2 6.4 %copy-start.1 = (s32[96,128]{1,0:T(8,128)S(1)}, s32[96,128]{1,0:T(8,128)}, u32[]{:S(2)}) copy-start(s32[96,128]{1,0:T(8,128)} %land_ref.7) | copy-start | bytes 147460
  47.2 6.3 %copy-start.3 = (s32[96,128]{1,0:T(8,128)S(1)}, s32[96,128]{1,0:T(8,128)}, u32[]{:S(2)}) copy-start(s32[96,128]{1,0:T(8,128)} %refs_7_.1) | copy-start | bytes 147460
  54.1 6.0 %collective-permute-start.10 = (bf16[2,96,128]{2,1,0:T(8,128)(2,1)S(1)}, bf16[2,96,128]{2,1,0:T(8,128)(2,1)S(1)}, u32[]{:S(2)}, u32[]{:S(2)}) collective-permute-start(bf16[2,96,128]{2,1,0:T(8,128)(2,1)S(1)} %get-tuple-element.59), channel_id=1, source_target_pairs={{0,3},{1,2},{2,1},{3,0},{4,7},{5,6},{6,5},{7,4},{8,11},{9,10},{10,... | collective-permute-start | bytes 147464 | tf_op jit(solution)/shard_map/ppermute | solution.py:97
  55.4 4.7 %collective-permute-start.9 = (bf16[2,96,128]{2,1,0:T(8,128)(2,1)S(1)}, bf16[2,96,128]{2,1,0:T(8,128)(2,1)S(1)}, u32[]{:S(2)}, u32[]{:S(2)}) collective-permute-start(bf16[2,96,128]{2,1,0:T(8,128)(2,1)S(1)} %get-tuple-element.59), channel_id=1, source_target_pairs={{0,1},{1,0},{2,3},{3,2},{4,5},{5,4},{6,7},{7,6},{8,9},{9,8},{10,11... | collective-permute-start | bytes 147464 | tf_op jit(solution)/shard_map/ppermute | solution.py:97
  55.4 4.7 %copy-start.2 = (bf16[384,96]{0,1:T(8,128)(2,1)S(1)}, bf16[384,96]{0,1:T(8,128)(2,1)}, u32[]{:S(2)}) copy-start(bf16[384,96]{0,1:T(8,128)(2,1)} %param.32) | copy-start | bytes 221188
  55.4 4.7 %copy-start.5 = (bf16[96,8]{0,1:T(8,128)(2,1)S(1)}, bf16[96,8]{0,1:T(8,128)(2,1)}, u32[]{:S(2)}) copy-start(bf16[96,8]{0,1:T(8,128)(2,1)} %param.34) | copy-start | bytes 4612
  60.1 7.1 %copy-start.4 = (bf16[8,96]{1,0:T(8,128)(2,1)S(1)}, bf16[8,96]{1,0:T(8,128)(2,1)}, u32[]{:S(2)}) copy-start(bf16[8,96]{1,0:T(8,128)(2,1)} %bw_ref.5) | copy-start | bytes 4612
  62.5 1.2 %collective-permute-start.11 = (bf16[12,8,128]{2,1,0:T(8,128)(2,1)S(1)}, bf16[12,8,128]{2,1,0:T(8,128)(2,1)S(1)}, u32[]{:S(2)}, u32[]{:S(2)}) collective-permute-start(bf16[12,8,128]{2,1,0:T(8,128)(2,1)S(1)} %get-tuple-element.64.own_ref), channel_id=1, source_target_pairs={{0,4},{4,0},{8,12},{12,8},{16,20},{20,16},{24,28},{28,24},{1,5},{5... | collective-permute-start | bytes 73736 | tf_op jit(solution)/shard_map/ppermute | solution.py:521
  63.7 5.2 %collective-permute-start.14 = (bf16[2,12,8,128]{3,2,1,0:T(8,128)(2,1)S(1)}, bf16[2,12,8,128]{3,2,1,0:T(8,128)(2,1)S(1)}, u32[]{:S(2)}, u32[]{:S(2)}) collective-permute-start(bf16[2,12,8,128]{3,2,1,0:T(8,128)(2,1)S(1)} %surface_pair.1.refs_0_), channel_id=1, source_target_pairs={{0,24},{4,28},{8,16},{12,20},{16,8},{20,12},{24,0},{28,4},{1,25},{... | collective-permute-start | bytes 147464 | tf_op jit(solution)/shard_map/ppermute | solution.py:521
  65.4 4.7 %collective-permute-start.13 = (bf16[2,12,8,128]{3,2,1,0:T(8,128)(2,1)S(1)}, bf16[2,12,8,128]{3,2,1,0:T(8,128)(2,1)S(1)}, u32[]{:S(2)}, u32[]{:S(2)}) collective-permute-start(bf16[2,12,8,128]{3,2,1,0:T(8,128)(2,1)S(1)} %surface_pair.1.refs_0_), channel_id=1, source_target_pairs={{0,8},{4,12},{8,0},{12,4},{16,24},{20,28},{24,16},{28,20},{1,9},{5... | collective-permute-start | bytes 147464 | tf_op jit(solution)/shard_map/ppermute | solution.py:521
  66.7 4.1 %collective-permute-start.12 = (bf16[2,12,8,128]{3,2,1,0:T(8,128)(2,1)S(1)}, bf16[2,12,8,128]{3,2,1,0:T(8,128)(2,1)S(1)}, u32[]{:S(2)}, u32[]{:S(2)}) collective-permute-start(bf16[2,12,8,128]{3,2,1,0:T(8,128)(2,1)S(1)} %surface_pair.1.refs_0_), channel_id=1, source_target_pairs={{0,16},{4,20},{8,24},{12,28},{16,0},{20,4},{24,8},{28,12},{1,17},{... | collective-permute-start | bytes 147464 | tf_op jit(solution)/shard_map/ppermute | solution.py:521
